TPU v7x, 32 devices: a whole 2x2x4 slice. The times are simulated.
32 devices in a mesh: node: 4 (over y, x), local: 4 (over z), edata: 2 (over core).
Axes of the slice: x: 2, y: 2, z: 4, core: 2. Of those that a mesh axis runs over, the one named last changes fastest.
Arguments:
- tokens: bfloat16 [8192, 2048], P(('node', 'local', 'edata')), may hold values from -6 to 6
- out_grad: bfloat16 [8192, 2048], P(('node', 'local', 'edata')), may hold values from -6 to 6
- expert_ids: int32 [8192, 8], P(('node', 'local', 'edata')), may hold values from 0 to 63, as said below
- gates: float32 [8192, 8], P(('node', 'local', 'edata')), may hold values from 0.05 to 0.45
- w_gate_up: bfloat16 [16, 2048, 1536], P(('node', 'local'), 'edata'), may hold values from -0.125 to 0.125
- w_down: bfloat16 [16, 2048, 768], P(('node', 'local'), 'edata'), may hold values from -0.21875 to 0.21875
Outputs:
- mixed: bfloat16 [8192, 2048], P(('node', 'local', 'edata'))
- token_grad: bfloat16 [8192, 2048], P(('node', 'local', 'edata'))
- gate_grad: float32 [8192, 8], P(('node', 'local', 'edata'))
- grad_gate_up: float32 [16, 2048, 1536], P(('node', 'local'), 'edata')
- grad_down: float32 [16, 2048, 768], P(('node', 'local'), 'edata')
Inputs may be any that keep to these rules, and one draw needn't show every extreme that they name: `expert_ids`: each row names 8 different experts. Expert e is held by node (e mod 16) // 4, and the experts of one row lie on at most 2 nodes.
All inputs are finite; a program needn't handle non-finite values.
Results may differ from a plain program's by a relative error of at most 0.0064.
Values may be sent and summed in bfloat16 or wider, within the bound.
No kernel may reach another device: no remote copies, remote signals or barrier semaphores. Data moves between devices by JAX's collectives and lax.ppermute only.
A program may use at most 128 MiB of HBM per device.

v0:
```python
import jax
import jax.numpy as jnp
from jax import lax
from jax.sharding import PartitionSpec as P

EXP_DEV = 4


def slot_tables(expert_ids, gates, groups, capacity):
    tok_rows = expert_ids.shape[0]
    numbers = jnp.arange(groups, dtype=jnp.int32)
    chosen = expert_ids[:, :, None] == numbers[None, None, :]
    routed = jnp.sum(chosen.astype(jnp.int32), axis=1)
    order_in = jnp.cumsum(routed, axis=0) - routed
    retained = (routed > 0) & (order_in < capacity)
    weight = jnp.sum(jnp.where(chosen, gates[:, :, None], jnp.zeros((), jnp.float32)), axis=1)
    weight = jnp.where(retained, weight, jnp.zeros((), jnp.float32))
    slot_ids = jnp.arange(capacity, dtype=jnp.int32)
    slot_hits = retained.T[:, None, :] & (order_in.T[:, None, :] == slot_ids[None, :, None])
    positions = jnp.arange(tok_rows, dtype=jnp.int32)
    slot_token = jnp.sum(jnp.where(slot_hits, positions[None, None, :], 0), axis=2)
    slot_live = jnp.any(slot_hits, axis=2)
    slot_weight = jnp.sum(
        jnp.where(slot_hits, weight.T[:, None, :], jnp.zeros((), jnp.float32)), axis=2
    )
    return (chosen, slot_token, slot_live, slot_weight)


def expert_rows(x_rows, dy_rows, w_in, w_out):
    hidden = w_out.shape[1]
    activation = jnp.dot(x_rows, w_in, preferred_element_type=jnp.float32)
    act_gate = activation[:, :hidden]
    act_up = activation[:, hidden:]
    sigmoid_gate = jax.nn.sigmoid(act_gate)
    swished = act_gate * sigmoid_gate
    inner_act = (swished * act_up).astype(jnp.bfloat16)
    expert_out = lax.dot_general(
        inner_act, w_out, (((1,), (1,)), ((), ())), preferred_element_type=jnp.float32
    ).astype(jnp.bfloat16)
    inner_grad = jnp.dot(dy_rows, w_out, preferred_element_type=jnp.float32)
    grad_gate_part = inner_grad * act_up * sigmoid_gate * (1.0 + act_gate * (1.0 - sigmoid_gate))
    grad_up_part = inner_grad * swished
    act_grad = jnp.concatenate([grad_gate_part, grad_up_part], axis=1).astype(jnp.bfloat16)
    copy_grad = lax.dot_general(
        act_grad, w_in, (((1,), (1,)), ((), ())), preferred_element_type=jnp.float32
    ).astype(jnp.bfloat16)
    return (inner_act, expert_out, act_grad, copy_grad)


def shards(tokens, out_grad, expert_ids, gates, w_gate_up, w_down):
    node_count = lax.axis_size("node")
    local_size = lax.axis_size("local")
    groups = node_count * local_size
    tok_rows, model_width = tokens.shape
    hidden = w_down.shape[2]
    capacity = tok_rows * expert_ids.shape[1] // (EXP_DEV * groups)
    row_count = groups * capacity
    chosen, slot_token, slot_live, slot_weight = slot_tables(expert_ids, gates, groups, capacity)
    flat_token = slot_token.reshape(-1)
    live_rows = slot_live.reshape(-1)[:, None]
    weight_flat = slot_weight.reshape(-1)
    x_send = jnp.where(live_rows, tokens[flat_token], jnp.zeros((), jnp.bfloat16))
    grad_rows = out_grad[flat_token]
    dy_send = (weight_flat[:, None] * grad_rows.astype(jnp.float32)).astype(jnp.bfloat16)
    whole_in, whole_out = (
        lax.all_gather(w_gate_up, "edata", axis=1, tiled=True),
        lax.all_gather(w_down, "edata", axis=1, tiled=True),
    )
    w_in = whole_in[0]
    w_out = whole_out[0]
    x_recv, dy_recv = (
        lax.all_to_all(
            x_send.reshape(groups, capacity, model_width),
            ("node", "local"),
            split_axis=0,
            concat_axis=0,
            tiled=True,
        ),
        lax.all_to_all(
            dy_send.reshape(groups, capacity, model_width),
            ("node", "local"),
            split_axis=0,
            concat_axis=0,
            tiled=True,
        ),
    )
    x_recv = x_recv.reshape(row_count, model_width)
    dy_recv = dy_recv.reshape(row_count, model_width)
    inner_act, expert_out, act_grad, copy_grad = expert_rows(x_recv, dy_recv, w_in, w_out)
    y_back, dx_back = (
        lax.all_to_all(
            expert_out.reshape(groups, capacity, model_width),
            ("node", "local"),
            split_axis=0,
            concat_axis=0,
            tiled=True,
        ),
        lax.all_to_all(
            copy_grad.reshape(groups, capacity, model_width),
            ("node", "local"),
            split_axis=0,
            concat_axis=0,
            tiled=True,
        ),
    )
    y_back = y_back.reshape(row_count, model_width)
    dx_back = dx_back.reshape(row_count, model_width)
    grad_first = lax.dot_general(
        x_recv, act_grad, (((0,), (0,)), ((), ())), preferred_element_type=jnp.float32
    )
    second = lax.dot_general(
        dy_recv, inner_act, (((0,), (0,)), ((), ())), preferred_element_type=jnp.float32
    )
    owned = lax.psum_scatter(
        jnp.concatenate([grad_first, second], axis=1).astype(jnp.bfloat16),
        "edata",
        scatter_dimension=0,
        tiled=True,
    ).astype(jnp.float32)
    grad_gate_up = owned[:, : 2 * hidden][None]
    grad_down = owned[:, 2 * hidden :][None]
    out_wide = y_back.astype(jnp.float32)
    mixed = (
        jnp.zeros((tok_rows, model_width), jnp.float32)
        .at[flat_token]
        .add(weight_flat[:, None] * out_wide)
    )
    token_grad = (
        jnp.zeros((tok_rows, model_width), jnp.float32)
        .at[flat_token]
        .add(jnp.where(live_rows, dx_back.astype(jnp.float32), jnp.zeros((), jnp.float32)))
    )
    slot_dots = jnp.where(
        slot_live.reshape(-1),
        jnp.sum(out_wide * grad_rows.astype(jnp.float32), axis=1),
        jnp.zeros((), jnp.float32),
    )
    expert_cols = jnp.broadcast_to(jnp.arange(groups, dtype=jnp.int32)[:, None], (groups, capacity))
    token_dots = (
        jnp.zeros((tok_rows, groups), jnp.float32)
        .at[slot_token, expert_cols]
        .add(slot_dots.reshape(groups, capacity))
    )
    gate_grad = jnp.sum(
        jnp.where(chosen, token_dots[:, None, :], jnp.zeros((), jnp.float32)), axis=2
    )
    return (
        mixed.astype(jnp.bfloat16),
        token_grad.astype(jnp.bfloat16),
        gate_grad,
        grad_gate_up,
        grad_down,
    )


def solution(mesh):
    in_specs = (
        P(("node", "local", "edata"), None),
        P(("node", "local", "edata"), None),
        P(("node", "local", "edata"), None),
        P(("node", "local", "edata"), None),
        P(("node", "local"), "edata", None),
        P(("node", "local"), "edata", None),
    )
    out_specs = (
        P(("node", "local", "edata"), None),
        P(("node", "local", "edata"), None),
        P(("node", "local", "edata"), None),
        P(("node", "local"), "edata", None),
        P(("node", "local"), "edata", None),
    )
    return jax.shard_map(shards, mesh=mesh, in_specs=in_specs, out_specs=out_specs, check_vma=False)
```

profile of v0, /device:TPU:0, one launch (start us, length us, event | category | flops | bytes accessed | tf_op | source)
XLA Modules:
  0.0 339.4 jit_solution(16488727330894904784)
XLA Ops:
  9.4 2.5 gather_fusion
  12.2 1.5 broadcast_select_fusion
  13.7 8.3 %all-to-all-start = ((bf16[16,32,2048]{2,1,0:T(8,128)(2,1)}), bf16[16,32,2048]{2,1,0:T(8,128)(2,1)S(1)}, u32[]{:S(2)}, u32[]{:S(2)}) async-start(bf16[16,32,2048]{2,1,0:T(8,128)(2,1)} %broadcast_select_fusion), calls=%async_computation | async-start | bytes 4194304 | tf_op jit(solution)/shard_map/all_to_all | solution.py:72
  22.8 49.2 %all-to-all-done = bf16[16,32,2048]{2,1,0:T(8,128)(2,1)S(1)} async-done(((bf16[16,32,2048]{2,1,0:T(8,128)(2,1)}), bf16[16,32,2048]{2,1,0:T(8,128)(2,1)S(1)}, u32[]{:S(2)}, u32[]{:S(2)}) %all-to-all-start) | async-done | bytes 2097184 | tf_op jit(solution)/shard_map/all_to_all | solution.py:72
  72.0 6.3 %fusion.2 = f32[512,1536]{1,0:T(8,128)S(1)} fusion(bf16[512,2048]{1,0:T(8,128)(2,1)S(1)} %bitcast.67, bf16[1,2048,1536]{2,1,0:T(8,128)(2,1)} %all-gather.3.cloned.1.call-done), kind=kOutput, calls=%fused_computation.10 | convolution fusion | flops 3221225472 | bytes 11534336 | tf_op jit(solution)/shard_map/dot_general | solution.py:31
  78.3 1.7 copy-done.5
  80.5 5.1 %fusion.11 = bf16[512,2048]{1,0:T(8,128)(2,1)} fusion(bf16[512,768]{1,0:T(8,128)(2,1)S(1)} %multiply_convert_fusion.2, bf16[1,2048,768]{2,1,0:T(8,128)(2,1)} %all-gather.5.cloned.1.call-done), kind=kOutput, calls=%fused_computation.25 | convolution fusion | flops 1611661312 | bytes 6029312 | tf_op jit(solution)/shard_map/dot_general | solution.py:37
  85.5 4.6 %all-to-all-start.1 = ((bf16[16,32,2048]{2,1,0:T(8,128)(2,1)}), bf16[16,32,2048]{2,1,0:T(8,128)(2,1)}, u32[]{:S(2)}, u32[]{:S(2)}) async-start(bf16[16,32,2048]{2,1,0:T(8,128)(2,1)} %bitcast.70), calls=%async_computation.1 | async-start | bytes 4194304 | tf_op jit(solution)/shard_map/all_to_all | solution.py:91
  90.2 3.3 gather_fusion.1
  93.5 46.0 %all-to-all-done.1 = bf16[16,32,2048]{2,1,0:T(8,128)(2,1)} async-done(((bf16[16,32,2048]{2,1,0:T(8,128)(2,1)}), bf16[16,32,2048]{2,1,0:T(8,128)(2,1)}, u32[]{:S(2)}, u32[]{:S(2)}) %all-to-all-start.1) | async-done | bytes 2097184 | tf_op jit(solution)/shard_map/all_to_all | solution.py:91
  139.6 2.8 fusion.5
  142.5 25.9 %scatter_fusion = f32[256,16]{0,1:T(8,128)S(1)} fusion(f32[256,16]{0,1:T(8,128)S(1)} %broadcast_in_dim.122, s32[512]{0:T(512)S(1)} %reshape.166, f32[512]{0:T(512)S(1)} %reshape.168), kind=kCustom, calls=%fused_computation.4 | custom fusion | flops 512 | bytes 10240 | tf_op jit(solution)/shard_map/scatter-add | solution.py:142
  169.6 52.7 %all_to_all.20 = bf16[16,32,2048]{2,1,0:T(8,128)(2,1)S(1)} all-to-all(bf16[16,32,2048]{2,1,0:T(8,128)(2,1)S(1)} %fusion.4), channel_id=1, replica_groups=mesh['node'=4,'local'=4,'edata'=2] {'node','local'}, dimensions={0} | all-to-all | bytes 4194304 | tf_op jit(solution)/shard_map/all_to_all | solution.py:79
  222.3 1.9 convolution_convert_fusion.1
  224.2 0.9 copy-done.11
  225.2 2.2 multiply_convert_fusion.1
  227.4 3.8 %convolution_convert_fusion = bf16[2048,1536]{0,1:T(8,128)(2,1)S(1)} fusion(bf16[512,2048]{1,0:T(8,128)(2,1)S(1)} %bitcast.68, bf16[512,768]{1,0:T(8,128)(2,1)S(1)} %get-tuple-element.25, bf16[512,768]{1,0:T(8,128)(2,1)S(1)} %get-tuple-element.24), kind=kOutput, calls=%fused_computation.6 | convolution fusion | flops 3227516928 | bytes 9961472 | tf_op jit(solution)/shard_map/dot_general | solution.py:108
  231.2 11.4 %pad_maximum_fusion = bf16[2048,2304]{0,1:T(8,128)(2,1)} fusion(bf16[2048,768]{0,1:T(8,128)(2,1)S(1)} %convolution_convert_fusion.1, bf16[2048,1536]{0,1:T(8,128)(2,1)S(1)} %convolution_convert_fusion), kind=kLoop, calls=%fused_computation.5 | loop fusion | flops 18874368 | bytes 18874368 | tf_op jit(solution)/shard_map/concatenate | solution.py:115
  242.6 7.4 %fusion.14 = bf16[512,2048]{1,0:T(8,128)(2,1)} fusion(bf16[1,2048,1536]{2,1,0:T(8,128)(2,1)} %all-gather.3.cloned.1.call-done, bf16[512,768]{1,0:T(8,128)(2,1)S(1)} %get-tuple-element.25, bf16[512,768]{1,0:T(8,128)(2,1)S(1)} %get-tuple-element.24), kind=kOutput, calls=%fused_computation.26 | convolution fusion | flops 3225419776 | bytes 9961472 | tf_op jit(solution)/shard_map/dot_general | solution.py:44
  250.0 4.0 %all-to-all-start.3 = ((bf16[16,32,2048]{2,1,0:T(8,128)(2,1)}), bf16[16,32,2048]{2,1,0:T(8,128)(2,1)S(1)}, u32[]{:S(2)}, u32[]{:S(2)}) async-start(bf16[16,32,2048]{2,1,0:T(8,128)(2,1)} %bitcast.69), calls=%async_computation.3 | async-start | bytes 4194304 | tf_op jit(solution)/shard_map/all_to_all | solution.py:98
  254.2 4.5 %bitcast_multiply_fusion = f32[512,2048]{1,0:T(8,128)} fusion(f32[512]{0:T(512)S(1)} %mul.44, bf16[16,32,2048]{2,1,0:T(8,128)(2,1)} %all-to-all-done.1), kind=kLoop, calls=%fused_computation.18 | loop fusion | flops 2097152 | bytes 6293504 | tf_op jit(solution)/shard_map/mul | solution.py:126
  258.6 9.8 %scatter_custom_fusion = f32[256,2048]{1,0:T(8,128)} fusion(s32[512]{0:T(512)S(1)} %bitcast.74, f32[512,2048]{1,0:T(8,128)} %bitcast_multiply_fusion, f32[]{:T(128)} %constant.7.clone.1), kind=kCustom, calls=%fused_computation.37 | custom fusion | flops 1048576 | bytes 2097664 | tf_op jit(solution)/shard_map/scatter-add | solution.py:126
  268.5 2.7 convert_element_type.56
  271.2 31.8 %all-to-all-done.3 = bf16[16,32,2048]{2,1,0:T(8,128)(2,1)S(1)} async-done(((bf16[16,32,2048]{2,1,0:T(8,128)(2,1)}), bf16[16,32,2048]{2,1,0:T(8,128)(2,1)S(1)}, u32[]{:S(2)}, u32[]{:S(2)}) %all-to-all-start.3) | async-done | bytes 2097184 | tf_op jit(solution)/shard_map/all_to_all | solution.py:98
  302.9 1.3 copy-done.4
  304.3 8.7 %scatter_custom_fusion.1 = f32[256,2048]{1,0:T(8,128)S(1)} fusion(s32[512]{0:T(512)S(1)} %bitcast.75, bf16[512,2048]{1,0:T(8,128)(2,1)} %bitcast.65, f32[]{:T(128)} %constant.7.clone.1, pred[512]{0:T(512)(128)(4,1)S(1)} %broadcast_in_dim.119), kind=kCustom, calls=%fused_computation.17 | custom fusion | flops 3145728 | bytes 4195840 | tf_op jit(solution)/shard_map/scatter-add | solution.py:131
  313.0 1.1 convert_element_type.63
  314.1 3.5 %convert_element_type.65 = f32[1024,2304]{0,1:T(8,128)S(1)} convert(bf16[1024,2304]{0,1:T(8,128)(2,1)} %reduce-scatter.2.cloned.1.call-done) | non-fusion elementwise | flops 2359296 | bytes 14155776 | tf_op jit(solution)/shard_map/convert_element_type | solution.py:119
  317.6 1.9 slice_bitcast_fusion.1
  319.5 3.2 slice_bitcast_fusion
  322.7 6.6 %copy.28 = f32[1,1024,1536]{2,1,0:T(8,128)} copy(f32[1,1024,1536]{1,2,0:T(8,128)} %slice_bitcast_fusion) | data formatting | bytes 12582912
  329.4 3.5 %copy.29 = f32[1,1024,768]{2,1,0:T(8,128)} copy(f32[1,1024,768]{1,2,0:T(8,128)} %slice_bitcast_fusion.1) | data formatting | bytes 6291456
  (54 shorter events, 5.4 us)
Async XLA Ops:
  7.2 2.2 copy-start
  7.2 0.8 copy-start.9
  7.2 64.8 %all-gather.3.cloned.1.call-start = ((), (), s32[]{:S(2)}) async-start(), calls=%async_computation.5 | async-start | bytes 9437184 | tf_op jit(solution)/shard_map/all_gather | solution.py:66
  13.7 58.3 %all-to-all-start = ((bf16[16,32,2048]{2,1,0:T(8,128)(2,1)}), bf16[16,32,2048]{2,1,0:T(8,128)(2,1)S(1)}, u32[]{:S(2)}, u32[]{:S(2)}) async-start(bf16[16,32,2048]{2,1,0:T(8,128)(2,1)} %broadcast_select_fusion), calls=%async_computation | async-start | bytes 4194304 | tf_op jit(solution)/shard_map/all_to_all | solution.py:72
  22.1 58.4 %all-gather.5.cloned.1.call-start = ((), (), s32[]{:S(2)}) async-start(), calls=%async_computation.6 | async-start | bytes 4718592 | tf_op jit(solution)/shard_map/all_gather | solution.py:67
  72.0 6.3 %copy-start.7 = (bf16[16,32,2048]{2,1,0:T(8,128)(2,1)}, bf16[16,32,2048]{2,1,0:T(8,128)(2,1)S(1)}, u32[]{:S(2)}) copy-start(bf16[16,32,2048]{2,1,0:T(8,128)(2,1)S(1)} %all-to-all-done) | copy-start | bytes 6291460
  78.3 1.7 copy-start.5
  85.5 4.7 %copy-start.2 = (bf16[256,2048]{1,0:T(8,128)(2,1)S(1)}, bf16[256,2048]{1,0:T(8,128)(2,1)}, u32[]{:S(2)}) copy-start(bf16[256,2048]{1,0:T(8,128)(2,1)} %param.7) | copy-start | bytes 3145732
  85.5 54.0 %all-to-all-start.1 = ((bf16[16,32,2048]{2,1,0:T(8,128)(2,1)}), bf16[16,32,2048]{2,1,0:T(8,128)(2,1)}, u32[]{:S(2)}, u32[]{:S(2)}) async-start(bf16[16,32,2048]{2,1,0:T(8,128)(2,1)} %bitcast.70), calls=%async_computation.1 | async-start | bytes 4194304 | tf_op jit(solution)/shard_map/all_to_all | solution.py:91
  90.1 224.0 %reduce-scatter.2.cloned.1.call-start = ((), (), s32[]{:S(2)}) async-start(), calls=%async_computation.7 | async-start | bytes 14155776 | tf_op jit(solution)/shard_map/reduce_scatter | solution.py:114
  142.5 25.9 %copy-start.10 = (f32[256,8]{0,1:T(8,128)S(1)}, f32[256,8]{0,1:T(8,128)}, u32[]{:S(2)}) copy-start(f32[256,8]{0,1:T(8,128)} %param.9) | copy-start | bytes 24580
  142.5 26.7 %copy-start.3 = (bf16[512,2048]{1,0:T(8,128)(2,1)S(1)}, bf16[512,2048]{1,0:T(8,128)(2,1)}, u32[]{:S(2)}) copy-start(bf16[512,2048]{1,0:T(8,128)(2,1)} %gather_fusion.1) | copy-start | bytes 6291460
  222.3 1.9 copy-start.6
  222.3 2.8 copy-start.11
  225.2 2.2 copy-start.8
  250.0 52.9 %all-to-all-start.3 = ((bf16[16,32,2048]{2,1,0:T(8,128)(2,1)}), bf16[16,32,2048]{2,1,0:T(8,128)(2,1)S(1)}, u32[]{:S(2)}, u32[]{:S(2)}) async-start(bf16[16,32,2048]{2,1,0:T(8,128)(2,1)} %bitcast.69), calls=%async_computation.3 | async-start | bytes 4194304 | tf_op jit(solution)/shard_map/all_to_all | solution.py:98
  302.9 1.3 copy-start.4
  322.7 10.2 %copy-start.1 = (bf16[256,2048]{1,0:T(8,128)(2,1)S(1)}, bf16[256,2048]{1,0:T(8,128)(2,1)}, u32[]{:S(2)}) copy-start(bf16[256,2048]{1,0:T(8,128)(2,1)} %param.6) | copy-start | bytes 3145732
Sparse Core Ops, SparseCore 0:
  9.6 19.4 all-gather.2
  30.6 13.2 all-gather.4
  242.7 14.9 reduce-scatter.1
where the time goes:
time: 340 us; the launch traced here: 339 us
  waiting for transfers between devices  128 us (38%)
  other arithmetic  75.1 us (22%)
  blocking collectives  52.7 us (16%)
  matrix products  26.6 us (8%)
  local copies, waits for them, and re-layouts  25.7 us (8%)
  starting transfers between devices  17 us (5%)
  between operations  14 us (4%)
    all_to_all x1, blocking collectives, shards(): lax.all_to_all(dy_send.reshape(groups, capacity, model_width), ('node', '...  52.7 us
    all_to_all x1, waiting for transfers between devices, shards(): lax.all_to_all(x_send.reshape(groups, capacity, model_width), ('node', 'l...  49.2 us
    all_to_all x1, waiting for transfers between devices, shards(): lax.all_to_all(expert_out.reshape(groups, capacity, model_width), ('node'...  46 us
    all_to_all x1, waiting for transfers between devices, shards(): lax.all_to_all(copy_grad.reshape(groups, capacity, model_width), ('node',...  31.8 us
    scatter-add x1, other arithmetic, shards(): token_dots = jnp.zeros((tok_rows, groups), jnp.float32).at[slot_token, ex...  25.9 us
    unnamed x26, local copies, waits for them, and re-layouts  14.2 us
    concatenate x1, other arithmetic, shards(): jnp.concatenate([grad_first, second], axis=1).astype(jnp.bfloat16)  11.4 us
    scatter-add x1, other arithmetic, shards(): mixed = jnp.zeros((tok_rows, model_width), jnp.float32).at[flat_token].ad...  9.84 us
  transfers between devices with their start and end apart: 6, of which 3 were waited for; matrix products, arithmetic and copies ran while one was open for 15% of the time, Pallas kernels for 0%

commit v1 on v0

v1 whole, which is shorter than its diff:
```python
import jax
import jax.numpy as jnp
from jax import lax
from jax.sharding import PartitionSpec as P

EXP_DEV = 4
BF = jnp.bfloat16
F32 = jnp.float32


def slot_tables(expert_ids, gates, groups, capacity):
    tok_rows = expert_ids.shape[0]
    ids_t = expert_ids.T
    numbers = jnp.arange(groups, dtype=jnp.int32)
    chosen = ids_t[None, :, :] == numbers[:, None, None]
    routed = jnp.any(chosen, axis=1)
    earlier = jnp.arange(tok_rows)[:, None] < jnp.arange(tok_rows)[None, :]
    order_in = jnp.dot(
        routed.astype(BF), earlier.astype(BF), preferred_element_type=F32
    ).astype(jnp.int32)
    weight = jnp.sum(jnp.where(chosen, gates.T[None, :, :], 0.0), axis=1)
    slot_ids = jnp.arange(capacity, dtype=jnp.int32)
    hits = routed[:, None, :] & (order_in[:, None, :] == slot_ids[None, :, None])
    slot_weight = jnp.sum(jnp.where(hits, weight[:, None, :], 0.0), axis=2)
    return chosen, hits.reshape(groups * capacity, tok_rows), slot_weight.reshape(-1)


def exchange(rows, groups):
    shaped = rows.reshape(groups, rows.shape[0] // groups, rows.shape[1])
    out = lax.all_to_all(shaped, ("node", "local"), split_axis=0, concat_axis=0, tiled=True)
    return out.reshape(rows.shape)


def shards(tokens, out_grad, expert_ids, gates, w_gate_up, w_down):
    groups = lax.axis_size("node") * lax.axis_size("local")
    tok_rows, model_width = tokens.shape
    hidden = w_down.shape[2]
    capacity = tok_rows * expert_ids.shape[1] // (EXP_DEV * groups)
    chosen, hits, slot_weight = slot_tables(expert_ids, gates, groups, capacity)
    pick = hits.astype(BF)
    x_send = jnp.dot(pick, tokens, preferred_element_type=F32).astype(BF)
    x_recv = exchange(x_send, groups)
    grad_rows = jnp.dot(pick, out_grad, preferred_element_type=F32)
    dy_send = (slot_weight[:, None] * grad_rows).astype(BF)
    dy_recv = exchange(dy_send, groups)
    w_in = lax.all_gather(w_gate_up, "edata", axis=1, tiled=True)[0]
    w_out = lax.all_gather(w_down, "edata", axis=1, tiled=True)[0]

    activation = jnp.dot(x_recv, w_in, preferred_element_type=F32)
    act_gate = activation[:, :hidden]
    act_up = activation[:, hidden:]
    sigmoid_gate = jax.nn.sigmoid(act_gate)
    swished = act_gate * sigmoid_gate
    inner_act = (swished * act_up).astype(BF)
    expert_out = lax.dot_general(
        inner_act, w_out, (((1,), (1,)), ((), ())), preferred_element_type=F32
    ).astype(BF)
    y_back = exchange(expert_out, groups)

    inner_grad = jnp.dot(dy_recv, w_out, preferred_element_type=F32)
    grad_gate_part = inner_grad * act_up * sigmoid_gate * (1.0 + act_gate * (1.0 - sigmoid_gate))
    grad_up_part = inner_grad * swished
    act_grad = jnp.concatenate([grad_gate_part, grad_up_part], axis=1).astype(BF)
    copy_grad = lax.dot_general(
        act_grad, w_in, (((1,), (1,)), ((), ())), preferred_element_type=F32
    ).astype(BF)
    dx_back = exchange(copy_grad, groups)

    part_down = lax.dot_general(
        dy_recv, inner_act, (((0,), (0,)), ((), ())), preferred_element_type=F32
    ).astype(BF)
    grad_down = lax.psum_scatter(part_down, "edata", scatter_dimension=0, tiled=True).astype(F32)
    part_in = lax.dot_general(
        x_recv, act_grad, (((0,), (0,)), ((), ())), preferred_element_type=F32
    ).astype(BF)
    grad_in = lax.psum_scatter(part_in, "edata", scatter_dimension=0, tiled=True).astype(F32)

    spread = jnp.where(hits, slot_weight[:, None], 0.0)
    high = spread.astype(BF)
    rest = spread - high.astype(F32)
    middle = rest.astype(BF)
    low = (rest - middle.astype(F32)).astype(BF)
    over_slots = (((0,), (0,)), ((), ()))
    mixed = (
        lax.dot_general(high, y_back, over_slots, preferred_element_type=F32)
        + lax.dot_general(middle, y_back, over_slots, preferred_element_type=F32)
        + lax.dot_general(low, y_back, over_slots, preferred_element_type=F32)
    )
    slot_dots = jnp.sum(y_back.astype(F32) * grad_rows, axis=1)
    token_dots = jnp.sum(
        jnp.where(hits, slot_dots[:, None], 0.0).reshape(groups, capacity, tok_rows), axis=1
    )
    gate_grad = jnp.sum(jnp.where(chosen, token_dots[:, None, :], 0.0), axis=0).T
    token_grad = lax.dot_general(pick, dx_back, over_slots, preferred_element_type=F32)
    return (mixed.astype(BF), token_grad.astype(BF), gate_grad, grad_in[None], grad_down[None])


def solution(mesh):
    rows = P(("node", "local", "edata"), None)
    weights = P(("node", "local"), "edata", None)
    return jax.shard_map(
        shards,
        mesh=mesh,
        in_specs=(rows, rows, rows, rows, weights, weights),
        out_specs=(rows, rows, rows, weights, weights),
        check_vma=False,
    )
```

time: 340 us -> 293 us (0.86)
  other arithmetic: 75.1 us -> 13.9 us
  local copies, waits for them, and re-layouts: 25.7 us -> 4.24 us
  matrix products: 26.6 us -> 46.4 us
  waiting for transfers between devices: 128 us -> 144 us
    scatter-add x3 -> x0, other arithmetic: 44.4 us -> none  [the longest x1 25.9 us: shards(): token_dots = jnp.zeros((tok_rows, groups), jnp.float32).at[slot_token, ex...]
    dot_general x4 -> x11, matrix products: 20.9 us -> 37.3 us  [the longest x1 7.81 us: shards(): lax.dot_general(act_grad, w_in, (((1,), (1,)), ((), ())), preferred_eleme...]
    all_to_all x3, waiting for transfers between devices: 127 us -> 143 us  [exchange(): lax.all_to_all(shaped, ('node', 'local'), split_axis=0, concat_axis=0, ti...]
    concatenate x2 -> x0, other arithmetic: 11.4 us -> none  [the longest x1 11.4 us: shards(): jnp.concatenate([grad_first, second], axis=1).astype(jnp.bfloat16)]
    unnamed x26 -> x22, local copies, waits for them, and re-layouts: 14.2 us -> 4 us
    broadcast_in_dim x0 -> x2, other arithmetic: none -> 8.86 us  [the longest x1 5.55 us: shards(): grad_in[None]]
    gather x2 -> x0, local copies, waits for them, and re-layouts: 5.74 us -> none  [the longest x1 3.28 us: shards(): grad_rows = out_grad[flat_token]]
    broadcast_in_dim x4 -> x2, local copies, waits for them, and re-layouts: 5.24 us -> 0.16 us  [the longest x1 0.08 us: shards(): jnp.where(hits, slot_dots[:, None], 0.0).reshape(groups, capacity, tok_rows)]
  transfers between devices with their start and end apart: 6 -> 7, of which waited for: 3 -> 3; matrix products, arithmetic and copies ran while one was open for 15% -> 14% of each run, Pallas kernels for 0% -> 0%
where the time goes in v1:
time: 293 us
  waiting for transfers between devices  144 us (49%)
  blocking collectives  52.8 us (18%)
  matrix products  46.4 us (16%)
  starting transfers between devices  17 us (6%)
  other arithmetic  13.9 us (5%)
  between operations  13.9 us (5%)
  local copies, waits for them, and re-layouts  4.24 us (1%)
    all_to_all x3, waiting for transfers between devices, exchange(): lax.all_to_all(shaped, ('node', 'local'), split_axis=0, concat_axis=0, ti...  143 us
    all_to_all x1, blocking collectives, exchange(): lax.all_to_all(shaped, ('node', 'local'), split_axis=0, concat_axis=0, ti...  52.8 us
    all_to_all x3, starting transfers between devices, exchange(): lax.all_to_all(shaped, ('node', 'local'), split_axis=0, concat_axis=0, ti...  16.6 us
    dot_general x1, matrix products, shards(): lax.dot_general(act_grad, w_in, (((1,), (1,)), ((), ())), preferred_eleme...  7.81 us
    dot_general x1, matrix products, shards(): activation = jnp.dot(x_recv, w_in, preferred_element_type=F32)  6.26 us
    dot_general x1, matrix products, shards(): inner_grad = jnp.dot(dy_recv, w_out, preferred_element_type=F32)  6.24 us
  transfers between devices with their start and end apart: 7, of which 3 were waited for; matrix products, arithmetic and copies ran while one was open for 14% of the time, Pallas kernels for 0%

profile of v1, /device:TPU:0, one launch (start us, length us, event | category | flops | bytes accessed | tf_op | source)
XLA Modules:
  0.0 292.8 jit_solution(9444704985090784406)
XLA Ops:
  7.2 0.7 all-gather.3.cloned.1.call-update
  8.2 0.2 fusion.23
  8.5 2.0 convolution_convert_fusion.2
  10.5 8.3 %all-to-all-start = ((bf16[16,32,2048]{2,1,0:T(8,128)(2,1)}), bf16[16,32,2048]{2,1,0:T(8,128)(2,1)S(1)}, u32[]{:S(2)}, u32[]{:S(2)}) async-start(bf16[16,32,2048]{2,1,0:T(8,128)(2,1)} %bitcast.4), calls=%async_computation | async-start | bytes 4194304 | tf_op jit(solution)/shard_map/all_to_all | solution.py:30
  18.9 0.7 all-gather.5.cloned.1.call-update
  19.6 49.2 %all-to-all-done = bf16[16,32,2048]{2,1,0:T(8,128)(2,1)S(1)} async-done(((bf16[16,32,2048]{2,1,0:T(8,128)(2,1)}), bf16[16,32,2048]{2,1,0:T(8,128)(2,1)S(1)}, u32[]{:S(2)}, u32[]{:S(2)}) %all-to-all-start) | async-done | bytes 2097184 | tf_op jit(solution)/shard_map/all_to_all | solution.py:30
  68.8 6.3 %fusion.2 = f32[512,1536]{1,0:T(8,128)S(1)} fusion(bf16[512,2048]{1,0:T(8,128)(2,1)S(1)} %bitcast.72, bf16[1,2048,1536]{2,1,0:T(8,128)(2,1)} %all-gather.3.cloned.1.call-done), kind=kOutput, calls=%fused_computation.3 | convolution fusion | flops 3221225472 | bytes 11534336 | tf_op jit(solution)/shard_map/dot_general | solution.py:49
  75.1 1.7 copy-done.2
  76.8 1.4 multiply_convert_fusion.3
  78.1 5.3 %fusion.9 = bf16[512,2048]{1,0:T(8,128)(2,1)} fusion(bf16[512,768]{1,0:T(8,128)(2,1)} %multiply_convert_fusion.3, bf16[1,2048,768]{2,1,0:T(8,128)(2,1)} %all-gather.5.cloned.1.call-done), kind=kOutput, calls=%fused_computation.15 | convolution fusion | flops 1611661312 | bytes 6029312 | tf_op jit(solution)/shard_map/dot_general | solution.py:55
  83.4 3.9 %all-to-all-start.1 = ((bf16[16,32,2048]{2,1,0:T(8,128)(2,1)}), bf16[16,32,2048]{2,1,0:T(8,128)(2,1)S(1)}, u32[]{:S(2)}, u32[]{:S(2)}) async-start(bf16[16,32,2048]{2,1,0:T(8,128)(2,1)} %bitcast.77), calls=%async_computation.1 | async-start | bytes 4194304 | tf_op jit(solution)/shard_map/all_to_all | solution.py:30
  87.4 49.3 %all-to-all-done.1 = bf16[16,32,2048]{2,1,0:T(8,128)(2,1)S(1)} async-done(((bf16[16,32,2048]{2,1,0:T(8,128)(2,1)}), bf16[16,32,2048]{2,1,0:T(8,128)(2,1)S(1)}, u32[]{:S(2)}, u32[]{:S(2)}) %all-to-all-start.1) | async-done | bytes 2097184 | tf_op jit(solution)/shard_map/all_to_all | solution.py:30
  136.7 2.7 fusion.4
  139.5 0.3 select_reduce_fusion
  139.9 2.5 multiply_convert_fusion
  142.4 52.8 %all_to_all.20 = bf16[16,32,2048]{2,1,0:T(8,128)(2,1)S(1)} all-to-all(bf16[16,32,2048]{2,1,0:T(8,128)(2,1)S(1)} %bitcast.71), channel_id=1, replica_groups=mesh['node'=4,'local'=4,'edata'=2] {'node','local'}, dimensions={0} | all-to-all | bytes 4194304 | tf_op jit(solution)/shard_map/all_to_all | solution.py:30
  195.2 1.3 copy-done.5
  196.5 3.6 %convolution_convert_fusion.1 = bf16[2048,768]{1,0:T(8,128)(2,1)} fusion(bf16[512,2048]{1,0:T(8,128)(2,1)S(1)} %bitcast.74, bf16[512,768]{1,0:T(8,128)(2,1)S(1)} %copy-done.7), kind=kOutput, calls=%fused_computation.8 | convolution fusion | flops 1612185600 | bytes 6029312 | tf_op jit(solution)/shard_map/dot_general | solution.py:69
  200.1 0.2 reduce-scatter.3.cloned.1.call-start
  200.4 6.2 %multiply_convert_fusion.2 = (bf16[512,768]{1,0:T(8,128)(2,1)S(1)}, bf16[512,768]{1,0:T(8,128)(2,1)S(1)}) fusion(f32[512,1536]{1,0:T(8,128)} %copy-done.2, bf16[512,2048]{1,0:T(8,128)(2,1)} %bitcast.75, bf16[1,2048,768]{2,1,0:T(8,128)(2,1)} %all-gather.5.cloned.1.call-done), kind=kOutput, calls=%fused_computation.28 | convolution fusion | flops 1615724544 | bytes 9961472 | tf_op jit(solution)/shard_map/dot_general | solution.py:60
  206.6 0.9 copy-done.10
  207.5 5.5 %convolution_convert_fusion = bf16[2048,1536]{1,0:T(8,128)(2,1)} fusion(bf16[512,2048]{1,0:T(8,128)(2,1)S(1)} %bitcast.73, bf16[512,768]{1,0:T(8,128)(2,1)S(1)} %get-tuple-element.8, bf16[512,768]{1,0:T(8,128)(2,1)S(1)} %get-tuple-element.7), kind=kOutput, calls=%fused_computation | convolution fusion | flops 3227516928 | bytes 9961472 | tf_op jit(solution)/shard_map/dot_general | solution.py:73
  213.0 7.8 %fusion.12 = bf16[512,2048]{1,0:T(8,128)(2,1)} fusion(bf16[1,2048,1536]{2,1,0:T(8,128)(2,1)} %all-gather.3.cloned.1.call-done, bf16[512,768]{1,0:T(8,128)(2,1)} %copy-done.10, bf16[512,768]{1,0:T(8,128)(2,1)S(1)} %get-tuple-element.7), kind=kOutput, calls=%fused_computation.16 | convolution fusion | flops 3225419776 | bytes 9961472 | tf_op jit(solution)/shard_map/dot_general | solution.py:64
  220.8 4.5 %all-to-all-start.3 = ((bf16[16,32,2048]{2,1,0:T(8,128)(2,1)}), bf16[16,32,2048]{2,1,0:T(8,128)(2,1)}, u32[]{:S(2)}, u32[]{:S(2)}) async-start(bf16[16,32,2048]{2,1,0:T(8,128)(2,1)} %bitcast.76), calls=%async_computation.3 | async-start | bytes 4194304 | tf_op jit(solution)/shard_map/all_to_all | solution.py:30
  225.3 0.6 select_reduce_fusion.2
  225.9 0.8 convolution_bitcast_fusion.2
  226.8 0.8 convolution_bitcast_fusion.1
  227.6 1.8 fusion.17
  229.5 44.6 %all-to-all-done.3 = bf16[16,32,2048]{2,1,0:T(8,128)(2,1)} async-done(((bf16[16,32,2048]{2,1,0:T(8,128)(2,1)}), bf16[16,32,2048]{2,1,0:T(8,128)(2,1)}, u32[]{:S(2)}, u32[]{:S(2)}) %all-to-all-start.3) | async-done | bytes 2097184 | tf_op jit(solution)/shard_map/all_to_all | solution.py:30
  274.0 3.3 %fusion.18 = bf16[256,2048]{1,0:T(8,128)(2,1)} fusion(bf16[16,32,2048]{2,1,0:T(8,128)(2,1)} %all-to-all-done.3, s32[16,256]{1,0:T(8,128)S(1)} %convolution_convert_fusion.3, pred[16,256]{1,0:T(8,128)(4,1)S(1)} %fusion.36), kind=kOutput, calls=%fused_computation.24 | convolution fusion | flops 537657344 | bytes 3166208 | tf_op jit(solution)/shard_map/dot_general | solution.py:94
  277.4 3.3 %bitcast_convert_fusion.1 = f32[1,1024,768]{2,1,0:T(8,128)} fusion(bf16[1024,768]{1,0:T(8,128)(2,1)} %reduce-scatter.5.cloned.1.call-done), kind=kLoop, calls=%fused_computation.26 | loop fusion | flops 786432 | bytes 4718592 | tf_op jit(solution)/shard_map/broadcast_in_dim | solution.py:95
  280.7 5.6 %bitcast_convert_fusion = f32[1,1024,1536]{2,1,0:T(8,128)} fusion(bf16[1024,1536]{1,0:T(8,128)(2,1)} %reduce-scatter.3.cloned.1.call-done), kind=kLoop, calls=%fused_computation.9 | loop fusion | flops 1572864 | bytes 9437184 | tf_op jit(solution)/shard_map/broadcast_in_dim | solution.py:95
  (35 shorter events, 0.8 us)
Async XLA Ops:
  7.2 129.5 %copy-start = (bf16[256,2048]{1,0:T(8,128)(2,1)S(1)}, bf16[256,2048]{1,0:T(8,128)(2,1)}, u32[]{:S(2)}) copy-start(bf16[256,2048]{1,0:T(8,128)(2,1)} %param.7) | copy-start | bytes 3145732
  7.2 0.8 copy-start.8
  7.2 1.3 copy-start.6
  7.2 61.6 %all-gather.3.cloned.1.call-start = ((), (), s32[]{:S(2)}) async-start(), calls=%async_computation.6 | async-start | bytes 9437184 | tf_op jit(solution)/shard_map/all_gather | solution.py:46
  10.5 58.3 %all-to-all-start = ((bf16[16,32,2048]{2,1,0:T(8,128)(2,1)}), bf16[16,32,2048]{2,1,0:T(8,128)(2,1)S(1)}, u32[]{:S(2)}, u32[]{:S(2)}) async-start(bf16[16,32,2048]{2,1,0:T(8,128)(2,1)} %bitcast.4), calls=%async_computation | async-start | bytes 4194304 | tf_op jit(solution)/shard_map/all_to_all | solution.py:30
  18.9 59.2 %all-gather.5.cloned.1.call-start = ((), (), s32[]{:S(2)}) async-start(), calls=%async_computation.7 | async-start | bytes 4718592 | tf_op jit(solution)/shard_map/all_gather | solution.py:47
  68.8 6.3 %copy-start.3 = (bf16[16,32,2048]{2,1,0:T(8,128)(2,1)}, bf16[16,32,2048]{2,1,0:T(8,128)(2,1)S(1)}, u32[]{:S(2)}) copy-start(bf16[16,32,2048]{2,1,0:T(8,128)(2,1)S(1)} %all-to-all-done) | copy-start | bytes 6291460
  75.1 1.7 copy-start.2
  83.4 3.9 %copy-start.9 = (f32[256,8]{0,1:T(8,128)S(1)}, f32[256,8]{0,1:T(8,128)}, u32[]{:S(2)}) copy-start(f32[256,8]{0,1:T(8,128)} %param.9) | copy-start | bytes 24580
  83.4 53.3 %all-to-all-start.1 = ((bf16[16,32,2048]{2,1,0:T(8,128)(2,1)}), bf16[16,32,2048]{2,1,0:T(8,128)(2,1)S(1)}, u32[]{:S(2)}, u32[]{:S(2)}) async-start(bf16[16,32,2048]{2,1,0:T(8,128)(2,1)} %bitcast.77), calls=%async_computation.1 | async-start | bytes 4194304 | tf_op jit(solution)/shard_map/all_to_all | solution.py:30
  87.3 190.1 %reduce-scatter.5.cloned.1.call-start = ((), (), s32[]{:S(2)}) async-start(), calls=%async_computation.9 | async-start | bytes 4718592 | tf_op jit(solution)/shard_map/reduce_scatter | solution.py:72
  142.4 54.1 %copy-start.7 = (bf16[512,768]{1,0:T(8,128)(2,1)S(1)}, bf16[512,768]{1,0:T(8,128)(2,1)}, u32[]{:S(2)}) copy-start(bf16[512,768]{1,0:T(8,128)(2,1)} %multiply_convert_fusion.3) | copy-start | bytes 2359300
  195.2 1.3 copy-start.5
  200.1 80.5 %reduce-scatter.3.cloned.1.call-start = ((), (), s32[]{:S(2)}) async-start(), calls=%async_computation.8 | async-start | bytes 9437184 | tf_op jit(solution)/shard_map/reduce_scatter | solution.py:76
  200.4 7.1 %copy-start.4 = (bf16[16,32,2048]{2,1,0:T(8,128)(2,1)S(1)}, bf16[16,32,2048]{2,1,0:T(8,128)(2,1)}, u32[]{:S(2)}) copy-start(bf16[16,32,2048]{2,1,0:T(8,128)(2,1)} %copy-done.3) | copy-start | bytes 6291460
  206.6 0.9 copy-start.10
  220.8 53.2 %all-to-all-start.3 = ((bf16[16,32,2048]{2,1,0:T(8,128)(2,1)}), bf16[16,32,2048]{2,1,0:T(8,128)(2,1)}, u32[]{:S(2)}, u32[]{:S(2)}) async-start(bf16[16,32,2048]{2,1,0:T(8,128)(2,1)} %bitcast.76), calls=%async_computation.3 | async-start | bytes 4194304 | tf_op jit(solution)/shard_map/all_to_all | solution.py:30
  280.7 5.6 %copy-start.1 = (bf16[256,2048]{1,0:T(8,128)(2,1)S(1)}, bf16[256,2048]{1,0:T(8,128)(2,1)}, u32[]{:S(2)}) copy-start(bf16[256,2048]{1,0:T(8,128)(2,1)} %param.7) | copy-start | bytes 3145732
Sparse Core Ops, SparseCore 0:
  9.6 19.4 all-gather.2
  30.6 13.2 all-gather.4
  200.2 8.1 reduce-scatter.4
  213.2 13.7 reduce-scatter.2

commit v2 on v1

--- a/solution.py
+++ b/solution.py
@@ -55,6 +55,7 @@
     expert_out = lax.dot_general(
         inner_act, w_out, (((1,), (1,)), ((), ())), preferred_element_type=F32
     ).astype(BF)
+    expert_out, dy_recv = lax.optimization_barrier((expert_out, dy_recv))
     y_back = exchange(expert_out, groups)
 
     inner_grad = jnp.dot(dy_recv, w_out, preferred_element_type=F32)
@@ -64,6 +65,7 @@
     copy_grad = lax.dot_general(
         act_grad, w_in, (((1,), (1,)), ((), ())), preferred_element_type=F32
     ).astype(BF)
+    copy_grad, y_back = lax.optimization_barrier((copy_grad, y_back))
     dx_back = exchange(copy_grad, groups)
 
     part_down = lax.dot_general(
@@ -76,10 +78,10 @@
     grad_in = lax.psum_scatter(part_in, "edata", scatter_dimension=0, tiled=True).astype(F32)
 
     spread = jnp.where(hits, slot_weight[:, None], 0.0)
-    high = spread.astype(BF)
-    rest = spread - high.astype(F32)
-    middle = rest.astype(BF)
-    low = (rest - middle.astype(F32)).astype(BF)
+    high = lax.reduce_precision(spread, 8, 7)
+    middle = lax.reduce_precision(spread - high, 8, 7)
+    low = spread - high - middle
+    high, middle, low = high.astype(BF), middle.astype(BF), low.astype(BF)
     over_slots = (((0,), (0,)), ((), ()))
     mixed = (
         lax.dot_general(high, y_back, over_slots, preferred_element_type=F32)
@@ -91,6 +93,7 @@
         jnp.where(hits, slot_dots[:, None], 0.0).reshape(groups, capacity, tok_rows), axis=1
     )
     gate_grad = jnp.sum(jnp.where(chosen, token_dots[:, None, :], 0.0), axis=0).T
+    dx_back, grad_in, grad_down = lax.optimization_barrier((dx_back, grad_in, grad_down))
     token_grad = lax.dot_general(pick, dx_back, over_slots, preferred_element_type=F32)
     return (mixed.astype(BF), token_grad.astype(BF), gate_grad, grad_in[None], grad_down[None])
 

time: 293 us -> 257 us (0.88)
  blocking collectives: 52.8 us -> 0 us
  waiting for transfers between devices: 144 us -> 157 us
  starting transfers between devices: 17 us -> 21.4 us
    all_to_all x1 -> x0, blocking collectives: 52.8 us -> none  [exchange(): lax.all_to_all(shaped, ('node', 'local'), split_axis=0, concat_axis=0, ti...]
    broadcast_in_dim x2 -> x0, other arithmetic: 8.86 us -> none  [the longest x1 5.55 us: shards(): grad_in[None]]
    all_gather x1, waiting for transfers between devices: 0.01 us -> 7.26 us  [shards(): w_out = lax.all_gather(w_down, 'edata', axis=1, tiled=True)[0]]
    convert_element_type x1 -> x2, other arithmetic: 2.47 us -> 8.86 us  [the longest x1 5.55 us: shards(): lax.psum_scatter(part_in, 'edata', scatter_dimension=0, tiled=True)]
    all_to_all x3 -> x4, waiting for transfers between devices: 143 us -> 148 us  [exchange(): lax.all_to_all(shaped, ('node', 'local'), split_axis=0, concat_axis=0, ti...]
    all_to_all x3 -> x4, starting transfers between devices: 16.6 us -> 21.2 us  [exchange(): lax.all_to_all(shaped, ('node', 'local'), split_axis=0, concat_axis=0, ti...]
  transfers between devices with their start and end apart: 7 -> 8, of which waited for: 3 -> 5; matrix products, arithmetic and copies ran while one was open for 14% -> 21% of each run, Pallas kernels for 0% -> 0%
where the time goes in v2:
time: 257 us
  waiting for transfers between devices  157 us (61%)
  matrix products  48.8 us (19%)
  starting transfers between devices  21.4 us (8%)
  between operations  13.9 us (5%)
  other arithmetic  13.3 us (5%)
  local copies, waits for them, and re-layouts  2.91 us (1%)
    all_to_all x4, waiting for transfers between devices, exchange(): lax.all_to_all(shaped, ('node', 'local'), split_axis=0, concat_axis=0, ti...  148 us
    all_to_all x4, starting transfers between devices, exchange(): lax.all_to_all(shaped, ('node', 'local'), split_axis=0, concat_axis=0, ti...  21.2 us
    dot_general x1, matrix products, shards(): lax.dot_general(act_grad, w_in, (((1,), (1,)), ((), ())), preferred_eleme...  8.81 us
    all_gather x1, waiting for transfers between devices, shards(): w_out = lax.all_gather(w_down, 'edata', axis=1, tiled=True)[0]  7.26 us
    dot_general x1, matrix products, shards(): inner_grad = jnp.dot(dy_recv, w_out, preferred_element_type=F32)  5.82 us
    convert_element_type x1, other arithmetic, shards(): lax.psum_scatter(part_in, 'edata', scatter_dimension=0, tiled=True)  5.55 us
    dot_general x1, matrix products, shards(): activation = jnp.dot(x_recv, w_in, preferred_element_type=F32)  5.5 us
    dot_general x1, matrix products, shards(): lax.dot_general(x_recv, act_grad, (((0,), (0,)), ((), ())), preferred_ele...  5.47 us
  transfers between devices with their start and end apart: 8, of which 5 were waited for; matrix products, arithmetic and copies ran while one was open for 21% of the time, Pallas kernels for 0%

profile of v2, /device:TPU:0, one launch (start us, length us, event | category | flops | bytes accessed | tf_op | source)
XLA Modules:
  0.0 256.8 jit_solution(5871562692754874069)
XLA Ops:
  7.2 0.7 all-gather.3.cloned.1.call-update
  8.5 2.0 convolution_convert_fusion.2
  10.5 8.4 %all-to-all-start = ((bf16[16,32,2048]{2,1,0:T(8,128)(2,1)}), bf16[16,32,2048]{2,1,0:T(8,128)(2,1)S(1)}, u32[]{:S(2)}, u32[]{:S(2)}) async-start(bf16[16,32,2048]{2,1,0:T(8,128)(2,1)} %bitcast.4), calls=%async_computation | async-start | bytes 4194304 | tf_op jit(solution)/shard_map/all_to_all | solution.py:30
  19.1 0.2 select_reduce_fusion.1
  19.3 3.9 %multiply_convert_fusion = (bf16[512,2048]{1,0:T(8,128)(2,1)}, f32[512,2048]{1,0:T(8,128)}) fusion(f32[512]{0:T(512)S(1)} %broadcast_in_dim.77, pred[512,256]{1,0:T(32,128)(4,1)S(1)} %fusion.18, bf16[256,2048]{1,0:T(8,128)(2,1)S(1)} %copy-done), kind=kOutput, calls=%fused_computation.6 | convolution fusion | flops 538968064 | bytes 7473152 | tf_op jit(solution)/shard_map/dot_general | solution.py:43
  23.3 45.7 %all-to-all-done = bf16[16,32,2048]{2,1,0:T(8,128)(2,1)S(1)} async-done(((bf16[16,32,2048]{2,1,0:T(8,128)(2,1)}), bf16[16,32,2048]{2,1,0:T(8,128)(2,1)S(1)}, u32[]{:S(2)}, u32[]{:S(2)}) %all-to-all-start) | async-done | bytes 2097184 | tf_op jit(solution)/shard_map/all_to_all | solution.py:30
  68.9 4.4 %all-to-all-start.1 = ((bf16[16,32,2048]{2,1,0:T(8,128)(2,1)}), bf16[16,32,2048]{2,1,0:T(8,128)(2,1)}, u32[]{:S(2)}, u32[]{:S(2)}) async-start(bf16[16,32,2048]{2,1,0:T(8,128)(2,1)} %bitcast.8), calls=%async_computation.1 | async-start | bytes 4194304 | tf_op jit(solution)/shard_map/all_to_all | solution.py:30
  73.4 0.7 all-gather.5.cloned.1.call-update
  74.2 5.5 %fusion.2 = f32[512,1536]{1,0:T(8,128)S(1)} fusion(bf16[512,2048]{1,0:T(8,128)(2,1)S(1)} %bitcast.57, bf16[1,2048,1536]{2,1,0:T(8,128)(2,1)} %all-gather.3.cloned.1.call-done), kind=kOutput, calls=%fused_computation.3 | convolution fusion | flops 3221225472 | bytes 11534336 | tf_op jit(solution)/shard_map/dot_general | solution.py:49
  79.7 1.7 copy-done.2
  81.4 0.5 multiply_convert_fusion.3
  81.9 7.3 %all-gather.5.cloned.1.call-done = bf16[1,2048,768]{2,1,0:T(8,128)(2,1)} async-done(((bf16[1,1024,768]{2,1,0:T(8,128)(2,1)}), bf16[1,2048,768]{2,1,0:T(8,128)(2,1)}) %all-gather.5.cloned.1.call-update) | async-done | bytes 3145744 | tf_op jit(solution)/shard_map/all_gather | solution.py:47
  89.1 5.1 %fusion.8 = bf16[512,2048]{1,0:T(8,128)(2,1)} fusion(bf16[512,768]{1,0:T(8,128)(2,1)S(1)} %multiply_convert_fusion.3, bf16[1,2048,768]{2,1,0:T(8,128)(2,1)} %all-gather.5.cloned.1.call-done), kind=kOutput, calls=%fused_computation.13 | convolution fusion | flops 1611661312 | bytes 6029312 | tf_op jit(solution)/shard_map/dot_general | solution.py:55
  94.2 28.7 %all-to-all-done.1 = bf16[16,32,2048]{2,1,0:T(8,128)(2,1)} async-done(((bf16[16,32,2048]{2,1,0:T(8,128)(2,1)}), bf16[16,32,2048]{2,1,0:T(8,128)(2,1)}, u32[]{:S(2)}, u32[]{:S(2)}) %all-to-all-start.1) | async-done | bytes 2097184 | tf_op jit(solution)/shard_map/all_to_all | solution.py:30
  122.8 5.2 %convolution_convert_fusion.1 = bf16[2048,768]{1,0:T(8,128)(2,1)} fusion(bf16[512,2048]{1,0:T(8,128)(2,1)} %bitcast.9, bf16[512,768]{1,0:T(8,128)(2,1)S(1)} %multiply_convert_fusion.3), kind=kOutput, calls=%fused_computation.7 | convolution fusion | flops 1612185600 | bytes 6029312 | tf_op jit(solution)/shard_map/dot_general | solution.py:71
  128.1 5.8 %multiply_convert_fusion.2 = (bf16[512,768]{1,0:T(8,128)(2,1)S(1)}, bf16[512,768]{1,0:T(8,128)(2,1)S(1)}) fusion(f32[512,1536]{1,0:T(8,128)} %copy-done.2, bf16[512,2048]{1,0:T(8,128)(2,1)} %bitcast.9, bf16[1,2048,768]{2,1,0:T(8,128)(2,1)} %all-gather.5.cloned.1.call-done), kind=kOutput, calls=%fused_computation.21 | convolution fusion | flops 1615724544 | bytes 9961472 | tf_op jit(solution)/shard_map/dot_general | solution.py:61
  133.9 0.9 copy-done.6
  134.8 5.5 %convolution_convert_fusion = bf16[2048,1536]{1,0:T(8,128)(2,1)} fusion(bf16[512,2048]{1,0:T(8,128)(2,1)S(1)} %bitcast.58, bf16[512,768]{1,0:T(8,128)(2,1)S(1)} %get-tuple-element.20, bf16[512,768]{1,0:T(8,128)(2,1)S(1)} %get-tuple-element.19), kind=kOutput, calls=%fused_computation | convolution fusion | flops 3227516928 | bytes 9961472 | tf_op jit(solution)/shard_map/dot_general | solution.py:75
  140.3 3.9 %all-to-all-start.2 = ((bf16[16,32,2048]{2,1,0:T(8,128)(2,1)}), bf16[16,32,2048]{2,1,0:T(8,128)(2,1)S(1)}, u32[]{:S(2)}, u32[]{:S(2)}) async-start(bf16[16,32,2048]{2,1,0:T(8,128)(2,1)} %bitcast.59), calls=%async_computation.2 | async-start | bytes 4194304 | tf_op jit(solution)/shard_map/all_to_all | solution.py:30
  144.2 8.8 %fusion.11 = bf16[512,2048]{1,0:T(8,128)(2,1)} fusion(bf16[1,2048,1536]{2,1,0:T(8,128)(2,1)} %all-gather.3.cloned.1.call-done, bf16[512,768]{1,0:T(8,128)(2,1)} %copy-done.6, bf16[512,768]{1,0:T(8,128)(2,1)S(1)} %get-tuple-element.19), kind=kOutput, calls=%fused_computation.14 | convolution fusion | flops 3225419776 | bytes 9961472 | tf_op jit(solution)/shard_map/dot_general | solution.py:65
  153.0 40.1 %all-to-all-done.2 = bf16[16,32,2048]{2,1,0:T(8,128)(2,1)S(1)} async-done(((bf16[16,32,2048]{2,1,0:T(8,128)(2,1)}), bf16[16,32,2048]{2,1,0:T(8,128)(2,1)S(1)}, u32[]{:S(2)}, u32[]{:S(2)}) %all-to-all-start.2) | async-done | bytes 2097184 | tf_op jit(solution)/shard_map/all_to_all | solution.py:30
  193.1 4.4 %all-to-all-start.3 = ((bf16[16,32,2048]{2,1,0:T(8,128)(2,1)}), bf16[16,32,2048]{2,1,0:T(8,128)(2,1)}, u32[]{:S(2)}, u32[]{:S(2)}) async-start(bf16[16,32,2048]{2,1,0:T(8,128)(2,1)} %bitcast.60), calls=%async_computation.3 | async-start | bytes 4194304 | tf_op jit(solution)/shard_map/all_to_all | solution.py:30
  197.6 2.7 %multiply_reduce_fusion = f32[512]{0:T(512)S(1)} fusion(f32[512,2048]{1,0:T(8,128)} %get-tuple-element.22, bf16[512,2048]{1,0:T(8,128)(2,1)S(1)} %bitcast.51), kind=kLoop, calls=%fused_computation.5 | loop fusion | flops 3145216 | bytes 6293504 | tf_op jit(solution)/shard_map/reduce_sum | solution.py:91
  200.3 0.2 select_reduce_fusion
  200.6 0.6 select_reduce_fusion.2
  201.2 0.8 fusion.20
  202.0 0.9 convolution_add_fusion.1
  202.9 1.8 fusion.14
  204.7 3.3 %convert_element_type.65 = f32[1024,768]{1,0:T(8,128)} convert(bf16[1024,768]{1,0:T(8,128)(2,1)} %reduce-scatter.5.cloned.1.call-done) | non-fusion elementwise | flops 786432 | bytes 4718592 | tf_op jit(solution)/shard_map/convert_element_type | solution.py:74
  208.0 5.6 %convert_element_type.63 = f32[1024,1536]{1,0:T(8,128)} convert(bf16[1024,1536]{1,0:T(8,128)(2,1)} %reduce-scatter.3.cloned.1.call-done) | non-fusion elementwise | flops 1572864 | bytes 9437184 | tf_op jit(solution)/shard_map/convert_element_type | solution.py:78
  213.6 33.4 %all-to-all-done.3 = bf16[16,32,2048]{2,1,0:T(8,128)(2,1)} async-done(((bf16[16,32,2048]{2,1,0:T(8,128)(2,1)}), bf16[16,32,2048]{2,1,0:T(8,128)(2,1)}, u32[]{:S(2)}, u32[]{:S(2)}) %all-to-all-start.3) | async-done | bytes 2097184 | tf_op jit(solution)/shard_map/all_to_all | solution.py:30
  246.9 3.3 %convolution_convert_fusion.3 = bf16[256,2048]{1,0:T(8,128)(2,1)} fusion(pred[512,256]{1,0:T(32,128)(4,1)S(1)} %fusion.18, bf16[512,2048]{1,0:T(8,128)(2,1)} %bitcast.13), kind=kOutput, calls=%fused_computation.18 | convolution fusion | flops 537395200 | bytes 3276800 | tf_op jit(solution)/shard_map/dot_general | solution.py:97
  (29 shorter events, 1.0 us)
Async XLA Ops:
  7.2 12.2 %copy-start = (bf16[256,2048]{1,0:T(8,128)(2,1)S(1)}, bf16[256,2048]{1,0:T(8,128)(2,1)}, u32[]{:S(2)}) copy-start(bf16[256,2048]{1,0:T(8,128)(2,1)} %param.7) | copy-start | bytes 3145732
  7.2 0.8 copy-start.4
  7.2 1.3 copy-start.3
  7.2 67.0 %all-gather.3.cloned.1.call-start = ((), (), s32[]{:S(2)}) async-start(), calls=%async_computation.6 | async-start | bytes 9437184 | tf_op jit(solution)/shard_map/all_gather | solution.py:46
  10.5 8.5 %copy-start.5 = (f32[256,8]{0,1:T(8,128)S(1)}, f32[256,8]{0,1:T(8,128)}, u32[]{:S(2)}) copy-start(f32[256,8]{0,1:T(8,128)} %param.9) | copy-start | bytes 24580
  10.5 58.4 %all-to-all-start = ((bf16[16,32,2048]{2,1,0:T(8,128)(2,1)}), bf16[16,32,2048]{2,1,0:T(8,128)(2,1)S(1)}, u32[]{:S(2)}, u32[]{:S(2)}) async-start(bf16[16,32,2048]{2,1,0:T(8,128)(2,1)} %bitcast.4), calls=%async_computation | async-start | bytes 4194304 | tf_op jit(solution)/shard_map/all_to_all | solution.py:30
  68.9 53.9 %all-to-all-start.1 = ((bf16[16,32,2048]{2,1,0:T(8,128)(2,1)}), bf16[16,32,2048]{2,1,0:T(8,128)(2,1)}, u32[]{:S(2)}, u32[]{:S(2)}) async-start(bf16[16,32,2048]{2,1,0:T(8,128)(2,1)} %bitcast.8), calls=%async_computation.1 | async-start | bytes 4194304 | tf_op jit(solution)/shard_map/all_to_all | solution.py:30
  73.4 15.7 %all-gather.5.cloned.1.call-start = ((), (), s32[]{:S(2)}) async-start(), calls=%async_computation.7 | async-start | bytes 4718592 | tf_op jit(solution)/shard_map/all_gather | solution.py:47
  74.1 130.6 %reduce-scatter.5.cloned.1.call-start = ((), (), s32[]{:S(2)}) async-start(), calls=%async_computation.9 | async-start | bytes 4718592 | tf_op jit(solution)/shard_map/reduce_scatter | solution.py:74
  79.7 1.7 copy-start.2
  128.0 80.0 %reduce-scatter.3.cloned.1.call-start = ((), (), s32[]{:S(2)}) async-start(), calls=%async_computation.8 | async-start | bytes 9437184 | tf_op jit(solution)/shard_map/reduce_scatter | solution.py:78
  133.9 0.9 copy-start.6
  140.3 52.9 %all-to-all-start.2 = ((bf16[16,32,2048]{2,1,0:T(8,128)(2,1)}), bf16[16,32,2048]{2,1,0:T(8,128)(2,1)S(1)}, u32[]{:S(2)}, u32[]{:S(2)}) async-start(bf16[16,32,2048]{2,1,0:T(8,128)(2,1)} %bitcast.59), calls=%async_computation.2 | async-start | bytes 4194304 | tf_op jit(solution)/shard_map/all_to_all | solution.py:30
  193.1 53.8 %all-to-all-start.3 = ((bf16[16,32,2048]{2,1,0:T(8,128)(2,1)}), bf16[16,32,2048]{2,1,0:T(8,128)(2,1)}, u32[]{:S(2)}, u32[]{:S(2)}) async-start(bf16[16,32,2048]{2,1,0:T(8,128)(2,1)} %bitcast.60), calls=%async_computation.3 | async-start | bytes 4194304 | tf_op jit(solution)/shard_map/all_to_all | solution.py:30
  208.0 42.2 %copy-start.1 = (bf16[256,2048]{1,0:T(8,128)(2,1)S(1)}, bf16[256,2048]{1,0:T(8,128)(2,1)}, u32[]{:S(2)}) copy-start(bf16[256,2048]{1,0:T(8,128)(2,1)} %param.7) | copy-start | bytes 3145732
Sparse Core Ops, SparseCore 0:
  9.6 19.4 all-gather.2
  75.8 13.3 all-gather.4
  128.2 8.0 reduce-scatter.4
  140.4 14.3 reduce-scatter.2

commit v3 on v2

v3 whole, which is shorter than its diff:
```python
import jax
import jax.numpy as jnp
from jax import lax
from jax.sharding import PartitionSpec as P

EXP_DEV = 4
BF = jnp.bfloat16
F32 = jnp.float32
ROWS_IN = (((0,), (0,)), ((), ()))
COLS_IN = (((1,), (1,)), ((), ()))


def slot_tables(expert_ids, gates, numbers, capacity):
    tok_rows = expert_ids.shape[0]
    groups = numbers.shape[0]
    ids_t = expert_ids.T
    chosen = ids_t[None, :, :] == numbers[:, None, None]
    routed = jnp.any(chosen, axis=1)
    earlier = jnp.arange(tok_rows)[:, None] < jnp.arange(tok_rows)[None, :]
    order_in = jnp.dot(
        routed.astype(BF), earlier.astype(BF), preferred_element_type=F32
    ).astype(jnp.int32)
    weight = jnp.sum(jnp.where(chosen, gates.T[None, :, :], 0.0), axis=1)
    slot_ids = jnp.arange(capacity, dtype=jnp.int32)
    hits = routed[:, None, :] & (order_in[:, None, :] == slot_ids[None, :, None])
    slot_weight = jnp.sum(jnp.where(hits, weight[:, None, :], 0.0), axis=2)
    return chosen, hits.reshape(groups * capacity, tok_rows), slot_weight.reshape(-1)


def exchange(rows, groups):
    size = rows.shape[0] // groups
    blocks = [rows[:size]]
    for j in range(1, groups):
        pairs = [(i, i ^ j) for i in range(groups)]
        blocks.append(lax.ppermute(rows[j * size : (j + 1) * size], ("node", "local"), pairs))
    return jnp.concatenate(blocks, axis=0)


def gathered(shard):
    count = lax.axis_size("edata")
    shards = [shard]
    for step in range(1, count):
        pairs = [((i + step) % count, i) for i in range(count)]
        shards.append(lax.ppermute(shard, "edata", pairs))
    return jnp.concatenate(shards, axis=0)


def reduced(part):
    count = lax.axis_size("edata")
    size = part.shape[0] // count
    total = part[:size].astype(F32)
    for step in range(1, count):
        pairs = [(i, (i + step) % count) for i in range(count)]
        piece = lax.ppermute(part[step * size : (step + 1) * size], "edata", pairs)
        total = total + piece.astype(F32)
    return total


def shards(tokens, out_grad, expert_ids, gates, w_gate_up, w_down):
    groups = lax.axis_size("node") * lax.axis_size("local")
    tok_rows, model_width = tokens.shape
    hidden = w_down.shape[2]
    capacity = tok_rows * expert_ids.shape[1] // (EXP_DEV * groups)
    me = lax.axis_index(("node", "local"))
    turn = lax.axis_index("edata") * w_down.shape[1]
    numbers = me ^ jnp.arange(groups, dtype=jnp.int32)
    w_in = gathered(w_gate_up[0])
    w_out = gathered(w_down[0])
    chosen, hits, slot_weight = slot_tables(expert_ids, gates, numbers, capacity)
    pick = hits.astype(BF)
    tokens = jnp.roll(tokens, -turn, axis=1)
    out_grad = jnp.roll(out_grad, -turn, axis=1)
    x_send = jnp.dot(pick, tokens, preferred_element_type=F32).astype(BF)
    x_recv = exchange(x_send, groups)
    grad_rows = jnp.dot(pick, out_grad, preferred_element_type=F32)
    dy_send = (slot_weight[:, None] * grad_rows).astype(BF)
    dy_recv = exchange(dy_send, groups)

    activation = jnp.dot(x_recv, w_in, preferred_element_type=F32)
    act_gate = activation[:, :hidden]
    act_up = activation[:, hidden:]
    sigmoid_gate = jax.nn.sigmoid(act_gate)
    swished = act_gate * sigmoid_gate
    inner_act = (swished * act_up).astype(BF)
    expert_out = lax.dot_general(inner_act, w_out, COLS_IN, preferred_element_type=F32).astype(BF)
    expert_out, dy_recv = lax.optimization_barrier((expert_out, dy_recv))
    y_back = exchange(expert_out, groups)

    inner_grad = jnp.dot(dy_recv, w_out, preferred_element_type=F32)
    grad_gate_part = inner_grad * act_up * sigmoid_gate * (1.0 + act_gate * (1.0 - sigmoid_gate))
    grad_up_part = inner_grad * swished
    act_grad = jnp.concatenate([grad_gate_part, grad_up_part], axis=1).astype(BF)
    copy_grad = lax.dot_general(act_grad, w_in, COLS_IN, preferred_element_type=F32).astype(BF)
    copy_grad, y_back = lax.optimization_barrier((copy_grad, y_back))
    dx_back = exchange(copy_grad, groups)

    part_down = lax.dot_general(dy_recv, inner_act, ROWS_IN, preferred_element_type=F32).astype(BF)
    grad_down = reduced(part_down)
    part_in = lax.dot_general(x_recv, act_grad, ROWS_IN, preferred_element_type=F32).astype(BF)
    grad_in = reduced(part_in)

    spread = jnp.where(hits, slot_weight[:, None], 0.0)
    high = lax.reduce_precision(spread, 8, 7)
    middle = lax.reduce_precision(spread - high, 8, 7)
    low = spread - high - middle
    high, middle, low = high.astype(BF), middle.astype(BF), low.astype(BF)
    mixed = (
        lax.dot_general(high, y_back, ROWS_IN, preferred_element_type=F32)
        + lax.dot_general(middle, y_back, ROWS_IN, preferred_element_type=F32)
        + lax.dot_general(low, y_back, ROWS_IN, preferred_element_type=F32)
    ).astype(BF)
    slot_dots = jnp.sum(y_back.astype(F32) * grad_rows, axis=1)
    token_dots = jnp.sum(
        jnp.where(hits, slot_dots[:, None], 0.0).reshape(groups, capacity, tok_rows), axis=1
    )
    gate_grad = jnp.sum(jnp.where(chosen, token_dots[:, None, :], 0.0), axis=0).T
    dx_back, grad_in, grad_down = lax.optimization_barrier((dx_back, grad_in, grad_down))
    token_grad = lax.dot_general(pick, dx_back, ROWS_IN, preferred_element_type=F32).astype(BF)
    mixed = jnp.roll(mixed, turn, axis=1)
    token_grad = jnp.roll(token_grad, turn, axis=1)
    return (mixed, token_grad, gate_grad, grad_in[None], grad_down[None])


def solution(mesh):
    rows = P(("node", "local", "edata"), None)
    weights = P(("node", "local"), "edata", None)
    return jax.shard_map(
        shards,
        mesh=mesh,
        in_specs=(rows, rows, rows, rows, weights, weights),
        out_specs=(rows, rows, rows, weights, weights),
        check_vma=False,
    )
```

time: 257 us -> 423 us (1.65)
  waiting for transfers between devices: 157 us -> 253 us
  starting transfers between devices: 21.4 us -> 96.3 us
  local copies, waits for them, and re-layouts: 2.91 us -> 23.1 us
  matrix products: 48.8 us -> 34.7 us
  between operations: 13.9 us -> 1.23 us
    ppermute x0 -> x64, waiting for transfers between devices: none -> 253 us  [the longest x60 253 us: exchange(): lax.ppermute(rows[j * size:(j + 1) * size], ('node', 'local'), pairs)]
    all_to_all x4 -> x0, waiting for transfers between devices: 148 us -> none  [exchange(): lax.all_to_all(shaped, ('node', 'local'), split_axis=0, concat_axis=0, ti...]
    ppermute x0 -> x64, starting transfers between devices: none -> 96.3 us  [the longest x60 95.2 us: exchange(): lax.ppermute(rows[j * size:(j + 1) * size], ('node', 'local'), pairs)]
    all_to_all x4 -> x0, starting transfers between devices: 21.2 us -> none  [exchange(): lax.all_to_all(shaped, ('node', 'local'), split_axis=0, concat_axis=0, ti...]
    unnamed x14 -> x86, local copies, waits for them, and re-layouts: 2.67 us -> 14.2 us
    add x0 -> x2, other arithmetic: none -> 8.97 us  [reduced(): total = total + piece.astype(F32)]
    convert_element_type x2 -> x0, other arithmetic: 8.86 us -> none  [the longest x1 5.55 us: shards(): lax.psum_scatter(part_in, 'edata', scatter_dimension=0, tiled=True)]
    dot_general x8, matrix products: 31.3 us -> 22.7 us  [the longest x1 9.03 us: shards(): lax.dot_general(act_grad, w_in, COLS_IN, preferred_element_type=F32)]
  transfers between devices with their start and end apart: 8 -> 64, of which waited for: 5 -> 48; matrix products, arithmetic and copies ran while one was open for 21% -> 14% of each run, Pallas kernels for 0% -> 0%
where the time goes in v3:
time: 423 us
  waiting for transfers between devices  253 us (60%)
  starting transfers between devices  96.3 us (23%)
  matrix products  34.7 us (8%)
  local copies, waits for them, and re-layouts  23.1 us (5%)
  other arithmetic  14.6 us (3%)
    ppermute x60, waiting for transfers between devices, exchange(): lax.ppermute(rows[j * size:(j + 1) * size], ('node', 'local'), pairs)  253 us
    ppermute x60, starting transfers between devices, exchange(): lax.ppermute(rows[j * size:(j + 1) * size], ('node', 'local'), pairs)  95.2 us
    unnamed x86, local copies, waits for them, and re-layouts  14.2 us
    dot_general x1, matrix products, shards(): lax.dot_general(act_grad, w_in, COLS_IN, preferred_element_type=F32)  9.03 us
    add x2, other arithmetic, reduced(): total = total + piece.astype(F32)  8.97 us
  transfers between devices with their start and end apart: 64, of which 48 were waited for; matrix products, arithmetic and copies ran while one was open for 14% of the time, Pallas kernels for 0%

profile of v3, /device:TPU:0, one launch (start us, length us, event | category | flops | bytes accessed | tf_op | source)
XLA Modules:
  0.0 422.7 jit_solution(4863954907399771069)
XLA Ops:
  5.4 6.5 %collective-permute-start.14 = (bf16[32,2048]{1,0:T(8,128)(2,1)S(1)}, bf16[32,2048]{1,0:T(8,128)(2,1)}, u32[]{:S(2)}, u32[]{:S(2)}) collective-permute-start(bf16[32,2048]{1,0:T(8,128)(2,1)S(1)} %get-tuple-element.70), channel_id=1, source_target_pairs={{0,30},{2,28},{4,26},{6,24},{8,22},{10,20},{12,18},{14,16},{16,14}... | collective-permute-start | bytes 393224 | tf_op jit(solution)/shard_map/ppermute | solution.py:35
  19.2 5.4 %collective-permute-done = bf16[32,2048]{1,0:T(8,128)(2,1)} collective-permute-done((bf16[32,2048]{1,0:T(8,128)(2,1)}, bf16[32,2048]{1,0:T(8,128)(2,1)}, u32[]{:S(2)}, u32[]{:S(2)}) %collective-permute-start) | collective-permute-done | bytes 131104 | tf_op jit(solution)/shard_map/ppermute | solution.py:35
  27.9 5.6 %collective-permute-done.1 = bf16[32,2048]{1,0:T(8,128)(2,1)S(1)} collective-permute-done((bf16[32,2048]{1,0:T(8,128)(2,1)}, bf16[32,2048]{1,0:T(8,128)(2,1)S(1)}, u32[]{:S(2)}, u32[]{:S(2)}) %collective-permute-start.1) | collective-permute-done | bytes 131104 | tf_op jit(solution)/shard_map/ppermute | solution.py:35
  54.3 7.4 %collective-permute-done.5 = bf16[32,2048]{1,0:T(8,128)(2,1)S(1)} collective-permute-done((bf16[32,2048]{1,0:T(8,128)(2,1)S(1)}, bf16[32,2048]{1,0:T(8,128)(2,1)S(1)}, u32[]{:S(2)}, u32[]{:S(2)}) %collective-permute-start.5) | collective-permute-done | bytes 131104 | tf_op jit(solution)/shard_map/ppermute | solution.py:35
  75.0 5.2 %collective-permute-done.8 = bf16[32,2048]{1,0:T(8,128)(2,1)S(1)} collective-permute-done((bf16[32,2048]{1,0:T(8,128)(2,1)S(1)}, bf16[32,2048]{1,0:T(8,128)(2,1)S(1)}, u32[]{:S(2)}, u32[]{:S(2)}) %collective-permute-start.8) | collective-permute-done | bytes 131104 | tf_op jit(solution)/shard_map/ppermute | solution.py:35
  80.9 6.3 %collective-permute-done.9 = bf16[32,2048]{1,0:T(8,128)(2,1)S(1)} collective-permute-done((bf16[32,2048]{1,0:T(8,128)(2,1)S(1)}, bf16[32,2048]{1,0:T(8,128)(2,1)S(1)}, u32[]{:S(2)}, u32[]{:S(2)}) %collective-permute-start.9) | collective-permute-done | bytes 131104 | tf_op jit(solution)/shard_map/ppermute | solution.py:35
  117.0 7.2 %collective-permute-done.18 = bf16[32,2048]{1,0:T(8,128)(2,1)S(1)} collective-permute-done((bf16[32,2048]{1,0:T(8,128)(2,1)S(1)}, bf16[32,2048]{1,0:T(8,128)(2,1)S(1)}, u32[]{:S(2)}, u32[]{:S(2)}) %collective-permute-start.18) | collective-permute-done | bytes 131104 | tf_op jit(solution)/shard_map/ppermute | solution.py:35
  125.3 5.7 %collective-permute-done.19 = bf16[32,2048]{1,0:T(8,128)(2,1)S(1)} collective-permute-done((bf16[32,2048]{1,0:T(8,128)(2,1)S(1)}, bf16[32,2048]{1,0:T(8,128)(2,1)S(1)}, u32[]{:S(2)}, u32[]{:S(2)}) %collective-permute-start.19) | collective-permute-done | bytes 131104 | tf_op jit(solution)/shard_map/ppermute | solution.py:35
  137.2 5.8 %collective-permute-done.21 = bf16[32,2048]{1,0:T(8,128)(2,1)S(1)} collective-permute-done((bf16[32,2048]{1,0:T(8,128)(2,1)S(1)}, bf16[32,2048]{1,0:T(8,128)(2,1)S(1)}, u32[]{:S(2)}, u32[]{:S(2)}) %collective-permute-start.21) | collective-permute-done | bytes 131104 | tf_op jit(solution)/shard_map/ppermute | solution.py:35
  143.7 8.9 %collective-permute-done.22 = bf16[32,2048]{1,0:T(8,128)(2,1)S(1)} collective-permute-done((bf16[32,2048]{1,0:T(8,128)(2,1)S(1)}, bf16[32,2048]{1,0:T(8,128)(2,1)S(1)}, u32[]{:S(2)}, u32[]{:S(2)}) %collective-permute-start.22) | collective-permute-done | bytes 131104 | tf_op jit(solution)/shard_map/ppermute | solution.py:35
  154.3 5.9 %collective-permute-done.23 = bf16[32,2048]{1,0:T(8,128)(2,1)S(1)} collective-permute-done((bf16[32,2048]{1,0:T(8,128)(2,1)S(1)}, bf16[32,2048]{1,0:T(8,128)(2,1)S(1)}, u32[]{:S(2)}, u32[]{:S(2)}) %collective-permute-start.23) | collective-permute-done | bytes 131104 | tf_op jit(solution)/shard_map/ppermute | solution.py:35
  165.4 5.8 %collective-permute-done.25 = bf16[32,2048]{1,0:T(8,128)(2,1)S(1)} collective-permute-done((bf16[32,2048]{1,0:T(8,128)(2,1)S(1)}, bf16[32,2048]{1,0:T(8,128)(2,1)S(1)}, u32[]{:S(2)}, u32[]{:S(2)}) %collective-permute-start.25) | collective-permute-done | bytes 131104 | tf_op jit(solution)/shard_map/ppermute | solution.py:35
  171.7 7.7 %collective-permute-done.26 = bf16[32,2048]{1,0:T(8,128)(2,1)S(1)} collective-permute-done((bf16[32,2048]{1,0:T(8,128)(2,1)S(1)}, bf16[32,2048]{1,0:T(8,128)(2,1)S(1)}, u32[]{:S(2)}, u32[]{:S(2)}) %collective-permute-start.26) | collective-permute-done | bytes 131104 | tf_op jit(solution)/shard_map/ppermute | solution.py:35
  181.3 6.3 %collective-permute-done.27 = bf16[32,2048]{1,0:T(8,128)(2,1)S(1)} collective-permute-done((bf16[32,2048]{1,0:T(8,128)(2,1)S(1)}, bf16[32,2048]{1,0:T(8,128)(2,1)S(1)}, u32[]{:S(2)}, u32[]{:S(2)}) %collective-permute-start.27) | collective-permute-done | bytes 131104 | tf_op jit(solution)/shard_map/ppermute | solution.py:35
  193.5 6.7 %collective-permute-done.29 = bf16[32,2048]{1,0:T(8,128)(2,1)S(1)} collective-permute-done((bf16[32,2048]{1,0:T(8,128)(2,1)S(1)}, bf16[32,2048]{1,0:T(8,128)(2,1)S(1)}, u32[]{:S(2)}, u32[]{:S(2)}) %collective-permute-start.29) | collective-permute-done | bytes 131104 | tf_op jit(solution)/shard_map/ppermute | solution.py:35
  224.9 9.0 %fusion.2 = bf16[512,2048]{1,0:T(8,128)(2,1)} fusion(bf16[1024,1536]{1,0:T(8,128)(2,1)} %copy-done.11, bf16[1024,1536]{1,0:T(8,128)(2,1)S(1)} %bitcast.38, bf16[512,768]{1,0:T(8,128)(2,1)S(1)} %get-tuple-element.21, bf16[512,768]{1,0:T(8,128)(2,1)S(1)} %get-tuple-element.20), kind=kOutput, calls=%fused_computation.11 | convolution fusion | flops 3238002688 | bytes 9961472 | tf_op jit(solution)/shard_map/dot_general | solution.py:93
  247.2 5.0 %collective-permute-done.34 = bf16[32,2048]{1,0:T(8,128)(2,1)S(1)} collective-permute-done((bf16[32,2048]{1,0:T(8,128)(2,1)S(1)}, bf16[32,2048]{1,0:T(8,128)(2,1)S(1)}, u32[]{:S(2)}, u32[]{:S(2)}) %collective-permute-start.34) | collective-permute-done | bytes 131104 | tf_op jit(solution)/shard_map/ppermute | solution.py:35
  273.2 5.6 %collective-permute-done.38 = bf16[32,2048]{1,0:T(8,128)(2,1)S(1)} collective-permute-done((bf16[32,2048]{1,0:T(8,128)(2,1)S(1)}, bf16[32,2048]{1,0:T(8,128)(2,1)S(1)}, u32[]{:S(2)}, u32[]{:S(2)}) %collective-permute-start.38) | collective-permute-done | bytes 131104 | tf_op jit(solution)/shard_map/ppermute | solution.py:35
  292.4 6.4 %collective-permute-done.41 = bf16[32,2048]{1,0:T(8,128)(2,1)S(1)} collective-permute-done((bf16[32,2048]{1,0:T(8,128)(2,1)S(1)}, bf16[32,2048]{1,0:T(8,128)(2,1)S(1)}, u32[]{:S(2)}, u32[]{:S(2)}) %collective-permute-start.41) | collective-permute-done | bytes 131104 | tf_op jit(solution)/shard_map/ppermute | solution.py:35
  301.5 5.0 %collective-permute-done.42 = bf16[32,2048]{1,0:T(8,128)(2,1)S(1)} collective-permute-done((bf16[32,2048]{1,0:T(8,128)(2,1)S(1)}, bf16[32,2048]{1,0:T(8,128)(2,1)S(1)}, u32[]{:S(2)}, u32[]{:S(2)}) %collective-permute-start.42) | collective-permute-done | bytes 131104 | tf_op jit(solution)/shard_map/ppermute | solution.py:35
  325.0 7.3 %collective-permute-done.48 = bf16[32,2048]{1,0:T(8,128)(2,1)S(1)} collective-permute-done((bf16[32,2048]{1,0:T(8,128)(2,1)S(1)}, bf16[32,2048]{1,0:T(8,128)(2,1)S(1)}, u32[]{:S(2)}, u32[]{:S(2)}) %collective-permute-start.48) | collective-permute-done | bytes 131104 | tf_op jit(solution)/shard_map/ppermute | solution.py:35
  334.1 4.9 %collective-permute-done.49 = bf16[32,2048]{1,0:T(8,128)(2,1)S(1)} collective-permute-done((bf16[32,2048]{1,0:T(8,128)(2,1)S(1)}, bf16[32,2048]{1,0:T(8,128)(2,1)S(1)}, u32[]{:S(2)}, u32[]{:S(2)}) %collective-permute-start.49) | collective-permute-done | bytes 131104 | tf_op jit(solution)/shard_map/ppermute | solution.py:35
  344.8 5.8 %collective-permute-done.51 = bf16[32,2048]{1,0:T(8,128)(2,1)S(1)} collective-permute-done((bf16[32,2048]{1,0:T(8,128)(2,1)S(1)}, bf16[32,2048]{1,0:T(8,128)(2,1)S(1)}, u32[]{:S(2)}, u32[]{:S(2)}) %collective-permute-start.51) | collective-permute-done | bytes 131104 | tf_op jit(solution)/shard_map/ppermute | solution.py:35
  351.3 10.3 %collective-permute-done.52 = bf16[32,2048]{1,0:T(8,128)(2,1)S(1)} collective-permute-done((bf16[32,2048]{1,0:T(8,128)(2,1)S(1)}, bf16[32,2048]{1,0:T(8,128)(2,1)S(1)}, u32[]{:S(2)}, u32[]{:S(2)}) %collective-permute-start.52) | collective-permute-done | bytes 131104 | tf_op jit(solution)/shard_map/ppermute | solution.py:35
  363.1 7.0 %collective-permute-done.53 = bf16[32,2048]{1,0:T(8,128)(2,1)S(1)} collective-permute-done((bf16[32,2048]{1,0:T(8,128)(2,1)S(1)}, bf16[32,2048]{1,0:T(8,128)(2,1)S(1)}, u32[]{:S(2)}, u32[]{:S(2)}) %collective-permute-start.53) | collective-permute-done | bytes 131104 | tf_op jit(solution)/shard_map/ppermute | solution.py:35
  370.2 5.8 %collective-permute-done.54 = bf16[32,2048]{1,0:T(8,128)(2,1)S(1)} collective-permute-done((bf16[32,2048]{1,0:T(8,128)(2,1)S(1)}, bf16[32,2048]{1,0:T(8,128)(2,1)S(1)}, u32[]{:S(2)}, u32[]{:S(2)}) %collective-permute-start.54) | collective-permute-done | bytes 131104 | tf_op jit(solution)/shard_map/ppermute | solution.py:35
  376.0 7.3 %collective-permute-done.55 = bf16[32,2048]{1,0:T(8,128)(2,1)S(1)} collective-permute-done((bf16[32,2048]{1,0:T(8,128)(2,1)S(1)}, bf16[32,2048]{1,0:T(8,128)(2,1)S(1)}, u32[]{:S(2)}, u32[]{:S(2)}) %collective-permute-start.55) | collective-permute-done | bytes 131104 | tf_op jit(solution)/shard_map/ppermute | solution.py:35
  383.2 6.7 %collective-permute-done.56 = bf16[32,2048]{1,0:T(8,128)(2,1)S(1)} collective-permute-done((bf16[32,2048]{1,0:T(8,128)(2,1)S(1)}, bf16[32,2048]{1,0:T(8,128)(2,1)S(1)}, u32[]{:S(2)}, u32[]{:S(2)}) %collective-permute-start.56) | collective-permute-done | bytes 131104 | tf_op jit(solution)/shard_map/ppermute | solution.py:35
  391.5 6.2 %collective-permute-done.57 = bf16[32,2048]{1,0:T(8,128)(2,1)S(1)} collective-permute-done((bf16[32,2048]{1,0:T(8,128)(2,1)S(1)}, bf16[32,2048]{1,0:T(8,128)(2,1)S(1)}, u32[]{:S(2)}, u32[]{:S(2)}) %collective-permute-start.57) | collective-permute-done | bytes 131104 | tf_op jit(solution)/shard_map/ppermute | solution.py:35
  397.7 5.8 %collective-permute-done.58 = bf16[32,2048]{1,0:T(8,128)(2,1)S(1)} collective-permute-done((bf16[32,2048]{1,0:T(8,128)(2,1)S(1)}, bf16[32,2048]{1,0:T(8,128)(2,1)S(1)}, u32[]{:S(2)}, u32[]{:S(2)}) %collective-permute-start.58) | collective-permute-done | bytes 131104 | tf_op jit(solution)/shard_map/ppermute | solution.py:35
  403.5 6.7 %collective-permute-done.59 = bf16[32,2048]{1,0:T(8,128)(2,1)S(1)} collective-permute-done((bf16[32,2048]{1,0:T(8,128)(2,1)S(1)}, bf16[32,2048]{1,0:T(8,128)(2,1)S(1)}, u32[]{:S(2)}, u32[]{:S(2)}) %collective-permute-start.59) | collective-permute-done | bytes 131104 | tf_op jit(solution)/shard_map/ppermute | solution.py:35
  413.8 5.6 %convert_add_fusion = f32[1024,1536]{1,0:T(8,128)} fusion(bf16[1024,1536]{1,0:T(8,128)(2,1)} %collective-permute-done.62, bf16[2048,1536]{1,0:T(8,128)(2,1)S(1)} %bitcast.29), kind=kLoop, calls=%fused_computation.2 | loop fusion | flops 4718592 | bytes 12582912 | tf_op jit(solution)/shard_map/add | solution.py:55
  (222 shorter events, 214.3 us)
Async XLA Ops:
  0.6 203.6 %collective-permute-start.16 = (bf16[1024,768]{1,0:T(8,128)(2,1)}, bf16[1024,768]{1,0:T(8,128)(2,1)}, u32[]{:S(2)}, u32[]{:S(2)}) collective-permute-start(bf16[1024,768]{1,0:T(8,128)(2,1)} %bitcast.39), channel_id=1, source_target_pairs={{1,0},{0,1},{3,2},{2,3},{5,4},{4,5},{7,6},{6,7},{9,8},{8,9},{11,10... | collective-permute-start | bytes 4718600 | tf_op jit(solution)/shard_map/ppermute | solution.py:44
  5.4 102.3 %collective-permute-start.14 = (bf16[32,2048]{1,0:T(8,128)(2,1)S(1)}, bf16[32,2048]{1,0:T(8,128)(2,1)}, u32[]{:S(2)}, u32[]{:S(2)}) collective-permute-start(bf16[32,2048]{1,0:T(8,128)(2,1)S(1)} %get-tuple-element.70), channel_id=1, source_target_pairs={{0,30},{2,28},{4,26},{6,24},{8,22},{10,20},{12,18},{14,16},{16,14}... | collective-permute-start | bytes 393224 | tf_op jit(solution)/shard_map/ppermute | solution.py:35
  11.9 94.2 %collective-permute-start.13 = (bf16[32,2048]{1,0:T(8,128)(2,1)S(1)}, bf16[32,2048]{1,0:T(8,128)(2,1)}, u32[]{:S(2)}, u32[]{:S(2)}) collective-permute-start(bf16[32,2048]{1,0:T(8,128)(2,1)S(1)} %get-tuple-element.71), channel_id=1, source_target_pairs={{0,28},{2,30},{4,24},{6,26},{8,20},{10,22},{12,16},{14,18},{16,12}... | collective-permute-start | bytes 393224 | tf_op jit(solution)/shard_map/ppermute | solution.py:35
  11.9 89.5 %collective-permute-start.12 = (bf16[32,2048]{1,0:T(8,128)(2,1)S(1)}, bf16[32,2048]{1,0:T(8,128)(2,1)}, u32[]{:S(2)}, u32[]{:S(2)}) collective-permute-start(bf16[32,2048]{1,0:T(8,128)(2,1)S(1)} %get-tuple-element.72), channel_id=1, source_target_pairs={{0,26},{2,24},{4,30},{6,28},{8,18},{10,16},{12,22},{14,20},{16,10}... | collective-permute-start | bytes 393224 | tf_op jit(solution)/shard_map/ppermute | solution.py:35
  14.5 10.1 %collective-permute-start = (bf16[32,2048]{1,0:T(8,128)(2,1)}, bf16[32,2048]{1,0:T(8,128)(2,1)}, u32[]{:S(2)}, u32[]{:S(2)}) collective-permute-start(bf16[32,2048]{1,0:T(8,128)(2,1)} %get-tuple-element.84), channel_id=1, source_target_pairs={{0,2},{2,0},{4,6},{6,4},{8,10},{10,8},{12,14},{14,12},{16,18},{18,... | collective-permute-start | bytes 393224 | tf_op jit(solution)/shard_map/ppermute | solution.py:35
  24.6 8.9 %collective-permute-start.1 = (bf16[32,2048]{1,0:T(8,128)(2,1)}, bf16[32,2048]{1,0:T(8,128)(2,1)S(1)}, u32[]{:S(2)}, u32[]{:S(2)}) collective-permute-start(bf16[32,2048]{1,0:T(8,128)(2,1)} %get-tuple-element.83), channel_id=1, source_target_pairs={{0,4},{2,6},{4,0},{6,2},{8,12},{10,14},{12,8},{14,10},{16,20},{18,... | collective-permute-start | bytes 393224 | tf_op jit(solution)/shard_map/ppermute | solution.py:35
  51.8 9.8 %collective-permute-start.5 = (bf16[32,2048]{1,0:T(8,128)(2,1)S(1)}, bf16[32,2048]{1,0:T(8,128)(2,1)S(1)}, u32[]{:S(2)}, u32[]{:S(2)}) collective-permute-start(bf16[32,2048]{1,0:T(8,128)(2,1)S(1)} %get-tuple-element.79), channel_id=1, source_target_pairs={{0,12},{2,14},{4,8},{6,10},{8,4},{10,6},{12,0},{14,2},{16,28},{18,... | collective-permute-start | bytes 393224 | tf_op jit(solution)/shard_map/ppermute | solution.py:35
  61.6 7.7 %collective-permute-start.6 = (bf16[32,2048]{1,0:T(8,128)(2,1)S(1)}, bf16[32,2048]{1,0:T(8,128)(2,1)S(1)}, u32[]{:S(2)}, u32[]{:S(2)}) collective-permute-start(bf16[32,2048]{1,0:T(8,128)(2,1)S(1)} %get-tuple-element.78), channel_id=1, source_target_pairs={{0,14},{2,12},{4,10},{6,8},{8,6},{10,4},{12,2},{14,0},{16,30},{18,... | collective-permute-start | bytes 393224 | tf_op jit(solution)/shard_map/ppermute | solution.py:35
  87.2 7.7 %collective-permute-start.10 = (bf16[32,2048]{1,0:T(8,128)(2,1)S(1)}, bf16[32,2048]{1,0:T(8,128)(2,1)S(1)}, u32[]{:S(2)}, u32[]{:S(2)}) collective-permute-start(bf16[32,2048]{1,0:T(8,128)(2,1)S(1)} %get-tuple-element.74), channel_id=1, source_target_pairs={{0,22},{2,20},{4,18},{6,16},{8,30},{10,28},{12,26},{14,24},{16,6},... | collective-permute-start | bytes 393224 | tf_op jit(solution)/shard_map/ppermute | solution.py:35
  100.7 99.6 %collective-permute-start.15 = (bf16[1024,1536]{1,0:T(8,128)(2,1)}, bf16[1024,1536]{1,0:T(8,128)(2,1)S(1)}, u32[]{:S(2)}, u32[]{:S(2)}) collective-permute-start(bf16[1024,1536]{1,0:T(8,128)(2,1)} %bitcast.36), channel_id=1, source_target_pairs={{1,0},{0,1},{3,2},{2,3},{5,4},{4,5},{7,6},{6,7},{9,8},{8,9},{11,10... | collective-permute-start | bytes 9437192 | tf_op jit(solution)/shard_map/ppermute | solution.py:44
  101.4 98.9 %collective-permute-start.31 = (bf16[32,2048]{1,0:T(8,128)(2,1)S(1)}, bf16[32,2048]{1,0:T(8,128)(2,1)S(1)}, u32[]{:S(2)}, u32[]{:S(2)}) collective-permute-start(bf16[32,2048]{1,0:T(8,128)(2,1)S(1)} %get-tuple-element.54), channel_id=1, source_target_pairs={{0,30},{2,28},{4,26},{6,24},{8,22},{10,20},{12,18},{14,16},{16,14}... | collective-permute-start | bytes 393224 | tf_op jit(solution)/shard_map/ppermute | solution.py:35
  106.1 94.2 %collective-permute-start.30 = (bf16[32,2048]{1,0:T(8,128)(2,1)S(1)}, bf16[32,2048]{1,0:T(8,128)(2,1)S(1)}, u32[]{:S(2)}, u32[]{:S(2)}) collective-permute-start(bf16[32,2048]{1,0:T(8,128)(2,1)S(1)} %get-tuple-element.55), channel_id=1, source_target_pairs={{0,28},{2,30},{4,24},{6,26},{8,20},{10,22},{12,16},{14,18},{16,12}... | collective-permute-start | bytes 393224 | tf_op jit(solution)/shard_map/ppermute | solution.py:35
  107.6 9.4 %collective-permute-start.17 = (bf16[32,2048]{1,0:T(8,128)(2,1)S(1)}, bf16[32,2048]{1,0:T(8,128)(2,1)S(1)}, u32[]{:S(2)}, u32[]{:S(2)}) collective-permute-start(bf16[32,2048]{1,0:T(8,128)(2,1)S(1)} %get-tuple-element.68), channel_id=1, source_target_pairs={{0,2},{2,0},{4,6},{6,4},{8,10},{10,8},{12,14},{14,12},{16,18},{18,... | collective-permute-start | bytes 393224 | tf_op jit(solution)/shard_map/ppermute | solution.py:35
  143.1 9.5 %collective-permute-start.22 = (bf16[32,2048]{1,0:T(8,128)(2,1)S(1)}, bf16[32,2048]{1,0:T(8,128)(2,1)S(1)}, u32[]{:S(2)}, u32[]{:S(2)}) collective-permute-start(bf16[32,2048]{1,0:T(8,128)(2,1)S(1)} %get-tuple-element.63), channel_id=1, source_target_pairs={{0,12},{2,14},{4,8},{6,10},{8,4},{10,6},{12,0},{14,2},{16,28},{18,... | collective-permute-start | bytes 393224 | tf_op jit(solution)/shard_map/ppermute | solution.py:35
  152.6 7.7 %collective-permute-start.23 = (bf16[32,2048]{1,0:T(8,128)(2,1)S(1)}, bf16[32,2048]{1,0:T(8,128)(2,1)S(1)}, u32[]{:S(2)}, u32[]{:S(2)}) collective-permute-start(bf16[32,2048]{1,0:T(8,128)(2,1)S(1)} %get-tuple-element.62), channel_id=1, source_target_pairs={{0,14},{2,12},{4,10},{6,8},{8,6},{10,4},{12,2},{14,0},{16,30},{18,... | collective-permute-start | bytes 393224 | tf_op jit(solution)/shard_map/ppermute | solution.py:35
  171.2 8.2 %collective-permute-start.26 = (bf16[32,2048]{1,0:T(8,128)(2,1)S(1)}, bf16[32,2048]{1,0:T(8,128)(2,1)S(1)}, u32[]{:S(2)}, u32[]{:S(2)}) collective-permute-start(bf16[32,2048]{1,0:T(8,128)(2,1)S(1)} %get-tuple-element.59), channel_id=1, source_target_pairs={{0,20},{2,22},{4,16},{6,18},{8,28},{10,30},{12,24},{14,26},{16,4},... | collective-permute-start | bytes 393224 | tf_op jit(solution)/shard_map/ppermute | solution.py:35
  179.4 8.2 %collective-permute-start.27 = (bf16[32,2048]{1,0:T(8,128)(2,1)S(1)}, bf16[32,2048]{1,0:T(8,128)(2,1)S(1)}, u32[]{:S(2)}, u32[]{:S(2)}) collective-permute-start(bf16[32,2048]{1,0:T(8,128)(2,1)S(1)} %get-tuple-element.58), channel_id=1, source_target_pairs={{0,22},{2,20},{4,18},{6,16},{8,30},{10,28},{12,26},{14,24},{16,6},... | collective-permute-start | bytes 393224 | tf_op jit(solution)/shard_map/ppermute | solution.py:35
  208.7 98.5 %collective-permute-start.46 = (bf16[32,2048]{1,0:T(8,128)(2,1)S(1)}, bf16[32,2048]{1,0:T(8,128)(2,1)S(1)}, u32[]{:S(2)}, u32[]{:S(2)}) collective-permute-start(bf16[32,2048]{1,0:T(8,128)(2,1)S(1)} %get-tuple-element.38), channel_id=1, source_target_pairs={{0,30},{2,28},{4,26},{6,24},{8,22},{10,20},{12,18},{14,16},{16,14}... | collective-permute-start | bytes 393224 | tf_op jit(solution)/shard_map/ppermute | solution.py:35
  211.2 95.9 %collective-permute-start.45 = (bf16[32,2048]{1,0:T(8,128)(2,1)S(1)}, bf16[32,2048]{1,0:T(8,128)(2,1)S(1)}, u32[]{:S(2)}, u32[]{:S(2)}) collective-permute-start(bf16[32,2048]{1,0:T(8,128)(2,1)S(1)} %get-tuple-element.39), channel_id=1, source_target_pairs={{0,28},{2,30},{4,24},{6,26},{8,20},{10,22},{12,16},{14,18},{16,12}... | collective-permute-start | bytes 393224 | tf_op jit(solution)/shard_map/ppermute | solution.py:35
  212.3 94.8 %collective-permute-start.44 = (bf16[32,2048]{1,0:T(8,128)(2,1)S(1)}, bf16[32,2048]{1,0:T(8,128)(2,1)S(1)}, u32[]{:S(2)}, u32[]{:S(2)}) collective-permute-start(bf16[32,2048]{1,0:T(8,128)(2,1)S(1)} %get-tuple-element.40), channel_id=1, source_target_pairs={{0,26},{2,24},{4,30},{6,28},{8,18},{10,16},{12,22},{14,20},{16,10}... | collective-permute-start | bytes 393224 | tf_op jit(solution)/shard_map/ppermute | solution.py:35
  216.6 89.9 %collective-permute-start.43 = (bf16[32,2048]{1,0:T(8,128)(2,1)S(1)}, bf16[32,2048]{1,0:T(8,128)(2,1)S(1)}, u32[]{:S(2)}, u32[]{:S(2)}) collective-permute-start(bf16[32,2048]{1,0:T(8,128)(2,1)S(1)} %get-tuple-element.41), channel_id=1, source_target_pairs={{0,24},{2,26},{4,28},{6,30},{8,16},{10,18},{12,20},{14,22},{16,8},... | collective-permute-start | bytes 393224 | tf_op jit(solution)/shard_map/ppermute | solution.py:35
  217.3 21.7 %collective-permute-start.32 = (bf16[32,2048]{1,0:T(8,128)(2,1)S(1)}, bf16[32,2048]{1,0:T(8,128)(2,1)S(1)}, u32[]{:S(2)}, u32[]{:S(2)}) collective-permute-start(bf16[32,2048]{1,0:T(8,128)(2,1)S(1)} %get-tuple-element.52), channel_id=1, source_target_pairs={{0,2},{2,0},{4,6},{6,4},{8,10},{10,8},{12,14},{14,12},{16,18},{18,... | collective-permute-start | bytes 393224 | tf_op jit(solution)/shard_map/ppermute | solution.py:35
  271.0 7.8 %collective-permute-start.38 = (bf16[32,2048]{1,0:T(8,128)(2,1)S(1)}, bf16[32,2048]{1,0:T(8,128)(2,1)S(1)}, u32[]{:S(2)}, u32[]{:S(2)}) collective-permute-start(bf16[32,2048]{1,0:T(8,128)(2,1)S(1)} %get-tuple-element.46), channel_id=1, source_target_pairs={{0,14},{2,12},{4,10},{6,8},{8,6},{10,4},{12,2},{14,0},{16,30},{18,... | collective-permute-start | bytes 393224 | tf_op jit(solution)/shard_map/ppermute | solution.py:35
  290.6 8.2 %collective-permute-start.41 = (bf16[32,2048]{1,0:T(8,128)(2,1)S(1)}, bf16[32,2048]{1,0:T(8,128)(2,1)S(1)}, u32[]{:S(2)}, u32[]{:S(2)}) collective-permute-start(bf16[32,2048]{1,0:T(8,128)(2,1)S(1)} %get-tuple-element.43), channel_id=1, source_target_pairs={{0,20},{2,22},{4,16},{6,18},{8,28},{10,30},{12,24},{14,26},{16,4},... | collective-permute-start | bytes 393224 | tf_op jit(solution)/shard_map/ppermute | solution.py:35
  306.5 103.9 %collective-permute-start.63 = (bf16[1024,768]{1,0:T(8,128)(2,1)}, bf16[1024,768]{1,0:T(8,128)(2,1)}, u32[]{:S(2)}, u32[]{:S(2)}) collective-permute-start(bf16[1024,768]{1,0:T(8,128)(2,1)} %slice.317), channel_id=1, source_target_pairs={{0,1},{1,0},{2,3},{3,2},{4,5},{5,4},{6,7},{7,6},{8,9},{9,8},{10,11... | collective-permute-start | bytes 4718600 | tf_op jit(solution)/shard_map/ppermute | solution.py:54
  306.5 107.2 %collective-permute-start.62 = (bf16[1024,1536]{1,0:T(8,128)(2,1)}, bf16[1024,1536]{1,0:T(8,128)(2,1)}, u32[]{:S(2)}, u32[]{:S(2)}) collective-permute-start(bf16[1024,1536]{1,0:T(8,128)(2,1)} %slice.315), channel_id=1, source_target_pairs={{0,1},{1,0},{2,3},{3,2},{4,5},{5,4},{6,7},{7,6},{8,9},{9,8},{10,11... | collective-permute-start | bytes 9437192 | tf_op jit(solution)/shard_map/ppermute | solution.py:54
  312.6 97.7 %collective-permute-start.61 = (bf16[32,2048]{1,0:T(8,128)(2,1)S(1)}, bf16[32,2048]{1,0:T(8,128)(2,1)S(1)}, u32[]{:S(2)}, u32[]{:S(2)}) collective-permute-start(bf16[32,2048]{1,0:T(8,128)(2,1)S(1)} %get-tuple-element.22), channel_id=1, source_target_pairs={{0,30},{2,28},{4,26},{6,24},{8,22},{10,20},{12,18},{14,16},{16,14}... | collective-permute-start | bytes 393224 | tf_op jit(solution)/shard_map/ppermute | solution.py:35
  313.3 97.0 %collective-permute-start.60 = (bf16[32,2048]{1,0:T(8,128)(2,1)S(1)}, bf16[32,2048]{1,0:T(8,128)(2,1)S(1)}, u32[]{:S(2)}, u32[]{:S(2)}) collective-permute-start(bf16[32,2048]{1,0:T(8,128)(2,1)S(1)} %get-tuple-element.23), channel_id=1, source_target_pairs={{0,28},{2,30},{4,24},{6,26},{8,20},{10,22},{12,16},{14,18},{16,12}... | collective-permute-start | bytes 393224 | tf_op jit(solution)/shard_map/ppermute | solution.py:35
  314.4 7.9 %collective-permute-start.47 = (bf16[32,2048]{1,0:T(8,128)(2,1)S(1)}, bf16[32,2048]{1,0:T(8,128)(2,1)S(1)}, u32[]{:S(2)}, u32[]{:S(2)}) collective-permute-start(bf16[32,2048]{1,0:T(8,128)(2,1)S(1)} %get-tuple-element.36), channel_id=1, source_target_pairs={{0,2},{2,0},{4,6},{6,4},{8,10},{10,8},{12,14},{14,12},{16,18},{18,... | collective-permute-start | bytes 393224 | tf_op jit(solution)/shard_map/ppermute | solution.py:35
  322.3 10.0 %collective-permute-start.48 = (bf16[32,2048]{1,0:T(8,128)(2,1)S(1)}, bf16[32,2048]{1,0:T(8,128)(2,1)S(1)}, u32[]{:S(2)}, u32[]{:S(2)}) collective-permute-start(bf16[32,2048]{1,0:T(8,128)(2,1)S(1)} %get-tuple-element.35), channel_id=1, source_target_pairs={{0,4},{2,6},{4,0},{6,2},{8,12},{10,14},{12,8},{14,10},{16,20},{18,... | collective-permute-start | bytes 393224 | tf_op jit(solution)/shard_map/ppermute | solution.py:35
  350.7 10.9 %collective-permute-start.52 = (bf16[32,2048]{1,0:T(8,128)(2,1)S(1)}, bf16[32,2048]{1,0:T(8,128)(2,1)S(1)}, u32[]{:S(2)}, u32[]{:S(2)}) collective-permute-start(bf16[32,2048]{1,0:T(8,128)(2,1)S(1)} %get-tuple-element.31), channel_id=1, source_target_pairs={{0,12},{2,14},{4,8},{6,10},{8,4},{10,6},{12,0},{14,2},{16,28},{18,... | collective-permute-start | bytes 393224 | tf_op jit(solution)/shard_map/ppermute | solution.py:35
  361.6 8.5 %collective-permute-start.53 = (bf16[32,2048]{1,0:T(8,128)(2,1)S(1)}, bf16[32,2048]{1,0:T(8,128)(2,1)S(1)}, u32[]{:S(2)}, u32[]{:S(2)}) collective-permute-start(bf16[32,2048]{1,0:T(8,128)(2,1)S(1)} %get-tuple-element.30), channel_id=1, source_target_pairs={{0,14},{2,12},{4,10},{6,8},{8,6},{10,4},{12,2},{14,0},{16,30},{18,... | collective-permute-start | bytes 393224 | tf_op jit(solution)/shard_map/ppermute | solution.py:35
  (47 other events, 763.0 us)

commit v4 on v3

v4 whole, which is shorter than its diff:
```python
import jax
import jax.numpy as jnp
from jax import lax
from jax.experimental import pallas as pl
from jax.experimental.pallas import tpu as pltpu
from jax.sharding import PartitionSpec as P

EXP_DEV = 4
BF = jnp.bfloat16
F32 = jnp.float32
ROWS_IN = (((0,), (0,)), ((), ()))
COLS_IN = (((1,), (1,)), ((), ()))
LIMIT = 48 * 1024 * 1024
CHEAP = pl.CostEstimate(flops=1, bytes_accessed=1, transcendentals=0)


def slot_tables(expert_ids, gates, groups, capacity):
    tok_rows = expert_ids.shape[0]
    numbers = jnp.arange(groups, dtype=jnp.int32)
    ids_t = expert_ids.T
    chosen = ids_t[None, :, :] == numbers[:, None, None]
    routed = jnp.any(chosen, axis=1)
    earlier = jnp.arange(tok_rows)[:, None] < jnp.arange(tok_rows)[None, :]
    order_in = jnp.dot(
        routed.astype(BF), earlier.astype(BF), preferred_element_type=F32
    ).astype(jnp.int32)
    weight = jnp.sum(jnp.where(chosen, gates.T[None, :, :], 0.0), axis=1)
    slot_ids = jnp.arange(capacity, dtype=jnp.int32)
    hits = routed[:, None, :] & (order_in[:, None, :] == slot_ids[None, :, None])
    slot_weight = jnp.sum(jnp.where(hits, weight[:, None, :], 0.0), axis=2)
    return chosen, hits.reshape(groups * capacity, tok_rows), slot_weight.reshape(-1)


def exchange(rows, groups):
    shaped = rows.reshape(groups, rows.shape[0] // groups, rows.shape[1])
    out = lax.all_to_all(shaped, ("node", "local"), split_axis=0, concat_axis=0, tiled=True)
    return out.reshape(rows.shape)


def gathered(shard):
    count = lax.axis_size("edata")
    shards = [shard]
    for step in range(1, count):
        pairs = [((i + step) % count, i) for i in range(count)]
        shards.append(lax.ppermute(shard, "edata", pairs))
    return shards


def reduced(part):
    count = lax.axis_size("edata")
    size = part.shape[0] // count
    total = part[:size].astype(F32)
    for step in range(1, count):
        pairs = [(i, (i + step) % count) for i in range(count)]
        piece = lax.ppermute(part[step * size : (step + 1) * size], "edata", pairs)
        total = total + piece.astype(F32)
    return total


def backward_kernel(count, act_ref, dy_ref, *refs):
    outs, ins = refs[:count], refs[count : 2 * count]
    act_grad_ref, dx_ref = refs[2 * count :]
    hidden = act_ref.shape[1] // 2
    width = dy_ref.shape[1] // count
    inner_grad = jnp.dot(dy_ref[:, :width], outs[0][...], preferred_element_type=F32)
    for s in range(1, count):
        inner_grad += jnp.dot(
            dy_ref[:, s * width : (s + 1) * width], outs[s][...], preferred_element_type=F32
        )
    act_gate = act_ref[:, :hidden]
    act_up = act_ref[:, hidden:]
    sig = jax.nn.sigmoid(act_gate)
    act_grad_ref[:, :hidden] = (
        inner_grad * act_up * sig * (1.0 + act_gate * (1.0 - sig))
    ).astype(BF)
    act_grad_ref[:, hidden:] = (inner_grad * (act_gate * sig)).astype(BF)
    for s in range(count):
        dx_ref[:, s * width : (s + 1) * width] = lax.dot_general(
            act_grad_ref[...], ins[s][...], COLS_IN, preferred_element_type=F32
        ).astype(BF)


def expert_backward(activation, dy_recv, w_outs, w_ins):
    rows, width = dy_recv.shape
    double = activation.shape[1]
    block = min(rows, 256)

    def whole(shard):
        return pl.BlockSpec(shard.shape, lambda i: (0, 0), pipeline_mode=pl.Buffered(1))

    def band(columns):
        return pl.BlockSpec((block, columns), lambda i: (i, 0))

    return pl.pallas_call(
        lambda *refs: backward_kernel(len(w_ins), *refs),
        grid=(rows // block,),
        in_specs=[band(double), band(width)] + [whole(s) for s in (*w_outs, *w_ins)],
        out_specs=[band(double), band(width)],
        out_shape=[
            jax.ShapeDtypeStruct((rows, double), BF),
            jax.ShapeDtypeStruct((rows, width), BF),
        ],
        compiler_params=pltpu.CompilerParams(vmem_limit_bytes=LIMIT),
        cost_estimate=CHEAP,
        name="expert_backward",
    )(activation, dy_recv, *w_outs, *w_ins)


def combine_kernel(turn_ref, pick_ref, rows_ref, out_ref):
    out_ref[...] = lax.dot_general(
        pick_ref[...], rows_ref[...], ROWS_IN, preferred_element_type=F32
    ).astype(BF)


def combine(pick, rows, position):
    slots, tok_rows = pick.shape
    width = rows.shape[1]
    count = lax.axis_size("edata")
    tile = min(512, width // count)
    steps = width // tile
    per_shard = steps // count
    return pl.pallas_call(
        combine_kernel,
        grid_spec=pltpu.PrefetchScalarGridSpec(
            num_scalar_prefetch=1,
            grid=(steps,),
            in_specs=[
                pl.BlockSpec((slots, tok_rows), lambda i, t: (0, 0)),
                pl.BlockSpec((slots, tile), lambda i, t: (0, i)),
            ],
            out_specs=pl.BlockSpec((tok_rows, tile), lambda i, t: (0, (i + t[0]) % steps)),
        ),
        out_shape=jax.ShapeDtypeStruct((tok_rows, width), BF),
        compiler_params=pltpu.CompilerParams(vmem_limit_bytes=LIMIT),
        cost_estimate=CHEAP,
        name="combine",
    )((position * per_shard).astype(jnp.int32).reshape(1), pick, rows)


def shards(tokens, out_grad, expert_ids, gates, w_gate_up, w_down):
    groups = lax.axis_size("node") * lax.axis_size("local")
    tok_rows, model_width = tokens.shape
    hidden = w_down.shape[2]
    capacity = tok_rows * expert_ids.shape[1] // (EXP_DEV * groups)
    position = lax.axis_index("edata")
    turn = position * w_down.shape[1]
    w_ins = gathered(w_gate_up[0])
    w_outs = gathered(w_down[0])
    chosen, hits, slot_weight = slot_tables(expert_ids, gates, groups, capacity)
    pick = hits.astype(BF)
    x_send = jnp.dot(pick, jnp.roll(tokens, -turn, axis=1), preferred_element_type=F32).astype(BF)
    x_recv = exchange(x_send, groups)
    grad_rows = jnp.dot(pick, jnp.roll(out_grad, -turn, axis=1), preferred_element_type=F32)
    dy_send = (slot_weight[:, None] * grad_rows).astype(BF)
    dy_recv = exchange(dy_send, groups)

    w_in = jnp.concatenate(w_ins, axis=0)
    w_out = jnp.concatenate(w_outs, axis=0)
    activation = jnp.dot(x_recv, w_in, preferred_element_type=F32)
    act_gate = activation[:, :hidden]
    act_up = activation[:, hidden:]
    inner_act = (act_gate * jax.nn.sigmoid(act_gate) * act_up).astype(BF)
    expert_out = lax.dot_general(inner_act, w_out, COLS_IN, preferred_element_type=F32).astype(BF)
    expert_out, dy_recv = lax.optimization_barrier((expert_out, dy_recv))
    y_back = exchange(expert_out, groups)

    act_grad, copy_grad = expert_backward(activation, dy_recv, w_outs, w_ins)
    copy_grad, y_back = lax.optimization_barrier((copy_grad, y_back))
    dx_back = exchange(copy_grad, groups)

    dy_recv, act_grad = lax.optimization_barrier((dy_recv, act_grad))
    part_down = lax.dot_general(dy_recv, inner_act, ROWS_IN, preferred_element_type=F32).astype(BF)
    grad_down = reduced(part_down)
    part_in = lax.dot_general(x_recv, act_grad, ROWS_IN, preferred_element_type=F32).astype(BF)
    grad_in = reduced(part_in)

    spread = jnp.where(hits, slot_weight[:, None], 0.0)
    high = lax.reduce_precision(spread, 8, 7)
    middle = lax.reduce_precision(spread - high, 8, 7)
    low = spread - high - middle
    high, middle, low = high.astype(BF), middle.astype(BF), low.astype(BF)
    mixed = (
        lax.dot_general(high, y_back, ROWS_IN, preferred_element_type=F32)
        + lax.dot_general(middle, y_back, ROWS_IN, preferred_element_type=F32)
        + lax.dot_general(low, y_back, ROWS_IN, preferred_element_type=F32)
    ).astype(BF)
    mixed = jnp.roll(mixed, turn, axis=1)
    slot_dots = jnp.sum(y_back.astype(F32) * grad_rows, axis=1)
    token_dots = jnp.sum(
        jnp.where(hits, slot_dots[:, None], 0.0).reshape(groups, capacity, tok_rows), axis=1
    )
    gate_grad = jnp.sum(jnp.where(chosen, token_dots[:, None, :], 0.0), axis=0).T
    dx_back, grad_in, grad_down, mixed, gate_grad = lax.optimization_barrier(
        (dx_back, grad_in, grad_down, mixed, gate_grad)
    )
    token_grad = combine(pick, dx_back, position)
    return (mixed, token_grad, gate_grad, grad_in[None], grad_down[None])


def solution(mesh):
    rows = P(("node", "local", "edata"), None)
    weights = P(("node", "local"), "edata", None)
    return jax.shard_map(
        shards,
        mesh=mesh,
        in_specs=(rows, rows, rows, rows, weights, weights),
        out_specs=(rows, rows, rows, weights, weights),
        check_vma=False,
    )
```

time: 423 us -> 229 us (0.54)
  waiting for transfers between devices: 253 us -> 132 us
  starting transfers between devices: 96.3 us -> 22 us
  Pallas kernels: 0 us -> 14.1 us
  local copies, waits for them, and re-layouts: 23.1 us -> 10.1 us
    ppermute x60 -> x0, waiting for transfers between devices: 253 us -> none  [exchange(): lax.ppermute(rows[j * size:(j + 1) * size], ('node', 'local'), pairs)]
    all_to_all x0 -> x4, waiting for transfers between devices: none -> 132 us  [exchange(): lax.all_to_all(shaped, ('node', 'local'), split_axis=0, concat_axis=0, ti...]
    ppermute x60 -> x0, starting transfers between devices: 95.2 us -> none  [exchange(): lax.ppermute(rows[j * size:(j + 1) * size], ('node', 'local'), pairs)]
    all_to_all x0 -> x4, starting transfers between devices: none -> 21.4 us  [exchange(): lax.all_to_all(shaped, ('node', 'local'), split_axis=0, concat_axis=0, ti...]
    pallas_call x0 -> x2, Pallas kernels: none -> 14.1 us  [the longest x1 11.6 us: expert_backward(): pl.pallas_call(lambda *refs: backward_kernel(len(w_ins), *refs), grid=(ro...]
    dot_general x5 -> x2, matrix products: 18.2 us -> 6.98 us  [the longest x1 3.63 us: shards(): jnp.dot(pick, jnp.roll(out_grad, -turn, axis=1), preferred_element_type=F32)]
    unnamed x86 -> x30, local copies, waits for them, and re-layouts: 14.2 us -> 6.08 us
  transfers between devices with their start and end apart: 64 -> 8, of which waited for: 48 -> 4; matrix products, arithmetic and copies ran while one was open for 14% -> 21% of each run, Pallas kernels for 0% -> 5%
where the time goes in v4:
time: 229 us; the launch traced here: 228 us
  waiting for transfers between devices  132 us (58%)
  matrix products  30.9 us (13%)
  starting transfers between devices  22 us (10%)
  other arithmetic  18.7 us (8%)
  Pallas kernels  14.1 us (6%)
  local copies, waits for them, and re-layouts  10.1 us (4%)
    all_to_all x4, waiting for transfers between devices, exchange(): lax.all_to_all(shaped, ('node', 'local'), split_axis=0, concat_axis=0, ti...  132 us
    all_to_all x4, starting transfers between devices, exchange(): lax.all_to_all(shaped, ('node', 'local'), split_axis=0, concat_axis=0, ti...  21.4 us
    pallas_call x1, Pallas kernels, expert_backward(): pl.pallas_call(lambda *refs: backward_kernel(len(w_ins), *refs), grid=(ro...  11.6 us
    add x2, other arithmetic, reduced(): total = total + piece.astype(F32)  10.5 us
    dot_general x1, matrix products, shards(): activation = jnp.dot(x_recv, w_in, preferred_element_type=F32)  6.19 us
    unnamed x30, local copies, waits for them, and re-layouts  6.08 us
  transfers between devices with their start and end apart: 8, of which 4 were waited for; matrix products, arithmetic and copies ran while one was open for 21% of the time, Pallas kernels for 5%

profile of v4, /device:TPU:0, one launch (start us, length us, event | category | flops | bytes accessed | tf_op | source)
XLA Modules:
  0.0 228.5 jit_solution(16686984584679953575)
XLA Ops:
  1.8 3.3 %convolution_convert_fusion.2 = bf16[512,2048]{1,0:T(8,128)(2,1)} fusion(pred[512,256]{1,0:T(32,128)(4,1)S(1)} %get-tuple-element.33, s32[]{:T(128)S(6)} %select_n.40, bf16[256,2048]{1,0:T(8,128)(2,1)} %param.8), kind=kOutput, calls=%fused_computation.15 | convolution fusion | flops 540016640 | bytes 3276804 | tf_op jit(solution)/shard_map/dot_general | solution.py:151
  5.2 8.4 %all-to-all-start = ((bf16[16,32,2048]{2,1,0:T(8,128)(2,1)}), bf16[16,32,2048]{2,1,0:T(8,128)(2,1)S(1)}, u32[]{:S(2)}, u32[]{:S(2)}) async-start(bf16[16,32,2048]{2,1,0:T(8,128)(2,1)} %bitcast.49), calls=%async_computation | async-start | bytes 4194304 | tf_op jit(solution)/shard_map/all_to_all | solution.py:36
  13.7 0.8 select_reduce_fusion.3
  14.5 1.5 select_reduce_fusion.1
  16.0 0.8 mul.28
  16.7 3.6 %multiply_convert_fusion = (bf16[512,2048]{1,0:T(8,128)(2,1)}, f32[512,2048]{1,0:T(8,128)}) fusion(f32[512]{0:T(512)S(1)} %mul.28, pred[512,256]{1,0:T(32,128)(4,1)S(1)} %get-tuple-element.33, s32[]{:T(128)S(6)} %select_n.40, bf16[256,2048]{1,0:T(8,128)(2,1)S(1)} %copy-done.7), kind=kOutput, calls=%fused_computation.7 | convolution fusion | flops 541065216 | bytes 7473156 | tf_op jit(solution)/shard_map/dot_general | solution.py:153
  20.4 43.2 %all-to-all-done = bf16[16,32,2048]{2,1,0:T(8,128)(2,1)S(1)} async-done(((bf16[16,32,2048]{2,1,0:T(8,128)(2,1)}), bf16[16,32,2048]{2,1,0:T(8,128)(2,1)S(1)}, u32[]{:S(2)}, u32[]{:S(2)}) %all-to-all-start) | async-done | bytes 2097184 | tf_op jit(solution)/shard_map/all_to_all | solution.py:36
  63.6 1.3 copy-done.5
  64.9 4.6 %all-to-all-start.1 = ((bf16[16,32,2048]{2,1,0:T(8,128)(2,1)}), bf16[16,32,2048]{2,1,0:T(8,128)(2,1)}, u32[]{:S(2)}, u32[]{:S(2)}) async-start(bf16[16,32,2048]{2,1,0:T(8,128)(2,1)} %bitcast.42), calls=%async_computation.1 | async-start | bytes 4194304 | tf_op jit(solution)/shard_map/all_to_all | solution.py:36
  69.6 6.2 %fusion.refs_0_ = f32[512,1536]{1,0:T(8,128)S(1)} fusion(bf16[512,2048]{1,0:T(8,128)(2,1)} %bitcast.46, bf16[1024,1536]{1,0:T(8,128)(2,1)} %collective-permute-done.refs_5_, bf16[1024,1536]{1,0:T(8,128)(2,1)} %bitcast.5.refs_4_), kind=kOutput, calls=%fused_computation.1 | convolution fusion | flops 3233808384 | bytes 11534336 | tf_op jit(solution)/shard_map/dot_general | solution.py:159
  76.3 1.2 copy-done.2
  77.7 3.1 %fusion.8 = bf16[512,2048]{1,0:T(8,128)(2,1)} fusion(bf16[512,768]{1,0:T(8,128)(2,1)S(1)} %fusion.12, bf16[1024,768]{1,0:T(8,128)(2,1)S(1)} %collective-permute-done.1.refs_3_, bf16[1024,768]{1,0:T(8,128)(2,1)S(1)} %bitcast.40), kind=kOutput, calls=%fused_computation.14 | convolution fusion | flops 1617952768 | bytes 6029312 | tf_op jit(solution)/shard_map/dot_general | solution.py:163
  80.8 38.1 %all-to-all-done.1 = bf16[16,32,2048]{2,1,0:T(8,128)(2,1)} async-done(((bf16[16,32,2048]{2,1,0:T(8,128)(2,1)}), bf16[16,32,2048]{2,1,0:T(8,128)(2,1)}, u32[]{:S(2)}, u32[]{:S(2)}) %all-to-all-start.1) | async-done | bytes 2097184 | tf_op jit(solution)/shard_map/all_to_all | solution.py:36
  118.9 4.6 %all-to-all-start.2 = ((bf16[16,32,2048]{2,1,0:T(8,128)(2,1)}), bf16[16,32,2048]{2,1,0:T(8,128)(2,1)}, u32[]{:S(2)}, u32[]{:S(2)}) async-start(bf16[16,32,2048]{2,1,0:T(8,128)(2,1)} %bitcast.48), calls=%async_computation.2 | async-start | bytes 4194304 | tf_op jit(solution)/shard_map/all_to_all | solution.py:36
  123.6 11.6 %expert_backward.1 = (bf16[512,1536]{1,0:T(8,128)(2,1)S(1)}, bf16[512,2048]{1,0:T(8,128)(2,1)}) custom-call(f32[512,1536]{1,0:T(8,128)} %copy-done.2, bf16[512,2048]{1,0:T(8,128)(2,1)} %bitcast.9.refs_1_, bf16[1024,768]{1,0:T(8,128)(2,1)S(1)} %bitcast.41, bf16[1024,768]{1,0:T(8,128)(2,1)S(1)} %collective-permute-done.1.refs_3_, ...), custom_call_target="tpu_custom_call" | custom-call | flops 1 | bytes 1 | tf_op jit(solution)/shard_map/expert_backward/pallas_call | solution.py:94
  135.1 3.7 %convolution_convert_fusion = bf16[2048,1536]{1,0:T(8,128)(2,1)S(1)} fusion(bf16[512,2048]{1,0:T(8,128)(2,1)S(1)} %bitcast.47, bf16[512,1536]{1,0:T(8,128)(2,1)S(1)} %get-tuple-element.24), kind=kOutput, calls=%fused_computation | convolution fusion | flops 3224371200 | bytes 9961472 | tf_op jit(solution)/shard_map/dot_general | solution.py:174
  138.9 1.9 slice.27
  140.7 1.7 copy-done.3
  142.4 3.4 %convolution_convert_fusion.1 = bf16[2048,768]{1,0:T(8,128)(2,1)S(1)} fusion(bf16[512,2048]{1,0:T(8,128)(2,1)} %bitcast.9.refs_1_, bf16[512,768]{1,0:T(8,128)(2,1)S(1)} %copy-done.9), kind=kOutput, calls=%fused_computation.8 | convolution fusion | flops 1612185600 | bytes 6029312 | tf_op jit(solution)/shard_map/dot_general | solution.py:172
  145.9 1.6 copy-done.4
  147.5 1.2 slice.29
  149.2 23.6 %all-to-all-done.2 = bf16[16,32,2048]{2,1,0:T(8,128)(2,1)} async-done(((bf16[16,32,2048]{2,1,0:T(8,128)(2,1)}), bf16[16,32,2048]{2,1,0:T(8,128)(2,1)}, u32[]{:S(2)}, u32[]{:S(2)}) %all-to-all-start.2) | async-done | bytes 2097184 | tf_op jit(solution)/shard_map/all_to_all | solution.py:36
  172.8 3.7 %all-to-all-start.3 = ((bf16[16,32,2048]{2,1,0:T(8,128)(2,1)}), bf16[16,32,2048]{2,1,0:T(8,128)(2,1)S(1)}, u32[]{:S(2)}, u32[]{:S(2)}) async-start(bf16[16,32,2048]{2,1,0:T(8,128)(2,1)} %bitcast.45), calls=%async_computation.3 | async-start | bytes 4194304 | tf_op jit(solution)/shard_map/all_to_all | solution.py:36
  176.6 3.9 %convert_add_fusion.1 = f32[1024,768]{1,0:T(8,128)} fusion(bf16[1024,768]{1,0:T(8,128)(2,1)} %collective-permute-done.3, bf16[2048,768]{1,0:T(8,128)(2,1)} %copy-done.4), kind=kLoop, calls=%fused_computation.13 | loop fusion | flops 2359296 | bytes 6291456 | tf_op jit(solution)/shard_map/add | solution.py:56
  180.5 6.6 %convert_add_fusion = f32[1024,1536]{1,0:T(8,128)} fusion(bf16[1024,1536]{1,0:T(8,128)(2,1)} %collective-permute-done.2, bf16[2048,1536]{1,0:T(8,128)(2,1)} %copy-done.3), kind=kLoop, calls=%fused_computation.5 | loop fusion | flops 4718592 | bytes 12582912 | tf_op jit(solution)/shard_map/add | solution.py:56
  187.1 2.2 multiply_reduce_fusion
  190.2 2.4 %fusion.23 = f32[256,2048]{1,0:T(8,128)S(1)} fusion(bf16[512,2048]{1,0:T(8,128)(2,1)} %bitcast.11, pred[512,256]{1,0:T(32,128)(4,1)S(1)} %get-tuple-element.33, f32[512]{0:T(512)S(1)} %mul.28), kind=kOutput, calls=%fused_computation.43 | convolution fusion | flops 537264128 | bytes 4327424 | tf_op jit(solution)/shard_map/dot_general | solution.py:183
  192.6 2.4 %convolution_add_fusion.1 = f32[256,2048]{1,0:T(8,128)S(1)} fusion(f32[256,2048]{1,0:T(8,128)S(1)} %fusion.23, bf16[512,2048]{1,0:T(8,128)(2,1)} %bitcast.11, pred[512,256]{1,0:T(32,128)(4,1)S(1)} %get-tuple-element.33, f32[512]{0:T(512)S(1)} %mul.28), kind=kOutput, calls=%fused_computation.17 | convolution fusion | flops 538050560 | bytes 6424576 | tf_op jit(solution)/shard_map/dot_general | solution.py:184
  195.0 2.5 %fusion.11 = bf16[256,2048]{1,0:T(8,128)(2,1)S(1)} fusion(f32[256,2048]{1,0:T(8,128)S(1)} %convolution_add_fusion.1, bf16[512,2048]{1,0:T(8,128)(2,1)} %bitcast.11, pred[512,256]{1,0:T(32,128)(4,1)S(1)} %get-tuple-element.33, f32[512]{0:T(512)S(1)} %mul.28), kind=kOutput, calls=%fused_computation.18 | convolution fusion | flops 538705920 | bytes 5376000 | tf_op jit(solution)/shard_map/dot_general | solution.py:185
  197.5 1.6 fusion.13
  199.1 26.9 %all-to-all-done.3 = bf16[16,32,2048]{2,1,0:T(8,128)(2,1)S(1)} async-done(((bf16[16,32,2048]{2,1,0:T(8,128)(2,1)}), bf16[16,32,2048]{2,1,0:T(8,128)(2,1)S(1)}, u32[]{:S(2)}, u32[]{:S(2)}) %all-to-all-start.3) | async-done | bytes 2097184 | tf_op jit(solution)/shard_map/all_to_all | solution.py:36
  225.9 2.5 %combine.1 = bf16[256,2048]{1,0:T(8,128)(2,1)} custom-call(s32[1]{0:T(128)} %bitcast.15.turn_ref, bf16[512,256]{1,0:T(8,128)(2,1)S(1)} %get-tuple-element.32.pick_ref, bf16[512,2048]{1,0:T(8,128)(2,1)S(1)} %bitcast.38), custom_call_target="tpu_custom_call" | custom-call | flops 1 | bytes 1 | tf_op jit(solution)/shard_map/combine/pallas_call | solution.py:122
  (43 shorter events, 3.5 us)
Async XLA Ops:
  1.4 3.8 %copy-start.13 = (pred[16,256]{1,0:T(8,128)(4,1)}, pred[16,256]{1,0:T(8,128)(4,1)S(1)}, u32[]{:S(2)}) copy-start(pred[16,256]{1,0:T(8,128)(4,1)S(1)} %fusion.30) | copy-start | bytes 12292
  1.7 12.8 %copy-start.10 = (s32[16,256]{1,0:T(8,128)}, s32[16,256]{1,0:T(8,128)S(1)}, u32[]{:S(2)}) copy-start(s32[16,256]{1,0:T(8,128)S(1)} %convolution_convert_fusion.3) | copy-start | bytes 49156
  5.2 11.5 %copy-start.7 = (bf16[256,2048]{1,0:T(8,128)(2,1)S(1)}, bf16[256,2048]{1,0:T(8,128)(2,1)}, u32[]{:S(2)}) copy-start(bf16[256,2048]{1,0:T(8,128)(2,1)} %param.9) | copy-start | bytes 3145732
  5.2 58.4 %all-to-all-start = ((bf16[16,32,2048]{2,1,0:T(8,128)(2,1)}), bf16[16,32,2048]{2,1,0:T(8,128)(2,1)S(1)}, u32[]{:S(2)}, u32[]{:S(2)}) async-start(bf16[16,32,2048]{2,1,0:T(8,128)(2,1)} %bitcast.49), calls=%async_computation | async-start | bytes 4194304 | tf_op jit(solution)/shard_map/all_to_all | solution.py:36
  13.7 55.9 %collective-permute-start = (bf16[1024,1536]{1,0:T(8,128)(2,1)}, bf16[1024,1536]{1,0:T(8,128)(2,1)}, u32[]{:S(2)}, u32[]{:S(2)}) collective-permute-start(bf16[1024,1536]{1,0:T(8,128)(2,1)} %bitcast.5.refs_4_), channel_id=1, source_target_pairs={{1,0},{0,1},{3,2},{2,3},{5,4},{4,5},{7,6},{6,7},{9,8},{8,9},{11,10... | collective-permute-start | bytes 9437192 | tf_op jit(solution)/shard_map/ppermute | solution.py:45
  63.6 1.3 copy-start.5
  64.9 4.6 %copy-start = (bf16[1,1024,768]{2,1,0:T(8,128)(2,1)S(1)}, bf16[1,1024,768]{2,1,0:T(8,128)(2,1)}, u32[]{:S(2)}) copy-start(bf16[1,1024,768]{2,1,0:T(8,128)(2,1)} %param.13) | copy-start | bytes 4718596
  64.9 54.0 %all-to-all-start.1 = ((bf16[16,32,2048]{2,1,0:T(8,128)(2,1)}), bf16[16,32,2048]{2,1,0:T(8,128)(2,1)}, u32[]{:S(2)}, u32[]{:S(2)}) async-start(bf16[16,32,2048]{2,1,0:T(8,128)(2,1)} %bitcast.42), calls=%async_computation.1 | async-start | bytes 4194304 | tf_op jit(solution)/shard_map/all_to_all | solution.py:36
  69.5 6.8 %collective-permute-start.1 = (bf16[1024,768]{1,0:T(8,128)(2,1)S(1)}, bf16[1024,768]{1,0:T(8,128)(2,1)S(1)}, u32[]{:S(2)}, u32[]{:S(2)}) collective-permute-start(bf16[1024,768]{1,0:T(8,128)(2,1)S(1)} %bitcast.39), channel_id=1, source_target_pairs={{1,0},{0,1},{3,2},{2,3},{5,4},{4,5},{7,6},{6,7},{9,8},{8,9},{11,10... | collective-permute-start | bytes 4718600 | tf_op jit(solution)/shard_map/ppermute | solution.py:45
  75.8 1.7 copy-start.2
  76.3 1.4 copy-start.8
  118.9 53.9 %all-to-all-start.2 = ((bf16[16,32,2048]{2,1,0:T(8,128)(2,1)}), bf16[16,32,2048]{2,1,0:T(8,128)(2,1)}, u32[]{:S(2)}, u32[]{:S(2)}) async-start(bf16[16,32,2048]{2,1,0:T(8,128)(2,1)} %bitcast.48), calls=%async_computation.2 | async-start | bytes 4194304 | tf_op jit(solution)/shard_map/all_to_all | solution.py:36
  123.6 11.6 %copy-start.6 = (bf16[16,32,2048]{2,1,0:T(8,128)(2,1)S(1)}, bf16[16,32,2048]{2,1,0:T(8,128)(2,1)}, u32[]{:S(2)}) copy-start(bf16[16,32,2048]{2,1,0:T(8,128)(2,1)} %copy-done.5) | copy-start | bytes 6291460
  138.8 3.6 %copy-start.3 = (bf16[2048,1536]{1,0:T(8,128)(2,1)}, bf16[2048,1536]{1,0:T(8,128)(2,1)S(1)}, u32[]{:S(2)}) copy-start(bf16[2048,1536]{1,0:T(8,128)(2,1)S(1)} %convolution_convert_fusion) | copy-start | bytes 18874372
  138.8 3.6 %copy-start.9 = (bf16[512,768]{1,0:T(8,128)(2,1)S(1)}, bf16[512,768]{1,0:T(8,128)(2,1)}, u32[]{:S(2)}) copy-start(bf16[512,768]{1,0:T(8,128)(2,1)} %copy-done.8) | copy-start | bytes 2359300
  142.4 38.0 %collective-permute-start.2 = (bf16[1024,1536]{1,0:T(8,128)(2,1)}, bf16[1024,1536]{1,0:T(8,128)(2,1)}, u32[]{:S(2)}, u32[]{:S(2)}) collective-permute-start(bf16[1024,1536]{1,0:T(8,128)(2,1)} %slice.27), channel_id=1, source_target_pairs={{0,1},{1,0},{2,3},{3,2},{4,5},{5,4},{6,7},{7,6},{8,9},{9,8},{10,11... | collective-permute-start | bytes 9437192 | tf_op jit(solution)/shard_map/ppermute | solution.py:55
  145.9 1.6 copy-start.4
  148.7 27.8 %collective-permute-start.3 = (bf16[1024,768]{1,0:T(8,128)(2,1)}, bf16[1024,768]{1,0:T(8,128)(2,1)}, u32[]{:S(2)}, u32[]{:S(2)}) collective-permute-start(bf16[1024,768]{1,0:T(8,128)(2,1)} %slice.29), channel_id=1, source_target_pairs={{0,1},{1,0},{2,3},{3,2},{4,5},{5,4},{6,7},{7,6},{8,9},{9,8},{10,11... | collective-permute-start | bytes 4718600 | tf_op jit(solution)/shard_map/ppermute | solution.py:55
  172.8 53.1 %all-to-all-start.3 = ((bf16[16,32,2048]{2,1,0:T(8,128)(2,1)}), bf16[16,32,2048]{2,1,0:T(8,128)(2,1)S(1)}, u32[]{:S(2)}, u32[]{:S(2)}) async-start(bf16[16,32,2048]{2,1,0:T(8,128)(2,1)} %bitcast.45), calls=%async_computation.3 | async-start | bytes 4194304 | tf_op jit(solution)/shard_map/all_to_all | solution.py:36
  180.5 6.6 %copy-start.1 = (f32[512,2048]{1,0:T(8,128)S(1)}, f32[512,2048]{1,0:T(8,128)}, u32[]{:S(2)}) copy-start(f32[512,2048]{1,0:T(8,128)} %get-tuple-element.35) | copy-start | bytes 12582916
  187.1 2.3 copy-start.11
  187.1 2.3 copy-start.14
  187.1 2.5 %copy-start.12 = (s32[256,8]{0,1:T(8,128)S(1)}, s32[256,8]{0,1:T(8,128)}, u32[]{:S(2)}) copy-start(s32[256,8]{0,1:T(8,128)} %param.10) | copy-start | bytes 24580

commit v5 on v4

--- a/solution.py
+++ b/solution.py
@@ -14,9 +14,8 @@
 CHEAP = pl.CostEstimate(flops=1, bytes_accessed=1, transcendentals=0)
 
 
-def slot_tables(expert_ids, gates, groups, capacity):
+def slot_tables(expert_ids, gates, numbers, capacity):
     tok_rows = expert_ids.shape[0]
-    numbers = jnp.arange(groups, dtype=jnp.int32)
     ids_t = expert_ids.T
     chosen = ids_t[None, :, :] == numbers[:, None, None]
     routed = jnp.any(chosen, axis=1)
@@ -28,13 +27,39 @@
     slot_ids = jnp.arange(capacity, dtype=jnp.int32)
     hits = routed[:, None, :] & (order_in[:, None, :] == slot_ids[None, :, None])
     slot_weight = jnp.sum(jnp.where(hits, weight[:, None, :], 0.0), axis=2)
-    return chosen, hits.reshape(groups * capacity, tok_rows), slot_weight.reshape(-1)
-
-
-def exchange(rows, groups):
-    shaped = rows.reshape(groups, rows.shape[0] // groups, rows.shape[1])
-    out = lax.all_to_all(shaped, ("node", "local"), split_axis=0, concat_axis=0, tiled=True)
+    return chosen, hits.reshape(numbers.shape[0] * capacity, tok_rows), slot_weight.reshape(-1)
+
+
+def after(value, *others):
+    return lax.optimization_barrier((value, *others))[0]
+
+
+def to_plane(rows, distance):
+    if distance == 0:
+        return rows
+    pairs = [(i, i ^ distance) for i in range(lax.axis_size("local"))]
+    return lax.ppermute(rows, "local", pairs)
+
+
+def over_nodes(rows):
+    nodes = lax.axis_size("node")
+    shaped = rows.reshape(nodes, rows.shape[0] // nodes, rows.shape[1])
+    out = lax.all_to_all(shaped, "node", split_axis=0, concat_axis=0, tiled=True)
     return out.reshape(rows.shape)
+
+
+def joined(planes):
+    nodes = lax.axis_size("node")
+    width = planes[0].shape[1]
+    parts = [p.reshape(nodes, -1, width) for p in planes]
+    return jnp.concatenate(parts, axis=1).reshape(-1, width)
+
+
+def parted(rows, count):
+    nodes = lax.axis_size("node")
+    width = rows.shape[1]
+    shaped = rows.reshape(nodes, count, -1, width)
+    return [shaped[:, i].reshape(-1, width) for i in range(count)]
 
 
 def gathered(shard):
@@ -55,6 +80,54 @@
         piece = lax.ppermute(part[step * size : (step + 1) * size], "edata", pairs)
         total = total + piece.astype(F32)
     return total
+
+
+def whole(array):
+    return pl.BlockSpec(array.shape, lambda i: (0, 0), pipeline_mode=pl.Buffered(1))
+
+
+def forward_kernel(count, x_ref, *refs):
+    ins, outs = refs[:count], refs[count : 2 * count]
+    act_ref, inner_ref, y_ref = refs[2 * count :]
+    hidden = inner_ref.shape[1]
+    width = x_ref.shape[1] // count
+    activation = jnp.dot(x_ref[:, :width], ins[0][...], preferred_element_type=F32)
+    for s in range(1, count):
+        activation += jnp.dot(
+            x_ref[:, s * width : (s + 1) * width], ins[s][...], preferred_element_type=F32
+        )
+    act_ref[...] = activation
+    act_gate = act_ref[:, :hidden]
+    inner_ref[...] = (act_gate * jax.nn.sigmoid(act_gate) * act_ref[:, hidden:]).astype(BF)
+    for s in range(count):
+        y_ref[:, s * width : (s + 1) * width] = lax.dot_general(
+            inner_ref[...], outs[s][...], COLS_IN, preferred_element_type=F32
+        ).astype(BF)
+
+
+def expert_forward(x_recv, w_ins, w_outs):
+    rows, width = x_recv.shape
+    double = w_ins[0].shape[1]
+    hidden = w_outs[0].shape[1]
+    block = min(rows, 256)
+
+    def band(columns):
+        return pl.BlockSpec((block, columns), lambda i: (i, 0))
+
+    return pl.pallas_call(
+        lambda *refs: forward_kernel(len(w_ins), *refs),
+        grid=(rows // block,),
+        in_specs=[band(width)] + [whole(s) for s in (*w_ins, *w_outs)],
+        out_specs=[band(double), band(hidden), band(width)],
+        out_shape=[
+            jax.ShapeDtypeStruct((rows, double), F32),
+            jax.ShapeDtypeStruct((rows, hidden), BF),
+            jax.ShapeDtypeStruct((rows, width), BF),
+        ],
+        compiler_params=pltpu.CompilerParams(vmem_limit_bytes=LIMIT),
+        cost_estimate=CHEAP,
+        name="expert_forward",
+    )(x_recv, *w_ins, *w_outs)
 
 
 def backward_kernel(count, act_ref, dy_ref, *refs):
@@ -80,13 +153,10 @@
         ).astype(BF)
 
 
-def expert_backward(activation, dy_recv, w_outs, w_ins):
+def expert_backward(activation, dy_recv, w_ins, w_outs):
     rows, width = dy_recv.shape
     double = activation.shape[1]
     block = min(rows, 256)
-
-    def whole(shard):
-        return pl.BlockSpec(shard.shape, lambda i: (0, 0), pipeline_mode=pl.Buffered(1))
 
     def band(columns):
         return pl.BlockSpec((block, columns), lambda i: (i, 0))
@@ -106,15 +176,21 @@
     )(activation, dy_recv, *w_outs, *w_ins)
 
 
-def combine_kernel(turn_ref, pick_ref, rows_ref, out_ref):
-    out_ref[...] = lax.dot_general(
-        pick_ref[...], rows_ref[...], ROWS_IN, preferred_element_type=F32
-    ).astype(BF)
-
-
-def combine(pick, rows, position):
+def combine_kernel(turn_ref, pick_ref, *refs):
+    planes, out_ref = refs[:-1], refs[-1]
+    size = planes[0].shape[0]
+    total = None
+    for i, plane in enumerate(planes):
+        part = lax.dot_general(
+            pick_ref[i * size : (i + 1) * size], plane[...], ROWS_IN, preferred_element_type=F32
+        )
+        total = part if total is None else total + part
+    out_ref[...] = total.astype(BF)
+
+
+def combine(pick, planes, position):
     slots, tok_rows = pick.shape
-    width = rows.shape[1]
+    size, width = planes[0].shape
     count = lax.axis_size("edata")
     tile = min(512, width // count)
     steps = width // tile
@@ -124,54 +200,79 @@
         grid_spec=pltpu.PrefetchScalarGridSpec(
             num_scalar_prefetch=1,
             grid=(steps,),
-            in_specs=[
-                pl.BlockSpec((slots, tok_rows), lambda i, t: (0, 0)),
-                pl.BlockSpec((slots, tile), lambda i, t: (0, i)),
-            ],
+            in_specs=[pl.BlockSpec((slots, tok_rows), lambda i, t: (0, 0))]
+            + [pl.BlockSpec((size, tile), lambda i, t: (0, i)) for _ in planes],
             out_specs=pl.BlockSpec((tok_rows, tile), lambda i, t: (0, (i + t[0]) % steps)),
         ),
         out_shape=jax.ShapeDtypeStruct((tok_rows, width), BF),
         compiler_params=pltpu.CompilerParams(vmem_limit_bytes=LIMIT),
         cost_estimate=CHEAP,
         name="combine",
-    )((position * per_shard).astype(jnp.int32).reshape(1), pick, rows)
+    )((position * per_shard).astype(jnp.int32).reshape(1), pick, *planes)
 
 
 def shards(tokens, out_grad, expert_ids, gates, w_gate_up, w_down):
-    groups = lax.axis_size("node") * lax.axis_size("local")
+    nodes, planes = lax.axis_size("node"), lax.axis_size("local")
+    groups = nodes * planes
     tok_rows, model_width = tokens.shape
-    hidden = w_down.shape[2]
     capacity = tok_rows * expert_ids.shape[1] // (EXP_DEV * groups)
+    half = planes // 2
+    near, far = range(half), range(half, planes)
+    size = nodes * capacity
     position = lax.axis_index("edata")
     turn = position * w_down.shape[1]
     w_ins = gathered(w_gate_up[0])
     w_outs = gathered(w_down[0])
-    chosen, hits, slot_weight = slot_tables(expert_ids, gates, groups, capacity)
+    numbers = (
+        (lax.axis_index("local") ^ jnp.arange(planes, dtype=jnp.int32))[:, None]
+        + planes * jnp.arange(nodes, dtype=jnp.int32)[None, :]
+    ).reshape(-1)
+    chosen, hits, slot_weight = slot_tables(expert_ids, gates, numbers, capacity)
     pick = hits.astype(BF)
+
+    def cut(rows, d):
+        return rows[d * size : (d + 1) * size]
+
     x_send = jnp.dot(pick, jnp.roll(tokens, -turn, axis=1), preferred_element_type=F32).astype(BF)
-    x_recv = exchange(x_send, groups)
+    x_far = [to_plane(cut(x_send, d), d) for d in far]
+    x_near = [to_plane(cut(x_send, d), d) for d in near]
     grad_rows = jnp.dot(pick, jnp.roll(out_grad, -turn, axis=1), preferred_element_type=F32)
     dy_send = (slot_weight[:, None] * grad_rows).astype(BF)
-    dy_recv = exchange(dy_send, groups)
-
-    w_in = jnp.concatenate(w_ins, axis=0)
-    w_out = jnp.concatenate(w_outs, axis=0)
-    activation = jnp.dot(x_recv, w_in, preferred_element_type=F32)
-    act_gate = activation[:, :hidden]
-    act_up = activation[:, hidden:]
-    inner_act = (act_gate * jax.nn.sigmoid(act_gate) * act_up).astype(BF)
-    expert_out = lax.dot_general(inner_act, w_out, COLS_IN, preferred_element_type=F32).astype(BF)
-    expert_out, dy_recv = lax.optimization_barrier((expert_out, dy_recv))
-    y_back = exchange(expert_out, groups)
-
-    act_grad, copy_grad = expert_backward(activation, dy_recv, w_outs, w_ins)
-    copy_grad, y_back = lax.optimization_barrier((copy_grad, y_back))
-    dx_back = exchange(copy_grad, groups)
-
-    dy_recv, act_grad = lax.optimization_barrier((dy_recv, act_grad))
-    part_down = lax.dot_general(dy_recv, inner_act, ROWS_IN, preferred_element_type=F32).astype(BF)
+    dy_near = [to_plane(cut(dy_send, d), d) for d in near]
+
+    x1 = over_nodes(joined(x_near))
+    act1, inner1, y1 = expert_forward(x1, w_ins, w_outs)
+    dy1 = over_nodes(after(joined(dy_near), x1))
+    act_grad1, dx1 = expert_backward(act1, dy1, w_ins, w_outs)
+
+    dy_far = [to_plane(after(cut(dy_send, d), x), d) for d, x in zip(far, x_far)]
+    x2 = over_nodes(after(joined(x_far), dx1))
+    act2, inner2, y2 = expert_forward(x2, w_ins, w_outs)
+    y_parts = parted(over_nodes(y2), len(far))
+    y_far = [to_plane(after(y, dy), d) for d, y, dy in zip(far, y_parts, dy_far)]
+
+    dy2 = over_nodes(after(joined(dy_far), *y_parts))
+    act_grad2, dx2 = expert_backward(act2, dy2, w_ins, w_outs)
+    dx_parts = parted(over_nodes(dx2), len(far))
+    dx_far = [to_plane(after(dx, y), d) for d, dx, y in zip(far, dx_parts, y_far)]
+
+    y1 = after(y1, *dx_parts)
+    y_near = [to_plane(y, d) for d, y in zip(near, parted(over_nodes(y1), len(near)))]
+    dx1 = after(dx1, *y_near)
+    dx_near = [to_plane(dx, d) for d, dx in zip(near, parted(over_nodes(dx1), len(near)))]
+
+    dy1, dy2, act_grad1, act_grad2 = lax.optimization_barrier(
+        (dy1, dy2, act_grad1, act_grad2, *dx_parts)
+    )[:4]
+    part_down = (
+        lax.dot_general(dy1, inner1, ROWS_IN, preferred_element_type=F32)
+        + lax.dot_general(dy2, inner2, ROWS_IN, preferred_element_type=F32)
+    ).astype(BF)
     grad_down = reduced(part_down)
-    part_in = lax.dot_general(x_recv, act_grad, ROWS_IN, preferred_element_type=F32).astype(BF)
+    part_in = (
+        lax.dot_general(x1, act_grad1, ROWS_IN, preferred_element_type=F32)
+        + lax.dot_general(x2, act_grad2, ROWS_IN, preferred_element_type=F32)
+    ).astype(BF)
     grad_in = reduced(part_in)
 
     spread = jnp.where(hits, slot_weight[:, None], 0.0)
@@ -179,6 +280,7 @@
     middle = lax.reduce_precision(spread - high, 8, 7)
     low = spread - high - middle
     high, middle, low = high.astype(BF), middle.astype(BF), low.astype(BF)
+    y_back = jnp.concatenate(y_near + y_far, axis=0)
     mixed = (
         lax.dot_general(high, y_back, ROWS_IN, preferred_element_type=F32)
         + lax.dot_general(middle, y_back, ROWS_IN, preferred_element_type=F32)
@@ -190,10 +292,10 @@
         jnp.where(hits, slot_dots[:, None], 0.0).reshape(groups, capacity, tok_rows), axis=1
     )
     gate_grad = jnp.sum(jnp.where(chosen, token_dots[:, None, :], 0.0), axis=0).T
-    dx_back, grad_in, grad_down, mixed, gate_grad = lax.optimization_barrier(
-        (dx_back, grad_in, grad_down, mixed, gate_grad)
+    *dx_far, grad_in, grad_down, mixed, gate_grad = lax.optimization_barrier(
+        (*dx_far, grad_in, grad_down, mixed, gate_grad)
     )
-    token_grad = combine(pick, dx_back, position)
+    token_grad = combine(pick, dx_near + dx_far, position)
     return (mixed, token_grad, gate_grad, grad_in[None], grad_down[None])
 
 

time: 229 us -> 359 us (1.57)
  waiting for transfers between devices: 132 us -> 175 us
  blocking collectives: 0 us -> 30.7 us
  starting transfers between devices: 22 us -> 48.6 us
  Pallas kernels: 14.1 us -> 33.2 us
  local copies, waits for them, and re-layouts: 10.1 us -> 23.8 us
  matrix products: 30.9 us -> 22.8 us
  other arithmetic: 18.7 us -> 22.9 us
    ppermute x0 -> x12, waiting for transfers between devices: none -> 170 us  [to_plane(): return lax.ppermute(rows, 'local', pairs)]
    all_to_all x4 -> x6, waiting for transfers between devices: 132 us -> 4.65 us  [over_nodes(): lax.all_to_all(shaped, 'node', split_axis=0, concat_axis=0, tiled=True)]
    all_to_all x0 -> x2, blocking collectives: none -> 30.7 us  [over_nodes(): lax.all_to_all(shaped, 'node', split_axis=0, concat_axis=0, tiled=True)]
    ppermute x0 -> x12, starting transfers between devices: none -> 23.6 us  [to_plane(): return lax.ppermute(rows, 'local', pairs)]
    pallas_call x0 -> x2, Pallas kernels: none -> 14.1 us  [expert_forward(): pl.pallas_call(lambda *refs: forward_kernel(len(w_ins), *refs), grid=(row...]
    slice x0 -> x6, local copies, waits for them, and re-layouts: none -> 9.25 us  [the longest x4 6.87 us: parted(): return [shaped[:, i].reshape(-1, width) for i in range(count)]]
    dot_general x4, matrix products: 16.4 us -> 9.65 us  [the longest x1 4.52 us: shards(): lax.dot_general(x2, act_grad2, ROWS_IN, preferred_element_type=F32)]
    concatenate x0 -> x4, other arithmetic: none -> 5.41 us  [joined(): return jnp.concatenate(parts, axis=1).reshape(-1, width)]
  transfers between devices with their start and end apart: 8 -> 22, of which waited for: 4 -> 11; matrix products, arithmetic and copies ran while one was open for 21% -> 17% of each run, Pallas kernels for 5% -> 2%
where the time goes in v5:
time: 359 us; the launch traced here: 358 us
  waiting for transfers between devices  175 us (49%)
  starting transfers between devices  48.6 us (14%)
  Pallas kernels  33.2 us (9%)
  blocking collectives  30.7 us (9%)
  local copies, waits for them, and re-layouts  23.8 us (7%)
  other arithmetic  22.9 us (6%)
  matrix products  22.8 us (6%)
    ppermute x12, waiting for transfers between devices, to_plane(): return lax.ppermute(rows, 'local', pairs)  170 us
    all_to_all x2, blocking collectives, over_nodes(): lax.all_to_all(shaped, 'node', split_axis=0, concat_axis=0, tiled=True)  30.7 us
    all_to_all x6, starting transfers between devices, over_nodes(): lax.all_to_all(shaped, 'node', split_axis=0, concat_axis=0, tiled=True)  24.1 us
    ppermute x12, starting transfers between devices, to_plane(): return lax.ppermute(rows, 'local', pairs)  23.6 us
    pallas_call x2, Pallas kernels, expert_backward(): pl.pallas_call(lambda *refs: backward_kernel(len(w_ins), *refs), grid=(ro...  14.8 us
    pallas_call x2, Pallas kernels, expert_forward(): pl.pallas_call(lambda *refs: forward_kernel(len(w_ins), *refs), grid=(row...  14.1 us
    add x2, other arithmetic, reduced(): total = total + piece.astype(F32)  9.84 us
    unnamed x64, local copies, waits for them, and re-layouts  7.9 us
  transfers between devices with their start and end apart: 22, of which 11 were waited for; matrix products, arithmetic and copies ran while one was open for 17% of the time, Pallas kernels for 2%

profile of v5, /device:TPU:0, one launch (start us, length us, event | category | flops | bytes accessed | tf_op | source)
XLA Modules:
  0.0 357.8 jit_solution(11561617660663283056)
XLA Ops:
  9.4 4.1 %multiply_convert_fusion = (bf16[512,2048]{1,0:T(8,128)(2,1)S(1)}, f32[512,2048]{1,0:T(8,128)}) fusion(f32[512]{0:T(512)S(1)} %mul.29, pred[512,256]{1,0:T(32,128)(4,1)S(1)} %get-tuple-element.85, s32[]{:T(128)S(6)} %select_n.40, bf16[256,2048]{1,0:T(8,128)(2,1)} %param.9), kind=kOutput, calls=%fused_computation.4 | convolution fusion | flops 541065216 | bytes 7473156 | tf_op jit(solution)/shard_map/dot_general | solution.py:239
  13.4 8.0 %collective-permute-done.2 = bf16[128,2048]{1,0:T(8,128)(2,1)} collective-permute-done((bf16[128,2048]{1,0:T(8,128)(2,1)}, bf16[128,2048]{1,0:T(8,128)(2,1)}, u32[]{:S(2)}, u32[]{:S(2)}) %collective-permute-start.2) | collective-permute-done | bytes 524320 | tf_op jit(solution)/shard_map/ppermute | solution.py:41
  23.5 3.9 %all-to-all-start = ((bf16[4,64,2048]{2,1,0:T(8,128)(2,1)}), bf16[4,64,2048]{2,1,0:T(8,128)(2,1)S(1)}, u32[]{:S(2)}, u32[]{:S(2)}) async-start(bf16[4,64,2048]{2,1,0:T(8,128)(2,1)} %pad_maximum_fusion.2), calls=%async_computation | async-start | bytes 2097152 | tf_op jit(solution)/shard_map/all_to_all | solution.py:47
  30.2 11.4 %collective-permute-done.5 = bf16[128,2048]{1,0:T(8,128)(2,1)S(1)} collective-permute-done((bf16[128,2048]{1,0:T(8,128)(2,1)S(1)}, bf16[128,2048]{1,0:T(8,128)(2,1)S(1)}, u32[]{:S(2)}, u32[]{:S(2)}) %collective-permute-start.5) | collective-permute-done | bytes 524320 | tf_op jit(solution)/shard_map/ppermute | solution.py:41
  42.7 4.5 %all-to-all-start.1 = ((bf16[4,64,2048]{2,1,0:T(8,128)(2,1)}), bf16[4,64,2048]{2,1,0:T(8,128)(2,1)}, u32[]{:S(2)}, u32[]{:S(2)}) async-start(bf16[4,64,2048]{2,1,0:T(8,128)(2,1)} %pad_maximum_fusion.3), calls=%async_computation.1 | async-start | bytes 2097152 | tf_op jit(solution)/shard_map/all_to_all | solution.py:47
  47.2 3.5 collective-permute-start.1
  50.7 13.5 %collective-permute-done.1 = bf16[128,2048]{1,0:T(8,128)(2,1)S(1)} collective-permute-done((bf16[128,2048]{1,0:T(8,128)(2,1)}, bf16[128,2048]{1,0:T(8,128)(2,1)S(1)}, u32[]{:S(2)}, u32[]{:S(2)}) %collective-permute-start.1) | collective-permute-done | bytes 524320 | tf_op jit(solution)/shard_map/ppermute | solution.py:41
  64.2 29.8 %collective-permute-done = bf16[128,2048]{1,0:T(8,128)(2,1)S(1)} collective-permute-done((bf16[128,2048]{1,0:T(8,128)(2,1)}, bf16[128,2048]{1,0:T(8,128)(2,1)S(1)}, u32[]{:S(2)}, u32[]{:S(2)}) %collective-permute-start) | collective-permute-done | bytes 524320 | tf_op jit(solution)/shard_map/ppermute | solution.py:41
  95.1 6.9 %expert_forward.2 = (f32[256,1536]{1,0:T(8,128)S(1)}, bf16[256,768]{1,0:T(8,128)(2,1)S(1)}, bf16[256,2048]{1,0:T(8,128)(2,1)}) custom-call(bf16[256,2048]{1,0:T(8,128)(2,1)S(1)} %bitcast.78, bf16[1024,1536]{1,0:T(8,128)(2,1)} %bitcast.85, bf16[1024,1536]{1,0:T(8,128)(2,1)} %collective-permute-done.3.refs_2_.refs_5_, bf16[1024,768]{1,0:T(8,128)(2,1)S(1)} %bitcast.72, ...), custom_call_target="tpu_custom_call" | custom-call | flops 1 | bytes 1 | tf_op jit(solution)/shard_map/expert_forward/pallas_call | solution.py:117
  105.2 8.1 %expert_backward.2 = (bf16[256,1536]{1,0:T(8,128)(2,1)S(1)}, bf16[256,2048]{1,0:T(8,128)(2,1)}) custom-call(f32[256,1536]{1,0:T(8,128)S(1)} %copy-done.8, bf16[256,2048]{1,0:T(8,128)(2,1)} %bitcast.16.refs_1_, bf16[1024,768]{1,0:T(8,128)(2,1)S(1)} %bitcast.73, bf16[1024,768]{1,0:T(8,128)(2,1)} %collective-permute-done.4.refs_4_.refs_3_, ...), custom_call_target="tpu_custom_call" | custom-call | flops 1 | bytes 1 | tf_op jit(solution)/shard_map/expert_backward/pallas_call | solution.py:164
  113.3 16.8 %all_to_all.40 = bf16[4,64,2048]{2,1,0:T(8,128)(2,1)S(1)} all-to-all(bf16[4,64,2048]{2,1,0:T(8,128)(2,1)S(1)} %copy-done.17), channel_id=1, replica_groups=mesh['node'=4,'local'=4,'edata'=2] {'node'}, dimensions={0} | all-to-all | bytes 2097152 | tf_op jit(solution)/shard_map/all_to_all | solution.py:47
  130.1 7.2 %expert_forward.3 = (f32[256,1536]{1,0:T(8,128)S(1)}, bf16[256,768]{1,0:T(8,128)(2,1)S(1)}, bf16[256,2048]{1,0:T(8,128)(2,1)}) custom-call(bf16[256,2048]{1,0:T(8,128)(2,1)S(1)} %bitcast.80, bf16[1024,1536]{1,0:T(8,128)(2,1)} %bitcast.87, bf16[1024,1536]{1,0:T(8,128)(2,1)} %collective-permute-done.3.refs_2_.refs_5_, bf16[1024,768]{1,0:T(8,128)(2,1)S(1)} %bitcast.74, ...), custom_call_target="tpu_custom_call" | custom-call | flops 1 | bytes 1 | tf_op jit(solution)/shard_map/expert_forward/pallas_call | solution.py:117
  138.5 3.5 all-to-all-start.3
  143.7 15.3 %collective-permute-done.7 = bf16[128,2048]{1,0:T(8,128)(2,1)S(1)} collective-permute-done((bf16[128,2048]{1,0:T(8,128)(2,1)}, bf16[128,2048]{1,0:T(8,128)(2,1)S(1)}, u32[]{:S(2)}, u32[]{:S(2)}) %collective-permute-start.7) | collective-permute-done | bytes 524320 | tf_op jit(solution)/shard_map/ppermute | solution.py:41
  159.0 26.0 %collective-permute-done.6 = bf16[128,2048]{1,0:T(8,128)(2,1)S(1)} collective-permute-done((bf16[128,2048]{1,0:T(8,128)(2,1)}, bf16[128,2048]{1,0:T(8,128)(2,1)S(1)}, u32[]{:S(2)}, u32[]{:S(2)}) %collective-permute-start.6) | collective-permute-done | bytes 524320 | tf_op jit(solution)/shard_map/ppermute | solution.py:41
  187.8 14.0 %all_to_all.41 = bf16[4,64,2048]{2,1,0:T(8,128)(2,1)S(1)} all-to-all(bf16[4,64,2048]{2,1,0:T(8,128)(2,1)S(1)} %copy-done.18), channel_id=1, replica_groups=mesh['node'=4,'local'=4,'edata'=2] {'node'}, dimensions={0} | all-to-all | bytes 2097152 | tf_op jit(solution)/shard_map/all_to_all | solution.py:47
  201.8 6.7 %expert_backward.3 = (bf16[256,1536]{1,0:T(8,128)(2,1)S(1)}, bf16[256,2048]{1,0:T(8,128)(2,1)S(1)}) custom-call(f32[256,1536]{1,0:T(8,128)S(1)} %copy-done.6, bf16[256,2048]{1,0:T(8,128)(2,1)S(1)} %bitcast.76, bf16[1024,768]{1,0:T(8,128)(2,1)S(1)} %bitcast.75, bf16[1024,768]{1,0:T(8,128)(2,1)} %collective-permute-done.4.refs_4_.refs_3_, ...), custom_call_target="tpu_custom_call" | custom-call | flops 1 | bytes 1 | tf_op jit(solution)/shard_map/expert_backward/pallas_call | solution.py:164
  210.3 3.5 all-to-all-start.5
  213.9 4.8 %collective-permute-start.10 = (bf16[128,2048]{1,0:T(8,128)(2,1)}, bf16[128,2048]{1,0:T(8,128)(2,1)}, u32[]{:S(2)}, u32[]{:S(2)}) collective-permute-start(bf16[128,2048]{1,0:T(8,128)(2,1)} %bitcast.25), channel_id=1, source_target_pairs={{0,6},{2,4},{4,2},{6,0},{1,7},{3,5},{5,3},{7,1},{8,14},{10,12},{12... | collective-permute-start | bytes 1572872 | tf_op jit(solution)/shard_map/ppermute | solution.py:41
  218.6 4.6 %all-to-all-done.5 = bf16[4,64,2048]{2,1,0:T(8,128)(2,1)S(1)} async-done(((bf16[4,64,2048]{2,1,0:T(8,128)(2,1)}), bf16[4,64,2048]{2,1,0:T(8,128)(2,1)S(1)}, u32[]{:S(2)}, u32[]{:S(2)}) %all-to-all-start.5) | async-done | bytes 1048608 | tf_op jit(solution)/shard_map/all_to_all | solution.py:47
  226.7 4.2 %all-to-all-start.6 = ((bf16[4,64,2048]{2,1,0:T(8,128)(2,1)}), bf16[4,64,2048]{2,1,0:T(8,128)(2,1)}, u32[]{:S(2)}, u32[]{:S(2)}) async-start(bf16[4,64,2048]{2,1,0:T(8,128)(2,1)} %bitcast.32), calls=%async_computation.6 | async-start | bytes 2097152 | tf_op jit(solution)/shard_map/all_to_all | solution.py:47
  231.8 4.9 %collective-permute-start.11 = (bf16[128,2048]{1,0:T(8,128)(2,1)}, bf16[128,2048]{1,0:T(8,128)(2,1)}, u32[]{:S(2)}, u32[]{:S(2)}) collective-permute-start(bf16[128,2048]{1,0:T(8,128)(2,1)} %bitcast.100), channel_id=1, source_target_pairs={{0,6},{2,4},{4,2},{6,0},{1,7},{3,5},{5,3},{7,1},{8,14},{10,12},{12... | collective-permute-start | bytes 1572872 | tf_op jit(solution)/shard_map/ppermute | solution.py:41
  236.7 41.3 %collective-permute-done.8 = bf16[128,2048]{1,0:T(8,128)(2,1)} collective-permute-done((bf16[128,2048]{1,0:T(8,128)(2,1)}, bf16[128,2048]{1,0:T(8,128)(2,1)}, u32[]{:S(2)}, u32[]{:S(2)}) %collective-permute-start.8) | collective-permute-done | bytes 524320 | tf_op jit(solution)/shard_map/ppermute | solution.py:41
  280.0 4.5 %add_convert_fusion = bf16[2048,1536]{1,0:T(8,128)(2,1)} fusion(f32[2048,1536]{1,0:T(8,128)S(1)} %fusion.36, bf16[256,2048]{1,0:T(8,128)(2,1)S(1)} %bitcast.81, bf16[256,1536]{1,0:T(8,128)(2,1)S(1)} %copy-done.13), kind=kOutput, calls=%fused_computation | convolution fusion | flops 1616904192 | bytes 20709376 | tf_op jit(solution)/shard_map/dot_general | solution.py:274
  284.5 3.8 %slice.93 = bf16[1024,1536]{1,0:T(8,128)(2,1)} slice(bf16[2048,1536]{1,0:T(8,128)(2,1)} %add_convert_fusion), slice={[1024:2048], [0:1536]} | slice | bytes 6291456 | tf_op jit(solution)/shard_map/slice | solution.py:80
  290.4 4.1 %collective-permute-start.14 = (bf16[128,2048]{1,0:T(8,128)(2,1)S(1)}, bf16[128,2048]{1,0:T(8,128)(2,1)}, u32[]{:S(2)}, u32[]{:S(2)}) collective-permute-start(bf16[128,2048]{1,0:T(8,128)(2,1)S(1)} %bitcast.102), channel_id=1, source_target_pairs={{0,2},{2,0},{4,6},{6,4},{1,3},{3,1},{5,7},{7,5},{8,10},{10,8},{12,... | collective-permute-start | bytes 1572872 | tf_op jit(solution)/shard_map/ppermute | solution.py:41
  299.3 16.4 %collective-permute-done.14 = bf16[128,2048]{1,0:T(8,128)(2,1)} collective-permute-done((bf16[128,2048]{1,0:T(8,128)(2,1)S(1)}, bf16[128,2048]{1,0:T(8,128)(2,1)}, u32[]{:S(2)}, u32[]{:S(2)}) %collective-permute-start.14) | collective-permute-done | bytes 524320 | tf_op jit(solution)/shard_map/ppermute | solution.py:41
  315.7 4.5 %all-to-all-start.7 = ((bf16[4,64,2048]{2,1,0:T(8,128)(2,1)}), bf16[4,64,2048]{2,1,0:T(8,128)(2,1)}, u32[]{:S(2)}, u32[]{:S(2)}) async-start(bf16[4,64,2048]{2,1,0:T(8,128)(2,1)} %bitcast.38), calls=%async_computation.7 | async-start | bytes 2097152 | tf_op jit(solution)/shard_map/all_to_all | solution.py:47
  320.2 3.9 %multiply_reduce_fusion = f32[512]{0:T(512)} fusion(f32[512,2048]{1,0:T(8,128)} %get-tuple-element.87, bf16[128,2048]{1,0:T(8,128)(2,1)} %collective-permute-done.10, bf16[128,2048]{1,0:T(8,128)(2,1)} %collective-permute-done.8, bf16[128,2048]{1,0:T(8,128)(2,1)} %collective-permute-done.14, bf16[128,2048]{1,0:T(8,128)(2,1)} %bitcast.93), kind=kLoop, calls=%fused_computation.3 | loop fusion | flops 10485248 | bytes 6293504 | tf_op jit(solution)/shard_map/reduce_sum | solution.py:290
  339.5 6.5 %convert_add_fusion = f32[1024,1536]{1,0:T(8,128)} fusion(bf16[1024,1536]{1,0:T(8,128)(2,1)} %collective-permute-done.12, bf16[2048,1536]{1,0:T(8,128)(2,1)} %add_convert_fusion), kind=kLoop, calls=%fused_computation.2 | loop fusion | flops 4718592 | bytes 12582912 | tf_op jit(solution)/shard_map/add | solution.py:81
  346.0 7.4 %collective-permute-done.15.refs_1_ = bf16[128,2048]{1,0:T(8,128)(2,1)S(1)} collective-permute-done((bf16[128,2048]{1,0:T(8,128)(2,1)S(1)}, bf16[128,2048]{1,0:T(8,128)(2,1)S(1)}, u32[]{:S(2)}, u32[]{:S(2)}) %collective-permute-start.15) | collective-permute-done | bytes 524320 | tf_op jit(solution)/shard_map/ppermute | solution.py:41
  353.4 4.3 %combine.1 = bf16[256,2048]{1,0:T(8,128)(2,1)} custom-call(s32[1]{0:T(128)} %bitcast.37.turn_ref, bf16[512,256]{1,0:T(8,128)(2,1)S(1)} %get-tuple-element.84.pick_ref, bf16[128,2048]{1,0:T(8,128)(2,1)S(1)} %bitcast.82, bf16[128,2048]{1,0:T(8,128)(2,1)S(1)} %collective-permute-done.15.refs_1_, bf16[128,2048]{1,0:T(8,128)(2,1)} %collective-permute-done.9.refs_2_, ...), custom_call_target="tpu_custom_call" | custom-call | flops 1 | bytes 1 | tf_op jit(solution)/shard_map/combine/pallas_call | solution.py:198
  (122 shorter events, 54.9 us)
Async XLA Ops:
  0.6 94.4 %collective-permute-start.4 = (bf16[1024,768]{1,0:T(8,128)(2,1)}, bf16[1024,768]{1,0:T(8,128)(2,1)}, u32[]{:S(2)}, u32[]{:S(2)}) collective-permute-start(bf16[1024,768]{1,0:T(8,128)(2,1)} %bitcast.71), channel_id=1, source_target_pairs={{1,0},{0,1},{3,2},{2,3},{5,4},{4,5},{7,6},{6,7},{9,8},{8,9},{11,10... | collective-permute-start | bytes 4718600 | tf_op jit(solution)/shard_map/ppermute | solution.py:70
  1.1 93.9 %collective-permute-start.3 = (bf16[1024,1536]{1,0:T(8,128)(2,1)}, bf16[1024,1536]{1,0:T(8,128)(2,1)}, u32[]{:S(2)}, u32[]{:S(2)}) collective-permute-start(bf16[1024,1536]{1,0:T(8,128)(2,1)} %bitcast.84), channel_id=1, source_target_pairs={{1,0},{0,1},{3,2},{2,3},{5,4},{4,5},{7,6},{6,7},{9,8},{8,9},{11,10... | collective-permute-start | bytes 9437192 | tf_op jit(solution)/shard_map/ppermute | solution.py:70
  1.4 7.6 %copy-start.29 = (s32[16]{0:T(128)}, s32[16]{0:T(128)S(1)}, u32[]{:S(2)}) copy-start(s32[16]{0:T(128)S(1)} %add.49) | copy-start | bytes 196
  5.9 15.5 %collective-permute-start.2 = (bf16[128,2048]{1,0:T(8,128)(2,1)}, bf16[128,2048]{1,0:T(8,128)(2,1)}, u32[]{:S(2)}, u32[]{:S(2)}) collective-permute-start(bf16[128,2048]{1,0:T(8,128)(2,1)} %get-tuple-element.73), channel_id=1, source_target_pairs={{0,2},{2,0},{4,6},{6,4},{1,3},{3,1},{5,7},{7,5},{8,10},{10,8},{12,... | collective-permute-start | bytes 1572872 | tf_op jit(solution)/shard_map/ppermute | solution.py:41
  23.5 19.2 %all-to-all-start = ((bf16[4,64,2048]{2,1,0:T(8,128)(2,1)}), bf16[4,64,2048]{2,1,0:T(8,128)(2,1)S(1)}, u32[]{:S(2)}, u32[]{:S(2)}) async-start(bf16[4,64,2048]{2,1,0:T(8,128)(2,1)} %pad_maximum_fusion.2), calls=%async_computation | async-start | bytes 2097152 | tf_op jit(solution)/shard_map/all_to_all | solution.py:47
  28.6 13.0 %collective-permute-start.5 = (bf16[128,2048]{1,0:T(8,128)(2,1)S(1)}, bf16[128,2048]{1,0:T(8,128)(2,1)S(1)}, u32[]{:S(2)}, u32[]{:S(2)}) collective-permute-start(bf16[128,2048]{1,0:T(8,128)(2,1)S(1)} %get-tuple-element.70), channel_id=1, source_target_pairs={{0,2},{2,0},{4,6},{6,4},{1,3},{3,1},{5,7},{7,5},{8,10},{10,8},{12,... | collective-permute-start | bytes 1572872 | tf_op jit(solution)/shard_map/ppermute | solution.py:41
  42.7 52.4 %copy-start.1 = (bf16[4,64,2048]{2,1,0:T(8,128)(2,1)}, bf16[4,64,2048]{2,1,0:T(8,128)(2,1)S(1)}, u32[]{:S(2)}) copy-start(bf16[4,64,2048]{2,1,0:T(8,128)(2,1)S(1)} %all-to-all-done) | copy-start | bytes 3145732
  42.7 52.4 %copy-start = (bf16[1,1024,768]{2,1,0:T(8,128)(2,1)S(1)}, bf16[1,1024,768]{2,1,0:T(8,128)(2,1)}, u32[]{:S(2)}) copy-start(bf16[1,1024,768]{2,1,0:T(8,128)(2,1)} %param.13) | copy-start | bytes 4718596
  42.7 61.2 %all-to-all-start.1 = ((bf16[4,64,2048]{2,1,0:T(8,128)(2,1)}), bf16[4,64,2048]{2,1,0:T(8,128)(2,1)}, u32[]{:S(2)}, u32[]{:S(2)}) async-start(bf16[4,64,2048]{2,1,0:T(8,128)(2,1)} %pad_maximum_fusion.3), calls=%async_computation.1 | async-start | bytes 2097152 | tf_op jit(solution)/shard_map/all_to_all | solution.py:47
  47.2 17.0 %collective-permute-start.1 = (bf16[128,2048]{1,0:T(8,128)(2,1)}, bf16[128,2048]{1,0:T(8,128)(2,1)S(1)}, u32[]{:S(2)}, u32[]{:S(2)}) collective-permute-start(bf16[128,2048]{1,0:T(8,128)(2,1)} %get-tuple-element.74), channel_id=1, source_target_pairs={{0,6},{2,4},{4,2},{6,0},{1,7},{3,5},{5,3},{7,1},{8,14},{10,12},{12... | collective-permute-start | bytes 1572872 | tf_op jit(solution)/shard_map/ppermute | solution.py:41
  50.7 43.3 %collective-permute-start = (bf16[128,2048]{1,0:T(8,128)(2,1)}, bf16[128,2048]{1,0:T(8,128)(2,1)S(1)}, u32[]{:S(2)}, u32[]{:S(2)}) collective-permute-start(bf16[128,2048]{1,0:T(8,128)(2,1)} %get-tuple-element.75), channel_id=1, source_target_pairs={{0,4},{2,6},{4,0},{6,2},{1,5},{3,7},{5,1},{7,3},{8,12},{10,14},{12... | collective-permute-start | bytes 1572872 | tf_op jit(solution)/shard_map/ppermute | solution.py:41
  105.2 8.1 %copy-start.17 = (bf16[4,64,2048]{2,1,0:T(8,128)(2,1)S(1)}, bf16[4,64,2048]{2,1,0:T(8,128)(2,1)}, u32[]{:S(2)}) copy-start(bf16[4,64,2048]{2,1,0:T(8,128)(2,1)} %pad_maximum_fusion.1) | copy-start | bytes 3145732
  113.3 16.8 %copy-start.10 = (bf16[256,1536]{1,0:T(8,128)(2,1)}, bf16[256,1536]{1,0:T(8,128)(2,1)S(1)}, u32[]{:S(2)}) copy-start(bf16[256,1536]{1,0:T(8,128)(2,1)S(1)} %get-tuple-element.53) | copy-start | bytes 2359300
  138.5 47.7 %all-to-all-start.3 = ((bf16[4,64,2048]{2,1,0:T(8,128)(2,1)}), bf16[4,64,2048]{2,1,0:T(8,128)(2,1)S(1)}, u32[]{:S(2)}, u32[]{:S(2)}) async-start(bf16[4,64,2048]{2,1,0:T(8,128)(2,1)} %bitcast.22), calls=%async_computation.3 | async-start | bytes 2097152 | tf_op jit(solution)/shard_map/all_to_all | solution.py:47
  142.0 17.0 %collective-permute-start.7 = (bf16[128,2048]{1,0:T(8,128)(2,1)}, bf16[128,2048]{1,0:T(8,128)(2,1)S(1)}, u32[]{:S(2)}, u32[]{:S(2)}) collective-permute-start(bf16[128,2048]{1,0:T(8,128)(2,1)} %get-tuple-element.43), channel_id=1, source_target_pairs={{0,6},{2,4},{4,2},{6,0},{1,7},{3,5},{5,3},{7,1},{8,14},{10,12},{12... | collective-permute-start | bytes 1572872 | tf_op jit(solution)/shard_map/ppermute | solution.py:41
  143.7 41.3 %collective-permute-start.6 = (bf16[128,2048]{1,0:T(8,128)(2,1)}, bf16[128,2048]{1,0:T(8,128)(2,1)S(1)}, u32[]{:S(2)}, u32[]{:S(2)}) collective-permute-start(bf16[128,2048]{1,0:T(8,128)(2,1)} %get-tuple-element.42), channel_id=1, source_target_pairs={{0,4},{2,6},{4,0},{6,2},{1,5},{3,7},{5,1},{7,3},{8,12},{10,14},{12... | collective-permute-start | bytes 1572872 | tf_op jit(solution)/shard_map/ppermute | solution.py:41
  186.2 15.6 %copy-start.6 = (f32[256,1536]{1,0:T(8,128)S(1)}, f32[256,1536]{1,0:T(8,128)}, u32[]{:S(2)}) copy-start(f32[256,1536]{1,0:T(8,128)} %copy-done.5) | copy-start | bytes 4718596
  210.3 12.9 %all-to-all-start.5 = ((bf16[4,64,2048]{2,1,0:T(8,128)(2,1)}), bf16[4,64,2048]{2,1,0:T(8,128)(2,1)S(1)}, u32[]{:S(2)}, u32[]{:S(2)}) async-start(bf16[4,64,2048]{2,1,0:T(8,128)(2,1)} %bitcast.83), calls=%async_computation.5 | async-start | bytes 2097152 | tf_op jit(solution)/shard_map/all_to_all | solution.py:47
  213.9 18.0 %collective-permute-start.10 = (bf16[128,2048]{1,0:T(8,128)(2,1)}, bf16[128,2048]{1,0:T(8,128)(2,1)}, u32[]{:S(2)}, u32[]{:S(2)}) collective-permute-start(bf16[128,2048]{1,0:T(8,128)(2,1)} %bitcast.25), channel_id=1, source_target_pairs={{0,6},{2,4},{4,2},{6,0},{1,7},{3,5},{5,3},{7,1},{8,14},{10,12},{12... | collective-permute-start | bytes 1572872 | tf_op jit(solution)/shard_map/ppermute | solution.py:41
  218.6 59.5 %collective-permute-start.8 = (bf16[128,2048]{1,0:T(8,128)(2,1)}, bf16[128,2048]{1,0:T(8,128)(2,1)}, u32[]{:S(2)}, u32[]{:S(2)}) collective-permute-start(bf16[128,2048]{1,0:T(8,128)(2,1)} %bitcast.24), channel_id=1, source_target_pairs={{0,4},{2,6},{4,0},{6,2},{1,5},{3,7},{5,1},{7,3},{8,12},{10,14},{12... | collective-permute-start | bytes 1572872 | tf_op jit(solution)/shard_map/ppermute | solution.py:41
  224.2 53.9 %copy-start.2 = (bf16[4,64,2048]{2,1,0:T(8,128)(2,1)S(1)}, bf16[4,64,2048]{2,1,0:T(8,128)(2,1)}, u32[]{:S(2)}) copy-start(bf16[4,64,2048]{2,1,0:T(8,128)(2,1)} %copy-done.1) | copy-start | bytes 3145732
  224.2 53.9 %copy-start.11 = (bf16[256,1536]{1,0:T(8,128)(2,1)S(1)}, bf16[256,1536]{1,0:T(8,128)(2,1)}, u32[]{:S(2)}) copy-start(bf16[256,1536]{1,0:T(8,128)(2,1)} %copy-done.10) | copy-start | bytes 2359300
  226.7 61.7 %all-to-all-start.6 = ((bf16[4,64,2048]{2,1,0:T(8,128)(2,1)}), bf16[4,64,2048]{2,1,0:T(8,128)(2,1)}, u32[]{:S(2)}, u32[]{:S(2)}) async-start(bf16[4,64,2048]{2,1,0:T(8,128)(2,1)} %bitcast.32), calls=%async_computation.6 | async-start | bytes 2097152 | tf_op jit(solution)/shard_map/all_to_all | solution.py:47
  230.9 49.0 %copy-start.4 = (bf16[4,64,2048]{2,1,0:T(8,128)(2,1)S(1)}, bf16[4,64,2048]{2,1,0:T(8,128)(2,1)}, u32[]{:S(2)}) copy-start(bf16[4,64,2048]{2,1,0:T(8,128)(2,1)} %copy-done.3) | copy-start | bytes 3145732
  230.9 49.0 %copy-start.13 = (bf16[256,1536]{1,0:T(8,128)(2,1)S(1)}, bf16[256,1536]{1,0:T(8,128)(2,1)}, u32[]{:S(2)}) copy-start(bf16[256,1536]{1,0:T(8,128)(2,1)} %copy-done.12) | copy-start | bytes 2359300
  231.8 114.2 %collective-permute-start.11 = (bf16[128,2048]{1,0:T(8,128)(2,1)}, bf16[128,2048]{1,0:T(8,128)(2,1)}, u32[]{:S(2)}, u32[]{:S(2)}) collective-permute-start(bf16[128,2048]{1,0:T(8,128)(2,1)} %bitcast.100), channel_id=1, source_target_pairs={{0,6},{2,4},{4,2},{6,0},{1,7},{3,5},{5,3},{7,1},{8,14},{10,12},{12... | collective-permute-start | bytes 1572872 | tf_op jit(solution)/shard_map/ppermute | solution.py:41
  278.1 67.9 %collective-permute-start.9 = (bf16[128,2048]{1,0:T(8,128)(2,1)}, bf16[128,2048]{1,0:T(8,128)(2,1)}, u32[]{:S(2)}, u32[]{:S(2)}) collective-permute-start(bf16[128,2048]{1,0:T(8,128)(2,1)} %bitcast.99), channel_id=1, source_target_pairs={{0,4},{2,6},{4,0},{6,2},{1,5},{3,7},{5,1},{7,3},{8,12},{10,14},{12... | collective-permute-start | bytes 1572872 | tf_op jit(solution)/shard_map/ppermute | solution.py:41
  288.3 51.2 %collective-permute-start.12 = (bf16[1024,1536]{1,0:T(8,128)(2,1)}, bf16[1024,1536]{1,0:T(8,128)(2,1)}, u32[]{:S(2)}, u32[]{:S(2)}) collective-permute-start(bf16[1024,1536]{1,0:T(8,128)(2,1)} %slice.93), channel_id=1, source_target_pairs={{0,1},{1,0},{2,3},{3,2},{4,5},{5,4},{6,7},{7,6},{8,9},{9,8},{10,11... | collective-permute-start | bytes 9437192 | tf_op jit(solution)/shard_map/ppermute | solution.py:80
  290.4 25.3 %collective-permute-start.14 = (bf16[128,2048]{1,0:T(8,128)(2,1)S(1)}, bf16[128,2048]{1,0:T(8,128)(2,1)}, u32[]{:S(2)}, u32[]{:S(2)}) collective-permute-start(bf16[128,2048]{1,0:T(8,128)(2,1)S(1)} %bitcast.102), channel_id=1, source_target_pairs={{0,2},{2,0},{4,6},{6,4},{1,3},{3,1},{5,7},{7,5},{8,10},{10,8},{12,... | collective-permute-start | bytes 1572872 | tf_op jit(solution)/shard_map/ppermute | solution.py:41
  299.1 35.7 %collective-permute-start.13 = (bf16[1024,768]{1,0:T(8,128)(2,1)}, bf16[1024,768]{1,0:T(8,128)(2,1)}, u32[]{:S(2)}, u32[]{:S(2)}) collective-permute-start(bf16[1024,768]{1,0:T(8,128)(2,1)} %slice.95), channel_id=1, source_target_pairs={{0,1},{1,0},{2,3},{3,2},{4,5},{5,4},{6,7},{7,6},{8,9},{9,8},{10,11... | collective-permute-start | bytes 4718600 | tf_op jit(solution)/shard_map/ppermute | solution.py:80
  315.7 22.4 %all-to-all-start.7 = ((bf16[4,64,2048]{2,1,0:T(8,128)(2,1)}), bf16[4,64,2048]{2,1,0:T(8,128)(2,1)}, u32[]{:S(2)}, u32[]{:S(2)}) async-start(bf16[4,64,2048]{2,1,0:T(8,128)(2,1)} %bitcast.38), calls=%async_computation.7 | async-start | bytes 2097152 | tf_op jit(solution)/shard_map/all_to_all | solution.py:47
  339.4 14.0 %collective-permute-start.15 = (bf16[128,2048]{1,0:T(8,128)(2,1)S(1)}, bf16[128,2048]{1,0:T(8,128)(2,1)S(1)}, u32[]{:S(2)}, u32[]{:S(2)}) collective-permute-start(bf16[128,2048]{1,0:T(8,128)(2,1)S(1)} %bitcast.101), channel_id=1, source_target_pairs={{0,2},{2,0},{4,6},{6,4},{1,3},{3,1},{5,7},{7,5},{8,10},{10,8},{12,... | collective-permute-start | bytes 1572872 | tf_op jit(solution)/shard_map/ppermute | solution.py:41
  (22 other events, 62.6 us)

commit v6 on v1

v6 whole, which is shorter than its diff:
```python
import jax
import jax.numpy as jnp
from jax import lax
from jax.experimental import pallas as pl
from jax.experimental.pallas import tpu as pltpu
from jax.sharding import PartitionSpec as P

EXP_DEV = 4
BF = jnp.bfloat16
F32 = jnp.float32
ROWS_IN = (((0,), (0,)), ((), ()))
COLS_IN = (((1,), (1,)), ((), ()))
LIMIT = 56 * 1024 * 1024
CHEAP = pl.CostEstimate(flops=1, bytes_accessed=1, transcendentals=0)


def params():
    return pltpu.CompilerParams(vmem_limit_bytes=LIMIT)


def slot_tables(expert_ids, gates, numbers, capacity):
    tok_rows = expert_ids.shape[0]
    ids_t = expert_ids.T
    chosen = ids_t[None, :, :] == numbers[:, None, None]
    routed = jnp.any(chosen, axis=1)
    earlier = jnp.arange(tok_rows)[:, None] < jnp.arange(tok_rows)[None, :]
    order_in = jnp.dot(
        routed.astype(BF), earlier.astype(BF), preferred_element_type=F32
    ).astype(jnp.int32)
    weight = jnp.sum(jnp.where(chosen, gates.T[None, :, :], 0.0), axis=1)
    slot_ids = jnp.arange(capacity, dtype=jnp.int32)
    hits = routed[:, None, :] & (order_in[:, None, :] == slot_ids[None, :, None])
    slot_weight = jnp.sum(jnp.where(hits, weight[:, None, :], 0.0), axis=2)
    return hits.reshape(numbers.shape[0] * capacity, tok_rows).astype(BF), slot_weight.reshape(-1, 1)


def after(value, *others):
    return lax.optimization_barrier((value, *others))[0]


def to_plane(rows, distance):
    if distance == 0:
        return rows
    pairs = [(i, i ^ distance) for i in range(lax.axis_size("local"))]
    return lax.ppermute(rows, "local", pairs)


def over_nodes(rows):
    return lax.all_to_all(rows, "node", split_axis=0, concat_axis=0, tiled=True)


def to_nodes(blocks):
    count = len(blocks)
    return [blocks[0]] + [
        lax.ppermute(blocks[d], "node", [(i, i ^ d) for i in range(count)]) for d in range(1, count)
    ]


def gathered(shard):
    count = lax.axis_size("edata")
    shards = [shard]
    for step in range(1, count):
        pairs = [((i + step) % count, i) for i in range(count)]
        shards.append(lax.ppermute(shard, "edata", pairs))
    return shards


def from_owner(piece, step):
    count = lax.axis_size("edata")
    return lax.ppermute(piece, "edata", [(i, (i + step) % count) for i in range(count)])


def dispatch_kernel(turn_ref, pick_ref, weight_ref, x_ref, dy_ref, *out_refs):
    nodes, _, capacity, tile = out_refs[0].shape
    size = nodes * capacity
    for i, out_ref in enumerate(out_refs):
        here = slice(i * size, (i + 1) * size)
        pick = pick_ref[here]
        x = jnp.dot(pick, x_ref[...], preferred_element_type=F32).astype(BF)
        out_ref[:, 0] = x.reshape(nodes, capacity, tile)
        dy = jnp.dot(pick, dy_ref[...], preferred_element_type=F32)
        out_ref[:, 1] = (weight_ref[here] * dy).astype(BF).reshape(nodes, capacity, tile)


def dispatch(turn, pick, weight, tokens, out_grad, nodes, capacity):
    slots, tok_rows = pick.shape
    width = tokens.shape[1]
    count = lax.axis_size("edata")
    tile = min(1024, width // count)
    steps = width // tile
    planes = slots // (nodes * capacity)
    turned = pl.BlockSpec((tok_rows, tile), lambda i, t: (0, (i + t[0] * (steps // count)) % steps))
    return pl.pallas_call(
        dispatch_kernel,
        grid_spec=pltpu.PrefetchScalarGridSpec(
            num_scalar_prefetch=1,
            grid=(steps,),
            in_specs=[
                pl.BlockSpec((slots, tok_rows), lambda i, t: (0, 0)),
                pl.BlockSpec((slots, 1), lambda i, t: (0, 0)),
                turned,
                turned,
            ],
            out_specs=[pl.BlockSpec((nodes, 2, capacity, tile), lambda i, t: (0, 0, 0, i))] * planes,
        ),
        out_shape=[jax.ShapeDtypeStruct((nodes, 2, capacity, width), BF)] * planes,
        compiler_params=params(),
        cost_estimate=CHEAP,
        name="dispatch",
    )(turn, pick, weight, tokens, out_grad)


def expert_kernel(count, rows_ref, *refs):
    ins, outs = refs[:count], refs[count : 2 * count]
    back_ref, inner_ref, act_grad_ref, act_ref = refs[2 * count :]
    nodes, _, capacity, model = rows_ref.shape
    rows = nodes * capacity
    hidden = inner_ref.shape[1]
    width = model // count

    def part(kind, s):
        return rows_ref[:, kind, :, s * width : (s + 1) * width].reshape(rows, width)

    activation = jnp.dot(part(0, 0), ins[0][...], preferred_element_type=F32)
    for s in range(1, count):
        activation += jnp.dot(part(0, s), ins[s][...], preferred_element_type=F32)
    act_ref[...] = activation
    act_gate = act_ref[:, :hidden]
    act_up = act_ref[:, hidden:]
    sig = jax.nn.sigmoid(act_gate)
    swished = act_gate * sig
    inner_ref[...] = (swished * act_up).astype(BF)
    inner_grad = jnp.dot(part(1, 0), outs[0][...], preferred_element_type=F32)
    for s in range(1, count):
        inner_grad += jnp.dot(part(1, s), outs[s][...], preferred_element_type=F32)
    act_grad_ref[:, :hidden] = (
        inner_grad * act_up * sig * (1.0 + act_gate * (1.0 - sig))
    ).astype(BF)
    act_grad_ref[:, hidden:] = (inner_grad * swished).astype(BF)
    for s in range(count):
        here = slice(s * width, (s + 1) * width)
        y = lax.dot_general(inner_ref[...], outs[s][...], COLS_IN, preferred_element_type=F32)
        back_ref[:, 0, :, here] = y.astype(BF).reshape(nodes, capacity, width)
        dx = lax.dot_general(act_grad_ref[...], ins[s][...], COLS_IN, preferred_element_type=F32)
        back_ref[:, 1, :, here] = dx.astype(BF).reshape(nodes, capacity, width)


def expert(arrived, w_ins, w_outs):
    nodes, pieces, capacity, width = arrived.shape
    double = w_ins[0].shape[1]
    hidden = w_outs[0].shape[1]
    rows = nodes * capacity

    def whole(shard):
        return pl.BlockSpec(shard.shape, lambda i: (0, 0), pipeline_mode=pl.Buffered(1))

    def band(columns):
        return pl.BlockSpec((rows, columns), lambda i: (i, 0))

    moved = pl.BlockSpec((nodes, 2, capacity, width), lambda i: (0, i, 0, 0))
    planes = pieces // 2
    return pl.pallas_call(
        lambda *refs: expert_kernel(len(w_ins), *refs),
        grid=(planes,),
        in_specs=[moved] + [whole(s) for s in (*w_ins, *w_outs)],
        out_specs=[moved, band(hidden), band(double)],
        out_shape=[
            jax.ShapeDtypeStruct(arrived.shape, BF),
            jax.ShapeDtypeStruct((planes * rows, hidden), BF),
            jax.ShapeDtypeStruct((planes * rows, double), BF),
        ],
        scratch_shapes=[pltpu.VMEM((rows, double), F32)],
        compiler_params=params(),
        cost_estimate=CHEAP,
        name="expert",
    )(arrived, *w_ins, *w_outs)


def weight_kernel(count, *refs):
    arrived, inners, act_grads = refs[:count], refs[count : 2 * count], refs[2 * count : 3 * count]
    in_ref, out_ref = refs[3 * count :]
    total_in = total_out = None
    for rows_ref, inner, act_grad in zip(arrived, inners, act_grads):
        nodes, pieces, capacity, tile = rows_ref.shape
        rows = nodes * capacity
        for i in range(pieces // 2):
            x = rows_ref[:, 2 * i].reshape(rows, tile)
            dy = rows_ref[:, 2 * i + 1].reshape(rows, tile)
            here = slice(i * rows, (i + 1) * rows)
            one = lax.dot_general(x, act_grad[here], ROWS_IN, preferred_element_type=F32)
            two = lax.dot_general(dy, inner[here], ROWS_IN, preferred_element_type=F32)
            total_in = one if total_in is None else total_in + one
            total_out = two if total_out is None else total_out + two
    in_ref[...] = total_in.astype(BF)
    out_ref[...] = total_out.astype(BF)


def weight_grads(shard, arrived, inners, act_grads):
    width = arrived[0].shape[3]
    size = width // lax.axis_size("edata")
    double, hidden = act_grads[0].shape[1], inners[0].shape[1]
    tile = min(256, size)
    steps = size // tile

    def columns(array):
        return pl.BlockSpec(array.shape[:3] + (tile,), lambda i: (0, 0, 0, shard * steps + i))

    def whole(array):
        return pl.BlockSpec(array.shape, lambda i: (0, 0), pipeline_mode=pl.Buffered(1))

    return pl.pallas_call(
        lambda *refs: weight_kernel(len(arrived), *refs),
        grid=(steps,),
        in_specs=[columns(a) for a in arrived] + [whole(a) for a in (*inners, *act_grads)],
        out_specs=[
            pl.BlockSpec((tile, double), lambda i: (i, 0)),
            pl.BlockSpec((tile, hidden), lambda i: (i, 0)),
        ],
        out_shape=[
            jax.ShapeDtypeStruct((size, double), BF),
            jax.ShapeDtypeStruct((size, hidden), BF),
        ],
        compiler_params=params(),
        cost_estimate=CHEAP,
        name="weight_grads",
    )(*arrived, *inners, *act_grads)


def all_weight_grads(arrived, results):
    inners = [r[1] for r in results]
    act_grads = [r[2] for r in results]
    parts = []
    for shard in range(lax.axis_size("edata")):
        parts += weight_grads(shard, arrived, inners, act_grads)
    return parts


def combine_kernel(
    planes, groups, turn_ref, number_ref, pick_ref, weight_ref, ids_ref, grad_ref, *refs
):
    backs = refs[:planes]
    mixed_ref, token_grad_ref, gate_grad_ref, high_ref, middle_ref, dots_ref = refs[planes:]
    step = pl.program_id(0)
    nodes, _, capacity, tile = backs[0].shape
    size = nodes * capacity

    @pl.when(step == 0)
    def _():
        spread = pick_ref[...].astype(F32) * weight_ref[...]
        high = spread.astype(BF)
        high_ref[...] = high
        middle_ref[...] = (spread - high.astype(F32)).astype(BF)
        dots_ref[...] = jnp.zeros_like(dots_ref)

    mixed = token_grad = None
    for i, back in enumerate(backs):
        here = slice(i * size, (i + 1) * size)
        pick = pick_ref[here]
        y = back[:, 0].reshape(size, tile)
        dx = back[:, 1].reshape(size, tile)
        one = lax.dot_general(high_ref[here], y, ROWS_IN, preferred_element_type=F32)
        one += lax.dot_general(middle_ref[here], y, ROWS_IN, preferred_element_type=F32)
        two = lax.dot_general(pick, dx, ROWS_IN, preferred_element_type=F32)
        mixed = one if mixed is None else mixed + one
        token_grad = two if token_grad is None else token_grad + two
        grad_rows = jnp.dot(pick, grad_ref[...], preferred_element_type=F32)
        dots_ref[here] += jnp.sum(y.astype(F32) * grad_rows, axis=1, keepdims=True)
    mixed_ref[...] = mixed.astype(BF)
    token_grad_ref[...] = token_grad.astype(BF)

    @pl.when(step == pl.num_programs(0) - 1)
    def _():
        tok_rows = pick_ref.shape[1]
        by_token = pick_ref[...].astype(F32) * dots_ref[...]
        by_token = jnp.sum(by_token.reshape(groups, capacity, tok_rows), axis=1)
        ids = ids_ref[...]
        total = jnp.zeros(ids.shape, F32)
        for g in range(groups):
            total += jnp.where(ids == number_ref[g], by_token[g : g + 1], 0.0)
        gate_grad_ref[...] = total


def combine(turn, numbers, pick, weight, ids_t, out_grad, backs):
    slots, tok_rows = pick.shape
    nodes, _, capacity, width = backs[0].shape
    count = lax.axis_size("edata")
    tile = min(512, width // count)
    steps = width // tile
    turned = pl.BlockSpec(
        (tok_rows, tile), lambda i, t, n: (0, (i + t[0] * (steps // count)) % steps)
    )

    def whole(array):
        return pl.BlockSpec(array.shape, lambda i, t, n: (0, 0))

    return pl.pallas_call(
        lambda *refs: combine_kernel(len(backs), numbers.shape[0], *refs),
        grid_spec=pltpu.PrefetchScalarGridSpec(
            num_scalar_prefetch=2,
            grid=(steps,),
            in_specs=[whole(pick), whole(weight), whole(ids_t), turned]
            + [pl.BlockSpec((nodes, 2, capacity, tile), lambda i, t, n: (0, 0, 0, i))] * len(backs),
            out_specs=[turned, turned, whole(ids_t)],
            scratch_shapes=[
                pltpu.VMEM((slots, tok_rows), BF),
                pltpu.VMEM((slots, tok_rows), BF),
                pltpu.VMEM((slots, 1), F32),
            ],
        ),
        out_shape=[
            jax.ShapeDtypeStruct((tok_rows, width), BF),
            jax.ShapeDtypeStruct((tok_rows, width), BF),
            jax.ShapeDtypeStruct(ids_t.shape, F32),
        ],
        compiler_params=params(),
        cost_estimate=CHEAP,
        name="combine",
    )(turn, numbers, pick, weight, ids_t, out_grad, *backs)


def shards(tokens, out_grad, expert_ids, gates, w_gate_up, w_down):
    nodes, planes = lax.axis_size("node"), lax.axis_size("local")
    groups = nodes * planes
    tok_rows = tokens.shape[0]
    capacity = tok_rows * expert_ids.shape[1] // (EXP_DEV * groups)
    half = planes // 2
    near, far = list(range(half)), list(range(half, planes))
    split = half * nodes * capacity
    turn = lax.axis_index("edata").astype(jnp.int32).reshape(1)
    w_ins = gathered(w_gate_up[0])
    w_outs = gathered(w_down[0])
    plane = (lax.axis_index("local") ^ jnp.arange(planes, dtype=jnp.int32))[:, None]
    node = jnp.arange(nodes, dtype=jnp.int32)[None, :]
    node = jnp.where(jnp.arange(planes)[:, None] < half, node, lax.axis_index("node") ^ node)
    numbers = (plane + planes * node).reshape(-1)
    pick, slot_weight = slot_tables(expert_ids, gates, numbers, capacity)

    sent_far = dispatch(
        turn, pick[split:], slot_weight[split:], tokens, out_grad, nodes, capacity
    )
    sent_near = dispatch(
        turn, after(pick[:split], *sent_far), slot_weight[:split], tokens, out_grad, nodes, capacity
    )
    far_in = [to_plane(rows, d) for d, rows in zip(far, sent_far)]
    near_mid = over_nodes(jnp.concatenate(sent_near, axis=1))

    backs = [None] * planes
    arrived, results, back, near_result = [], [], None, None
    far_in[0] = after(far_in[0], *w_ins[1:], *w_outs[1:])
    for d, rows in zip(far, far_in):
        if back is not None:
            rows = after(rows, back)
        blocks = to_nodes([rows[i : i + 1] for i in range(nodes)])
        if back is not None and near_result is None:
            near_in = after(near_in, rows)
            near_result = expert(near_in, w_ins, w_outs)
            blocks[0] = after(blocks[0], near_result[0])
        arrived.append(jnp.concatenate(blocks, axis=0))
        results.append(expert(arrived[-1], w_ins, w_outs))
        if back is None:
            near_mid = after(near_mid, results[0][0])
            near_in = [to_plane(near_mid[:, 2 * i : 2 * i + 2], i) for i in near]
            near_in = jnp.concatenate(near_in, axis=1)
        back = [results[-1][0][i : i + 1] for i in range(nodes)]
        back = jnp.concatenate(to_nodes(back), axis=0)
        if len(results) == len(far):
            parts = all_weight_grads([near_in, *arrived], [near_result, *results])
            back, *parts = lax.optimization_barrier((back, *parts, backs[far[-2]]))[:-1]
        backs[d] = to_plane(back, d)
    near_out = [to_plane(near_result[0][:, 2 * i : 2 * i + 2], i) for i in near]
    near_out = over_nodes(jnp.concatenate(near_out, axis=1))
    for i, d in enumerate(near):
        backs[d] = near_out[:, 2 * i : 2 * i + 2]
    sums = [parts[0].astype(F32), parts[1].astype(F32)]
    for step in range(1, len(w_ins)):
        for i in (0, 1):
            sums[i] = sums[i] + from_owner(parts[2 * step + i], step).astype(F32)

    *backs, sums[0], sums[1] = lax.optimization_barrier((*backs, *sums))
    mixed, token_grad, gate_grad = combine(
        turn, numbers, pick, slot_weight, expert_ids.T, out_grad, backs
    )
    return (mixed, token_grad, gate_grad.T, sums[0][None], sums[1][None])


def solution(mesh):
    rows = P(("node", "local", "edata"), None)
    weights = P(("node", "local"), "edata", None)
    return jax.shard_map(
        shards,
        mesh=mesh,
        in_specs=(rows, rows, rows, rows, weights, weights),
        out_specs=(rows, rows, rows, weights, weights),
        check_vma=False,
    )
```

time: 293 us -> 262 us (0.89)
  the two profiles are of different devices: /device:TPU:0 before, /device:TPU:18 now
where the time goes in v6:
time: 262 us; the launch traced here: 261 us
  waiting for transfers between devices  128 us (49%)
  Pallas kernels  65 us (25%)
  starting transfers between devices  32.3 us (12%)
  other arithmetic  19.9 us (8%)
  local copies, waits for them, and re-layouts  14.9 us (6%)
    ppermute x6, waiting for transfers between devices, to_plane(): return lax.ppermute(rows, 'local', pairs)  91.1 us
    pallas_call x3, Pallas kernels, expert(): pl.pallas_call(lambda *refs: expert_kernel(len(w_ins), *refs), grid=(plan...  33 us
    ppermute x12, waiting for transfers between devices, to_nodes(): lax.ppermute(blocks[d], 'node', [(i, i ^ d) for i in range(count)])  20.7 us
    pallas_call x2, Pallas kernels, weight_grads(): pl.pallas_call(lambda *refs: weight_kernel(len(arrived), *refs), grid=(st...  17.2 us
    all_to_all x2, waiting for transfers between devices, over_nodes(): return lax.all_to_all(rows, 'node', split_axis=0, concat_axis=0, tiled=True)  16.4 us
    ppermute x12, starting transfers between devices, to_nodes(): lax.ppermute(blocks[d], 'node', [(i, i ^ d) for i in range(count)])  14.2 us
    add x2, other arithmetic, shards(): sums[i] = sums[i] + from_owner(parts[2 * step + i], step).astype(F32)  9.38 us
    all_to_all x2, starting transfers between devices, over_nodes(): return lax.all_to_all(rows, 'node', split_axis=0, concat_axis=0, tiled=True)  8.81 us
  transfers between devices with their start and end apart: 24, of which 12 were waited for; matrix products, arithmetic and copies ran while one was open for 12% of the time, Pallas kernels for 22%

profile of v6, /device:TPU:18, one launch (start us, length us, event | category | flops | bytes accessed | tf_op | source)
XLA Modules:
  0.0 261.4 jit_solution(16127284343538806982)
XLA Ops:
  5.2 3.1 %dispatch.2 = (bf16[4,2,32,2048]{3,2,1,0:T(8,128)(2,1)}, bf16[4,2,32,2048]{3,2,1,0:T(8,128)(2,1)}) custom-call(s32[1]{0:T(128)} %bitcast.turn_ref.refs_0_, bf16[256,256]{1,0:T(8,128)(2,1)} %get-tuple-element.101.pick_ref, f32[256,1]{1,0:T(8,128)} %slice.112.weight_ref, bf16[256,2048]{1,0:T(8,128)(2,1)} %x_ref.3, bf16[256,2048]{1,0:T(8,128)(2,1)} %refs_5_.1), custom_call_target="tpu_custom_call" | custom-call | flops 1 | bytes 1 | tf_op jit(solution)/shard_map/dispatch/pallas_call | solution.py:93
  9.4 3.1 %dispatch.3 = (bf16[4,2,32,2048]{3,2,1,0:T(8,128)(2,1)}, bf16[4,2,32,2048]{3,2,1,0:T(8,128)(2,1)}) custom-call(s32[1]{0:T(128)} %bitcast.turn_ref.refs_0_, bf16[256,256]{1,0:T(8,128)(2,1)} %get-tuple-element.44.pick_ref, f32[256,1]{1,0:T(8,128)} %slice.113.weight_ref, bf16[256,2048]{1,0:T(8,128)(2,1)} %x_ref.3, bf16[256,2048]{1,0:T(8,128)(2,1)} %refs_5_.1), custom_call_target="tpu_custom_call" | custom-call | flops 1 | bytes 1 | tf_op jit(solution)/shard_map/dispatch/pallas_call | solution.py:93
  12.5 3.0 %pad_maximum_fusion = bf16[4,4,32,2048]{3,2,1,0:T(8,128)(2,1)} fusion(bf16[4,2,32,2048]{3,2,1,0:T(8,128)(2,1)} %get-tuple-element.46, bf16[4,2,32,2048]{3,2,1,0:T(8,128)(2,1)} %get-tuple-element.45), kind=kLoop, calls=%fused_computation.2 | loop fusion | flops 1048576 | bytes 4194304 | tf_op jit(solution)/shard_map/concatenate | solution.py:345
  15.5 4.6 %all-to-all-start = ((bf16[4,4,32,2048]{3,2,1,0:T(8,128)(2,1)}), bf16[4,4,32,2048]{3,2,1,0:T(8,128)(2,1)}, u32[]{:S(2)}, u32[]{:S(2)}) async-start(bf16[4,4,32,2048]{3,2,1,0:T(8,128)(2,1)} %pad_maximum_fusion), calls=%async_computation | async-start | bytes 4194304 | tf_op jit(solution)/shard_map/all_to_all | solution.py:49
  20.2 33.9 %collective-permute-done = bf16[4,2,32,2048]{3,2,1,0:T(8,128)(2,1)} collective-permute-done((bf16[4,2,32,2048]{3,2,1,0:T(8,128)(2,1)}, bf16[4,2,32,2048]{3,2,1,0:T(8,128)(2,1)}, u32[]{:S(2)}, u32[]{:S(2)}) %collective-permute-start) | collective-permute-done | bytes 1048608 | tf_op jit(solution)/shard_map/ppermute | solution.py:45
  54.1 2.0 fusion.10
  59.7 5.8 %collective-permute-done.3 = bf16[1,2,32,2048]{3,2,1,0:T(8,128)(2,1)S(1)} collective-permute-done((bf16[1,2,32,2048]{3,2,1,0:T(8,128)(2,1)S(1)}, bf16[1,2,32,2048]{3,2,1,0:T(8,128)(2,1)S(1)}, u32[]{:S(2)}, u32[]{:S(2)}) %collective-permute-start.3) | collective-permute-done | bytes 262176 | tf_op jit(solution)/shard_map/ppermute | solution.py:55
  65.4 3.1 %collective-permute-done.4 = bf16[1,2,32,2048]{3,2,1,0:T(8,128)(2,1)S(1)} collective-permute-done((bf16[1,2,32,2048]{3,2,1,0:T(8,128)(2,1)S(1)}, bf16[1,2,32,2048]{3,2,1,0:T(8,128)(2,1)S(1)}, u32[]{:S(2)}, u32[]{:S(2)}) %collective-permute-start.4) | collective-permute-done | bytes 262176 | tf_op jit(solution)/shard_map/ppermute | solution.py:55
  68.6 1.6 collective-permute-done.5
  71.3 3.4 %collective-permute-start.7 = (bf16[4,2,32,2048]{3,2,1,0:T(8,128)(2,1)}, bf16[4,2,32,2048]{3,2,1,0:T(8,128)(2,1)}, u32[]{:S(2)}, u32[]{:S(2)}) collective-permute-start(bf16[4,2,32,2048]{3,2,1,0:T(8,128)(2,1)} %get-tuple-element.43), channel_id=1, source_target_pairs={{0,6},{2,4},{4,2},{6,0},{1,7},{3,5},{5,3},{7,1},{8,14},{10,12},{12... | collective-permute-start | bytes 3145736 | tf_op jit(solution)/shard_map/ppermute | solution.py:45
  74.7 9.4 %expert.3 = (bf16[4,2,32,2048]{3,2,1,0:T(8,128)(2,1)}, bf16[128,768]{1,0:T(8,128)(2,1)}, bf16[128,1536]{1,0:T(8,128)(2,1)}) custom-call(bf16[4,2,32,2048]{3,2,1,0:T(8,128)(2,1)} %pad_maximum_fusion.3.refs_0_.refs_1_, bf16[1024,1536]{1,0:T(8,128)(2,1)} %bitcast.18, bf16[1024,1536]{1,0:T(8,128)(2,1)} %copy-done, bf16[1024,768]{1,0:T(8,128)(2,1)} %bitcast.22, ...), custom_call_target="tpu_custom_call" | custom-call | flops 1 | bytes 1 | tf_op jit(solution)/shard_map/expert/pallas_call | solution.py:162
  84.1 1.8 fusion.6
  86.0 2.0 collective-permute-start.6
  88.1 1.8 collective-permute-start.10
  91.6 6.7 %collective-permute-done.10 = bf16[1,2,32,2048]{3,2,1,0:T(8,128)(2,1)S(1)} collective-permute-done((bf16[1,2,32,2048]{3,2,1,0:T(8,128)(2,1)S(1)}, bf16[1,2,32,2048]{3,2,1,0:T(8,128)(2,1)S(1)}, u32[]{:S(2)}, u32[]{:S(2)}) %collective-permute-start.10) | collective-permute-done | bytes 262176 | tf_op jit(solution)/shard_map/ppermute | solution.py:55
  98.3 2.6 collective-permute-done.8
  101.9 18.1 %collective-permute-done.7 = bf16[4,2,32,2048]{3,2,1,0:T(8,128)(2,1)} collective-permute-done((bf16[4,2,32,2048]{3,2,1,0:T(8,128)(2,1)}, bf16[4,2,32,2048]{3,2,1,0:T(8,128)(2,1)}, u32[]{:S(2)}, u32[]{:S(2)}) %collective-permute-start.7) | collective-permute-done | bytes 1048608 | tf_op jit(solution)/shard_map/ppermute | solution.py:45
  122.4 2.4 collective-permute-start.15
  126.4 14.1 %expert.4 = (bf16[4,4,32,2048]{3,2,1,0:T(8,128)(2,1)}, bf16[256,768]{1,0:T(8,128)(2,1)}, bf16[256,1536]{1,0:T(8,128)(2,1)}) custom-call(bf16[4,4,32,2048]{3,2,1,0:T(8,128)(2,1)} %pad_maximum_fusion.1.refs_0_, bf16[1024,1536]{1,0:T(8,128)(2,1)} %bitcast.19, bf16[1024,1536]{1,0:T(8,128)(2,1)} %copy-done, bf16[1024,768]{1,0:T(8,128)(2,1)} %bitcast.23, ...), custom_call_target="tpu_custom_call" | custom-call | flops 1 | bytes 1 | tf_op jit(solution)/shard_map/expert/pallas_call | solution.py:162
  141.6 9.4 %expert.5 = (bf16[4,2,32,2048]{3,2,1,0:T(8,128)(2,1)}, bf16[128,768]{1,0:T(8,128)(2,1)}, bf16[128,1536]{1,0:T(8,128)(2,1)}) custom-call(bf16[4,2,32,2048]{3,2,1,0:T(8,128)(2,1)} %copy-done.1, bf16[1024,1536]{1,0:T(8,128)(2,1)} %bitcast.20, bf16[1024,1536]{1,0:T(8,128)(2,1)} %copy-done, bf16[1024,768]{1,0:T(8,128)(2,1)} %bitcast.24, ...), custom_call_target="tpu_custom_call" | custom-call | flops 1 | bytes 1 | tf_op jit(solution)/shard_map/expert/pallas_call | solution.py:162
  153.6 2.4 collective-permute-start.18
  156.2 2.4 collective-permute-start.11
  158.6 8.6 %weight_grads.3 = (bf16[1024,1536]{1,0:T(8,128)(2,1)}, bf16[1024,768]{1,0:T(8,128)(2,1)}) custom-call(bf16[4,4,32,2048]{3,2,1,0:T(8,128)(2,1)} %pad_maximum_fusion.1.refs_0_, bf16[4,2,32,2048]{3,2,1,0:T(8,128)(2,1)} %pad_maximum_fusion.3.refs_0_.refs_1_, bf16[4,2,32,2048]{3,2,1,0:T(8,128)(2,1)} %copy-done.1, bf16[256,768]{1,0:T(8,128)(2,1)} %get-tuple-element.55.refs_3_, ...), custom_call_target="tpu_custom_call" | custom-call | flops 1 | bytes 1 | tf_op jit(solution)/shard_map/weight_grads/pallas_call | solution.py:211
  167.1 8.6 %weight_grads.2 = (bf16[1024,1536]{1,0:T(8,128)(2,1)}, bf16[1024,768]{1,0:T(8,128)(2,1)}) custom-call(bf16[4,4,32,2048]{3,2,1,0:T(8,128)(2,1)} %pad_maximum_fusion.1.refs_0_, bf16[4,2,32,2048]{3,2,1,0:T(8,128)(2,1)} %pad_maximum_fusion.3.refs_0_.refs_1_, bf16[4,2,32,2048]{3,2,1,0:T(8,128)(2,1)} %copy-done.1, bf16[256,768]{1,0:T(8,128)(2,1)} %get-tuple-element.55.refs_3_, ...), custom_call_target="tpu_custom_call" | custom-call | flops 1 | bytes 1 | tf_op jit(solution)/shard_map/weight_grads/pallas_call | solution.py:211
  176.9 8.3 %collective-permute-done.12.refs_8_ = bf16[4,2,32,2048]{3,2,1,0:T(8,128)(2,1)S(1)} collective-permute-done((bf16[4,2,32,2048]{3,2,1,0:T(8,128)(2,1)S(1)}, bf16[4,2,32,2048]{3,2,1,0:T(8,128)(2,1)S(1)}, u32[]{:S(2)}, u32[]{:S(2)}) %collective-permute-start.12) | collective-permute-done | bytes 1048608 | tf_op jit(solution)/shard_map/ppermute | solution.py:45
  185.7 15.3 %collective-permute-done.11 = bf16[4,2,32,2048]{3,2,1,0:T(8,128)(2,1)S(1)} collective-permute-done((bf16[4,2,32,2048]{3,2,1,0:T(8,128)(2,1)S(1)}, bf16[4,2,32,2048]{3,2,1,0:T(8,128)(2,1)S(1)}, u32[]{:S(2)}, u32[]{:S(2)}) %collective-permute-start.11) | collective-permute-done | bytes 1048608 | tf_op jit(solution)/shard_map/ppermute | solution.py:45
  202.6 4.2 %all-to-all-start.1 = ((bf16[4,4,32,2048]{3,2,1,0:T(8,128)(2,1)}), bf16[4,4,32,2048]{3,2,1,0:T(8,128)(2,1)S(1)}, u32[]{:S(2)}, u32[]{:S(2)}) async-start(bf16[4,4,32,2048]{3,2,1,0:T(8,128)(2,1)} %pad_maximum_fusion.2), calls=%async_computation.1 | async-start | bytes 4194304 | tf_op jit(solution)/shard_map/all_to_all | solution.py:49
  207.7 3.9 %convert_add_fusion.1 = f32[1024,768]{1,0:T(8,128)} fusion(bf16[1024,768]{1,0:T(8,128)(2,1)} %collective-permute-done.21, bf16[1024,768]{1,0:T(8,128)(2,1)} %get-tuple-element.68), kind=kLoop, calls=%fused_computation.1 | loop fusion | flops 2359296 | bytes 6291456 | tf_op jit(solution)/shard_map/add | solution.py:377
  211.6 16.4 %all-to-all-done.1 = bf16[4,4,32,2048]{3,2,1,0:T(8,128)(2,1)S(1)} async-done(((bf16[4,4,32,2048]{3,2,1,0:T(8,128)(2,1)}), bf16[4,4,32,2048]{3,2,1,0:T(8,128)(2,1)S(1)}, u32[]{:S(2)}, u32[]{:S(2)}) %all-to-all-start.1) | async-done | bytes 2097184 | tf_op jit(solution)/shard_map/all_to_all | solution.py:49
  230.7 5.5 %convert_add_fusion = f32[1024,1536]{1,0:T(8,128)} fusion(bf16[1024,1536]{1,0:T(8,128)(2,1)} %collective-permute-done.20, bf16[1024,1536]{1,0:T(8,128)(2,1)S(1)} %copy-done.2), kind=kLoop, calls=%fused_computation | loop fusion | flops 4718592 | bytes 12582912 | tf_op jit(solution)/shard_map/add | solution.py:377
  236.2 15.6 %collective-permute-done.19.refs_9_ = bf16[4,2,32,2048]{3,2,1,0:T(8,128)(2,1)S(1)} collective-permute-done((bf16[4,2,32,2048]{3,2,1,0:T(8,128)(2,1)}, bf16[4,2,32,2048]{3,2,1,0:T(8,128)(2,1)S(1)}, u32[]{:S(2)}, u32[]{:S(2)}) %collective-permute-start.19) | collective-permute-done | bytes 1048608 | tf_op jit(solution)/shard_map/ppermute | solution.py:45
  252.7 8.7 %combine.1 = (bf16[256,2048]{1,0:T(8,128)(2,1)}, bf16[256,2048]{1,0:T(8,128)(2,1)}, f32[8,256]{1,0:T(8,128)}) custom-call(s32[1]{0:T(128)} %bitcast.turn_ref.refs_0_, s32[16]{0:T(128)} %copy-done.8, bf16[512,256]{1,0:T(8,128)(2,1)} %copy-done.3, f32[512,1]{1,0:T(8,128)} %reshape.79.refs_3_, s32[8,256]{1,0:T(8,128)} %bitcast.29, bf16[256,2048]{1,0:T(8,128)(2,1)} %refs_5_.1, ...), custom_call_target="tpu_custom_call" | custom-call | flops 1 | bytes 1 | tf_op jit(solution)/shard_map/combine/pallas_call | solution.py:296
  (77 shorter events, 28.7 us)
Async XLA Ops:
  0.6 53.5 %collective-permute-start.1 = (bf16[1024,1536]{1,0:T(8,128)(2,1)}, bf16[1024,1536]{1,0:T(8,128)(2,1)S(1)}, u32[]{:S(2)}, u32[]{:S(2)}) collective-permute-start(bf16[1024,1536]{1,0:T(8,128)(2,1)} %bitcast.17), channel_id=1, source_target_pairs={{1,0},{0,1},{3,2},{2,3},{5,4},{4,5},{7,6},{6,7},{9,8},{8,9},{11,10... | collective-permute-start | bytes 9437192 | tf_op jit(solution)/shard_map/ppermute | solution.py:64
  0.7 53.4 %collective-permute-start.2 = (bf16[1024,768]{1,0:T(8,128)(2,1)}, bf16[1024,768]{1,0:T(8,128)(2,1)}, u32[]{:S(2)}, u32[]{:S(2)}) collective-permute-start(bf16[1024,768]{1,0:T(8,128)(2,1)} %bitcast.21), channel_id=1, source_target_pairs={{1,0},{0,1},{3,2},{2,3},{5,4},{4,5},{7,6},{6,7},{9,8},{8,9},{11,10... | collective-permute-start | bytes 4718600 | tf_op jit(solution)/shard_map/ppermute | solution.py:64
  1.4 11.1 %copy-start.8 = (s32[16]{0:T(128)}, s32[16]{0:T(128)S(1)}, u32[]{:S(2)}) copy-start(s32[16]{0:T(128)S(1)} %add.24.refs_1_) | copy-start | bytes 196
  4.4 8.1 %copy-start.3 = (bf16[512,256]{1,0:T(8,128)(2,1)}, bf16[512,256]{1,0:T(8,128)(2,1)S(1)}, u32[]{:S(2)}) copy-start(bf16[512,256]{1,0:T(8,128)(2,1)S(1)} %fusion.2.refs_2_) | copy-start | bytes 786436
  8.3 45.8 %collective-permute-start = (bf16[4,2,32,2048]{3,2,1,0:T(8,128)(2,1)}, bf16[4,2,32,2048]{3,2,1,0:T(8,128)(2,1)}, u32[]{:S(2)}, u32[]{:S(2)}) collective-permute-start(bf16[4,2,32,2048]{3,2,1,0:T(8,128)(2,1)} %get-tuple-element.42), channel_id=1, source_target_pairs={{0,4},{2,6},{4,0},{6,2},{1,5},{3,7},{5,1},{7,3},{8,12},{10,14},{12... | collective-permute-start | bytes 3145736 | tf_op jit(solution)/shard_map/ppermute | solution.py:45
  15.5 68.6 %all-to-all-start = ((bf16[4,4,32,2048]{3,2,1,0:T(8,128)(2,1)}), bf16[4,4,32,2048]{3,2,1,0:T(8,128)(2,1)}, u32[]{:S(2)}, u32[]{:S(2)}) async-start(bf16[4,4,32,2048]{3,2,1,0:T(8,128)(2,1)} %pad_maximum_fusion), calls=%async_computation | async-start | bytes 4194304 | tf_op jit(solution)/shard_map/all_to_all | solution.py:49
  54.1 17.2 %copy-start = (bf16[1024,1536]{1,0:T(8,128)(2,1)}, bf16[1024,1536]{1,0:T(8,128)(2,1)S(1)}, u32[]{:S(2)}) copy-start(bf16[1024,1536]{1,0:T(8,128)(2,1)S(1)} %collective-permute-done.1.refs_2_) | copy-start | bytes 9437188
  56.1 9.3 %collective-permute-start.3 = (bf16[1,2,32,2048]{3,2,1,0:T(8,128)(2,1)S(1)}, bf16[1,2,32,2048]{3,2,1,0:T(8,128)(2,1)S(1)}, u32[]{:S(2)}, u32[]{:S(2)}) collective-permute-start(bf16[1,2,32,2048]{3,2,1,0:T(8,128)(2,1)S(1)} %get-tuple-element.100), channel_id=1, source_target_pairs={{0,8},{8,0},{16,24},{24,16},{1,9},{9,1},{17,25},{25,17},{2,10},{10... | collective-permute-start | bytes 786440 | tf_op jit(solution)/shard_map/ppermute | solution.py:55
  56.7 11.9 %collective-permute-start.4 = (bf16[1,2,32,2048]{3,2,1,0:T(8,128)(2,1)S(1)}, bf16[1,2,32,2048]{3,2,1,0:T(8,128)(2,1)S(1)}, u32[]{:S(2)}, u32[]{:S(2)}) collective-permute-start(bf16[1,2,32,2048]{3,2,1,0:T(8,128)(2,1)S(1)} %get-tuple-element.99), channel_id=1, source_target_pairs={{0,16},{8,24},{16,0},{24,8},{1,17},{9,25},{17,1},{25,9},{2,18},{10... | collective-permute-start | bytes 786440 | tf_op jit(solution)/shard_map/ppermute | solution.py:55
  58.3 12.0 %collective-permute-start.5 = (bf16[1,2,32,2048]{3,2,1,0:T(8,128)(2,1)S(1)}, bf16[1,2,32,2048]{3,2,1,0:T(8,128)(2,1)S(1)}, u32[]{:S(2)}, u32[]{:S(2)}) collective-permute-start(bf16[1,2,32,2048]{3,2,1,0:T(8,128)(2,1)S(1)} %get-tuple-element.98), channel_id=1, source_target_pairs={{0,24},{8,16},{16,8},{24,0},{1,25},{9,17},{17,9},{25,1},{2,26},{10... | collective-permute-start | bytes 786440 | tf_op jit(solution)/shard_map/ppermute | solution.py:55
  71.3 48.7 %collective-permute-start.7 = (bf16[4,2,32,2048]{3,2,1,0:T(8,128)(2,1)}, bf16[4,2,32,2048]{3,2,1,0:T(8,128)(2,1)}, u32[]{:S(2)}, u32[]{:S(2)}) collective-permute-start(bf16[4,2,32,2048]{3,2,1,0:T(8,128)(2,1)} %get-tuple-element.43), channel_id=1, source_target_pairs={{0,6},{2,4},{4,2},{6,0},{1,7},{3,5},{5,3},{7,1},{8,14},{10,12},{12... | collective-permute-start | bytes 3145736 | tf_op jit(solution)/shard_map/ppermute | solution.py:45
  84.1 3.8 %copy-start.7 = (bf16[4,2,32,2048]{3,2,1,0:T(8,128)(2,1)S(1)}, bf16[4,2,32,2048]{3,2,1,0:T(8,128)(2,1)}, u32[]{:S(2)}) copy-start(bf16[4,2,32,2048]{3,2,1,0:T(8,128)(2,1)} %get-tuple-element.48) | copy-start | bytes 3145732
  86.0 38.9 %collective-permute-start.6 = (bf16[4,2,32,2048]{3,2,1,0:T(8,128)(2,1)S(1)}, bf16[4,2,32,2048]{3,2,1,0:T(8,128)(2,1)S(1)}, u32[]{:S(2)}, u32[]{:S(2)}) collective-permute-start(bf16[4,2,32,2048]{3,2,1,0:T(8,128)(2,1)S(1)} %get-tuple-element.84), channel_id=1, source_target_pairs={{0,2},{2,0},{4,6},{6,4},{1,3},{3,1},{5,7},{7,5},{8,10},{10,8},{12,... | collective-permute-start | bytes 3145736 | tf_op jit(solution)/shard_map/ppermute | solution.py:45
  88.1 10.2 %collective-permute-start.10 = (bf16[1,2,32,2048]{3,2,1,0:T(8,128)(2,1)S(1)}, bf16[1,2,32,2048]{3,2,1,0:T(8,128)(2,1)S(1)}, u32[]{:S(2)}, u32[]{:S(2)}) collective-permute-start(bf16[1,2,32,2048]{3,2,1,0:T(8,128)(2,1)S(1)} %get-tuple-element.94), channel_id=1, source_target_pairs={{0,24},{8,16},{16,8},{24,0},{1,25},{9,17},{17,9},{25,1},{2,26},{10... | collective-permute-start | bytes 786440 | tf_op jit(solution)/shard_map/ppermute | solution.py:55
  89.9 11.0 %collective-permute-start.8 = (bf16[1,2,32,2048]{3,2,1,0:T(8,128)(2,1)S(1)}, bf16[1,2,32,2048]{3,2,1,0:T(8,128)(2,1)S(1)}, u32[]{:S(2)}, u32[]{:S(2)}) collective-permute-start(bf16[1,2,32,2048]{3,2,1,0:T(8,128)(2,1)S(1)} %get-tuple-element.96), channel_id=1, source_target_pairs={{0,8},{8,0},{16,24},{24,16},{1,9},{9,1},{17,25},{25,17},{2,10},{10... | collective-permute-start | bytes 786440 | tf_op jit(solution)/shard_map/ppermute | solution.py:55
  90.4 11.3 %collective-permute-start.9 = (bf16[1,2,32,2048]{3,2,1,0:T(8,128)(2,1)S(1)}, bf16[1,2,32,2048]{3,2,1,0:T(8,128)(2,1)S(1)}, u32[]{:S(2)}, u32[]{:S(2)}) collective-permute-start(bf16[1,2,32,2048]{3,2,1,0:T(8,128)(2,1)S(1)} %get-tuple-element.95), channel_id=1, source_target_pairs={{0,16},{8,24},{16,0},{24,8},{1,17},{9,25},{17,1},{25,9},{2,18},{10... | collective-permute-start | bytes 786440 | tf_op jit(solution)/shard_map/ppermute | solution.py:55
  121.3 19.2 %collective-permute-start.13 = (bf16[1,2,32,2048]{3,2,1,0:T(8,128)(2,1)S(1)}, bf16[1,2,32,2048]{3,2,1,0:T(8,128)(2,1)S(1)}, u32[]{:S(2)}, u32[]{:S(2)}) collective-permute-start(bf16[1,2,32,2048]{3,2,1,0:T(8,128)(2,1)S(1)} %get-tuple-element.91), channel_id=1, source_target_pairs={{0,8},{8,0},{16,24},{24,16},{1,9},{9,1},{17,25},{25,17},{2,10},{10... | collective-permute-start | bytes 786440 | tf_op jit(solution)/shard_map/ppermute | solution.py:55
  121.9 18.6 %collective-permute-start.14 = (bf16[1,2,32,2048]{3,2,1,0:T(8,128)(2,1)S(1)}, bf16[1,2,32,2048]{3,2,1,0:T(8,128)(2,1)S(1)}, u32[]{:S(2)}, u32[]{:S(2)}) collective-permute-start(bf16[1,2,32,2048]{3,2,1,0:T(8,128)(2,1)S(1)} %get-tuple-element.90), channel_id=1, source_target_pairs={{0,16},{8,24},{16,0},{24,8},{1,17},{9,25},{17,1},{25,9},{2,18},{10... | collective-permute-start | bytes 786440 | tf_op jit(solution)/shard_map/ppermute | solution.py:55
  122.4 18.1 %collective-permute-start.15 = (bf16[1,2,32,2048]{3,2,1,0:T(8,128)(2,1)S(1)}, bf16[1,2,32,2048]{3,2,1,0:T(8,128)(2,1)S(1)}, u32[]{:S(2)}, u32[]{:S(2)}) collective-permute-start(bf16[1,2,32,2048]{3,2,1,0:T(8,128)(2,1)S(1)} %get-tuple-element.89), channel_id=1, source_target_pairs={{0,24},{8,16},{16,8},{24,0},{1,25},{9,17},{17,9},{25,1},{2,26},{10... | collective-permute-start | bytes 786440 | tf_op jit(solution)/shard_map/ppermute | solution.py:55
  140.6 44.6 %collective-permute-start.12 = (bf16[4,2,32,2048]{3,2,1,0:T(8,128)(2,1)S(1)}, bf16[4,2,32,2048]{3,2,1,0:T(8,128)(2,1)S(1)}, u32[]{:S(2)}, u32[]{:S(2)}) collective-permute-start(bf16[4,2,32,2048]{3,2,1,0:T(8,128)(2,1)S(1)} %pad_maximum_fusion.4), channel_id=1, source_target_pairs={{0,4},{2,6},{4,0},{6,2},{1,5},{3,7},{5,1},{7,3},{8,12},{10,14},{12... | collective-permute-start | bytes 3145736 | tf_op jit(solution)/shard_map/ppermute | solution.py:45
  151.0 5.0 %copy-start.4 = (bf16[4,4,32,2048]{3,2,1,0:T(8,128)(2,1)S(1)}, bf16[4,4,32,2048]{3,2,1,0:T(8,128)(2,1)}, u32[]{:S(2)}) copy-start(bf16[4,4,32,2048]{3,2,1,0:T(8,128)(2,1)} %get-tuple-element.52) | copy-start | bytes 6291460
  152.4 23.3 %collective-permute-start.16 = (bf16[1,2,32,2048]{3,2,1,0:T(8,128)(2,1)S(1)}, bf16[1,2,32,2048]{3,2,1,0:T(8,128)(2,1)S(1)}, u32[]{:S(2)}, u32[]{:S(2)}) collective-permute-start(bf16[1,2,32,2048]{3,2,1,0:T(8,128)(2,1)S(1)} %get-tuple-element.88), channel_id=1, source_target_pairs={{0,8},{8,0},{16,24},{24,16},{1,9},{9,1},{17,25},{25,17},{2,10},{10... | collective-permute-start | bytes 786440 | tf_op jit(solution)/shard_map/ppermute | solution.py:55
  153.1 22.7 %collective-permute-start.17 = (bf16[1,2,32,2048]{3,2,1,0:T(8,128)(2,1)S(1)}, bf16[1,2,32,2048]{3,2,1,0:T(8,128)(2,1)S(1)}, u32[]{:S(2)}, u32[]{:S(2)}) collective-permute-start(bf16[1,2,32,2048]{3,2,1,0:T(8,128)(2,1)S(1)} %get-tuple-element.87), channel_id=1, source_target_pairs={{0,16},{8,24},{16,0},{24,8},{1,17},{9,25},{17,1},{25,9},{2,18},{10... | collective-permute-start | bytes 786440 | tf_op jit(solution)/shard_map/ppermute | solution.py:55
  153.6 22.2 %collective-permute-start.18 = (bf16[1,2,32,2048]{3,2,1,0:T(8,128)(2,1)S(1)}, bf16[1,2,32,2048]{3,2,1,0:T(8,128)(2,1)S(1)}, u32[]{:S(2)}, u32[]{:S(2)}) collective-permute-start(bf16[1,2,32,2048]{3,2,1,0:T(8,128)(2,1)S(1)} %get-tuple-element.86), channel_id=1, source_target_pairs={{0,24},{8,16},{16,8},{24,0},{1,25},{9,17},{17,9},{25,1},{2,26},{10... | collective-permute-start | bytes 786440 | tf_op jit(solution)/shard_map/ppermute | solution.py:55
  156.2 44.8 %collective-permute-start.11 = (bf16[4,2,32,2048]{3,2,1,0:T(8,128)(2,1)S(1)}, bf16[4,2,32,2048]{3,2,1,0:T(8,128)(2,1)S(1)}, u32[]{:S(2)}, u32[]{:S(2)}) collective-permute-start(bf16[4,2,32,2048]{3,2,1,0:T(8,128)(2,1)S(1)} %get-tuple-element.82), channel_id=1, source_target_pairs={{0,2},{2,0},{4,6},{6,4},{1,3},{3,1},{5,7},{7,5},{8,10},{10,8},{12,... | collective-permute-start | bytes 3145736 | tf_op jit(solution)/shard_map/ppermute | solution.py:45
  185.2 17.4 %copy-start.5 = (bf16[4,2,32,2048]{3,2,1,0:T(8,128)(2,1)}, bf16[4,2,32,2048]{3,2,1,0:T(8,128)(2,1)S(1)}, u32[]{:S(2)}) copy-start(bf16[4,2,32,2048]{3,2,1,0:T(8,128)(2,1)S(1)} %collective-permute-done.12.refs_8_) | copy-start | bytes 3145732
  185.2 44.4 %collective-permute-start.20 = (bf16[1024,1536]{1,0:T(8,128)(2,1)}, bf16[1024,1536]{1,0:T(8,128)(2,1)}, u32[]{:S(2)}, u32[]{:S(2)}) collective-permute-start(bf16[1024,1536]{1,0:T(8,128)(2,1)} %get-tuple-element.67), channel_id=1, source_target_pairs={{0,1},{1,0},{2,3},{3,2},{4,5},{5,4},{6,7},{7,6},{8,9},{9,8},{10,11... | collective-permute-start | bytes 9437192 | tf_op jit(solution)/shard_map/ppermute | solution.py:70
  185.2 22.5 %collective-permute-start.21 = (bf16[1024,768]{1,0:T(8,128)(2,1)}, bf16[1024,768]{1,0:T(8,128)(2,1)}, u32[]{:S(2)}, u32[]{:S(2)}) collective-permute-start(bf16[1024,768]{1,0:T(8,128)(2,1)} %get-tuple-element.69), channel_id=1, source_target_pairs={{0,1},{1,0},{2,3},{3,2},{4,5},{5,4},{6,7},{7,6},{8,9},{9,8},{10,11... | collective-permute-start | bytes 4718600 | tf_op jit(solution)/shard_map/ppermute | solution.py:70
  202.6 25.5 %all-to-all-start.1 = ((bf16[4,4,32,2048]{3,2,1,0:T(8,128)(2,1)}), bf16[4,4,32,2048]{3,2,1,0:T(8,128)(2,1)S(1)}, u32[]{:S(2)}, u32[]{:S(2)}) async-start(bf16[4,4,32,2048]{3,2,1,0:T(8,128)(2,1)} %pad_maximum_fusion.2), calls=%async_computation.1 | async-start | bytes 4194304 | tf_op jit(solution)/shard_map/all_to_all | solution.py:49
  207.7 44.0 %collective-permute-start.19 = (bf16[4,2,32,2048]{3,2,1,0:T(8,128)(2,1)}, bf16[4,2,32,2048]{3,2,1,0:T(8,128)(2,1)S(1)}, u32[]{:S(2)}, u32[]{:S(2)}) collective-permute-start(bf16[4,2,32,2048]{3,2,1,0:T(8,128)(2,1)} %pad_maximum_fusion.5), channel_id=1, source_target_pairs={{0,6},{2,4},{4,2},{6,0},{1,7},{3,5},{5,3},{7,1},{8,14},{10,12},{12... | collective-permute-start | bytes 3145736 | tf_op jit(solution)/shard_map/ppermute | solution.py:45
  228.0 2.6 %copy-start.2 = (bf16[1024,1536]{1,0:T(8,128)(2,1)S(1)}, bf16[1024,1536]{1,0:T(8,128)(2,1)}, u32[]{:S(2)}) copy-start(bf16[1024,1536]{1,0:T(8,128)(2,1)} %get-tuple-element.66) | copy-start | bytes 9437188
  251.7 1.0 copy-start.6
  (1 other events, 1.0 us)

commit v7 on v3

v7 whole, which is shorter than its diff:
```python
import jax
import jax.numpy as jnp
from jax import lax
from jax.experimental import pallas as pl
from jax.experimental.pallas import tpu as pltpu
from jax.sharding import PartitionSpec as P

EXP_DEV = 4
BF = jnp.bfloat16
F32 = jnp.float32
ROWS_IN = (((0,), (0,)), ((), ()))
COLS_IN = (((1,), (1,)), ((), ()))
LIMIT = 56 * 1024 * 1024
CHEAP = pl.CostEstimate(flops=1, bytes_accessed=1, transcendentals=0)
VMEM = pl.BlockSpec(memory_space=pltpu.VMEM)


def call(kernel, name, **more):
    return pl.pallas_call(
        kernel,
        compiler_params=pltpu.CompilerParams(vmem_limit_bytes=LIMIT),
        cost_estimate=CHEAP,
        name=name,
        **more,
    )


def shape(*dims, kind=BF):
    return jax.ShapeDtypeStruct(dims, kind)


def after(value, *others):
    return lax.optimization_barrier((value, *others))[0]


def slot_tables(expert_ids, gates, numbers, capacity):
    tok_rows = expert_ids.shape[0]
    ids_t = expert_ids.T
    chosen = ids_t[None, :, :] == numbers[:, None, None]
    routed = jnp.any(chosen, axis=1)
    earlier = jnp.arange(tok_rows)[:, None] < jnp.arange(tok_rows)[None, :]
    order_in = jnp.dot(
        routed.astype(BF), earlier.astype(BF), preferred_element_type=F32
    ).astype(jnp.int32)
    weight = jnp.sum(jnp.where(chosen, gates.T[None, :, :], 0.0), axis=1)
    slot_ids = jnp.arange(capacity, dtype=jnp.int32)
    hits = routed[:, None, :] & (order_in[:, None, :] == slot_ids[None, :, None])
    slot_weight = jnp.sum(jnp.where(hits, weight[:, None, :], 0.0), axis=2)
    return hits.reshape(numbers.shape[0] * capacity, tok_rows).astype(BF), slot_weight.reshape(-1, 1)


class Ring:
    def __init__(self, nodes, planes):
        self.nodes, self.planes, self.half = nodes, planes, planes // 2
        self.cut = nodes // 2
        self.up_size = nodes * (self.half - 1) + self.cut
        self.down_size = nodes * (self.half - 1) + nodes - self.cut

    def shapes(self, capacity, width):
        return [
            shape(n, capacity, width) for n in (self.nodes, self.up_size, self.down_size)
        ]

    def place(self, refs, distance, value, columns=slice(None)):
        own, up, down = refs
        nodes, half = self.nodes, self.half
        if distance == 0:
            own[:, :, columns] = value
        elif distance < half:
            up[(distance - 1) * nodes : distance * nodes, :, columns] = value
        elif distance > half:
            back = self.planes - distance
            down[(back - 1) * nodes : back * nodes, :, columns] = value
        else:
            up[(half - 1) * nodes :, :, columns] = value[: self.cut]
            down[(half - 1) * nodes :, :, columns] = value[self.cut :]

    def send(self, own, up, down):
        got = [own]
        for first, way, last in ((up, 1, self.cut), (down, -1, self.nodes - self.cut)):
            now = first
            for step in range(1, self.half + 1):
                pairs = [(i, (i + way) % self.planes) for i in range(self.planes)]
                now = lax.ppermute(now, "local", pairs)
                got.append(now)
                if step < self.half:
                    now = now[self.nodes :]
        return got

    def take(self, got, distance):
        nodes, half = self.nodes, self.half
        if distance == 0:
            return got[0][...]
        if distance < half:
            return got[distance][:nodes]
        if distance > half:
            return got[half + self.planes - distance][:nodes]
        return jnp.concatenate([got[half][...], got[2 * half][...]], axis=0)


def over_nodes(rows):
    return lax.all_to_all(rows, "node", split_axis=0, concat_axis=0, tiled=True)


def gathered(shard):
    count = lax.axis_size("edata")
    shards = [shard]
    for step in range(1, count):
        pairs = [((i + step) % count, i) for i in range(count)]
        shards.append(lax.ppermute(shard, "edata", pairs))
    return shards


def from_owner(piece, step):
    count = lax.axis_size("edata")
    return lax.ppermute(piece, "edata", [(i, (i + step) % count) for i in range(count)])


def column_tiles(width, most):
    count = lax.axis_size("edata")
    tile = min(most, width // count)
    steps = width // tile
    return tile, steps, lambda i, turn: (i + turn * (steps // count)) % steps


def dispatch_x(ring, turn, pick, tokens, capacity):
    slots, tok_rows = pick.shape
    width = tokens.shape[1]
    tile, steps, turned = column_tiles(width, 1024)
    size = ring.nodes * capacity

    def kernel(turn_ref, pick_ref, x_ref, *refs):
        rows = jnp.dot(pick_ref[...], x_ref[...], preferred_element_type=F32).astype(BF)
        for d in range(ring.planes):
            part = rows[d * size : (d + 1) * size]
            ring.place(refs, d, part.reshape(ring.nodes, capacity, tile))

    shapes = ring.shapes(capacity, width)
    return call(
        kernel,
        "dispatch_x",
        grid_spec=pltpu.PrefetchScalarGridSpec(
            num_scalar_prefetch=1,
            grid=(steps,),
            in_specs=[
                pl.BlockSpec((slots, tok_rows), lambda i, t: (0, 0)),
                pl.BlockSpec((tok_rows, tile), lambda i, t: (0, turned(i, t[0]))),
            ],
            out_specs=[pl.BlockSpec(s.shape[:2] + (tile,), lambda i, t: (0, 0, i)) for s in shapes],
        ),
        out_shape=shapes,
    )(turn, pick, tokens)


def dispatch_dy(ring, turn, pick, weight, out_grad, capacity):
    slots, tok_rows = pick.shape
    width = out_grad.shape[1]
    tile, steps, turned = column_tiles(width, 1024)
    size = ring.nodes * capacity

    def kernel(turn_ref, pick_ref, weight_ref, grad_ref, out_ref, rows_ref):
        rows = jnp.dot(pick_ref[...], grad_ref[...], preferred_element_type=F32)
        rows_ref[...] = rows.astype(BF)
        scaled = (weight_ref[...] * rows).astype(BF)
        for d in range(ring.planes):
            part = scaled[d * size : (d + 1) * size]
            out_ref[:, d] = part.reshape(ring.nodes, capacity, tile)

    return call(
        kernel,
        "dispatch_dy",
        grid_spec=pltpu.PrefetchScalarGridSpec(
            num_scalar_prefetch=1,
            grid=(steps,),
            in_specs=[
                pl.BlockSpec((slots, tok_rows), lambda i, t: (0, 0)),
                pl.BlockSpec((slots, 1), lambda i, t: (0, 0)),
                pl.BlockSpec((tok_rows, tile), lambda i, t: (0, turned(i, t[0]))),
            ],
            out_specs=[
                pl.BlockSpec(
                    (ring.nodes, ring.planes, capacity, tile), lambda i, t: (0, 0, 0, i)
                ),
                pl.BlockSpec((slots, tile), lambda i, t: (0, i)),
            ],
        ),
        out_shape=[
            shape(ring.nodes, ring.planes, capacity, width),
            shape(slots, width),
        ],
    )(turn, pick, weight, out_grad)


def pack(ring, got):
    _, capacity, width = got[0].shape
    tile = min(1024, width)

    def kernel(*refs):
        for d in range(ring.planes):
            refs[-1][:, d] = ring.take(refs[:-1], d)

    used = [ring.nodes]
    for last in (ring.cut, ring.nodes - ring.cut):
        used += [ring.nodes] * (ring.half - 1) + [last]
    return call(
        kernel,
        "pack",
        grid=(width // tile,),
        in_specs=[pl.BlockSpec((n, capacity, tile), lambda i: (0, 0, i)) for n in used],
        out_specs=pl.BlockSpec(
            (ring.nodes, ring.planes, capacity, tile), lambda i: (0, 0, 0, i)
        ),
        out_shape=shape(ring.nodes, ring.planes, capacity, width),
    )(*got)


def unpack(ring, rows, back):
    _, _, capacity, width = rows.shape
    tile = min(1024, width)

    def kernel(rows_ref, *refs):
        for d in range(ring.planes):
            ring.place(refs, -d % ring.planes if back else d, rows_ref[:, d])

    shapes = ring.shapes(capacity, width)
    return call(
        kernel,
        "unpack",
        grid=(width // tile,),
        in_specs=[
            pl.BlockSpec((ring.nodes, ring.planes, capacity, tile), lambda i: (0, 0, 0, i))
        ],
        out_specs=[pl.BlockSpec(s.shape[:2] + (tile,), lambda i: (0, 0, i)) for s in shapes],
        out_shape=shapes,
    )(rows)


def expert(ring, x_rows, dy_got, w_ins, w_outs):
    nodes, planes, capacity, model = x_rows.shape
    size = nodes * capacity
    rows = planes * size
    count = len(w_ins)
    width = model // count
    double, hidden = w_ins[0].shape[1], w_outs[0].shape[1]
    many = max(1, min(256, rows) // size)

    def kernel(x_ref, *refs):
        got, refs = refs[: len(dy_got)], refs[len(dy_got) :]
        ins, outs, refs = refs[:count], refs[count : 2 * count], refs[2 * count :]
        y_refs, (dx_ref, inner_ref, act_grad_ref, xs_ref, dys_ref, act_ref) = refs[:3], refs[3:]
        for first in range(0, planes, many):
            band = slice(first * size, (first + many) * size)
            for d in range(first, first + many):
                here = slice(d * size, (d + 1) * size)
                xs_ref[here] = x_ref[:, d].reshape(size, model)
                dys_ref[here] = ring.take(got, d).reshape(size, model)

            def product(source, weights):
                total = None
                for s in range(count):
                    one = jnp.dot(
                        source[band, s * width : (s + 1) * width],
                        weights[s][...],
                        preferred_element_type=F32,
                    )
                    total = one if total is None else total + one
                return total

            act_ref[...] = product(xs_ref, ins)
            act_gate = act_ref[:, :hidden]
            act_up = act_ref[:, hidden:]
            sig = jax.nn.sigmoid(act_gate)
            swished = act_gate * sig
            inner_ref[band] = (swished * act_up).astype(BF)
            inner_grad = product(dys_ref, outs)
            act_grad_ref[band, :hidden] = (
                inner_grad * act_up * sig * (1.0 + act_gate * (1.0 - sig))
            ).astype(BF)
            act_grad_ref[band, hidden:] = (inner_grad * swished).astype(BF)
            for s in range(count):
                columns = slice(s * width, (s + 1) * width)
                y = lax.dot_general(
                    inner_ref[band], outs[s][...], COLS_IN, preferred_element_type=F32
                ).astype(BF)
                dx = lax.dot_general(
                    act_grad_ref[band], ins[s][...], COLS_IN, preferred_element_type=F32
                ).astype(BF)
                for i in range(many):
                    d = first + i
                    part = slice(i * size, (i + 1) * size)
                    ring.place(
                        y_refs, -d % planes, y[part].reshape(nodes, capacity, width), columns
                    )
                    dx_ref[:, d, :, columns] = dx[part].reshape(nodes, capacity, width)

    operands = (x_rows, *dy_got, *w_ins, *w_outs)
    out_shape = [
        *ring.shapes(capacity, model),
        shape(nodes, planes, capacity, model),
        shape(rows, hidden),
        shape(rows, double),
        shape(rows, model),
        shape(rows, model),
    ]
    return call(
        kernel,
        "expert",
        in_specs=[VMEM] * len(operands),
        out_specs=[VMEM] * len(out_shape),
        out_shape=out_shape,
        scratch_shapes=[pltpu.VMEM((many * size, double), F32)],
    )(*operands)


def weight_grads(shard, xs, dys, inner, act_grad):
    rows, width = xs.shape
    size = width // lax.axis_size("edata")
    double, hidden = act_grad.shape[1], inner.shape[1]
    tile = min(256, size)
    steps = size // tile

    def kernel(x_ref, dy_ref, inner_ref, act_grad_ref, out_ref):
        out_ref[:, :double] = lax.dot_general(
            x_ref[...], act_grad_ref[...], ROWS_IN, preferred_element_type=F32
        ).astype(BF)
        out_ref[:, double:] = lax.dot_general(
            dy_ref[...], inner_ref[...], ROWS_IN, preferred_element_type=F32
        ).astype(BF)

    columns = pl.BlockSpec((rows, tile), lambda i: (0, shard * steps + i))
    return call(
        kernel,
        "weight_grads",
        grid=(steps,),
        in_specs=[
            columns,
            columns,
            pl.BlockSpec((rows, hidden), lambda i: (0, 0)),
            pl.BlockSpec((rows, double), lambda i: (0, 0)),
        ],
        out_specs=pl.BlockSpec((tile, double + hidden), lambda i: (i, 0)),
        out_shape=shape(size, double + hidden),
    )(xs, dys, inner, act_grad)


def combine(ring, turn, numbers, picks, ids_t, grad_rows, y_rows, dx_got):
    pick, pick_t, high_t, middle_t = picks
    slots, tok_rows = pick.shape
    nodes, planes, capacity, width = y_rows.shape
    size = nodes * capacity
    groups = nodes * planes
    tile, steps, turned = column_tiles(width, 512)

    def kernel(turn_ref, number_ref, pick_ref, pick_t_ref, high_ref, middle_ref, *refs):
        ids_ref, grad_ref, y_ref, *got = refs[:-4]
        mixed_ref, token_grad_ref, gate_grad_ref, dots_ref = refs[-4:]
        step = pl.program_id(0)
        order = [-d % planes for d in range(planes)]
        y = jnp.concatenate([y_ref[:, e].reshape(size, tile) for e in order], axis=0)
        dx = jnp.concatenate([ring.take(got, e).reshape(size, tile) for e in order], axis=0)
        mixed_ref[...] = (
            jnp.dot(high_ref[...], y, preferred_element_type=F32)
            + jnp.dot(middle_ref[...], y, preferred_element_type=F32)
        ).astype(BF)
        token_grad_ref[...] = jnp.dot(
            pick_t_ref[...], dx, preferred_element_type=F32
        ).astype(BF)
        dots = jnp.sum(y.astype(F32) * grad_ref[...].astype(F32), axis=1, keepdims=True)

        @pl.when(step == 0)
        def _():
            dots_ref[...] = dots

        @pl.when(step > 0)
        def _():
            dots_ref[...] += dots

        @pl.when(step == steps - 1)
        def _():
            by_token = pick_ref[...].astype(F32) * dots_ref[...]
            by_token = jnp.sum(by_token.reshape(groups, capacity, tok_rows), axis=1)
            ids = ids_ref[...]
            total = jnp.zeros(ids.shape, F32)
            for g in range(groups):
                total += jnp.where(ids == number_ref[g], by_token[g : g + 1], 0.0)
            gate_grad_ref[...] = total

    def whole(array):
        return pl.BlockSpec(array.shape, lambda i, t, n: (0, 0))

    used = [nodes]
    for last in (ring.cut, nodes - ring.cut):
        used += [nodes] * (ring.half - 1) + [last]
    turned_spec = pl.BlockSpec((tok_rows, tile), lambda i, t, n: (0, turned(i, t[0])))
    return call(
        kernel,
        "combine",
        grid_spec=pltpu.PrefetchScalarGridSpec(
            num_scalar_prefetch=2,
            grid=(steps,),
            in_specs=[whole(p) for p in picks]
            + [
                whole(ids_t),
                pl.BlockSpec((slots, tile), lambda i, t, n: (0, i)),
                pl.BlockSpec((nodes, planes, capacity, tile), lambda i, t, n: (0, 0, 0, i)),
            ]
            + [pl.BlockSpec((u, capacity, tile), lambda i, t, n: (0, 0, i)) for u in used],
            out_specs=[turned_spec, turned_spec, whole(ids_t)],
            scratch_shapes=[pltpu.VMEM((slots, 1), F32)],
        ),
        out_shape=[
            shape(tok_rows, width),
            shape(tok_rows, width),
            shape(*ids_t.shape, kind=F32),
        ],
    )(turn, numbers, *picks, ids_t, grad_rows, y_rows, *dx_got)


def shards(tokens, out_grad, expert_ids, gates, w_gate_up, w_down):
    nodes, planes = lax.axis_size("node"), lax.axis_size("local")
    groups = nodes * planes
    tok_rows = tokens.shape[0]
    capacity = tok_rows * expert_ids.shape[1] // (EXP_DEV * groups)
    ring = Ring(nodes, planes)
    turn = lax.axis_index("edata").astype(jnp.int32).reshape(1)
    w_ins = gathered(w_gate_up[0])
    w_outs = gathered(w_down[0])
    plane = (lax.axis_index("local") + jnp.arange(planes, dtype=jnp.int32)) % planes
    numbers = (plane[:, None] + planes * jnp.arange(nodes, dtype=jnp.int32)[None, :]).reshape(-1)
    pick, slot_weight = slot_tables(expert_ids, gates, numbers, capacity)

    x_own, x_up, x_down = dispatch_x(ring, turn, pick, tokens, capacity)
    pick2 = after(pick, x_own, x_up, x_down)
    dy_sent, grad_rows = dispatch_dy(ring, turn, pick2, slot_weight, out_grad, capacity)
    x_got = ring.send(x_own, x_up, x_down)
    dy_mid = over_nodes(dy_sent)
    *x_got, dy_mid = lax.optimization_barrier((*x_got, dy_mid))
    x_rows = over_nodes(pack(ring, x_got))
    dy_got = ring.send(*unpack(ring, dy_mid, False))
    *y_sent, dx_sent, inner, act_grad, xs, dys = expert(ring, x_rows, dy_got, w_ins, w_outs)
    y_got = ring.send(*y_sent)
    dx_mid = over_nodes(dx_sent)
    *y_got, dx_mid = lax.optimization_barrier((*y_got, dx_mid))
    y_packed = pack(ring, y_got)
    y_rows = over_nodes(y_packed)
    dx_sent = unpack(ring, dx_mid, True)
    dx_got = ring.send(*dx_sent)
    inner = after(inner, y_packed, *dx_sent)
    parts = []
    for shard in [*range(1, len(w_ins)), 0]:
        parts.append(weight_grads(shard, xs, dys, inner, act_grad))

    parts = [parts[-1]] + [from_owner(p, step) for step, p in enumerate(parts[:-1], 1)]
    double = w_gate_up.shape[2]
    sums = [
        sum(p[:, columns].astype(F32) for p in parts)
        for columns in (slice(0, double), slice(double, None))
    ]

    spread = pick.astype(F32) * after(slot_weight, y_got[1])
    high = lax.reduce_precision(spread, 8, 7)
    middle = (spread - high).astype(BF)
    picks = (pick, pick.T, high.astype(BF).T, middle.T)
    *dx_got, sums[0], sums[1] = lax.optimization_barrier((*dx_got, *sums))
    mixed, token_grad, gate_grad = combine(
        ring, turn, numbers, picks, expert_ids.T, grad_rows, y_rows, dx_got
    )
    return (mixed, token_grad, gate_grad.T, sums[0][None], sums[1][None])


def solution(mesh):
    rows = P(("node", "local", "edata"), None)
    weights = P(("node", "local"), "edata", None)
    return jax.shard_map(
        shards,
        mesh=mesh,
        in_specs=(rows, rows, rows, rows, weights, weights),
        out_specs=(rows, rows, rows, weights, weights),
        check_vma=False,
    )
```

time: 423 us -> 271 us (0.64)
  waiting for transfers between devices: 253 us -> 149 us
  Pallas kernels: 0 us -> 55.2 us
  starting transfers between devices: 96.3 us -> 43.6 us
  matrix products: 34.7 us -> 0.15 us
  local copies, waits for them, and re-layouts: 23.1 us -> 8.58 us
    ppermute x62 -> x17, waiting for transfers between devices: 253 us -> 148 us  [the longest x16 148 us: send(): now = lax.ppermute(now, 'local', pairs)]
    ppermute x62 -> x17, starting transfers between devices: 95.8 us -> 26.3 us  [the longest x16 26.3 us: send(): now = lax.ppermute(now, 'local', pairs)]
    pallas_call x0 -> x10, Pallas kernels: none -> 55.2 us  [the longest x1 16.8 us: expert(): call(kernel, 'expert', in_specs=[VMEM] * len(operands), out_specs=[VMEM]...]
    dot_general x12 -> x0, matrix products: 34.6 us -> none  [the longest x1 9.03 us: shards(): lax.dot_general(act_grad, w_in, COLS_IN, preferred_element_type=F32)]
    all_to_all x0 -> x4, starting transfers between devices: none -> 17.3 us  [over_nodes(): return lax.all_to_all(rows, 'node', split_axis=0, concat_axis=0, tiled=True)]
    unnamed x86 -> x40, local copies, waits for them, and re-layouts: 14.2 us -> 4.15 us
    slice x6 -> x8, local copies, waits for them, and re-layouts: 7.05 us -> 1.09 us  [send(): now = now[self.nodes:]]
    add x2 -> x3, other arithmetic: 8.97 us -> 10.4 us  [the longest x2 10.4 us: shards(): sum((p[:, columns].astype(F32) for p in parts))]
  transfers between devices with their start and end apart: 64 -> 23, of which waited for: 48 -> 14; matrix products, arithmetic and copies ran while one was open for 14% -> 5% of each run, Pallas kernels for 0% -> 5%
where the time goes in v7:
time: 271 us; the launch traced here: 270 us
  waiting for transfers between devices  149 us (55%)
  Pallas kernels  55.2 us (20%)
  starting transfers between devices  43.6 us (16%)
  other arithmetic  12.6 us (5%)
  local copies, waits for them, and re-layouts  8.58 us (3%)
    ppermute x16, waiting for transfers between devices, send(): now = lax.ppermute(now, 'local', pairs)  148 us
    ppermute x16, starting transfers between devices, send(): now = lax.ppermute(now, 'local', pairs)  26.3 us
    all_to_all x4, starting transfers between devices, over_nodes(): return lax.all_to_all(rows, 'node', split_axis=0, concat_axis=0, tiled=True)  17.3 us
    pallas_call x1, Pallas kernels, expert(): call(kernel, 'expert', in_specs=[VMEM] * len(operands), out_specs=[VMEM]...  16.8 us
    pallas_call x2, Pallas kernels, weight_grads(): call(kernel, 'weight_grads', grid=(steps,), in_specs=[columns, columns, p...  13.7 us
    add x2, other arithmetic, shards(): sum((p[:, columns].astype(F32) for p in parts))  10.4 us
    pallas_call x1, Pallas kernels, combine(): call(kernel, 'combine', grid_spec=pltpu.PrefetchScalarGridSpec(num_scalar...  7.09 us
    pallas_call x2, Pallas kernels, pack(): call(kernel, 'pack', grid=(width // tile,), in_specs=[pl.BlockSpec((n, ca...  5.95 us
  transfers between devices with their start and end apart: 23, of which 14 were waited for; matrix products, arithmetic and copies ran while one was open for 5% of the time, Pallas kernels for 5%

profile of v7, /device:TPU:0, one launch (start us, length us, event | category | flops | bytes accessed | tf_op | source)
XLA Modules:
  0.0 269.7 jit_solution(920228670141691771)
XLA Ops:
  3.4 2.9 %dispatch_x.1 = (bf16[4,32,2048]{2,1,0:T(8,128)(2,1)}, bf16[6,32,2048]{2,1,0:T(8,128)(2,1)}, bf16[6,32,2048]{2,1,0:T(8,128)(2,1)}) custom-call(s32[1]{0:T(128)} %bitcast.turn_ref, bf16[512,256]{1,0:T(8,128)(2,1)} %copy.26.pick_ref, bf16[256,2048]{1,0:T(8,128)(2,1)} %x_ref.1), custom_call_target="tpu_custom_call" | custom-call | flops 1 | bytes 1 | tf_op jit(solution)/shard_map/dispatch_x/pallas_call | solution.py:139
  8.4 3.6 %dispatch_dy.1 = (bf16[4,4,32,2048]{3,2,1,0:T(8,128)(2,1)}, bf16[512,2048]{1,0:T(8,128)(2,1)}) custom-call(s32[1]{0:T(128)} %bitcast.turn_ref, bf16[512,256]{1,0:T(8,128)(2,1)} %copy.24.pick_ref, f32[512,1]{1,0:T(8,128)} %copy.25.weight_ref, bf16[256,2048]{1,0:T(8,128)(2,1)} %grad_ref.1), custom_call_target="tpu_custom_call" | custom-call | flops 1 | bytes 1 | tf_op jit(solution)/shard_map/dispatch_dy/pallas_call | solution.py:169
  12.1 5.2 %all-to-all-start = ((bf16[4,4,32,2048]{3,2,1,0:T(8,128)(2,1)}), bf16[4,4,32,2048]{3,2,1,0:T(8,128)(2,1)S(1)}, u32[]{:S(2)}, u32[]{:S(2)}) async-start(bf16[4,4,32,2048]{3,2,1,0:T(8,128)(2,1)} %get-tuple-element.53), calls=%async_computation | async-start | bytes 4194304 | tf_op jit(solution)/shard_map/all_to_all | solution.py:102
  21.1 18.6 %collective-permute-done.refs_1_ = bf16[6,32,2048]{2,1,0:T(8,128)(2,1)S(1)} collective-permute-done((bf16[6,32,2048]{2,1,0:T(8,128)(2,1)}, bf16[6,32,2048]{2,1,0:T(8,128)(2,1)S(1)}, u32[]{:S(2)}, u32[]{:S(2)}) %collective-permute-start) | collective-permute-done | bytes 786464 | tf_op jit(solution)/shard_map/ppermute | solution.py:84
  39.7 15.8 %collective-permute-done.2.refs_3_ = bf16[6,32,2048]{2,1,0:T(8,128)(2,1)S(1)} collective-permute-done((bf16[6,32,2048]{2,1,0:T(8,128)(2,1)}, bf16[6,32,2048]{2,1,0:T(8,128)(2,1)S(1)}, u32[]{:S(2)}, u32[]{:S(2)}) %collective-permute-start.2) | collective-permute-done | bytes 786464 | tf_op jit(solution)/shard_map/ppermute | solution.py:84
  58.2 6.5 %collective-permute-done.1.refs_2_ = bf16[2,32,2048]{2,1,0:T(8,128)(2,1)S(1)} collective-permute-done((bf16[2,32,2048]{2,1,0:T(8,128)(2,1)S(1)}, bf16[2,32,2048]{2,1,0:T(8,128)(2,1)S(1)}, u32[]{:S(2)}, u32[]{:S(2)}) %collective-permute-start.1) | collective-permute-done | bytes 262176 | tf_op jit(solution)/shard_map/ppermute | solution.py:84
  64.7 2.8 %collective-permute-done.3.refs_4_ = bf16[2,32,2048]{2,1,0:T(8,128)(2,1)} collective-permute-done((bf16[2,32,2048]{2,1,0:T(8,128)(2,1)S(1)}, bf16[2,32,2048]{2,1,0:T(8,128)(2,1)}, u32[]{:S(2)}, u32[]{:S(2)}) %collective-permute-start.3) | collective-permute-done | bytes 262176 | tf_op jit(solution)/shard_map/ppermute | solution.py:84
  67.5 3.3 %pack.2 = bf16[4,4,32,2048]{3,2,1,0:T(8,128)(2,1)} custom-call(bf16[4,32,2048]{2,1,0:T(8,128)(2,1)} %get-tuple-element.54.refs_0_, bf16[6,32,2048]{2,1,0:T(8,128)(2,1)} %copy-done.9, bf16[2,32,2048]{2,1,0:T(8,128)(2,1)} %copy-done.16, bf16[6,32,2048]{2,1,0:T(8,128)(2,1)} %copy-done.11, bf16[2,32,2048]{2,1,0:T(8,128)(2,1)} %collective-permute-done.3.refs_4_), custom_call_target="tpu_custom_call" | custom-call | flops 1 | bytes 1 | tf_op jit(solution)/shard_map/pack/pallas_call | solution.py:205
  70.9 4.2 %all-to-all-start.1 = ((bf16[4,4,32,2048]{3,2,1,0:T(8,128)(2,1)}), bf16[4,4,32,2048]{3,2,1,0:T(8,128)(2,1)S(1)}, u32[]{:S(2)}, u32[]{:S(2)}) async-start(bf16[4,4,32,2048]{3,2,1,0:T(8,128)(2,1)} %pack.2), calls=%async_computation.1 | async-start | bytes 4194304 | tf_op jit(solution)/shard_map/all_to_all | solution.py:102
  78.3 3.2 %collective-permute-start.6 = (bf16[6,32,2048]{2,1,0:T(8,128)(2,1)}, bf16[6,32,2048]{2,1,0:T(8,128)(2,1)S(1)}, u32[]{:S(2)}, u32[]{:S(2)}) collective-permute-start(bf16[6,32,2048]{2,1,0:T(8,128)(2,1)} %get-tuple-element.62), channel_id=1, source_target_pairs={{0,6},{2,0},{4,2},{6,4},{1,7},{3,1},{5,3},{7,5},{8,14},{10,8},{12,... | collective-permute-start | bytes 2359304 | tf_op jit(solution)/shard_map/ppermute | solution.py:84
  81.5 18.6 %collective-permute-done.4.refs_1_ = bf16[6,32,2048]{2,1,0:T(8,128)(2,1)S(1)} collective-permute-done((bf16[6,32,2048]{2,1,0:T(8,128)(2,1)}, bf16[6,32,2048]{2,1,0:T(8,128)(2,1)S(1)}, u32[]{:S(2)}, u32[]{:S(2)}) %collective-permute-start.4) | collective-permute-done | bytes 786464 | tf_op jit(solution)/shard_map/ppermute | solution.py:84
  100.2 13.6 %collective-permute-done.6.refs_3_ = bf16[6,32,2048]{2,1,0:T(8,128)(2,1)S(1)} collective-permute-done((bf16[6,32,2048]{2,1,0:T(8,128)(2,1)}, bf16[6,32,2048]{2,1,0:T(8,128)(2,1)S(1)}, u32[]{:S(2)}, u32[]{:S(2)}) %collective-permute-start.6) | collective-permute-done | bytes 786464 | tf_op jit(solution)/shard_map/ppermute | solution.py:84
  113.8 3.9 %collective-permute-start.7 = (bf16[2,32,2048]{2,1,0:T(8,128)(2,1)S(1)}, bf16[2,32,2048]{2,1,0:T(8,128)(2,1)}, u32[]{:S(2)}, u32[]{:S(2)}) collective-permute-start(bf16[2,32,2048]{2,1,0:T(8,128)(2,1)S(1)} %slice.51), channel_id=1, source_target_pairs={{0,6},{2,0},{4,2},{6,4},{1,7},{3,1},{5,3},{7,5},{8,14},{10,8},{12,... | collective-permute-start | bytes 786440 | tf_op jit(solution)/shard_map/ppermute | solution.py:84
  117.7 4.9 %collective-permute-done.5.refs_2_ = bf16[2,32,2048]{2,1,0:T(8,128)(2,1)S(1)} collective-permute-done((bf16[2,32,2048]{2,1,0:T(8,128)(2,1)S(1)}, bf16[2,32,2048]{2,1,0:T(8,128)(2,1)S(1)}, u32[]{:S(2)}, u32[]{:S(2)}) %collective-permute-start.5) | collective-permute-done | bytes 262176 | tf_op jit(solution)/shard_map/ppermute | solution.py:84
  122.6 3.1 %collective-permute-done.7.refs_4_ = bf16[2,32,2048]{2,1,0:T(8,128)(2,1)} collective-permute-done((bf16[2,32,2048]{2,1,0:T(8,128)(2,1)S(1)}, bf16[2,32,2048]{2,1,0:T(8,128)(2,1)}, u32[]{:S(2)}, u32[]{:S(2)}) %collective-permute-start.7) | collective-permute-done | bytes 262176 | tf_op jit(solution)/shard_map/ppermute | solution.py:84
  127.1 16.8 %expert.1 = (bf16[4,32,2048]{2,1,0:T(8,128)(2,1)}, bf16[6,32,2048]{2,1,0:T(8,128)(2,1)}, bf16[6,32,2048]{2,1,0:T(8,128)(2,1)}, bf16[4,4,32,2048]{3,2,1,0:T(8,128...) custom-call(bf16[4,4,32,2048]{3,2,1,0:T(8,128)(2,1)} %copy-done, ...), custom_call_target="tpu_custom_call" | custom-call | flops 1 | bytes 1 | tf_op jit(solution)/shard_map/expert/pallas_call | solution.py:305
  143.8 3.7 %all-to-all-start.2 = ((bf16[4,4,32,2048]{3,2,1,0:T(8,128)(2,1)}), bf16[4,4,32,2048]{3,2,1,0:T(8,128)(2,1)S(1)}, u32[]{:S(2)}, u32[]{:S(2)}) async-start(bf16[4,4,32,2048]{3,2,1,0:T(8,128)(2,1)} %get-tuple-element.66), calls=%async_computation.2 | async-start | bytes 4194304 | tf_op jit(solution)/shard_map/all_to_all | solution.py:102
  148.7 2.7 %collective-permute-start.12 = (bf16[6,32,2048]{2,1,0:T(8,128)(2,1)}, bf16[6,32,2048]{2,1,0:T(8,128)(2,1)S(1)}, u32[]{:S(2)}, u32[]{:S(2)}) collective-permute-start(bf16[6,32,2048]{2,1,0:T(8,128)(2,1)} %get-tuple-element.65), channel_id=1, source_target_pairs={{0,6},{2,0},{4,2},{6,4},{1,7},{3,1},{5,3},{7,5},{8,14},{10,8},{12,... | collective-permute-start | bytes 2359304 | tf_op jit(solution)/shard_map/ppermute | solution.py:84
  151.4 18.7 %collective-permute-done.10.refs_1_ = bf16[6,32,2048]{2,1,0:T(8,128)(2,1)S(1)} collective-permute-done((bf16[6,32,2048]{2,1,0:T(8,128)(2,1)}, bf16[6,32,2048]{2,1,0:T(8,128)(2,1)S(1)}, u32[]{:S(2)}, u32[]{:S(2)}) %collective-permute-start.10) | collective-permute-done | bytes 786464 | tf_op jit(solution)/shard_map/ppermute | solution.py:84
  170.2 16.3 %collective-permute-done.12.refs_3_ = bf16[6,32,2048]{2,1,0:T(8,128)(2,1)S(1)} collective-permute-done((bf16[6,32,2048]{2,1,0:T(8,128)(2,1)}, bf16[6,32,2048]{2,1,0:T(8,128)(2,1)S(1)}, u32[]{:S(2)}, u32[]{:S(2)}) %collective-permute-start.12) | collective-permute-done | bytes 786464 | tf_op jit(solution)/shard_map/ppermute | solution.py:84
  188.2 4.4 %collective-permute-done.11.refs_2_ = bf16[2,32,2048]{2,1,0:T(8,128)(2,1)S(1)} collective-permute-done((bf16[2,32,2048]{2,1,0:T(8,128)(2,1)S(1)}, bf16[2,32,2048]{2,1,0:T(8,128)(2,1)S(1)}, u32[]{:S(2)}, u32[]{:S(2)}) %collective-permute-start.11) | collective-permute-done | bytes 262176 | tf_op jit(solution)/shard_map/ppermute | solution.py:84
  192.6 3.6 %collective-permute-done.13.refs_4_ = bf16[2,32,2048]{2,1,0:T(8,128)(2,1)} collective-permute-done((bf16[2,32,2048]{2,1,0:T(8,128)(2,1)S(1)}, bf16[2,32,2048]{2,1,0:T(8,128)(2,1)}, u32[]{:S(2)}, u32[]{:S(2)}) %collective-permute-start.13) | collective-permute-done | bytes 262176 | tf_op jit(solution)/shard_map/ppermute | solution.py:84
  197.5 2.6 unpack.3
  202.8 6.9 %weight_grads.3 = bf16[1024,2304]{1,0:T(8,128)(2,1)} custom-call(bf16[512,2048]{1,0:T(8,128)(2,1)} %get-tuple-element.78.x_ref, bf16[512,2048]{1,0:T(8,128)(2,1)} %get-tuple-element.79.dy_ref, bf16[512,768]{1,0:T(8,128)(2,1)} %get-tuple-element.81.inner_ref, bf16[512,1536]{1,0:T(8,128)(2,1)} %get-tuple-element.82.act_grad_ref), custom_call_target="tpu_custom_call" | custom-call | flops 1 | bytes 1 | tf_op jit(solution)/shard_map/weight_grads/pallas_call | solution.py:331
  210.2 3.2 %collective-permute-start.16 = (bf16[6,32,2048]{2,1,0:T(8,128)(2,1)}, bf16[6,32,2048]{2,1,0:T(8,128)(2,1)}, u32[]{:S(2)}, u32[]{:S(2)}) collective-permute-start(bf16[6,32,2048]{2,1,0:T(8,128)(2,1)} %get-tuple-element.77), channel_id=1, source_target_pairs={{0,6},{2,0},{4,2},{6,4},{1,7},{3,1},{5,3},{7,5},{8,14},{10,8},{12,... | collective-permute-start | bytes 2359304 | tf_op jit(solution)/shard_map/ppermute | solution.py:84
  213.5 4.2 %all-to-all-start.3 = ((bf16[4,4,32,2048]{3,2,1,0:T(8,128)(2,1)}), bf16[4,4,32,2048]{3,2,1,0:T(8,128)(2,1)S(1)}, u32[]{:S(2)}, u32[]{:S(2)}) async-start(bf16[4,4,32,2048]{3,2,1,0:T(8,128)(2,1)} %pack.3), calls=%async_computation.3 | async-start | bytes 4194304 | tf_op jit(solution)/shard_map/all_to_all | solution.py:102
  217.6 6.8 %weight_grads.2 = bf16[1024,2304]{1,0:T(8,128)(2,1)} custom-call(bf16[512,2048]{1,0:T(8,128)(2,1)} %get-tuple-element.78.x_ref, bf16[512,2048]{1,0:T(8,128)(2,1)} %get-tuple-element.79.dy_ref, bf16[512,768]{1,0:T(8,128)(2,1)} %get-tuple-element.81.inner_ref, bf16[512,1536]{1,0:T(8,128)(2,1)} %get-tuple-element.82.act_grad_ref), custom_call_target="tpu_custom_call" | custom-call | flops 1 | bytes 1 | tf_op jit(solution)/shard_map/weight_grads/pallas_call | solution.py:331
  225.4 6.7 %collective-permute-done.14.refs_4_ = bf16[6,32,2048]{2,1,0:T(8,128)(2,1)S(1)} collective-permute-done((bf16[6,32,2048]{2,1,0:T(8,128)(2,1)}, bf16[6,32,2048]{2,1,0:T(8,128)(2,1)S(1)}, u32[]{:S(2)}, u32[]{:S(2)}) %collective-permute-start.14) | collective-permute-done | bytes 786464 | tf_op jit(solution)/shard_map/ppermute | solution.py:84
  232.1 15.0 %collective-permute-done.16.refs_6_ = bf16[6,32,2048]{2,1,0:T(8,128)(2,1)} collective-permute-done((bf16[6,32,2048]{2,1,0:T(8,128)(2,1)}, bf16[6,32,2048]{2,1,0:T(8,128)(2,1)}, u32[]{:S(2)}, u32[]{:S(2)}) %collective-permute-start.16) | collective-permute-done | bytes 786464 | tf_op jit(solution)/shard_map/ppermute | solution.py:84
  250.6 6.5 %convert_add_fusion = f32[1024,1536]{1,0:T(8,128)} fusion(bf16[1024,2304]{1,0:T(8,128)(2,1)} %collective-permute-done.18, bf16[1024,2304]{1,0:T(8,128)(2,1)} %weight_grads.2), kind=kLoop, calls=%fused_computation | loop fusion | flops 4718592 | bytes 12582912 | tf_op jit(solution)/shard_map/add | solution.py:456
  257.1 3.9 %convert_add_fusion.1 = f32[1024,768]{1,0:T(8,128)} fusion(bf16[1024,2304]{1,0:T(8,128)(2,1)} %collective-permute-done.18, bf16[1024,2304]{1,0:T(8,128)(2,1)} %weight_grads.2), kind=kLoop, calls=%fused_computation.1 | loop fusion | flops 2359296 | bytes 6291456 | tf_op jit(solution)/shard_map/add | solution.py:456
  262.5 7.1 %combine.1 = (bf16[256,2048]{1,0:T(8,128)(2,1)}, bf16[256,2048]{1,0:T(8,128)(2,1)}, f32[8,256]{1,0:T(8,128)}) custom-call(s32[1]{0:T(128)} %bitcast.turn_ref, s32[16]{0:T(128)} %copy-done.18, bf16[512,256]{1,0:T(8,128)(2,1)} %copy.26.pick_ref, bf16[256,512]{1,0:T(8,128)(2,1)} %bitcast.17, bf16[256,512]{1,0:T(8,128)(2,1)} %get-tuple-element.94.high_ref, ...), custom_call_target="tpu_custom_call" | custom-call | flops 1 | bytes 1 | tf_op jit(solution)/shard_map/combine/pallas_call | solution.py:395
  (93 shorter events, 29.5 us)
Async XLA Ops:
  0.8 11.2 %copy-start.18 = (s32[16]{0:T(128)}, s32[16]{0:T(128)S(1)}, u32[]{:S(2)}) copy-start(s32[16]{0:T(128)S(1)} %add.53.number_ref) | copy-start | bytes 196
  2.5 221.9 %copy-start.4 = (bf16[512,256]{0,1:T(8,128)(2,1)}, bf16[512,256]{0,1:T(8,128)(2,1)S(1)}, u32[]{:S(2)}) copy-start(bf16[512,256]{0,1:T(8,128)(2,1)S(1)} %and_convert_fusion) | copy-start | bytes 786436
  12.1 55.4 %all-to-all-start = ((bf16[4,4,32,2048]{3,2,1,0:T(8,128)(2,1)}), bf16[4,4,32,2048]{3,2,1,0:T(8,128)(2,1)S(1)}, u32[]{:S(2)}, u32[]{:S(2)}) async-start(bf16[4,4,32,2048]{3,2,1,0:T(8,128)(2,1)} %get-tuple-element.53), calls=%async_computation | async-start | bytes 4194304 | tf_op jit(solution)/shard_map/all_to_all | solution.py:102
  17.2 108.5 %collective-permute-start.8 = (bf16[1024,1536]{1,0:T(8,128)(2,1)}, bf16[1024,1536]{1,0:T(8,128)(2,1)}, u32[]{:S(2)}, u32[]{:S(2)}) collective-permute-start(bf16[1024,1536]{1,0:T(8,128)(2,1)} %bitcast.19), channel_id=1, source_target_pairs={{1,0},{0,1},{3,2},{2,3},{5,4},{4,5},{7,6},{6,7},{9,8},{8,9},{11,10... | collective-permute-start | bytes 9437192 | tf_op jit(solution)/shard_map/ppermute | solution.py:110
  17.2 22.4 %collective-permute-start = (bf16[6,32,2048]{2,1,0:T(8,128)(2,1)}, bf16[6,32,2048]{2,1,0:T(8,128)(2,1)S(1)}, u32[]{:S(2)}, u32[]{:S(2)}) collective-permute-start(bf16[6,32,2048]{2,1,0:T(8,128)(2,1)} %get-tuple-element.50), channel_id=1, source_target_pairs={{0,2},{2,4},{4,6},{6,0},{1,3},{3,5},{5,7},{7,1},{8,10},{10,12},{12... | collective-permute-start | bytes 2359304 | tf_op jit(solution)/shard_map/ppermute | solution.py:84
  18.8 36.7 %collective-permute-start.2 = (bf16[6,32,2048]{2,1,0:T(8,128)(2,1)}, bf16[6,32,2048]{2,1,0:T(8,128)(2,1)S(1)}, u32[]{:S(2)}, u32[]{:S(2)}) collective-permute-start(bf16[6,32,2048]{2,1,0:T(8,128)(2,1)} %get-tuple-element.51), channel_id=1, source_target_pairs={{0,6},{2,0},{4,2},{6,4},{1,7},{3,1},{5,3},{7,5},{8,14},{10,8},{12,... | collective-permute-start | bytes 2359304 | tf_op jit(solution)/shard_map/ppermute | solution.py:84
  39.6 27.9 %copy-start.9 = (bf16[6,32,2048]{2,1,0:T(8,128)(2,1)}, bf16[6,32,2048]{2,1,0:T(8,128)(2,1)S(1)}, u32[]{:S(2)}) copy-start(bf16[6,32,2048]{2,1,0:T(8,128)(2,1)S(1)} %collective-permute-done.refs_1_) | copy-start | bytes 2359300
  39.6 25.1 %collective-permute-start.1 = (bf16[2,32,2048]{2,1,0:T(8,128)(2,1)S(1)}, bf16[2,32,2048]{2,1,0:T(8,128)(2,1)S(1)}, u32[]{:S(2)}, u32[]{:S(2)}) collective-permute-start(bf16[2,32,2048]{2,1,0:T(8,128)(2,1)S(1)} %slice.48), channel_id=1, source_target_pairs={{0,2},{2,4},{4,6},{6,0},{1,3},{3,5},{5,7},{7,1},{8,10},{10,12},{12... | collective-permute-start | bytes 786440 | tf_op jit(solution)/shard_map/ppermute | solution.py:84
  55.5 9.2 %copy-start.11 = (bf16[6,32,2048]{2,1,0:T(8,128)(2,1)}, bf16[6,32,2048]{2,1,0:T(8,128)(2,1)S(1)}, u32[]{:S(2)}) copy-start(bf16[6,32,2048]{2,1,0:T(8,128)(2,1)S(1)} %collective-permute-done.2.refs_3_) | copy-start | bytes 2359300
  55.6 11.9 %collective-permute-start.3 = (bf16[2,32,2048]{2,1,0:T(8,128)(2,1)S(1)}, bf16[2,32,2048]{2,1,0:T(8,128)(2,1)}, u32[]{:S(2)}, u32[]{:S(2)}) collective-permute-start(bf16[2,32,2048]{2,1,0:T(8,128)(2,1)S(1)} %slice.49), channel_id=1, source_target_pairs={{0,6},{2,0},{4,2},{6,4},{1,7},{3,1},{5,3},{7,5},{8,14},{10,8},{12,... | collective-permute-start | bytes 786440 | tf_op jit(solution)/shard_map/ppermute | solution.py:84
  58.2 59.6 %collective-permute-start.9 = (bf16[1024,768]{1,0:T(8,128)(2,1)}, bf16[1024,768]{1,0:T(8,128)(2,1)}, u32[]{:S(2)}, u32[]{:S(2)}) collective-permute-start(bf16[1024,768]{1,0:T(8,128)(2,1)} %bitcast.23), channel_id=1, source_target_pairs={{1,0},{0,1},{3,2},{2,3},{5,4},{4,5},{7,6},{6,7},{9,8},{8,9},{11,10... | collective-permute-start | bytes 4718600 | tf_op jit(solution)/shard_map/ppermute | solution.py:110
  70.9 54.9 %all-to-all-start.1 = ((bf16[4,4,32,2048]{3,2,1,0:T(8,128)(2,1)}), bf16[4,4,32,2048]{3,2,1,0:T(8,128)(2,1)S(1)}, u32[]{:S(2)}, u32[]{:S(2)}) async-start(bf16[4,4,32,2048]{3,2,1,0:T(8,128)(2,1)} %pack.2), calls=%async_computation.1 | async-start | bytes 4194304 | tf_op jit(solution)/shard_map/all_to_all | solution.py:102
  77.6 22.5 %collective-permute-start.4 = (bf16[6,32,2048]{2,1,0:T(8,128)(2,1)}, bf16[6,32,2048]{2,1,0:T(8,128)(2,1)S(1)}, u32[]{:S(2)}, u32[]{:S(2)}) collective-permute-start(bf16[6,32,2048]{2,1,0:T(8,128)(2,1)} %get-tuple-element.61), channel_id=1, source_target_pairs={{0,2},{2,4},{4,6},{6,0},{1,3},{3,5},{5,7},{7,1},{8,10},{10,12},{12... | collective-permute-start | bytes 2359304 | tf_op jit(solution)/shard_map/ppermute | solution.py:84
  78.3 35.5 %collective-permute-start.6 = (bf16[6,32,2048]{2,1,0:T(8,128)(2,1)}, bf16[6,32,2048]{2,1,0:T(8,128)(2,1)S(1)}, u32[]{:S(2)}, u32[]{:S(2)}) collective-permute-start(bf16[6,32,2048]{2,1,0:T(8,128)(2,1)} %get-tuple-element.62), channel_id=1, source_target_pairs={{0,6},{2,0},{4,2},{6,4},{1,7},{3,1},{5,3},{7,5},{8,14},{10,8},{12,... | collective-permute-start | bytes 2359304 | tf_op jit(solution)/shard_map/ppermute | solution.py:84
  100.1 25.6 %copy-start.6 = (bf16[6,32,2048]{2,1,0:T(8,128)(2,1)}, bf16[6,32,2048]{2,1,0:T(8,128)(2,1)S(1)}, u32[]{:S(2)}) copy-start(bf16[6,32,2048]{2,1,0:T(8,128)(2,1)S(1)} %collective-permute-done.4.refs_1_) | copy-start | bytes 2359300
  100.1 22.5 %collective-permute-start.5 = (bf16[2,32,2048]{2,1,0:T(8,128)(2,1)S(1)}, bf16[2,32,2048]{2,1,0:T(8,128)(2,1)S(1)}, u32[]{:S(2)}, u32[]{:S(2)}) collective-permute-start(bf16[2,32,2048]{2,1,0:T(8,128)(2,1)S(1)} %slice.50), channel_id=1, source_target_pairs={{0,2},{2,4},{4,6},{6,0},{1,3},{3,5},{5,7},{7,1},{8,10},{10,12},{12... | collective-permute-start | bytes 786440 | tf_op jit(solution)/shard_map/ppermute | solution.py:84
  113.8 8.9 %copy-start.7 = (bf16[6,32,2048]{2,1,0:T(8,128)(2,1)}, bf16[6,32,2048]{2,1,0:T(8,128)(2,1)S(1)}, u32[]{:S(2)}) copy-start(bf16[6,32,2048]{2,1,0:T(8,128)(2,1)S(1)} %collective-permute-done.6.refs_3_) | copy-start | bytes 2359300
  113.8 12.0 %collective-permute-start.7 = (bf16[2,32,2048]{2,1,0:T(8,128)(2,1)S(1)}, bf16[2,32,2048]{2,1,0:T(8,128)(2,1)}, u32[]{:S(2)}, u32[]{:S(2)}) collective-permute-start(bf16[2,32,2048]{2,1,0:T(8,128)(2,1)S(1)} %slice.51), channel_id=1, source_target_pairs={{0,6},{2,0},{4,2},{6,4},{1,7},{3,1},{5,3},{7,5},{8,14},{10,8},{12,... | collective-permute-start | bytes 786440 | tf_op jit(solution)/shard_map/ppermute | solution.py:84
  143.8 52.4 %all-to-all-start.2 = ((bf16[4,4,32,2048]{3,2,1,0:T(8,128)(2,1)}), bf16[4,4,32,2048]{3,2,1,0:T(8,128)(2,1)S(1)}, u32[]{:S(2)}, u32[]{:S(2)}) async-start(bf16[4,4,32,2048]{3,2,1,0:T(8,128)(2,1)} %get-tuple-element.66), calls=%async_computation.2 | async-start | bytes 4194304 | tf_op jit(solution)/shard_map/all_to_all | solution.py:102
  147.6 22.5 %collective-permute-start.10 = (bf16[6,32,2048]{2,1,0:T(8,128)(2,1)}, bf16[6,32,2048]{2,1,0:T(8,128)(2,1)S(1)}, u32[]{:S(2)}, u32[]{:S(2)}) collective-permute-start(bf16[6,32,2048]{2,1,0:T(8,128)(2,1)} %get-tuple-element.64), channel_id=1, source_target_pairs={{0,2},{2,4},{4,6},{6,0},{1,3},{3,5},{5,7},{7,1},{8,10},{10,12},{12... | collective-permute-start | bytes 2359304 | tf_op jit(solution)/shard_map/ppermute | solution.py:84
  148.7 37.7 %collective-permute-start.12 = (bf16[6,32,2048]{2,1,0:T(8,128)(2,1)}, bf16[6,32,2048]{2,1,0:T(8,128)(2,1)S(1)}, u32[]{:S(2)}, u32[]{:S(2)}) collective-permute-start(bf16[6,32,2048]{2,1,0:T(8,128)(2,1)} %get-tuple-element.65), channel_id=1, source_target_pairs={{0,6},{2,0},{4,2},{6,4},{1,7},{3,1},{5,3},{7,5},{8,14},{10,8},{12,... | collective-permute-start | bytes 2359304 | tf_op jit(solution)/shard_map/ppermute | solution.py:84
  170.1 30.1 %copy-start.8 = (bf16[6,32,2048]{2,1,0:T(8,128)(2,1)}, bf16[6,32,2048]{2,1,0:T(8,128)(2,1)S(1)}, u32[]{:S(2)}) copy-start(bf16[6,32,2048]{2,1,0:T(8,128)(2,1)S(1)} %collective-permute-done.10.refs_1_) | copy-start | bytes 2359300
  170.1 22.4 %collective-permute-start.11 = (bf16[2,32,2048]{2,1,0:T(8,128)(2,1)S(1)}, bf16[2,32,2048]{2,1,0:T(8,128)(2,1)S(1)}, u32[]{:S(2)}, u32[]{:S(2)}) collective-permute-start(bf16[2,32,2048]{2,1,0:T(8,128)(2,1)S(1)} %slice.52), channel_id=1, source_target_pairs={{0,2},{2,4},{4,6},{6,0},{1,3},{3,5},{5,7},{7,1},{8,10},{10,12},{12... | collective-permute-start | bytes 786440 | tf_op jit(solution)/shard_map/ppermute | solution.py:84
  186.5 9.7 %collective-permute-start.13 = (bf16[2,32,2048]{2,1,0:T(8,128)(2,1)S(1)}, bf16[2,32,2048]{2,1,0:T(8,128)(2,1)}, u32[]{:S(2)}, u32[]{:S(2)}) collective-permute-start(bf16[2,32,2048]{2,1,0:T(8,128)(2,1)S(1)} %slice.53), channel_id=1, source_target_pairs={{0,6},{2,0},{4,2},{6,4},{1,7},{3,1},{5,3},{7,5},{8,14},{10,8},{12,... | collective-permute-start | bytes 786440 | tf_op jit(solution)/shard_map/ppermute | solution.py:84
  192.6 7.6 %copy-start.15 = (bf16[2,32,2048]{2,1,0:T(8,128)(2,1)}, bf16[2,32,2048]{2,1,0:T(8,128)(2,1)S(1)}, u32[]{:S(2)}) copy-start(bf16[2,32,2048]{2,1,0:T(8,128)(2,1)S(1)} %collective-permute-done.11.refs_2_) | copy-start | bytes 786436
  209.6 41.0 %collective-permute-start.18 = (bf16[1024,2304]{1,0:T(8,128)(2,1)}, bf16[1024,2304]{1,0:T(8,128)(2,1)}, u32[]{:S(2)}, u32[]{:S(2)}) collective-permute-start(bf16[1024,2304]{1,0:T(8,128)(2,1)} %weight_grads.3), channel_id=1, source_target_pairs={{0,1},{1,0},{2,3},{3,2},{4,5},{5,4},{6,7},{7,6},{8,9},{9,8},{10,11... | collective-permute-start | bytes 14155784 | tf_op jit(solution)/shard_map/ppermute | solution.py:116
  209.6 22.4 %collective-permute-start.14 = (bf16[6,32,2048]{2,1,0:T(8,128)(2,1)}, bf16[6,32,2048]{2,1,0:T(8,128)(2,1)S(1)}, u32[]{:S(2)}, u32[]{:S(2)}) collective-permute-start(bf16[6,32,2048]{2,1,0:T(8,128)(2,1)} %get-tuple-element.76), channel_id=1, source_target_pairs={{0,2},{2,4},{4,6},{6,0},{1,3},{3,5},{5,7},{7,1},{8,10},{10,12},{12... | collective-permute-start | bytes 2359304 | tf_op jit(solution)/shard_map/ppermute | solution.py:84
  210.2 36.8 %collective-permute-start.16 = (bf16[6,32,2048]{2,1,0:T(8,128)(2,1)}, bf16[6,32,2048]{2,1,0:T(8,128)(2,1)}, u32[]{:S(2)}, u32[]{:S(2)}) collective-permute-start(bf16[6,32,2048]{2,1,0:T(8,128)(2,1)} %get-tuple-element.77), channel_id=1, source_target_pairs={{0,6},{2,0},{4,2},{6,4},{1,7},{3,1},{5,3},{7,5},{8,14},{10,8},{12,... | collective-permute-start | bytes 2359304 | tf_op jit(solution)/shard_map/ppermute | solution.py:84
  213.5 47.5 %all-to-all-start.3 = ((bf16[4,4,32,2048]{3,2,1,0:T(8,128)(2,1)}), bf16[4,4,32,2048]{3,2,1,0:T(8,128)(2,1)S(1)}, u32[]{:S(2)}, u32[]{:S(2)}) async-start(bf16[4,4,32,2048]{3,2,1,0:T(8,128)(2,1)} %pack.3), calls=%async_computation.3 | async-start | bytes 4194304 | tf_op jit(solution)/shard_map/all_to_all | solution.py:102
  232.0 25.0 %copy-start.5 = (bf16[6,32,2048]{2,1,0:T(8,128)(2,1)}, bf16[6,32,2048]{2,1,0:T(8,128)(2,1)S(1)}, u32[]{:S(2)}) copy-start(bf16[6,32,2048]{2,1,0:T(8,128)(2,1)S(1)} %collective-permute-done.14.refs_4_) | copy-start | bytes 2359300
  232.1 28.9 %collective-permute-start.15 = (bf16[2,32,2048]{2,1,0:T(8,128)(2,1)S(1)}, bf16[2,32,2048]{2,1,0:T(8,128)(2,1)S(1)}, u32[]{:S(2)}, u32[]{:S(2)}) collective-permute-start(bf16[2,32,2048]{2,1,0:T(8,128)(2,1)S(1)} %slice.54), channel_id=1, source_target_pairs={{0,2},{2,4},{4,6},{6,0},{1,3},{3,5},{5,7},{7,1},{8,10},{10,12},{12... | collective-permute-start | bytes 786440 | tf_op jit(solution)/shard_map/ppermute | solution.py:84
  248.1 12.9 %collective-permute-start.17 = (bf16[2,32,2048]{2,1,0:T(8,128)(2,1)S(1)}, bf16[2,32,2048]{2,1,0:T(8,128)(2,1)S(1)}, u32[]{:S(2)}, u32[]{:S(2)}) collective-permute-start(bf16[2,32,2048]{2,1,0:T(8,128)(2,1)S(1)} %slice.55), channel_id=1, source_target_pairs={{0,6},{2,0},{4,2},{6,4},{1,7},{3,1},{5,3},{7,5},{8,14},{10,8},{12,... | collective-permute-start | bytes 786440 | tf_op jit(solution)/shard_map/ppermute | solution.py:84
  (11 other events, 34.0 us)

commit v8 on v7

--- a/solution.py
+++ b/solution.py
@@ -49,6 +49,10 @@
     return hits.reshape(numbers.shape[0] * capacity, tok_rows).astype(BF), slot_weight.reshape(-1, 1)
 
 
+def heading(e):
+    return 1 - 2 * (e % 2)
+
+
 class Ring:
     def __init__(self, nodes, planes):
         self.nodes, self.planes, self.half = nodes, planes, planes // 2
@@ -75,13 +79,20 @@
             up[(half - 1) * nodes :, :, columns] = value[: self.cut]
             down[(half - 1) * nodes :, :, columns] = value[self.cut :]
 
+    def pairs(self, way):
+        count = lax.axis_size("edata")
+        return [
+            (p * count + e, (p + way * heading(e)) % self.planes * count + e)
+            for p in range(self.planes)
+            for e in range(count)
+        ]
+
     def send(self, own, up, down):
         got = [own]
         for first, way, last in ((up, 1, self.cut), (down, -1, self.nodes - self.cut)):
             now = first
             for step in range(1, self.half + 1):
-                pairs = [(i, (i + way) % self.planes) for i in range(self.planes)]
-                now = lax.ppermute(now, "local", pairs)
+                now = lax.ppermute(now, ("local", "edata"), self.pairs(way))
                 got.append(now)
                 if step < self.half:
                     now = now[self.nodes :]
@@ -425,7 +436,8 @@
     turn = lax.axis_index("edata").astype(jnp.int32).reshape(1)
     w_ins = gathered(w_gate_up[0])
     w_outs = gathered(w_down[0])
-    plane = (lax.axis_index("local") + jnp.arange(planes, dtype=jnp.int32)) % planes
+    along = heading(lax.axis_index("edata")) * jnp.arange(planes, dtype=jnp.int32)
+    plane = (lax.axis_index("local") + along + planes) % planes
     numbers = (plane[:, None] + planes * jnp.arange(nodes, dtype=jnp.int32)[None, :]).reshape(-1)
     pick, slot_weight = slot_tables(expert_ids, gates, numbers, capacity)
 

time: 271 us -> 270 us (level)
  waiting for transfers between devices: 149 us -> 96.6 us
  starting transfers between devices: 43.6 us -> 95 us
    ppermute x16, waiting for transfers between devices: 148 us -> 96.6 us  [send(): now = lax.ppermute(now, ('local', 'edata'), self.pairs(way))]
    ppermute x16, starting transfers between devices: 26.3 us -> 77.9 us  [send(): now = lax.ppermute(now, ('local', 'edata'), self.pairs(way))]
  transfers between devices with their start and end apart: 23 -> 23, of which waited for: 14 -> 12; matrix products, arithmetic and copies ran while one was open for 5% -> 5% of each run, Pallas kernels for 5% -> 5%
where the time goes in v8:
time: 270 us; the launch traced here: 269 us
  waiting for transfers between devices  96.6 us (36%)
  starting transfers between devices  95 us (35%)
  Pallas kernels  55.2 us (20%)
  other arithmetic  12.6 us (5%)
  local copies, waits for them, and re-layouts  8.58 us (3%)
    ppermute x16, waiting for transfers between devices, send(): now = lax.ppermute(now, ('local', 'edata'), self.pairs(way))  96.6 us
    ppermute x16, starting transfers between devices, send(): now = lax.ppermute(now, ('local', 'edata'), self.pairs(way))  77.9 us
    all_to_all x4, starting transfers between devices, over_nodes(): return lax.all_to_all(rows, 'node', split_axis=0, concat_axis=0, tiled=True)  17.1 us
    pallas_call x1, Pallas kernels, expert(): call(kernel, 'expert', in_specs=[VMEM] * len(operands), out_specs=[VMEM]...  16.8 us
    pallas_call x2, Pallas kernels, weight_grads(): call(kernel, 'weight_grads', grid=(steps,), in_specs=[columns, columns, p...  13.7 us
    add x2, other arithmetic, shards(): sum((p[:, columns].astype(F32) for p in parts))  10.4 us
    pallas_call x1, Pallas kernels, combine(): call(kernel, 'combine', grid_spec=pltpu.PrefetchScalarGridSpec(num_scalar...  7.09 us
    pallas_call x2, Pallas kernels, pack(): call(kernel, 'pack', grid=(width // tile,), in_specs=[pl.BlockSpec((n, ca...  5.95 us
  transfers between devices with their start and end apart: 23, of which 12 were waited for; matrix products, arithmetic and copies ran while one was open for 5% of the time, Pallas kernels for 5%

profile of v8, /device:TPU:0, one launch (start us, length us, event | category | flops | bytes accessed | tf_op | source)
XLA Modules:
  0.0 269.2 jit_solution(9457124449989633999)
XLA Ops:
  8.4 3.6 %dispatch_dy.1 = (bf16[4,4,32,2048]{3,2,1,0:T(8,128)(2,1)}, bf16[512,2048]{1,0:T(8,128)(2,1)}) custom-call(s32[1]{0:T(128)} %bitcast.turn_ref, bf16[512,256]{1,0:T(8,128)(2,1)} %copy.24.pick_ref, f32[512,1]{1,0:T(8,128)} %copy.25.weight_ref, bf16[256,2048]{1,0:T(8,128)(2,1)} %grad_ref.1), custom_call_target="tpu_custom_call" | custom-call | flops 1 | bytes 1 | tf_op jit(solution)/shard_map/dispatch_dy/pallas_call | solution.py:180
  12.1 5.2 %all-to-all-start = ((bf16[4,4,32,2048]{3,2,1,0:T(8,128)(2,1)}), bf16[4,4,32,2048]{3,2,1,0:T(8,128)(2,1)S(1)}, u32[]{:S(2)}, u32[]{:S(2)}) async-start(bf16[4,4,32,2048]{3,2,1,0:T(8,128)(2,1)} %get-tuple-element.53), calls=%async_computation | async-start | bytes 4194304 | tf_op jit(solution)/shard_map/all_to_all | solution.py:113
  21.1 18.7 %collective-permute-done.refs_1_ = bf16[6,32,2048]{2,1,0:T(8,128)(2,1)S(1)} collective-permute-done((bf16[6,32,2048]{2,1,0:T(8,128)(2,1)}, bf16[6,32,2048]{2,1,0:T(8,128)(2,1)S(1)}, u32[]{:S(2)}, u32[]{:S(2)}) %collective-permute-start) | collective-permute-done | bytes 786464 | tf_op jit(solution)/shard_map/ppermute | solution.py:95
  39.8 15.4 %collective-permute-start.1 = (bf16[2,32,2048]{2,1,0:T(8,128)(2,1)S(1)}, bf16[2,32,2048]{2,1,0:T(8,128)(2,1)S(1)}, u32[]{:S(2)}, u32[]{:S(2)}) collective-permute-start(bf16[2,32,2048]{2,1,0:T(8,128)(2,1)S(1)} %slice.48), channel_id=1, source_target_pairs={{0,2},{1,7},{2,4},{3,1},{4,6},{5,3},{6,0},{7,5},{8,10},{9,15},{10,... | collective-permute-start | bytes 786440 | tf_op jit(solution)/shard_map/ppermute | solution.py:95
  55.3 2.9 %collective-permute-start.3 = (bf16[2,32,2048]{2,1,0:T(8,128)(2,1)S(1)}, bf16[2,32,2048]{2,1,0:T(8,128)(2,1)}, u32[]{:S(2)}, u32[]{:S(2)}) collective-permute-start(bf16[2,32,2048]{2,1,0:T(8,128)(2,1)S(1)} %slice.49), channel_id=1, source_target_pairs={{0,6},{1,3},{2,0},{3,5},{4,2},{5,7},{6,4},{7,1},{8,14},{9,11},{10,... | collective-permute-start | bytes 786440 | tf_op jit(solution)/shard_map/ppermute | solution.py:95
  58.2 6.6 %collective-permute-done.1.refs_2_ = bf16[2,32,2048]{2,1,0:T(8,128)(2,1)S(1)} collective-permute-done((bf16[2,32,2048]{2,1,0:T(8,128)(2,1)S(1)}, bf16[2,32,2048]{2,1,0:T(8,128)(2,1)S(1)}, u32[]{:S(2)}, u32[]{:S(2)}) %collective-permute-start.1) | collective-permute-done | bytes 262176 | tf_op jit(solution)/shard_map/ppermute | solution.py:95
  64.8 3.0 %collective-permute-done.3.refs_4_ = bf16[2,32,2048]{2,1,0:T(8,128)(2,1)} collective-permute-done((bf16[2,32,2048]{2,1,0:T(8,128)(2,1)S(1)}, bf16[2,32,2048]{2,1,0:T(8,128)(2,1)}, u32[]{:S(2)}, u32[]{:S(2)}) %collective-permute-start.3) | collective-permute-done | bytes 262176 | tf_op jit(solution)/shard_map/ppermute | solution.py:95
  67.8 3.3 %pack.2 = bf16[4,4,32,2048]{3,2,1,0:T(8,128)(2,1)} custom-call(bf16[4,32,2048]{2,1,0:T(8,128)(2,1)} %get-tuple-element.54.refs_0_, bf16[6,32,2048]{2,1,0:T(8,128)(2,1)} %copy-done.9, bf16[2,32,2048]{2,1,0:T(8,128)(2,1)} %copy-done.16, bf16[6,32,2048]{2,1,0:T(8,128)(2,1)} %copy-done.11, bf16[2,32,2048]{2,1,0:T(8,128)(2,1)} %collective-permute-done.3.refs_4_), custom_call_target="tpu_custom_call" | custom-call | flops 1 | bytes 1 | tf_op jit(solution)/shard_map/pack/pallas_call | solution.py:216
  71.2 4.2 %all-to-all-start.1 = ((bf16[4,4,32,2048]{3,2,1,0:T(8,128)(2,1)}), bf16[4,4,32,2048]{3,2,1,0:T(8,128)(2,1)S(1)}, u32[]{:S(2)}, u32[]{:S(2)}) async-start(bf16[4,4,32,2048]{3,2,1,0:T(8,128)(2,1)} %pack.2), calls=%async_computation.1 | async-start | bytes 4194304 | tf_op jit(solution)/shard_map/all_to_all | solution.py:113
  81.8 18.8 %collective-permute-done.4.refs_1_ = bf16[6,32,2048]{2,1,0:T(8,128)(2,1)S(1)} collective-permute-done((bf16[6,32,2048]{2,1,0:T(8,128)(2,1)}, bf16[6,32,2048]{2,1,0:T(8,128)(2,1)S(1)}, u32[]{:S(2)}, u32[]{:S(2)}) %collective-permute-start.4) | collective-permute-done | bytes 786464 | tf_op jit(solution)/shard_map/ppermute | solution.py:95
  100.6 7.1 %collective-permute-start.5 = (bf16[2,32,2048]{2,1,0:T(8,128)(2,1)S(1)}, bf16[2,32,2048]{2,1,0:T(8,128)(2,1)S(1)}, u32[]{:S(2)}, u32[]{:S(2)}) collective-permute-start(bf16[2,32,2048]{2,1,0:T(8,128)(2,1)S(1)} %slice.50), channel_id=1, source_target_pairs={{0,2},{1,7},{2,4},{3,1},{4,6},{5,3},{6,0},{7,5},{8,10},{9,15},{10,... | collective-permute-start | bytes 786440 | tf_op jit(solution)/shard_map/ppermute | solution.py:95
  107.7 6.5 %collective-permute-done.6.refs_3_ = bf16[6,32,2048]{2,1,0:T(8,128)(2,1)S(1)} collective-permute-done((bf16[6,32,2048]{2,1,0:T(8,128)(2,1)}, bf16[6,32,2048]{2,1,0:T(8,128)(2,1)S(1)}, u32[]{:S(2)}, u32[]{:S(2)}) %collective-permute-start.6) | collective-permute-done | bytes 786464 | tf_op jit(solution)/shard_map/ppermute | solution.py:95
  116.0 3.6 %collective-permute-done.5.refs_2_ = bf16[2,32,2048]{2,1,0:T(8,128)(2,1)S(1)} collective-permute-done((bf16[2,32,2048]{2,1,0:T(8,128)(2,1)S(1)}, bf16[2,32,2048]{2,1,0:T(8,128)(2,1)S(1)}, u32[]{:S(2)}, u32[]{:S(2)}) %collective-permute-start.5) | collective-permute-done | bytes 262176 | tf_op jit(solution)/shard_map/ppermute | solution.py:95
  119.6 4.0 %collective-permute-done.7.refs_4_ = bf16[2,32,2048]{2,1,0:T(8,128)(2,1)} collective-permute-done((bf16[2,32,2048]{2,1,0:T(8,128)(2,1)S(1)}, bf16[2,32,2048]{2,1,0:T(8,128)(2,1)}, u32[]{:S(2)}, u32[]{:S(2)}) %collective-permute-start.7) | collective-permute-done | bytes 262176 | tf_op jit(solution)/shard_map/ppermute | solution.py:95
  125.0 16.8 %expert.1 = (bf16[4,32,2048]{2,1,0:T(8,128)(2,1)}, bf16[6,32,2048]{2,1,0:T(8,128)(2,1)}, bf16[6,32,2048]{2,1,0:T(8,128)(2,1)}, bf16[4,4,32,2048]{3,2,1,0:T(8,128...) custom-call(bf16[4,4,32,2048]{3,2,1,0:T(8,128)(2,1)} %copy-done, ...), custom_call_target="tpu_custom_call" | custom-call | flops 1 | bytes 1 | tf_op jit(solution)/shard_map/expert/pallas_call | solution.py:316
  141.7 3.9 %all-to-all-start.2 = ((bf16[4,4,32,2048]{3,2,1,0:T(8,128)(2,1)}), bf16[4,4,32,2048]{3,2,1,0:T(8,128)(2,1)S(1)}, u32[]{:S(2)}, u32[]{:S(2)}) async-start(bf16[4,4,32,2048]{3,2,1,0:T(8,128)(2,1)} %get-tuple-element.66), calls=%async_computation.2 | async-start | bytes 4194304 | tf_op jit(solution)/shard_map/all_to_all | solution.py:113
  145.7 3.8 %collective-permute-start.12 = (bf16[6,32,2048]{2,1,0:T(8,128)(2,1)}, bf16[6,32,2048]{2,1,0:T(8,128)(2,1)S(1)}, u32[]{:S(2)}, u32[]{:S(2)}) collective-permute-start(bf16[6,32,2048]{2,1,0:T(8,128)(2,1)} %get-tuple-element.65), channel_id=1, source_target_pairs={{0,6},{1,3},{2,0},{3,5},{4,2},{5,7},{6,4},{7,1},{8,14},{9,11},{10,... | collective-permute-start | bytes 2359304 | tf_op jit(solution)/shard_map/ppermute | solution.py:95
  149.5 18.8 %collective-permute-done.10.refs_1_ = bf16[6,32,2048]{2,1,0:T(8,128)(2,1)S(1)} collective-permute-done((bf16[6,32,2048]{2,1,0:T(8,128)(2,1)}, bf16[6,32,2048]{2,1,0:T(8,128)(2,1)S(1)}, u32[]{:S(2)}, u32[]{:S(2)}) %collective-permute-start.10) | collective-permute-done | bytes 786464 | tf_op jit(solution)/shard_map/ppermute | solution.py:95
  168.3 10.2 %collective-permute-start.11 = (bf16[2,32,2048]{2,1,0:T(8,128)(2,1)S(1)}, bf16[2,32,2048]{2,1,0:T(8,128)(2,1)S(1)}, u32[]{:S(2)}, u32[]{:S(2)}) collective-permute-start(bf16[2,32,2048]{2,1,0:T(8,128)(2,1)S(1)} %slice.52), channel_id=1, source_target_pairs={{0,2},{1,7},{2,4},{3,1},{4,6},{5,3},{6,0},{7,5},{8,10},{9,15},{10,... | collective-permute-start | bytes 786440 | tf_op jit(solution)/shard_map/ppermute | solution.py:95
  180.7 4.3 %collective-permute-start.13 = (bf16[2,32,2048]{2,1,0:T(8,128)(2,1)S(1)}, bf16[2,32,2048]{2,1,0:T(8,128)(2,1)}, u32[]{:S(2)}, u32[]{:S(2)}) collective-permute-start(bf16[2,32,2048]{2,1,0:T(8,128)(2,1)S(1)} %slice.53), channel_id=1, source_target_pairs={{0,6},{1,3},{2,0},{3,5},{4,2},{5,7},{6,4},{7,1},{8,14},{9,11},{10,... | collective-permute-start | bytes 786440 | tf_op jit(solution)/shard_map/ppermute | solution.py:95
  185.0 4.1 %collective-permute-done.11.refs_2_ = bf16[2,32,2048]{2,1,0:T(8,128)(2,1)S(1)} collective-permute-done((bf16[2,32,2048]{2,1,0:T(8,128)(2,1)S(1)}, bf16[2,32,2048]{2,1,0:T(8,128)(2,1)S(1)}, u32[]{:S(2)}, u32[]{:S(2)}) %collective-permute-start.11) | collective-permute-done | bytes 262176 | tf_op jit(solution)/shard_map/ppermute | solution.py:95
  189.2 3.2 %collective-permute-done.13.refs_4_ = bf16[2,32,2048]{2,1,0:T(8,128)(2,1)} collective-permute-done((bf16[2,32,2048]{2,1,0:T(8,128)(2,1)S(1)}, bf16[2,32,2048]{2,1,0:T(8,128)(2,1)}, u32[]{:S(2)}, u32[]{:S(2)}) %collective-permute-start.13) | collective-permute-done | bytes 262176 | tf_op jit(solution)/shard_map/ppermute | solution.py:95
  199.0 6.9 %weight_grads.3 = bf16[1024,2304]{1,0:T(8,128)(2,1)} custom-call(bf16[512,2048]{1,0:T(8,128)(2,1)} %get-tuple-element.78.x_ref, bf16[512,2048]{1,0:T(8,128)(2,1)} %get-tuple-element.79.dy_ref, bf16[512,768]{1,0:T(8,128)(2,1)} %get-tuple-element.81.inner_ref, bf16[512,1536]{1,0:T(8,128)(2,1)} %get-tuple-element.82.act_grad_ref), custom_call_target="tpu_custom_call" | custom-call | flops 1 | bytes 1 | tf_op jit(solution)/shard_map/weight_grads/pallas_call | solution.py:342
  206.7 3.0 %collective-permute-start.16 = (bf16[6,32,2048]{2,1,0:T(8,128)(2,1)}, bf16[6,32,2048]{2,1,0:T(8,128)(2,1)}, u32[]{:S(2)}, u32[]{:S(2)}) collective-permute-start(bf16[6,32,2048]{2,1,0:T(8,128)(2,1)} %get-tuple-element.77), channel_id=1, source_target_pairs={{0,6},{1,3},{2,0},{3,5},{4,2},{5,7},{6,4},{7,1},{8,14},{9,11},{10,... | collective-permute-start | bytes 2359304 | tf_op jit(solution)/shard_map/ppermute | solution.py:95
  209.7 3.8 %all-to-all-start.3 = ((bf16[4,4,32,2048]{3,2,1,0:T(8,128)(2,1)}), bf16[4,4,32,2048]{3,2,1,0:T(8,128)(2,1)S(1)}, u32[]{:S(2)}, u32[]{:S(2)}) async-start(bf16[4,4,32,2048]{3,2,1,0:T(8,128)(2,1)} %pack.3), calls=%async_computation.3 | async-start | bytes 4194304 | tf_op jit(solution)/shard_map/all_to_all | solution.py:113
  213.5 6.8 %weight_grads.2 = bf16[1024,2304]{1,0:T(8,128)(2,1)} custom-call(bf16[512,2048]{1,0:T(8,128)(2,1)} %get-tuple-element.78.x_ref, bf16[512,2048]{1,0:T(8,128)(2,1)} %get-tuple-element.79.dy_ref, bf16[512,768]{1,0:T(8,128)(2,1)} %get-tuple-element.81.inner_ref, bf16[512,1536]{1,0:T(8,128)(2,1)} %get-tuple-element.82.act_grad_ref), custom_call_target="tpu_custom_call" | custom-call | flops 1 | bytes 1 | tf_op jit(solution)/shard_map/weight_grads/pallas_call | solution.py:342
  221.2 7.1 %collective-permute-done.14.refs_4_ = bf16[6,32,2048]{2,1,0:T(8,128)(2,1)S(1)} collective-permute-done((bf16[6,32,2048]{2,1,0:T(8,128)(2,1)}, bf16[6,32,2048]{2,1,0:T(8,128)(2,1)S(1)}, u32[]{:S(2)}, u32[]{:S(2)}) %collective-permute-start.14) | collective-permute-done | bytes 786464 | tf_op jit(solution)/shard_map/ppermute | solution.py:95
  228.3 14.5 %collective-permute-start.15 = (bf16[2,32,2048]{2,1,0:T(8,128)(2,1)S(1)}, bf16[2,32,2048]{2,1,0:T(8,128)(2,1)S(1)}, u32[]{:S(2)}, u32[]{:S(2)}) collective-permute-start(bf16[2,32,2048]{2,1,0:T(8,128)(2,1)S(1)} %slice.54), channel_id=1, source_target_pairs={{0,2},{1,7},{2,4},{3,1},{4,6},{5,3},{6,0},{7,5},{8,10},{9,15},{10,... | collective-permute-start | bytes 786440 | tf_op jit(solution)/shard_map/ppermute | solution.py:95
  243.9 6.2 %collective-permute-start.17 = (bf16[2,32,2048]{2,1,0:T(8,128)(2,1)S(1)}, bf16[2,32,2048]{2,1,0:T(8,128)(2,1)S(1)}, u32[]{:S(2)}, u32[]{:S(2)}) collective-permute-start(bf16[2,32,2048]{2,1,0:T(8,128)(2,1)S(1)} %slice.55), channel_id=1, source_target_pairs={{0,6},{1,3},{2,0},{3,5},{4,2},{5,7},{6,4},{7,1},{8,14},{9,11},{10,... | collective-permute-start | bytes 786440 | tf_op jit(solution)/shard_map/ppermute | solution.py:95
  250.1 6.5 %convert_add_fusion = f32[1024,1536]{1,0:T(8,128)} fusion(bf16[1024,2304]{1,0:T(8,128)(2,1)} %collective-permute-done.18, bf16[1024,2304]{1,0:T(8,128)(2,1)} %weight_grads.2), kind=kLoop, calls=%fused_computation | loop fusion | flops 4718592 | bytes 12582912 | tf_op jit(solution)/shard_map/add | solution.py:468
  256.6 3.9 %convert_add_fusion.1 = f32[1024,768]{1,0:T(8,128)} fusion(bf16[1024,2304]{1,0:T(8,128)(2,1)} %collective-permute-done.18, bf16[1024,2304]{1,0:T(8,128)(2,1)} %weight_grads.2), kind=kLoop, calls=%fused_computation.1 | loop fusion | flops 2359296 | bytes 6291456 | tf_op jit(solution)/shard_map/add | solution.py:468
  262.0 7.1 %combine.1 = (bf16[256,2048]{1,0:T(8,128)(2,1)}, bf16[256,2048]{1,0:T(8,128)(2,1)}, f32[8,256]{1,0:T(8,128)}) custom-call(s32[1]{0:T(128)} %bitcast.turn_ref, s32[16]{0:T(128)} %copy-done.18, bf16[512,256]{1,0:T(8,128)(2,1)} %copy.26.pick_ref, bf16[256,512]{1,0:T(8,128)(2,1)} %bitcast.17, bf16[256,512]{1,0:T(8,128)(2,1)} %get-tuple-element.94.high_ref, ...), custom_call_target="tpu_custom_call" | custom-call | flops 1 | bytes 1 | tf_op jit(solution)/shard_map/combine/pallas_call | solution.py:406
  (93 shorter events, 34.2 us)
Async XLA Ops:
  0.8 11.2 %copy-start.18 = (s32[16]{0:T(128)}, s32[16]{0:T(128)S(1)}, u32[]{:S(2)}) copy-start(s32[16]{0:T(128)S(1)} %add.66.number_ref) | copy-start | bytes 196
  2.5 217.8 %copy-start.4 = (bf16[512,256]{0,1:T(8,128)(2,1)}, bf16[512,256]{0,1:T(8,128)(2,1)S(1)}, u32[]{:S(2)}) copy-start(bf16[512,256]{0,1:T(8,128)(2,1)S(1)} %and_convert_fusion) | copy-start | bytes 786436
  12.1 55.7 %all-to-all-start = ((bf16[4,4,32,2048]{3,2,1,0:T(8,128)(2,1)}), bf16[4,4,32,2048]{3,2,1,0:T(8,128)(2,1)S(1)}, u32[]{:S(2)}, u32[]{:S(2)}) async-start(bf16[4,4,32,2048]{3,2,1,0:T(8,128)(2,1)} %get-tuple-element.53), calls=%async_computation | async-start | bytes 4194304 | tf_op jit(solution)/shard_map/all_to_all | solution.py:113
  17.2 106.4 %collective-permute-start.8 = (bf16[1024,1536]{1,0:T(8,128)(2,1)}, bf16[1024,1536]{1,0:T(8,128)(2,1)}, u32[]{:S(2)}, u32[]{:S(2)}) collective-permute-start(bf16[1024,1536]{1,0:T(8,128)(2,1)} %bitcast.19), channel_id=1, source_target_pairs={{1,0},{0,1},{3,2},{2,3},{5,4},{4,5},{7,6},{6,7},{9,8},{8,9},{11,10... | collective-permute-start | bytes 9437192 | tf_op jit(solution)/shard_map/ppermute | solution.py:121
  17.2 22.6 %collective-permute-start = (bf16[6,32,2048]{2,1,0:T(8,128)(2,1)}, bf16[6,32,2048]{2,1,0:T(8,128)(2,1)S(1)}, u32[]{:S(2)}, u32[]{:S(2)}) collective-permute-start(bf16[6,32,2048]{2,1,0:T(8,128)(2,1)} %get-tuple-element.50), channel_id=1, source_target_pairs={{0,2},{1,7},{2,4},{3,1},{4,6},{5,3},{6,0},{7,5},{8,10},{9,15},{10,... | collective-permute-start | bytes 2359304 | tf_op jit(solution)/shard_map/ppermute | solution.py:95
  18.8 36.4 %collective-permute-start.2 = (bf16[6,32,2048]{2,1,0:T(8,128)(2,1)}, bf16[6,32,2048]{2,1,0:T(8,128)(2,1)S(1)}, u32[]{:S(2)}, u32[]{:S(2)}) collective-permute-start(bf16[6,32,2048]{2,1,0:T(8,128)(2,1)} %get-tuple-element.51), channel_id=1, source_target_pairs={{0,6},{1,3},{2,0},{3,5},{4,2},{5,7},{6,4},{7,1},{8,14},{9,11},{10,... | collective-permute-start | bytes 2359304 | tf_op jit(solution)/shard_map/ppermute | solution.py:95
  39.8 28.0 %copy-start.9 = (bf16[6,32,2048]{2,1,0:T(8,128)(2,1)}, bf16[6,32,2048]{2,1,0:T(8,128)(2,1)S(1)}, u32[]{:S(2)}) copy-start(bf16[6,32,2048]{2,1,0:T(8,128)(2,1)S(1)} %collective-permute-done.refs_1_) | copy-start | bytes 2359300
  39.8 25.0 %collective-permute-start.1 = (bf16[2,32,2048]{2,1,0:T(8,128)(2,1)S(1)}, bf16[2,32,2048]{2,1,0:T(8,128)(2,1)S(1)}, u32[]{:S(2)}, u32[]{:S(2)}) collective-permute-start(bf16[2,32,2048]{2,1,0:T(8,128)(2,1)S(1)} %slice.48), channel_id=1, source_target_pairs={{0,2},{1,7},{2,4},{3,1},{4,6},{5,3},{6,0},{7,5},{8,10},{9,15},{10,... | collective-permute-start | bytes 786440 | tf_op jit(solution)/shard_map/ppermute | solution.py:95
  55.3 9.5 %copy-start.11 = (bf16[6,32,2048]{2,1,0:T(8,128)(2,1)}, bf16[6,32,2048]{2,1,0:T(8,128)(2,1)S(1)}, u32[]{:S(2)}) copy-start(bf16[6,32,2048]{2,1,0:T(8,128)(2,1)S(1)} %collective-permute-done.2.refs_3_) | copy-start | bytes 2359300
  55.3 12.5 %collective-permute-start.3 = (bf16[2,32,2048]{2,1,0:T(8,128)(2,1)S(1)}, bf16[2,32,2048]{2,1,0:T(8,128)(2,1)}, u32[]{:S(2)}, u32[]{:S(2)}) collective-permute-start(bf16[2,32,2048]{2,1,0:T(8,128)(2,1)S(1)} %slice.49), channel_id=1, source_target_pairs={{0,6},{1,3},{2,0},{3,5},{4,2},{5,7},{6,4},{7,1},{8,14},{9,11},{10,... | collective-permute-start | bytes 786440 | tf_op jit(solution)/shard_map/ppermute | solution.py:95
  58.2 57.8 %collective-permute-start.9 = (bf16[1024,768]{1,0:T(8,128)(2,1)}, bf16[1024,768]{1,0:T(8,128)(2,1)}, u32[]{:S(2)}, u32[]{:S(2)}) collective-permute-start(bf16[1024,768]{1,0:T(8,128)(2,1)} %bitcast.23), channel_id=1, source_target_pairs={{1,0},{0,1},{3,2},{2,3},{5,4},{4,5},{7,6},{6,7},{9,8},{8,9},{11,10... | collective-permute-start | bytes 4718600 | tf_op jit(solution)/shard_map/ppermute | solution.py:121
  71.2 52.5 %all-to-all-start.1 = ((bf16[4,4,32,2048]{3,2,1,0:T(8,128)(2,1)}), bf16[4,4,32,2048]{3,2,1,0:T(8,128)(2,1)S(1)}, u32[]{:S(2)}, u32[]{:S(2)}) async-start(bf16[4,4,32,2048]{3,2,1,0:T(8,128)(2,1)} %pack.2), calls=%async_computation.1 | async-start | bytes 4194304 | tf_op jit(solution)/shard_map/all_to_all | solution.py:113
  78.0 22.6 %collective-permute-start.4 = (bf16[6,32,2048]{2,1,0:T(8,128)(2,1)}, bf16[6,32,2048]{2,1,0:T(8,128)(2,1)S(1)}, u32[]{:S(2)}, u32[]{:S(2)}) collective-permute-start(bf16[6,32,2048]{2,1,0:T(8,128)(2,1)} %get-tuple-element.61), channel_id=1, source_target_pairs={{0,2},{1,7},{2,4},{3,1},{4,6},{5,3},{6,0},{7,5},{8,10},{9,15},{10,... | collective-permute-start | bytes 2359304 | tf_op jit(solution)/shard_map/ppermute | solution.py:95
  78.9 35.2 %collective-permute-start.6 = (bf16[6,32,2048]{2,1,0:T(8,128)(2,1)}, bf16[6,32,2048]{2,1,0:T(8,128)(2,1)S(1)}, u32[]{:S(2)}, u32[]{:S(2)}) collective-permute-start(bf16[6,32,2048]{2,1,0:T(8,128)(2,1)} %get-tuple-element.62), channel_id=1, source_target_pairs={{0,6},{1,3},{2,0},{3,5},{4,2},{5,7},{6,4},{7,1},{8,14},{9,11},{10,... | collective-permute-start | bytes 2359304 | tf_op jit(solution)/shard_map/ppermute | solution.py:95
  100.6 23.1 %copy-start.6 = (bf16[6,32,2048]{2,1,0:T(8,128)(2,1)}, bf16[6,32,2048]{2,1,0:T(8,128)(2,1)S(1)}, u32[]{:S(2)}) copy-start(bf16[6,32,2048]{2,1,0:T(8,128)(2,1)S(1)} %collective-permute-done.4.refs_1_) | copy-start | bytes 2359300
  100.6 19.0 %collective-permute-start.5 = (bf16[2,32,2048]{2,1,0:T(8,128)(2,1)S(1)}, bf16[2,32,2048]{2,1,0:T(8,128)(2,1)S(1)}, u32[]{:S(2)}, u32[]{:S(2)}) collective-permute-start(bf16[2,32,2048]{2,1,0:T(8,128)(2,1)S(1)} %slice.50), channel_id=1, source_target_pairs={{0,2},{1,7},{2,4},{3,1},{4,6},{5,3},{6,0},{7,5},{8,10},{9,15},{10,... | collective-permute-start | bytes 786440 | tf_op jit(solution)/shard_map/ppermute | solution.py:95
  114.2 9.5 %collective-permute-start.7 = (bf16[2,32,2048]{2,1,0:T(8,128)(2,1)S(1)}, bf16[2,32,2048]{2,1,0:T(8,128)(2,1)}, u32[]{:S(2)}, u32[]{:S(2)}) collective-permute-start(bf16[2,32,2048]{2,1,0:T(8,128)(2,1)S(1)} %slice.51), channel_id=1, source_target_pairs={{0,6},{1,3},{2,0},{3,5},{4,2},{5,7},{6,4},{7,1},{8,14},{9,11},{10,... | collective-permute-start | bytes 786440 | tf_op jit(solution)/shard_map/ppermute | solution.py:95
  141.7 50.7 %all-to-all-start.2 = ((bf16[4,4,32,2048]{3,2,1,0:T(8,128)(2,1)}), bf16[4,4,32,2048]{3,2,1,0:T(8,128)(2,1)S(1)}, u32[]{:S(2)}, u32[]{:S(2)}) async-start(bf16[4,4,32,2048]{3,2,1,0:T(8,128)(2,1)} %get-tuple-element.66), calls=%async_computation.2 | async-start | bytes 4194304 | tf_op jit(solution)/shard_map/all_to_all | solution.py:113
  145.6 22.6 %collective-permute-start.10 = (bf16[6,32,2048]{2,1,0:T(8,128)(2,1)}, bf16[6,32,2048]{2,1,0:T(8,128)(2,1)S(1)}, u32[]{:S(2)}, u32[]{:S(2)}) collective-permute-start(bf16[6,32,2048]{2,1,0:T(8,128)(2,1)} %get-tuple-element.64), channel_id=1, source_target_pairs={{0,2},{1,7},{2,4},{3,1},{4,6},{5,3},{6,0},{7,5},{8,10},{9,15},{10,... | collective-permute-start | bytes 2359304 | tf_op jit(solution)/shard_map/ppermute | solution.py:95
  145.7 35.0 %collective-permute-start.12 = (bf16[6,32,2048]{2,1,0:T(8,128)(2,1)}, bf16[6,32,2048]{2,1,0:T(8,128)(2,1)S(1)}, u32[]{:S(2)}, u32[]{:S(2)}) collective-permute-start(bf16[6,32,2048]{2,1,0:T(8,128)(2,1)} %get-tuple-element.65), channel_id=1, source_target_pairs={{0,6},{1,3},{2,0},{3,5},{4,2},{5,7},{6,4},{7,1},{8,14},{9,11},{10,... | collective-permute-start | bytes 2359304 | tf_op jit(solution)/shard_map/ppermute | solution.py:95
  168.3 28.1 %copy-start.8 = (bf16[6,32,2048]{2,1,0:T(8,128)(2,1)}, bf16[6,32,2048]{2,1,0:T(8,128)(2,1)S(1)}, u32[]{:S(2)}) copy-start(bf16[6,32,2048]{2,1,0:T(8,128)(2,1)S(1)} %collective-permute-done.10.refs_1_) | copy-start | bytes 2359300
  168.3 20.8 %collective-permute-start.11 = (bf16[2,32,2048]{2,1,0:T(8,128)(2,1)S(1)}, bf16[2,32,2048]{2,1,0:T(8,128)(2,1)S(1)}, u32[]{:S(2)}, u32[]{:S(2)}) collective-permute-start(bf16[2,32,2048]{2,1,0:T(8,128)(2,1)S(1)} %slice.52), channel_id=1, source_target_pairs={{0,2},{1,7},{2,4},{3,1},{4,6},{5,3},{6,0},{7,5},{8,10},{9,15},{10,... | collective-permute-start | bytes 786440 | tf_op jit(solution)/shard_map/ppermute | solution.py:95
  180.7 8.5 %copy-start.10 = (bf16[6,32,2048]{2,1,0:T(8,128)(2,1)}, bf16[6,32,2048]{2,1,0:T(8,128)(2,1)S(1)}, u32[]{:S(2)}) copy-start(bf16[6,32,2048]{2,1,0:T(8,128)(2,1)S(1)} %collective-permute-done.12.refs_3_) | copy-start | bytes 2359300
  180.7 11.7 %collective-permute-start.13 = (bf16[2,32,2048]{2,1,0:T(8,128)(2,1)S(1)}, bf16[2,32,2048]{2,1,0:T(8,128)(2,1)}, u32[]{:S(2)}, u32[]{:S(2)}) collective-permute-start(bf16[2,32,2048]{2,1,0:T(8,128)(2,1)S(1)} %slice.53), channel_id=1, source_target_pairs={{0,6},{1,3},{2,0},{3,5},{4,2},{5,7},{6,4},{7,1},{8,14},{9,11},{10,... | collective-permute-start | bytes 786440 | tf_op jit(solution)/shard_map/ppermute | solution.py:95
  189.1 7.2 %copy-start.15 = (bf16[2,32,2048]{2,1,0:T(8,128)(2,1)}, bf16[2,32,2048]{2,1,0:T(8,128)(2,1)S(1)}, u32[]{:S(2)}) copy-start(bf16[2,32,2048]{2,1,0:T(8,128)(2,1)S(1)} %collective-permute-done.11.refs_2_) | copy-start | bytes 786436
  205.8 44.2 %collective-permute-start.18 = (bf16[1024,2304]{1,0:T(8,128)(2,1)}, bf16[1024,2304]{1,0:T(8,128)(2,1)}, u32[]{:S(2)}, u32[]{:S(2)}) collective-permute-start(bf16[1024,2304]{1,0:T(8,128)(2,1)} %weight_grads.3), channel_id=1, source_target_pairs={{0,1},{1,0},{2,3},{3,2},{4,5},{5,4},{6,7},{7,6},{8,9},{9,8},{10,11... | collective-permute-start | bytes 14155784 | tf_op jit(solution)/shard_map/ppermute | solution.py:127
  205.8 22.5 %collective-permute-start.14 = (bf16[6,32,2048]{2,1,0:T(8,128)(2,1)}, bf16[6,32,2048]{2,1,0:T(8,128)(2,1)S(1)}, u32[]{:S(2)}, u32[]{:S(2)}) collective-permute-start(bf16[6,32,2048]{2,1,0:T(8,128)(2,1)} %get-tuple-element.76), channel_id=1, source_target_pairs={{0,2},{1,7},{2,4},{3,1},{4,6},{5,3},{6,0},{7,5},{8,10},{9,15},{10,... | collective-permute-start | bytes 2359304 | tf_op jit(solution)/shard_map/ppermute | solution.py:95
  206.7 36.2 %collective-permute-start.16 = (bf16[6,32,2048]{2,1,0:T(8,128)(2,1)}, bf16[6,32,2048]{2,1,0:T(8,128)(2,1)}, u32[]{:S(2)}, u32[]{:S(2)}) collective-permute-start(bf16[6,32,2048]{2,1,0:T(8,128)(2,1)} %get-tuple-element.77), channel_id=1, source_target_pairs={{0,6},{1,3},{2,0},{3,5},{4,2},{5,7},{6,4},{7,1},{8,14},{9,11},{10,... | collective-permute-start | bytes 2359304 | tf_op jit(solution)/shard_map/ppermute | solution.py:95
  209.7 50.8 %all-to-all-start.3 = ((bf16[4,4,32,2048]{3,2,1,0:T(8,128)(2,1)}), bf16[4,4,32,2048]{3,2,1,0:T(8,128)(2,1)S(1)}, u32[]{:S(2)}, u32[]{:S(2)}) async-start(bf16[4,4,32,2048]{3,2,1,0:T(8,128)(2,1)} %pack.3), calls=%async_computation.3 | async-start | bytes 4194304 | tf_op jit(solution)/shard_map/all_to_all | solution.py:113
  228.3 28.2 %copy-start.5 = (bf16[6,32,2048]{2,1,0:T(8,128)(2,1)}, bf16[6,32,2048]{2,1,0:T(8,128)(2,1)S(1)}, u32[]{:S(2)}) copy-start(bf16[6,32,2048]{2,1,0:T(8,128)(2,1)S(1)} %collective-permute-done.14.refs_4_) | copy-start | bytes 2359300
  228.3 32.1 %collective-permute-start.15 = (bf16[2,32,2048]{2,1,0:T(8,128)(2,1)S(1)}, bf16[2,32,2048]{2,1,0:T(8,128)(2,1)S(1)}, u32[]{:S(2)}, u32[]{:S(2)}) collective-permute-start(bf16[2,32,2048]{2,1,0:T(8,128)(2,1)S(1)} %slice.54), channel_id=1, source_target_pairs={{0,2},{1,7},{2,4},{3,1},{4,6},{5,3},{6,0},{7,5},{8,10},{9,15},{10,... | collective-permute-start | bytes 786440 | tf_op jit(solution)/shard_map/ppermute | solution.py:95
  243.9 16.6 %collective-permute-start.17 = (bf16[2,32,2048]{2,1,0:T(8,128)(2,1)S(1)}, bf16[2,32,2048]{2,1,0:T(8,128)(2,1)S(1)}, u32[]{:S(2)}, u32[]{:S(2)}) collective-permute-start(bf16[2,32,2048]{2,1,0:T(8,128)(2,1)S(1)} %slice.55), channel_id=1, source_target_pairs={{0,6},{1,3},{2,0},{3,5},{4,2},{5,7},{6,4},{7,1},{8,14},{9,11},{10,... | collective-permute-start | bytes 786440 | tf_op jit(solution)/shard_map/ppermute | solution.py:95
  (11 other events, 34.5 us)

commit v9 on v1

v9 whole, which is shorter than its diff:
```python
import jax
import jax.numpy as jnp
from jax import lax
from jax.experimental import pallas as pl
from jax.experimental.pallas import tpu as pltpu
from jax.sharding import PartitionSpec as P

EXP_DEV = 4
BF = jnp.bfloat16
F32 = jnp.float32
ROWS_IN = (((0,), (0,)), ((), ()))
COLS_IN = (((1,), (1,)), ((), ()))
LIMIT = 56 * 1024 * 1024
CHEAP = pl.CostEstimate(flops=1, bytes_accessed=1, transcendentals=0)
VMEM = pl.BlockSpec(memory_space=pltpu.VMEM)
SMEM = pl.BlockSpec(memory_space=pltpu.SMEM)
SHARE = 4


def call(kernel, name, **more):
    return pl.pallas_call(
        kernel,
        compiler_params=pltpu.CompilerParams(vmem_limit_bytes=LIMIT),
        cost_estimate=CHEAP,
        name=name,
        **more,
    )


def shape(*dims, kind=BF):
    return jax.ShapeDtypeStruct(dims, kind)


def after(value, *others):
    return lax.optimization_barrier((value, *others))[0]


def gathered(shard):
    count = lax.axis_size("edata")
    shards = [shard]
    for step in range(1, count):
        pairs = [((i + step) % count, i) for i in range(count)]
        shards.append(lax.ppermute(shard, "edata", pairs))
    return shards


def from_owner(piece, step):
    count = lax.axis_size("edata")
    return lax.ppermute(piece, "edata", [(i, (i + step) % count) for i in range(count)])


def exchange(everything, blocks):
    axes = ("node", "local")
    count = len(blocks)
    got = [blocks[0]]
    for j in range(1, count):
        got.append(lax.ppermute(blocks[j], axes, [(i, i ^ j) for i in range(count)]))
    return lax.all_to_all(everything, axes, split_axis=0, concat_axis=0, tiled=True), got


def slots_of(j, me, capacity):
    return pl.ds(pl.multiple_of((me ^ j) * capacity, capacity), capacity)


def shard_at(s, turn, count, width):
    return pl.ds(pl.multiple_of((turn + s) % count * width, width), width)


def dispatch(where, ids_t, gates_t, tokens, out_grad, groups, capacity):
    top, tok_rows = ids_t.shape
    model = tokens.shape[1]
    count = lax.axis_size("edata")
    width = model // count
    part = model // SHARE
    slots = groups * capacity

    def kernel(where_ref, ids_ref, gates_ref, x_ref, grad_ref, sent_ref, *refs):
        blocks, (rows_ref, pick_ref, weight_ref, dy_ref) = refs[:groups], refs[groups:]
        me, turn = where_ref[0], where_ref[1]
        numbers = lax.broadcasted_iota(jnp.int32, (groups, tok_rows), 0)
        routed = jnp.zeros((groups, tok_rows), F32)
        weight = jnp.zeros((groups, tok_rows), F32)
        for k in range(top):
            chosen = ids_ref[k : k + 1, :] == numbers
            routed = jnp.where(chosen, 1.0, routed)
            weight += jnp.where(chosen, gates_ref[k : k + 1, :], 0.0)
        first = lax.broadcasted_iota(jnp.int32, (tok_rows, tok_rows), 0)
        second = lax.broadcasted_iota(jnp.int32, (tok_rows, tok_rows), 1)
        earlier = jnp.where(first < second, 1.0, 0.0).astype(BF)
        order = jnp.dot(routed.astype(BF), earlier, preferred_element_type=F32)
        order = jnp.where(routed > 0.0, order, -1.0)
        places = lax.broadcasted_iota(jnp.int32, (capacity, tok_rows), 0).astype(F32)
        for g in range(groups):
            hits = order[g : g + 1, :] == places
            here = slice(g * capacity, (g + 1) * capacity)
            pick_ref[here] = jnp.where(hits, 1.0, 0.0).astype(BF)
            weight_ref[here] = jnp.sum(
                jnp.where(hits, weight[g : g + 1, :], 0.0), axis=1, keepdims=True
            )
        for s in range(count):
            source = shard_at(s, turn, count, width)
            here = slice(s * width, (s + 1) * width)
            x = jnp.dot(pick_ref[...], x_ref[:, source], preferred_element_type=F32).astype(BF)
            sent_ref[:, :, here] = x.reshape(groups, capacity, width)
            rows = jnp.dot(pick_ref[...], grad_ref[:, source], preferred_element_type=F32)
            rows_ref[:, here] = rows.astype(BF)
            dy_ref[:, here] = (weight_ref[...] * rows).astype(BF)
        sent_ref[:, :, model:] = dy_ref[:, :part].reshape(groups, capacity, part)
        for j, block in enumerate(blocks):
            block[...] = dy_ref[slots_of(j, me, capacity), part:]

    out_shape = [
        shape(groups, capacity, model + part),
        *[shape(capacity, model - part)] * groups,
        shape(slots, model),
        shape(slots, tok_rows),
        shape(slots, 1, kind=F32),
    ]
    sent, *blocks, rows, pick, weight = call(
        kernel,
        "dispatch",
        in_specs=[SMEM] + [VMEM] * 4,
        out_specs=[VMEM] * len(out_shape),
        out_shape=out_shape,
        scratch_shapes=[pltpu.VMEM((slots, model), BF)],
    )(where, ids_t, gates_t, tokens, out_grad)
    return sent, blocks, rows, pick, weight


def expert(where, got, got_blocks, w_ins, w_outs):
    groups, capacity, _ = got.shape
    count = len(w_ins)
    width = w_ins[0].shape[0]
    model = width * count
    part = model // SHARE
    double, hidden = w_ins[0].shape[1], w_outs[0].shape[1]
    slots = groups * capacity
    many = max(1, 256 // capacity)
    rows = many * capacity

    def kernel(where_ref, got_ref, *refs):
        got_blocks, refs = refs[:groups], refs[groups:]
        ins, outs, refs = refs[:count], refs[count : 2 * count], refs[2 * count :]
        back_ref, blocks, refs = refs[0], refs[1 : 1 + groups], refs[1 + groups :]
        inner_ref, act_grad_ref, dy_ref, dx_ref, act_ref = refs
        me = where_ref[0]
        dy_ref[:, :part] = got_ref[:, :, model:].reshape(slots, part)
        for j, block in enumerate(got_blocks):
            dy_ref[slots_of(j, me, capacity), part:] = block[...]
        for first in range(0, groups, many):
            theirs = slice(first, first + many)
            band = slice(first * capacity, first * capacity + rows)
            total = None
            for s in range(count):
                x = got_ref[theirs, :, s * width : (s + 1) * width].reshape(rows, width)
                one = jnp.dot(x, ins[s][...], preferred_element_type=F32)
                total = one if total is None else total + one
            act_ref[...] = total
            act_gate = act_ref[:, :hidden]
            act_up = act_ref[:, hidden:]
            sig = jax.nn.sigmoid(act_gate)
            swished = act_gate * sig
            inner_ref[band] = (swished * act_up).astype(BF)
            total = None
            for s in range(count):
                dy = dy_ref[band, s * width : (s + 1) * width]
                one = jnp.dot(dy, outs[s][...], preferred_element_type=F32)
                total = one if total is None else total + one
            act_grad_ref[band, :hidden] = (
                total * act_up * sig * (1.0 + act_gate * (1.0 - sig))
            ).astype(BF)
            act_grad_ref[band, hidden:] = (total * swished).astype(BF)
            for s in range(count):
                here = slice(s * width, (s + 1) * width)
                y = lax.dot_general(
                    inner_ref[band], outs[s][...], COLS_IN, preferred_element_type=F32
                )
                back_ref[theirs, :, here] = y.astype(BF).reshape(many, capacity, width)
                dx_ref[band, here] = lax.dot_general(
                    act_grad_ref[band], ins[s][...], COLS_IN, preferred_element_type=F32
                ).astype(BF)
        back_ref[:, :, model:] = dx_ref[:, :part].reshape(groups, capacity, part)
        for j, block in enumerate(blocks):
            block[...] = dx_ref[slots_of(j, me, capacity), part:]

    operands = (where, got, *got_blocks, *w_ins, *w_outs)
    out_shape = [
        shape(groups, capacity, model + part),
        *[shape(capacity, model - part)] * groups,
        shape(slots, hidden),
        shape(slots, double),
        shape(slots, model),
    ]
    back, *rest = call(
        kernel,
        "expert",
        in_specs=[SMEM] + [VMEM] * (len(operands) - 1),
        out_specs=[VMEM] * len(out_shape),
        out_shape=out_shape,
        scratch_shapes=[pltpu.VMEM((slots, model), BF), pltpu.VMEM((rows, double), F32)],
    )(*operands)
    return back, rest[:groups], *rest[groups:]


def weight_grads(shard, got, dys, inner, act_grad):
    groups, capacity, _ = got.shape
    slots, model = dys.shape
    size = model // lax.axis_size("edata")
    double, hidden = act_grad.shape[1], inner.shape[1]
    tile = min(256, size)
    steps = size // tile

    def kernel(x_ref, dy_ref, inner_ref, act_grad_ref, out_ref):
        x = x_ref[...].reshape(slots, tile)
        out_ref[:, :double] = lax.dot_general(
            x, act_grad_ref[...], ROWS_IN, preferred_element_type=F32
        ).astype(BF)
        out_ref[:, double:] = lax.dot_general(
            dy_ref[...], inner_ref[...], ROWS_IN, preferred_element_type=F32
        ).astype(BF)

    return call(
        kernel,
        "weight_grads",
        grid=(steps,),
        in_specs=[
            pl.BlockSpec((groups, capacity, tile), lambda i: (0, 0, shard * steps + i)),
            pl.BlockSpec((slots, tile), lambda i: (0, shard * steps + i)),
            pl.BlockSpec((slots, hidden), lambda i: (0, 0)),
            pl.BlockSpec((slots, double), lambda i: (0, 0)),
        ],
        out_specs=pl.BlockSpec((tile, double + hidden), lambda i: (i, 0)),
        out_shape=shape(size, double + hidden),
    )(got, dys, inner, act_grad)


def combine(where, picks, ids_t, grad_rows, back, back_blocks):
    groups, capacity, _ = back.shape
    slots, tok_rows = picks[0].shape
    model = grad_rows.shape[1]
    count = lax.axis_size("edata")
    width = model // count
    part = model // SHARE

    def kernel(where_ref, pick_ref, pick_t_ref, high_ref, middle_ref, ids_ref, *refs):
        rows_ref, back_ref, refs = refs[0], refs[1], refs[2:]
        blocks, (mixed_ref, token_grad_ref, gate_grad_ref, dx_ref) = refs[:groups], refs[groups:]
        me, turn = where_ref[0], where_ref[1]
        dx_ref[:, :part] = back_ref[:, :, model:].reshape(slots, part)
        for j, block in enumerate(blocks):
            dx_ref[slots_of(j, me, capacity), part:] = block[...]
        dots = jnp.zeros((slots, 1), F32)
        for s in range(count):
            here = slice(s * width, (s + 1) * width)
            target = shard_at(s, turn, count, width)
            y = back_ref[:, :, here].reshape(slots, width)
            mixed_ref[:, target] = (
                jnp.dot(high_ref[...], y, preferred_element_type=F32)
                + jnp.dot(middle_ref[...], y, preferred_element_type=F32)
            ).astype(BF)
            token_grad_ref[:, target] = jnp.dot(
                pick_t_ref[...], dx_ref[:, here], preferred_element_type=F32
            ).astype(BF)
            dots += jnp.sum(
                y.astype(F32) * rows_ref[:, here].astype(F32), axis=1, keepdims=True
            )
        by_token = pick_ref[...].astype(F32) * dots
        by_token = jnp.sum(by_token.reshape(groups, capacity, tok_rows), axis=1)
        ids = ids_ref[...]
        total = jnp.zeros(ids.shape, F32)
        for g in range(groups):
            total += jnp.where(ids == g, by_token[g : g + 1], 0.0)
        gate_grad_ref[...] = total

    operands = (where, *picks, ids_t, grad_rows, back, *back_blocks)
    return call(
        kernel,
        "combine",
        in_specs=[SMEM] + [VMEM] * (len(operands) - 1),
        out_specs=[VMEM] * 3,
        out_shape=[
            shape(tok_rows, model),
            shape(tok_rows, model),
            shape(*ids_t.shape, kind=F32),
        ],
        scratch_shapes=[pltpu.VMEM((slots, model), BF)],
    )(*operands)


def shards(tokens, out_grad, expert_ids, gates, w_gate_up, w_down):
    groups = lax.axis_size("node") * lax.axis_size("local")
    tok_rows = tokens.shape[0]
    capacity = tok_rows * expert_ids.shape[1] // (EXP_DEV * groups)
    where = jnp.stack([lax.axis_index(("node", "local")), lax.axis_index("edata")])
    where = where.astype(jnp.int32)
    w_ins = gathered(w_gate_up[0])
    w_outs = gathered(w_down[0])
    ids_t = expert_ids.T
    sent, blocks, grad_rows, pick, slot_weight = dispatch(
        where, ids_t, gates.T, tokens, out_grad, groups, capacity
    )
    for j in range(4, groups):
        blocks[j] = after(blocks[j], *w_ins[1:], *w_outs[1:])
    got, got_blocks = exchange(sent, blocks)
    sent, blocks, inner, act_grad, dys = expert(where, got, got_blocks, w_ins, w_outs)
    back, back_blocks = exchange(sent, blocks)

    inner = after(inner, back_blocks[1])
    parts = []
    for shard in [*range(1, len(w_ins)), 0]:
        parts.append(weight_grads(shard, got, dys, inner, act_grad))
    parts = [parts[-1]] + [from_owner(p, step) for step, p in enumerate(parts[:-1], 1)]
    double = w_gate_up.shape[2]
    sums = [
        sum(p[:, columns].astype(F32) for p in parts)
        for columns in (slice(0, double), slice(double, None))
    ]
    spread = pick.astype(F32) * after(slot_weight, inner)
    high = lax.reduce_precision(spread, 8, 7)
    middle = (spread - high).astype(BF)
    picks = (pick, pick.T, high.astype(BF).T, middle.T)
    *back_blocks, sums[0], sums[1] = lax.optimization_barrier((*back_blocks, *sums))
    mixed, token_grad, gate_grad = combine(where, picks, ids_t, grad_rows, back, back_blocks)
    return (mixed, token_grad, gate_grad.T, sums[0][None], sums[1][None])


def solution(mesh):
    rows = P(("node", "local", "edata"), None)
    weights = P(("node", "local"), "edata", None)
    return jax.shard_map(
        shards,
        mesh=mesh,
        in_specs=(rows, rows, rows, rows, weights, weights),
        out_specs=(rows, rows, rows, weights, weights),
        check_vma=False,
    )
```

time: 293 us -> 263 us (0.90)
  starting transfers between devices: 17 us -> 75.7 us
  blocking collectives: 52.8 us -> 0 us
  matrix products: 46.4 us -> 0 us
  Pallas kernels: 0 us -> 43.2 us
  waiting for transfers between devices: 144 us -> 126 us
  between operations: 13.9 us -> 1.13 us
    all_to_all x3 -> x2, waiting for transfers between devices: 143 us -> 0.01 us  [exchange(): lax.all_to_all(everything, axes, split_axis=0, concat_axis=0, tiled=True)]
    ppermute x0 -> x33, waiting for transfers between devices: none -> 126 us  [the longest x30 123 us: exchange(): lax.ppermute(blocks[j], axes, [(i, i ^ j) for i in range(count)])]
    ppermute x0 -> x33, starting transfers between devices: none -> 59.4 us  [the longest x30 58.8 us: exchange(): lax.ppermute(blocks[j], axes, [(i, i ^ j) for i in range(count)])]
    all_to_all x1 -> x0, blocking collectives: 52.8 us -> none  [exchange(): lax.all_to_all(shaped, ('node', 'local'), split_axis=0, concat_axis=0, ti...]
    dot_general x13 -> x0, matrix products: 46.4 us -> none  [the longest x1 7.81 us: shards(): lax.dot_general(act_grad, w_in, (((1,), (1,)), ((), ())), preferred_eleme...]
    pallas_call x0 -> x5, Pallas kernels: none -> 43.2 us  [the longest x1 17.7 us: expert(): call(kernel, 'expert', in_specs=[SMEM] + [VMEM] * (len(operands) - 1), ou...]
    add x0 -> x2, other arithmetic: none -> 10.4 us  [shards(): sum((p[:, columns].astype(F32) for p in parts))]
    broadcast_in_dim x2 -> x0, other arithmetic: 8.86 us -> none  [the longest x1 5.55 us: shards(): grad_in[None]]
  transfers between devices with their start and end apart: 7 -> 35, of which waited for: 3 -> 10; matrix products, arithmetic and copies ran while one was open for 14% -> 4% of each run, Pallas kernels for 0% -> 3%
where the time goes in v9:
time: 263 us
  waiting for transfers between devices  126 us (48%)
  starting transfers between devices  75.7 us (29%)
  Pallas kernels  43.2 us (16%)
  other arithmetic  12 us (5%)
  local copies, waits for them, and re-layouts  4.42 us (2%)
    ppermute x30, waiting for transfers between devices, exchange(): lax.ppermute(blocks[j], axes, [(i, i ^ j) for i in range(count)])  123 us
    ppermute x30, starting transfers between devices, exchange(): lax.ppermute(blocks[j], axes, [(i, i ^ j) for i in range(count)])  58.8 us
    pallas_call x1, Pallas kernels, expert(): call(kernel, 'expert', in_specs=[SMEM] + [VMEM] * (len(operands) - 1), ou...  17.7 us
    all_to_all x2, starting transfers between devices, exchange(): lax.all_to_all(everything, axes, split_axis=0, concat_axis=0, tiled=True)  16.2 us
    pallas_call x2, Pallas kernels, weight_grads(): call(kernel, 'weight_grads', grid=(steps,), in_specs=[pl.BlockSpec((group...  13.8 us
    add x2, other arithmetic, shards(): sum((p[:, columns].astype(F32) for p in parts))  10.4 us
    pallas_call x1, Pallas kernels, combine(): call(kernel, 'combine', in_specs=[SMEM] + [VMEM] * (len(operands) - 1), o...  6.15 us
    pallas_call x1, Pallas kernels, dispatch(): call(kernel, 'dispatch', in_specs=[SMEM] + [VMEM] * 4, out_specs=[VMEM] *...  5.57 us
  transfers between devices with their start and end apart: 35, of which 10 were waited for; matrix products, arithmetic and copies ran while one was open for 4% of the time, Pallas kernels for 3%

profile of v9, /device:TPU:0, one launch (start us, length us, event | category | flops | bytes accessed | tf_op | source)
XLA Modules:
  0.0 262.6 jit_solution(11435651514489848323)
XLA Ops:
  1.2 5.6 %dispatch.1 = (bf16[16,32,2560]{2,1,0:T(8,128)(2,1)}, bf16[32,1536]{1,0:T(8,128)(2,1)}, bf16[32,1536]{1,0:T(8,128)(2,1)}, bf16[32,1536]{1,0:T(8,128)(2,1)}, bf16...) custom-call(s32[2]{0:T(128)} %pad_add_fusion.where_ref, ...), custom_call_target="tpu_custom_call" | custom-call | flops 1 | bytes 1 | tf_op jit(solution)/shard_map/dispatch/pallas_call | solution.py:119
  6.9 8.5 %all-to-all-start = ((bf16[16,32,2560]{2,1,0:T(8,128)(2,1)}), bf16[16,32,2560]{2,1,0:T(8,128)(2,1)S(1)}, u32[]{:S(2)}, u32[]{:S(2)}) async-start(bf16[16,32,2560]{2,1,0:T(8,128)(2,1)} %get-tuple-element.82), calls=%async_computation | async-start | bytes 5242880 | tf_op jit(solution)/shard_map/all_to_all | solution.py:58
  17.8 2.4 collective-permute-start.1
  20.3 3.2 %collective-permute-done.4.refs_19_ = bf16[1024,768]{1,0:T(8,128)(2,1)S(1)} collective-permute-done((bf16[1024,768]{1,0:T(8,128)(2,1)}, bf16[1024,768]{1,0:T(8,128)(2,1)S(1)}, u32[]{:S(2)}, u32[]{:S(2)}) %collective-permute-start.4) | collective-permute-done | bytes 1572896 | tf_op jit(solution)/shard_map/ppermute | solution.py:43
  23.5 5.5 %collective-permute-start.16 = (bf16[32,1536]{1,0:T(8,128)(2,1)S(1)}, bf16[32,1536]{1,0:T(8,128)(2,1)S(1)}, u32[]{:S(2)}, u32[]{:S(2)}) collective-permute-start(bf16[32,1536]{1,0:T(8,128)(2,1)S(1)} %copy-done.45), channel_id=1, source_target_pairs={{0,30},{2,28},{4,26},{6,24},{8,22},{10,20},{12,18},{14,16},{16,14}... | collective-permute-start | bytes 294920 | tf_op jit(solution)/shard_map/ppermute | solution.py:57
  29.1 32.8 %collective-permute-done.refs_1_ = bf16[32,1536]{1,0:T(8,128)(2,1)S(1)} collective-permute-done((bf16[32,1536]{1,0:T(8,128)(2,1)S(1)}, bf16[32,1536]{1,0:T(8,128)(2,1)S(1)}, u32[]{:S(2)}, u32[]{:S(2)}) %collective-permute-start) | collective-permute-done | bytes 98336 | tf_op jit(solution)/shard_map/ppermute | solution.py:57
  61.9 3.9 %collective-permute-start.14 = (bf16[32,1536]{1,0:T(8,128)(2,1)}, bf16[32,1536]{1,0:T(8,128)(2,1)S(1)}, u32[]{:S(2)}, u32[]{:S(2)}) collective-permute-start(bf16[32,1536]{1,0:T(8,128)(2,1)} %get-tuple-element.106), channel_id=1, source_target_pairs={{0,26},{2,24},{4,30},{6,28},{8,18},{10,16},{12,22},{14,20},{16,10}... | collective-permute-start | bytes 294920 | tf_op jit(solution)/shard_map/ppermute | solution.py:57
  65.8 21.5 %collective-permute-done.1.refs_2_ = bf16[32,1536]{1,0:T(8,128)(2,1)S(1)} collective-permute-done((bf16[32,1536]{1,0:T(8,128)(2,1)S(1)}, bf16[32,1536]{1,0:T(8,128)(2,1)S(1)}, u32[]{:S(2)}, u32[]{:S(2)}) %collective-permute-start.1) | collective-permute-done | bytes 98336 | tf_op jit(solution)/shard_map/ppermute | solution.py:57
  89.0 2.1 collective-permute-start.12
  91.0 2.7 %collective-permute-start.11 = (bf16[32,1536]{1,0:T(8,128)(2,1)}, bf16[32,1536]{1,0:T(8,128)(2,1)S(1)}, u32[]{:S(2)}, u32[]{:S(2)}) collective-permute-start(bf16[32,1536]{1,0:T(8,128)(2,1)} %get-tuple-element.100), channel_id=1, source_target_pairs={{0,20},{2,22},{4,16},{6,18},{8,28},{10,30},{12,24},{14,26},{16,4},... | collective-permute-start | bytes 294920 | tf_op jit(solution)/shard_map/ppermute | solution.py:57
  93.8 1.9 collective-permute-done.15.refs_14_
  96.4 4.8 %collective-permute-start.8 = (bf16[32,1536]{1,0:T(8,128)(2,1)}, bf16[32,1536]{1,0:T(8,128)(2,1)S(1)}, u32[]{:S(2)}, u32[]{:S(2)}) collective-permute-start(bf16[32,1536]{1,0:T(8,128)(2,1)} %get-tuple-element.94), channel_id=1, source_target_pairs={{0,14},{2,12},{4,10},{6,8},{8,6},{10,4},{12,2},{14,0},{16,30},{18,... | collective-permute-start | bytes 294920 | tf_op jit(solution)/shard_map/ppermute | solution.py:57
  101.2 1.9 collective-permute-start.7
  103.1 2.5 collective-permute-done.11.refs_10_
  106.3 4.8 %collective-permute-done.7.refs_6_ = bf16[32,1536]{1,0:T(8,128)(2,1)S(1)} collective-permute-done((bf16[32,1536]{1,0:T(8,128)(2,1)}, bf16[32,1536]{1,0:T(8,128)(2,1)S(1)}, u32[]{:S(2)}, u32[]{:S(2)}) %collective-permute-start.7) | collective-permute-done | bytes 98336 | tf_op jit(solution)/shard_map/ppermute | solution.py:57
  114.3 17.7 %expert.1 = (bf16[16,32,2560]{2,1,0:T(8,128)(2,1)}, bf16[32,1536]{1,0:T(8,128)(2,1)}, bf16[32,1536]{1,0:T(8,128)(2,1)}, bf16[32,1536]{1,0:T(8,128)(2,1)}, bf16[3...) custom-call(s32[2]{0:T(128)} %pad_add_fusion.where_ref, ...), custom_call_target="tpu_custom_call" | custom-call | flops 1 | bytes 1 | tf_op jit(solution)/shard_map/expert/pallas_call | solution.py:194
  133.8 3.1 %collective-permute-done.17.refs_3_ = bf16[32,1536]{1,0:T(8,128)(2,1)S(1)} collective-permute-done((bf16[32,1536]{1,0:T(8,128)(2,1)}, bf16[32,1536]{1,0:T(8,128)(2,1)S(1)}, u32[]{:S(2)}, u32[]{:S(2)}) %collective-permute-start.17) | collective-permute-done | bytes 98336 | tf_op jit(solution)/shard_map/ppermute | solution.py:57
  136.9 6.9 %weight_grads.3 = bf16[1024,2304]{1,0:T(8,128)(2,1)} custom-call(bf16[16,32,2560]{2,1,0:T(8,128)(2,1)} %copy-done, bf16[512,2048]{1,0:T(8,128)(2,1)} %get-tuple-element.132.dy_ref, bf16[512,768]{1,0:T(8,128)(2,1)} %get-tuple-element.113.inner_ref, bf16[512,1536]{1,0:T(8,128)(2,1)} %get-tuple-element.133.act_grad_ref), custom_call_target="tpu_custom_call" | custom-call | flops 1 | bytes 1 | tf_op jit(solution)/shard_map/weight_grads/pallas_call | solution.py:222
  143.9 7.8 %all-to-all-start.1 = ((bf16[16,32,2560]{2,1,0:T(8,128)(2,1)}), bf16[16,32,2560]{2,1,0:T(8,128)(2,1)S(1)}, u32[]{:S(2)}, u32[]{:S(2)}) async-start(bf16[16,32,2560]{2,1,0:T(8,128)(2,1)} %get-tuple-element.116), calls=%async_computation.1 | async-start | bytes 5242880 | tf_op jit(solution)/shard_map/all_to_all | solution.py:58
  151.8 2.9 %collective-permute-start.18 = (bf16[32,1536]{1,0:T(8,128)(2,1)}, bf16[32,1536]{1,0:T(8,128)(2,1)S(1)}, u32[]{:S(2)}, u32[]{:S(2)}) collective-permute-start(bf16[32,1536]{1,0:T(8,128)(2,1)} %get-tuple-element.118), channel_id=1, source_target_pairs={{0,4},{2,6},{4,0},{6,2},{8,12},{10,14},{12,8},{14,10},{16,20},{18,... | collective-permute-start | bytes 294920 | tf_op jit(solution)/shard_map/ppermute | solution.py:57
  158.7 6.9 %weight_grads.2 = bf16[1024,2304]{1,0:T(8,128)(2,1)} custom-call(bf16[16,32,2560]{2,1,0:T(8,128)(2,1)} %copy-done, bf16[512,2048]{1,0:T(8,128)(2,1)} %get-tuple-element.132.dy_ref, bf16[512,768]{1,0:T(8,128)(2,1)} %get-tuple-element.113.inner_ref, bf16[512,1536]{1,0:T(8,128)(2,1)} %get-tuple-element.133.act_grad_ref), custom_call_target="tpu_custom_call" | custom-call | flops 1 | bytes 1 | tf_op jit(solution)/shard_map/weight_grads/pallas_call | solution.py:222
  165.6 53.8 %collective-permute-done.18.refs_4_ = bf16[32,1536]{1,0:T(8,128)(2,1)S(1)} collective-permute-done((bf16[32,1536]{1,0:T(8,128)(2,1)}, bf16[32,1536]{1,0:T(8,128)(2,1)S(1)}, u32[]{:S(2)}, u32[]{:S(2)}) %collective-permute-start.18) | collective-permute-done | bytes 98336 | tf_op jit(solution)/shard_map/ppermute | solution.py:57
  219.5 4.1 %collective-permute-start.22 = (bf16[32,1536]{1,0:T(8,128)(2,1)S(1)}, bf16[32,1536]{1,0:T(8,128)(2,1)S(1)}, u32[]{:S(2)}, u32[]{:S(2)}) collective-permute-start(bf16[32,1536]{1,0:T(8,128)(2,1)S(1)} %copy-done.44), channel_id=1, source_target_pairs={{0,12},{2,14},{4,8},{6,10},{8,4},{10,6},{12,0},{14,2},{16,28},{18,... | collective-permute-start | bytes 294920 | tf_op jit(solution)/shard_map/ppermute | solution.py:57
  225.4 3.6 %collective-permute-start.25 = (bf16[32,1536]{1,0:T(8,128)(2,1)S(1)}, bf16[32,1536]{1,0:T(8,128)(2,1)S(1)}, u32[]{:S(2)}, u32[]{:S(2)}) collective-permute-start(bf16[32,1536]{1,0:T(8,128)(2,1)S(1)} %copy-done.41), channel_id=1, source_target_pairs={{0,18},{2,16},{4,22},{6,20},{8,26},{10,24},{12,30},{14,28},{16,2},... | collective-permute-start | bytes 294920 | tf_op jit(solution)/shard_map/ppermute | solution.py:57
  229.0 2.2 collective-permute-start.26
  231.2 6.5 %convert_add_fusion = f32[1024,1536]{1,0:T(8,128)} fusion(bf16[1024,2304]{1,0:T(8,128)(2,1)} %collective-permute-done.32, bf16[1024,2304]{1,0:T(8,128)(2,1)} %weight_grads.2), kind=kLoop, calls=%fused_computation | loop fusion | flops 4718592 | bytes 12582912 | tf_op jit(solution)/shard_map/add | solution.py:315
  237.8 2.3 collective-permute-start.27
  240.7 2.4 collective-permute-start.29
  243.1 3.0 %collective-permute-start.30 = (bf16[32,1536]{1,0:T(8,128)(2,1)S(1)}, bf16[32,1536]{1,0:T(8,128)(2,1)S(1)}, u32[]{:S(2)}, u32[]{:S(2)}) collective-permute-start(bf16[32,1536]{1,0:T(8,128)(2,1)S(1)} %copy-done.36), channel_id=1, source_target_pairs={{0,28},{2,30},{4,24},{6,26},{8,20},{10,22},{12,16},{14,18},{16,12}... | collective-permute-start | bytes 294920 | tf_op jit(solution)/shard_map/ppermute | solution.py:57
  246.1 2.9 %collective-permute-start.31 = (bf16[32,1536]{1,0:T(8,128)(2,1)S(1)}, bf16[32,1536]{1,0:T(8,128)(2,1)S(1)}, u32[]{:S(2)}, u32[]{:S(2)}) collective-permute-start(bf16[32,1536]{1,0:T(8,128)(2,1)S(1)} %copy-done.35), channel_id=1, source_target_pairs={{0,30},{2,28},{4,26},{6,24},{8,22},{10,20},{12,18},{14,16},{16,14}... | collective-permute-start | bytes 294920 | tf_op jit(solution)/shard_map/ppermute | solution.py:57
  248.9 3.9 %convert_add_fusion.1 = f32[1024,768]{1,0:T(8,128)} fusion(bf16[1024,2304]{1,0:T(8,128)(2,1)} %collective-permute-done.32, bf16[1024,2304]{1,0:T(8,128)(2,1)} %weight_grads.2), kind=kLoop, calls=%fused_computation.1 | loop fusion | flops 2359296 | bytes 6291456 | tf_op jit(solution)/shard_map/add | solution.py:315
  256.4 6.2 %combine.1 = (bf16[256,2048]{1,0:T(8,128)(2,1)}, bf16[256,2048]{1,0:T(8,128)(2,1)}, f32[8,256]{1,0:T(8,128)}) custom-call(s32[2]{0:T(128)} %pad_add_fusion.where_ref, bf16[512,256]{1,0:T(8,128)(2,1)} %get-tuple-element.80.pick_ref, bf16[256,512]{1,0:T(8,128)(2,1)} %bitcast.18, bf16[256,512]{1,0:T(8,128)(2,1)} %get-tuple-element.156.high_ref, ...), custom_call_target="tpu_custom_call" | custom-call | flops 1 | bytes 1 | tf_op jit(solution)/shard_map/combine/pallas_call | solution.py:276
  (147 shorter events, 21.3 us)
Async XLA Ops:
  6.9 106.0 %all-to-all-start = ((bf16[16,32,2560]{2,1,0:T(8,128)(2,1)}), bf16[16,32,2560]{2,1,0:T(8,128)(2,1)S(1)}, u32[]{:S(2)}, u32[]{:S(2)}) async-start(bf16[16,32,2560]{2,1,0:T(8,128)(2,1)} %get-tuple-element.82), calls=%async_computation | async-start | bytes 5242880 | tf_op jit(solution)/shard_map/all_to_all | solution.py:58
  15.3 8.2 %collective-permute-start.3 = (bf16[1024,1536]{1,0:T(8,128)(2,1)}, bf16[1024,1536]{1,0:T(8,128)(2,1)S(1)}, u32[]{:S(2)}, u32[]{:S(2)}) collective-permute-start(bf16[1024,1536]{1,0:T(8,128)(2,1)} %bitcast.16), channel_id=1, source_target_pairs={{1,0},{0,1},{3,2},{2,3},{5,4},{4,5},{7,6},{6,7},{9,8},{8,9},{11,10... | collective-permute-start | bytes 9437192 | tf_op jit(solution)/shard_map/ppermute | solution.py:43
  15.4 8.1 %collective-permute-start.4 = (bf16[1024,768]{1,0:T(8,128)(2,1)}, bf16[1024,768]{1,0:T(8,128)(2,1)S(1)}, u32[]{:S(2)}, u32[]{:S(2)}) collective-permute-start(bf16[1024,768]{1,0:T(8,128)(2,1)} %bitcast.19), channel_id=1, source_target_pairs={{1,0},{0,1},{3,2},{2,3},{5,4},{4,5},{7,6},{6,7},{9,8},{8,9},{11,10... | collective-permute-start | bytes 4718600 | tf_op jit(solution)/shard_map/ppermute | solution.py:43
  15.9 46.0 %collective-permute-start = (bf16[32,1536]{1,0:T(8,128)(2,1)S(1)}, bf16[32,1536]{1,0:T(8,128)(2,1)S(1)}, u32[]{:S(2)}, u32[]{:S(2)}) collective-permute-start(bf16[32,1536]{1,0:T(8,128)(2,1)S(1)} %copy-done.48), channel_id=1, source_target_pairs={{0,2},{2,0},{4,6},{6,4},{8,10},{10,8},{12,14},{14,12},{16,18},{18,... | collective-permute-start | bytes 294920 | tf_op jit(solution)/shard_map/ppermute | solution.py:57
  17.8 69.5 %collective-permute-start.1 = (bf16[32,1536]{1,0:T(8,128)(2,1)S(1)}, bf16[32,1536]{1,0:T(8,128)(2,1)S(1)}, u32[]{:S(2)}, u32[]{:S(2)}) collective-permute-start(bf16[32,1536]{1,0:T(8,128)(2,1)S(1)} %copy-done.47), channel_id=1, source_target_pairs={{0,4},{2,6},{4,0},{6,2},{8,12},{10,14},{12,8},{14,10},{16,20},{18,... | collective-permute-start | bytes 294920 | tf_op jit(solution)/shard_map/ppermute | solution.py:57
  20.1 68.8 %collective-permute-start.2 = (bf16[32,1536]{1,0:T(8,128)(2,1)S(1)}, bf16[32,1536]{1,0:T(8,128)(2,1)S(1)}, u32[]{:S(2)}, u32[]{:S(2)}) collective-permute-start(bf16[32,1536]{1,0:T(8,128)(2,1)S(1)} %copy-done.46), channel_id=1, source_target_pairs={{0,6},{2,4},{4,2},{6,0},{8,14},{10,12},{12,10},{14,8},{16,22},{18,... | collective-permute-start | bytes 294920 | tf_op jit(solution)/shard_map/ppermute | solution.py:57
  23.5 67.5 %collective-permute-start.16 = (bf16[32,1536]{1,0:T(8,128)(2,1)S(1)}, bf16[32,1536]{1,0:T(8,128)(2,1)S(1)}, u32[]{:S(2)}, u32[]{:S(2)}) collective-permute-start(bf16[32,1536]{1,0:T(8,128)(2,1)S(1)} %copy-done.45), channel_id=1, source_target_pairs={{0,30},{2,28},{4,26},{6,24},{8,22},{10,20},{12,18},{14,16},{16,14}... | collective-permute-start | bytes 294920 | tf_op jit(solution)/shard_map/ppermute | solution.py:57
  29.1 66.6 %collective-permute-start.15 = (bf16[32,1536]{1,0:T(8,128)(2,1)}, bf16[32,1536]{1,0:T(8,128)(2,1)S(1)}, u32[]{:S(2)}, u32[]{:S(2)}) collective-permute-start(bf16[32,1536]{1,0:T(8,128)(2,1)} %get-tuple-element.108), channel_id=1, source_target_pairs={{0,28},{2,30},{4,24},{6,26},{8,20},{10,22},{12,16},{14,18},{16,12}... | collective-permute-start | bytes 294920 | tf_op jit(solution)/shard_map/ppermute | solution.py:57
  61.9 34.5 %collective-permute-start.14 = (bf16[32,1536]{1,0:T(8,128)(2,1)}, bf16[32,1536]{1,0:T(8,128)(2,1)S(1)}, u32[]{:S(2)}, u32[]{:S(2)}) collective-permute-start(bf16[32,1536]{1,0:T(8,128)(2,1)} %get-tuple-element.106), channel_id=1, source_target_pairs={{0,26},{2,24},{4,30},{6,28},{8,18},{10,16},{12,22},{14,20},{16,10}... | collective-permute-start | bytes 294920 | tf_op jit(solution)/shard_map/ppermute | solution.py:57
  87.3 9.2 %collective-permute-start.13 = (bf16[32,1536]{1,0:T(8,128)(2,1)}, bf16[32,1536]{1,0:T(8,128)(2,1)S(1)}, u32[]{:S(2)}, u32[]{:S(2)}) collective-permute-start(bf16[32,1536]{1,0:T(8,128)(2,1)} %get-tuple-element.104), channel_id=1, source_target_pairs={{0,24},{2,26},{4,28},{6,30},{8,16},{10,18},{12,20},{14,22},{16,8},... | collective-permute-start | bytes 294920 | tf_op jit(solution)/shard_map/ppermute | solution.py:57
  89.0 12.2 %collective-permute-start.12 = (bf16[32,1536]{1,0:T(8,128)(2,1)}, bf16[32,1536]{1,0:T(8,128)(2,1)S(1)}, u32[]{:S(2)}, u32[]{:S(2)}) collective-permute-start(bf16[32,1536]{1,0:T(8,128)(2,1)} %get-tuple-element.102), channel_id=1, source_target_pairs={{0,22},{2,20},{4,18},{6,16},{8,30},{10,28},{12,26},{14,24},{16,6},... | collective-permute-start | bytes 294920 | tf_op jit(solution)/shard_map/ppermute | solution.py:57
  91.0 14.6 %collective-permute-start.11 = (bf16[32,1536]{1,0:T(8,128)(2,1)}, bf16[32,1536]{1,0:T(8,128)(2,1)S(1)}, u32[]{:S(2)}, u32[]{:S(2)}) collective-permute-start(bf16[32,1536]{1,0:T(8,128)(2,1)} %get-tuple-element.100), channel_id=1, source_target_pairs={{0,20},{2,22},{4,16},{6,18},{8,28},{10,30},{12,24},{14,26},{16,4},... | collective-permute-start | bytes 294920 | tf_op jit(solution)/shard_map/ppermute | solution.py:57
  95.7 9.9 %collective-permute-start.10 = (bf16[32,1536]{1,0:T(8,128)(2,1)}, bf16[32,1536]{1,0:T(8,128)(2,1)S(1)}, u32[]{:S(2)}, u32[]{:S(2)}) collective-permute-start(bf16[32,1536]{1,0:T(8,128)(2,1)} %get-tuple-element.98), channel_id=1, source_target_pairs={{0,18},{2,16},{4,22},{6,20},{8,26},{10,24},{12,30},{14,28},{16,2},... | collective-permute-start | bytes 294920 | tf_op jit(solution)/shard_map/ppermute | solution.py:57
  96.4 9.9 %collective-permute-start.9 = (bf16[32,1536]{1,0:T(8,128)(2,1)}, bf16[32,1536]{1,0:T(8,128)(2,1)S(1)}, u32[]{:S(2)}, u32[]{:S(2)}) collective-permute-start(bf16[32,1536]{1,0:T(8,128)(2,1)} %get-tuple-element.96), channel_id=1, source_target_pairs={{0,16},{2,18},{4,20},{6,22},{8,24},{10,26},{12,28},{14,30},{16,0},... | collective-permute-start | bytes 294920 | tf_op jit(solution)/shard_map/ppermute | solution.py:57
  96.4 9.9 %collective-permute-start.8 = (bf16[32,1536]{1,0:T(8,128)(2,1)}, bf16[32,1536]{1,0:T(8,128)(2,1)S(1)}, u32[]{:S(2)}, u32[]{:S(2)}) collective-permute-start(bf16[32,1536]{1,0:T(8,128)(2,1)} %get-tuple-element.94), channel_id=1, source_target_pairs={{0,14},{2,12},{4,10},{6,8},{8,6},{10,4},{12,2},{14,0},{16,30},{18,... | collective-permute-start | bytes 294920 | tf_op jit(solution)/shard_map/ppermute | solution.py:57
  101.2 9.9 %collective-permute-start.7 = (bf16[32,1536]{1,0:T(8,128)(2,1)}, bf16[32,1536]{1,0:T(8,128)(2,1)S(1)}, u32[]{:S(2)}, u32[]{:S(2)}) collective-permute-start(bf16[32,1536]{1,0:T(8,128)(2,1)} %get-tuple-element.92), channel_id=1, source_target_pairs={{0,12},{2,14},{4,8},{6,10},{8,4},{10,6},{12,0},{14,2},{16,28},{18,... | collective-permute-start | bytes 294920 | tf_op jit(solution)/shard_map/ppermute | solution.py:57
  143.8 85.2 %collective-permute-start.32 = (bf16[1024,2304]{1,0:T(8,128)(2,1)}, bf16[1024,2304]{1,0:T(8,128)(2,1)}, u32[]{:S(2)}, u32[]{:S(2)}) collective-permute-start(bf16[1024,2304]{1,0:T(8,128)(2,1)} %weight_grads.3), channel_id=1, source_target_pairs={{0,1},{1,0},{2,3},{3,2},{4,5},{5,4},{6,7},{7,6},{8,9},{9,8},{10,11... | collective-permute-start | bytes 14155784 | tf_op jit(solution)/shard_map/ppermute | solution.py:49
  143.9 111.1 %all-to-all-start.1 = ((bf16[16,32,2560]{2,1,0:T(8,128)(2,1)}), bf16[16,32,2560]{2,1,0:T(8,128)(2,1)S(1)}, u32[]{:S(2)}, u32[]{:S(2)}) async-start(bf16[16,32,2560]{2,1,0:T(8,128)(2,1)} %get-tuple-element.116), calls=%async_computation.1 | async-start | bytes 5242880 | tf_op jit(solution)/shard_map/all_to_all | solution.py:58
  151.8 67.6 %collective-permute-start.18 = (bf16[32,1536]{1,0:T(8,128)(2,1)}, bf16[32,1536]{1,0:T(8,128)(2,1)S(1)}, u32[]{:S(2)}, u32[]{:S(2)}) collective-permute-start(bf16[32,1536]{1,0:T(8,128)(2,1)} %get-tuple-element.118), channel_id=1, source_target_pairs={{0,4},{2,6},{4,0},{6,2},{8,12},{10,14},{12,8},{14,10},{16,20},{18,... | collective-permute-start | bytes 294920 | tf_op jit(solution)/shard_map/ppermute | solution.py:57
  154.7 68.9 %collective-permute-start.19 = (bf16[32,1536]{1,0:T(8,128)(2,1)}, bf16[32,1536]{1,0:T(8,128)(2,1)S(1)}, u32[]{:S(2)}, u32[]{:S(2)}) collective-permute-start(bf16[32,1536]{1,0:T(8,128)(2,1)} %get-tuple-element.119), channel_id=1, source_target_pairs={{0,6},{2,4},{4,2},{6,0},{8,14},{10,12},{12,10},{14,8},{16,22},{18,... | collective-permute-start | bytes 294920 | tf_op jit(solution)/shard_map/ppermute | solution.py:57
  156.2 67.5 %collective-permute-start.20 = (bf16[32,1536]{1,0:T(8,128)(2,1)}, bf16[32,1536]{1,0:T(8,128)(2,1)S(1)}, u32[]{:S(2)}, u32[]{:S(2)}) collective-permute-start(bf16[32,1536]{1,0:T(8,128)(2,1)} %get-tuple-element.120), channel_id=1, source_target_pairs={{0,8},{2,10},{4,12},{6,14},{8,0},{10,2},{12,4},{14,6},{16,24},{18,... | collective-permute-start | bytes 294920 | tf_op jit(solution)/shard_map/ppermute | solution.py:57
  157.6 67.7 %collective-permute-start.21 = (bf16[32,1536]{1,0:T(8,128)(2,1)}, bf16[32,1536]{1,0:T(8,128)(2,1)}, u32[]{:S(2)}, u32[]{:S(2)}) collective-permute-start(bf16[32,1536]{1,0:T(8,128)(2,1)} %get-tuple-element.121), channel_id=1, source_target_pairs={{0,10},{2,8},{4,14},{6,12},{8,2},{10,0},{12,6},{14,4},{16,26},{18,... | collective-permute-start | bytes 294920 | tf_op jit(solution)/shard_map/ppermute | solution.py:57
  219.5 18.3 %collective-permute-start.22 = (bf16[32,1536]{1,0:T(8,128)(2,1)S(1)}, bf16[32,1536]{1,0:T(8,128)(2,1)S(1)}, u32[]{:S(2)}, u32[]{:S(2)}) collective-permute-start(bf16[32,1536]{1,0:T(8,128)(2,1)S(1)} %copy-done.44), channel_id=1, source_target_pairs={{0,12},{2,14},{4,8},{6,10},{8,4},{10,6},{12,0},{14,2},{16,28},{18,... | collective-permute-start | bytes 294920 | tf_op jit(solution)/shard_map/ppermute | solution.py:57
  223.6 16.5 %collective-permute-start.23 = (bf16[32,1536]{1,0:T(8,128)(2,1)S(1)}, bf16[32,1536]{1,0:T(8,128)(2,1)S(1)}, u32[]{:S(2)}, u32[]{:S(2)}) collective-permute-start(bf16[32,1536]{1,0:T(8,128)(2,1)S(1)} %copy-done.43), channel_id=1, source_target_pairs={{0,14},{2,12},{4,10},{6,8},{8,6},{10,4},{12,2},{14,0},{16,30},{18,... | collective-permute-start | bytes 294920 | tf_op jit(solution)/shard_map/ppermute | solution.py:57
  223.7 17.0 %collective-permute-start.24 = (bf16[32,1536]{1,0:T(8,128)(2,1)S(1)}, bf16[32,1536]{1,0:T(8,128)(2,1)S(1)}, u32[]{:S(2)}, u32[]{:S(2)}) collective-permute-start(bf16[32,1536]{1,0:T(8,128)(2,1)S(1)} %copy-done.42), channel_id=1, source_target_pairs={{0,16},{2,18},{4,20},{6,22},{8,24},{10,26},{12,28},{14,30},{16,0},... | collective-permute-start | bytes 294920 | tf_op jit(solution)/shard_map/ppermute | solution.py:57
  225.4 17.7 %collective-permute-start.25 = (bf16[32,1536]{1,0:T(8,128)(2,1)S(1)}, bf16[32,1536]{1,0:T(8,128)(2,1)S(1)}, u32[]{:S(2)}, u32[]{:S(2)}) collective-permute-start(bf16[32,1536]{1,0:T(8,128)(2,1)S(1)} %copy-done.41), channel_id=1, source_target_pairs={{0,18},{2,16},{4,22},{6,20},{8,26},{10,24},{12,30},{14,28},{16,2},... | collective-permute-start | bytes 294920 | tf_op jit(solution)/shard_map/ppermute | solution.py:57
  229.0 17.0 %collective-permute-start.26 = (bf16[32,1536]{1,0:T(8,128)(2,1)S(1)}, bf16[32,1536]{1,0:T(8,128)(2,1)S(1)}, u32[]{:S(2)}, u32[]{:S(2)}) collective-permute-start(bf16[32,1536]{1,0:T(8,128)(2,1)S(1)} %copy-done.40), channel_id=1, source_target_pairs={{0,20},{2,22},{4,16},{6,18},{8,28},{10,30},{12,24},{14,26},{16,4},... | collective-permute-start | bytes 294920 | tf_op jit(solution)/shard_map/ppermute | solution.py:57
  237.8 15.1 %collective-permute-start.27 = (bf16[32,1536]{1,0:T(8,128)(2,1)S(1)}, bf16[32,1536]{1,0:T(8,128)(2,1)S(1)}, u32[]{:S(2)}, u32[]{:S(2)}) collective-permute-start(bf16[32,1536]{1,0:T(8,128)(2,1)S(1)} %copy-done.39), channel_id=1, source_target_pairs={{0,22},{2,20},{4,18},{6,16},{8,30},{10,28},{12,26},{14,24},{16,6},... | collective-permute-start | bytes 294920 | tf_op jit(solution)/shard_map/ppermute | solution.py:57
  240.1 12.8 %collective-permute-start.28 = (bf16[32,1536]{1,0:T(8,128)(2,1)S(1)}, bf16[32,1536]{1,0:T(8,128)(2,1)S(1)}, u32[]{:S(2)}, u32[]{:S(2)}) collective-permute-start(bf16[32,1536]{1,0:T(8,128)(2,1)S(1)} %copy-done.38), channel_id=1, source_target_pairs={{0,24},{2,26},{4,28},{6,30},{8,16},{10,18},{12,20},{14,22},{16,8},... | collective-permute-start | bytes 294920 | tf_op jit(solution)/shard_map/ppermute | solution.py:57
  240.7 12.2 %collective-permute-start.29 = (bf16[32,1536]{1,0:T(8,128)(2,1)S(1)}, bf16[32,1536]{1,0:T(8,128)(2,1)S(1)}, u32[]{:S(2)}, u32[]{:S(2)}) collective-permute-start(bf16[32,1536]{1,0:T(8,128)(2,1)S(1)} %copy-done.37), channel_id=1, source_target_pairs={{0,26},{2,24},{4,30},{6,28},{8,18},{10,16},{12,22},{14,20},{16,10}... | collective-permute-start | bytes 294920 | tf_op jit(solution)/shard_map/ppermute | solution.py:57
  243.1 9.8 %collective-permute-start.30 = (bf16[32,1536]{1,0:T(8,128)(2,1)S(1)}, bf16[32,1536]{1,0:T(8,128)(2,1)S(1)}, u32[]{:S(2)}, u32[]{:S(2)}) collective-permute-start(bf16[32,1536]{1,0:T(8,128)(2,1)S(1)} %copy-done.36), channel_id=1, source_target_pairs={{0,28},{2,30},{4,24},{6,26},{8,20},{10,22},{12,16},{14,18},{16,12}... | collective-permute-start | bytes 294920 | tf_op jit(solution)/shard_map/ppermute | solution.py:57
  246.1 8.3 %collective-permute-start.31 = (bf16[32,1536]{1,0:T(8,128)(2,1)S(1)}, bf16[32,1536]{1,0:T(8,128)(2,1)S(1)}, u32[]{:S(2)}, u32[]{:S(2)}) collective-permute-start(bf16[32,1536]{1,0:T(8,128)(2,1)S(1)} %copy-done.35), channel_id=1, source_target_pairs={{0,30},{2,28},{4,26},{6,24},{8,22},{10,20},{12,18},{14,16},{16,14}... | collective-permute-start | bytes 294920 | tf_op jit(solution)/shard_map/ppermute | solution.py:57
  (52 other events, 1003.9 us)

commit v10 on v9

v10 whole, which is shorter than its diff:
```python
import jax
import jax.numpy as jnp
from jax import lax
from jax.experimental import pallas as pl
from jax.experimental.pallas import tpu as pltpu
from jax.sharding import PartitionSpec as P

EXP_DEV = 4
BF = jnp.bfloat16
F32 = jnp.float32
ROWS_IN = (((0,), (0,)), ((), ()))
COLS_IN = (((1,), (1,)), ((), ()))
LIMIT = 56 * 1024 * 1024
def work(flops):
    return pl.CostEstimate(flops=flops, bytes_accessed=flops // 400, transcendentals=0)


WINDOW = 4
CHEAP = pl.CostEstimate(flops=1, bytes_accessed=1, transcendentals=0)
VMEM = pl.BlockSpec(memory_space=pltpu.VMEM)
SMEM = pl.BlockSpec(memory_space=pltpu.SMEM)
def call(kernel, name, cost=CHEAP, **more):
    return pl.pallas_call(
        kernel,
        compiler_params=pltpu.CompilerParams(vmem_limit_bytes=LIMIT),
        cost_estimate=cost,
        name=name,
        **more,
    )


def shape(*dims, kind=BF):
    return jax.ShapeDtypeStruct(dims, kind)


def after(value, *others):
    return lax.optimization_barrier((value, *others))[0]


def gathered(shard):
    count = lax.axis_size("edata")
    shards = [shard]
    for step in range(1, count):
        pairs = [((i + step) % count, i) for i in range(count)]
        shards.append(lax.ppermute(shard, "edata", pairs))
    return shards


def from_owner(piece, step):
    count = lax.axis_size("edata")
    return lax.ppermute(piece, "edata", [(i, (i + step) % count) for i in range(count)])


def to_partner(block, j):
    if j == 0:
        return block
    count = lax.axis_size("node") * lax.axis_size("local")
    return lax.ppermute(block, ("node", "local"), [(i, i ^ j) for i in range(count)])


def shard_at(s, turn, count, width):
    return pl.ds(pl.multiple_of((turn + s) % count * width, width), width)


def dispatch(where, ids_t, gates_t, tokens, out_grad, groups, capacity):
    top, tok_rows = ids_t.shape
    model = tokens.shape[1]
    count = lax.axis_size("edata")
    width = model // count
    slots = groups * capacity

    def kernel(where_ref, ids_ref, gates_ref, x_ref, grad_ref, *refs):
        blocks, (rows_ref, pick_ref, weight_ref) = refs[:groups], refs[groups:]
        me, turn = where_ref[0], where_ref[1]
        numbers = me ^ lax.broadcasted_iota(jnp.int32, (groups, tok_rows), 0)
        routed = jnp.zeros((groups, tok_rows), F32)
        weight = jnp.zeros((groups, tok_rows), F32)
        for k in range(top):
            chosen = ids_ref[k : k + 1, :] == numbers
            routed = jnp.where(chosen, 1.0, routed)
            weight += jnp.where(chosen, gates_ref[k : k + 1, :], 0.0)
        first = lax.broadcasted_iota(jnp.int32, (tok_rows, tok_rows), 0)
        second = lax.broadcasted_iota(jnp.int32, (tok_rows, tok_rows), 1)
        earlier = jnp.where(first < second, 1.0, 0.0).astype(BF)
        order = jnp.dot(routed.astype(BF), earlier, preferred_element_type=F32)
        order = jnp.where(routed > 0.0, order, -1.0)
        places = lax.broadcasted_iota(jnp.int32, (capacity, tok_rows), 0).astype(F32)
        for g in range(groups):
            hits = order[g : g + 1, :] == places
            here = slice(g * capacity, (g + 1) * capacity)
            pick_ref[here] = jnp.where(hits, 1.0, 0.0).astype(BF)
            weight_ref[here] = jnp.sum(
                jnp.where(hits, weight[g : g + 1, :], 0.0), axis=1, keepdims=True
            )
        for s in range(count):
            source = shard_at(s, turn, count, width)
            here = slice(s * width, (s + 1) * width)
            x = jnp.dot(pick_ref[...], x_ref[:, source], preferred_element_type=F32).astype(BF)
            rows = jnp.dot(pick_ref[...], grad_ref[:, source], preferred_element_type=F32)
            rows_ref[:, here] = rows.astype(BF)
            dy = (weight_ref[...] * rows).astype(BF)
            for j, block in enumerate(blocks):
                block[0, :, here] = x[j * capacity : (j + 1) * capacity]
                block[1, :, here] = dy[j * capacity : (j + 1) * capacity]

    out_shape = [
        *[shape(2, capacity, model)] * groups,
        shape(slots, model),
        shape(slots, tok_rows),
        shape(slots, 1, kind=F32),
    ]
    *blocks, rows, pick, weight = call(
        kernel,
        "dispatch",
        in_specs=[SMEM] + [VMEM] * 4,
        out_specs=[VMEM] * len(out_shape),
        out_shape=out_shape,
    )(where, ids_t, gates_t, tokens, out_grad)
    return list(blocks), rows, pick, weight


def expert(got, w_ins, w_outs):
    _, capacity, model = got[0].shape
    many = len(got)
    count = len(w_ins)
    width = w_ins[0].shape[0]
    double, hidden = w_ins[0].shape[1], w_outs[0].shape[1]
    rows = many * capacity

    def kernel(*refs):
        got, refs = refs[:many], refs[many:]
        ins, outs, refs = refs[:count], refs[count : 2 * count], refs[2 * count :]
        blocks, (inner_ref, act_grad_ref, x_ref, dy_ref, act_ref) = refs[:many], refs[many:]
        for j, block in enumerate(got):
            x_ref[j * capacity : (j + 1) * capacity] = block[0]
            dy_ref[j * capacity : (j + 1) * capacity] = block[1]

        def product(source, weights):
            total = None
            for s in range(count):
                one = jnp.dot(
                    source[:, s * width : (s + 1) * width],
                    weights[s][...],
                    preferred_element_type=F32,
                )
                total = one if total is None else total + one
            return total

        act_ref[...] = product(x_ref, ins)
        act_gate = act_ref[:, :hidden]
        act_up = act_ref[:, hidden:]
        sig = jax.nn.sigmoid(act_gate)
        swished = act_gate * sig
        inner_ref[...] = (swished * act_up).astype(BF)
        inner_grad = product(dy_ref, outs)
        act_grad_ref[:, :hidden] = (
            inner_grad * act_up * sig * (1.0 + act_gate * (1.0 - sig))
        ).astype(BF)
        act_grad_ref[:, hidden:] = (inner_grad * swished).astype(BF)
        for s in range(count):
            here = slice(s * width, (s + 1) * width)
            y = lax.dot_general(
                inner_ref[...], outs[s][...], COLS_IN, preferred_element_type=F32
            ).astype(BF)
            dx = lax.dot_general(
                act_grad_ref[...], ins[s][...], COLS_IN, preferred_element_type=F32
            ).astype(BF)
            for j, block in enumerate(blocks):
                block[0, :, here] = y[j * capacity : (j + 1) * capacity]
                block[1, :, here] = dx[j * capacity : (j + 1) * capacity]

    operands = (*got, *w_ins, *w_outs)
    out_shape = [
        *[shape(2, capacity, model)] * many,
        shape(rows, hidden),
        shape(rows, double),
        shape(rows, model),
        shape(rows, model),
    ]
    results = call(
        kernel,
        "expert",
        cost=work(12 * rows * model * hidden),
        in_specs=[VMEM] * len(operands),
        out_specs=[VMEM] * len(out_shape),
        out_shape=out_shape,
        scratch_shapes=[pltpu.VMEM((rows, double), F32)],
    )(*operands)
    return list(results[:many]), results[many:]


def weight_grads(shard, bands):
    rows, model = bands[0][3].shape
    hidden, double = bands[0][0].shape[1], bands[0][1].shape[1]
    size = model // lax.axis_size("edata")
    tile = min(256, size)
    steps = size // tile
    count = len(bands)

    def kernel(*refs):
        inners, act_grads = refs[:count], refs[count : 2 * count]
        xs, dys, out_ref = refs[2 * count : 3 * count], refs[3 * count : 4 * count], refs[-1]
        for rights, lefts, columns in (
            (act_grads, xs, slice(0, double)),
            (inners, dys, slice(double, None)),
        ):
            total = None
            for left, right in zip(lefts, rights):
                one = lax.dot_general(
                    left[...], right[...], ROWS_IN, preferred_element_type=F32
                )
                total = one if total is None else total + one
            out_ref[:, columns] = total.astype(BF)

    tall = pl.BlockSpec((rows, tile), lambda i: (0, shard * steps + i))
    return call(
        kernel,
        "weight_grads",
        cost=work(6 * count * rows * size * hidden),
        grid=(steps,),
        in_specs=[pl.BlockSpec((rows, hidden), lambda i: (0, 0))] * count
        + [pl.BlockSpec((rows, double), lambda i: (0, 0))] * count
        + [tall] * (2 * count),
        out_specs=pl.BlockSpec((tile, double + hidden), lambda i: (i, 0)),
        out_shape=shape(size, double + hidden),
    )(*[band[i] for i in range(4) for band in bands])


def combine(where, picks, ids_t, grad_rows, blocks):
    groups = len(blocks)
    _, capacity, model = blocks[0].shape
    slots, tok_rows = picks[0].shape
    count = lax.axis_size("edata")
    width = model // count

    def kernel(where_ref, pick_ref, pick_t_ref, high_ref, middle_ref, ids_ref, rows_ref, *refs):
        blocks, (mixed_ref, token_grad_ref, gate_grad_ref) = refs[:groups], refs[groups:]
        me, turn = where_ref[0], where_ref[1]
        dots = jnp.zeros((slots, 1), F32)
        for s in range(count):
            here = slice(s * width, (s + 1) * width)
            target = shard_at(s, turn, count, width)
            y = jnp.concatenate([block[0, :, here] for block in blocks], axis=0)
            mixed_ref[:, target] = (
                jnp.dot(high_ref[...], y, preferred_element_type=F32)
                + jnp.dot(middle_ref[...], y, preferred_element_type=F32)
            ).astype(BF)
            dots += jnp.sum(
                y.astype(F32) * rows_ref[:, here].astype(F32), axis=1, keepdims=True
            )
            dx = jnp.concatenate([block[1, :, here] for block in blocks], axis=0)
            token_grad_ref[:, target] = jnp.dot(
                pick_t_ref[...], dx, preferred_element_type=F32
            ).astype(BF)
        by_token = pick_ref[...].astype(F32) * dots
        by_token = jnp.sum(by_token.reshape(groups, capacity, tok_rows), axis=1)
        ids = ids_ref[...]
        total = jnp.zeros(ids.shape, F32)
        for g in range(groups):
            total += jnp.where(ids == (me ^ g), by_token[g : g + 1], 0.0)
        gate_grad_ref[...] = total

    operands = (where, *picks, ids_t, grad_rows, *blocks)
    return call(
        kernel,
        "combine",
        in_specs=[SMEM] + [VMEM] * (len(operands) - 1),
        out_specs=[VMEM] * 3,
        out_shape=[
            shape(tok_rows, model),
            shape(tok_rows, model),
            shape(*ids_t.shape, kind=F32),
        ],
    )(*operands)


def shards(tokens, out_grad, expert_ids, gates, w_gate_up, w_down):
    groups = lax.axis_size("node") * lax.axis_size("local")
    half, quarter = groups // 2, groups // 4
    tok_rows = tokens.shape[0]
    capacity = tok_rows * expert_ids.shape[1] // (EXP_DEV * groups)
    where = jnp.stack([lax.axis_index(("node", "local")), lax.axis_index("edata")])
    where = where.astype(jnp.int32)
    w_ins = gathered(w_gate_up[0])
    w_outs = gathered(w_down[0])
    ids_t = expert_ids.T
    blocks, grad_rows, pick, slot_weight = dispatch(
        where, ids_t, gates.T, tokens, out_grad, groups, capacity
    )
    for j in range(quarter, groups):
        blocks[j] = after(blocks[j], *w_ins[1:], *w_outs[1:])
    got = [to_partner(blocks[j], j) for j in range(half + quarter)]
    sent, first = expert(got[:half], w_ins, w_outs)
    for j in range(half + quarter, groups):
        got.append(to_partner(after(blocks[j], sent[0]), j))
    more, second = expert(got[half:], w_ins, w_outs)
    back = []
    for j, block in enumerate([*sent, *more]):
        if j == 1:
            block = after(block, got[half + quarter - 1])
        elif j > WINDOW:
            block = after(block, *back[max(1, j - WINDOW - 1) : j - WINDOW + 1])
        back.append(to_partner(block, j))

    parts = []
    for shard in [*range(1, len(w_ins)), 0]:
        hint = back[1:half] if shard > 0 else back[half : half + quarter]
        band = [after(first[0], *hint), *first[1:]]
        parts.append(weight_grads(shard, [band, second]))
    parts = [parts[-1]] + [from_owner(p, step) for step, p in enumerate(parts[:-1], 1)]
    double = w_gate_up.shape[2]
    sums = [
        sum(p[:, columns].astype(F32) for p in parts)
        for columns in (slice(0, double), slice(double, None))
    ]
    spread = pick.astype(F32) * after(slot_weight, first[0])
    high = lax.reduce_precision(spread, 8, 7)
    middle = (spread - high).astype(BF)
    picks = (pick, pick.T, high.astype(BF).T, middle.T)
    *back, sums[0], sums[1] = lax.optimization_barrier((*back, *sums))
    mixed, token_grad, gate_grad = combine(where, picks, ids_t, grad_rows, back)
    return (mixed, token_grad, gate_grad.T, sums[0][None], sums[1][None])


def solution(mesh):
    rows = P(("node", "local", "edata"), None)
    weights = P(("node", "local"), "edata", None)
    return jax.shard_map(
        shards,
        mesh=mesh,
        in_specs=(rows, rows, rows, rows, weights, weights),
        out_specs=(rows, rows, rows, weights, weights),
        check_vma=False,
    )
```

time: 263 us -> 243 us (0.924)
  waiting for transfers between devices: 126 us -> 95.3 us
  starting transfers between devices: 75.7 us -> 81.4 us
  Pallas kernels: 43.2 us -> 48.1 us
    ppermute x30, waiting for transfers between devices: 123 us -> 95.3 us  [to_partner(): lax.ppermute(block, ('node', 'local'), [(i, i ^ j) for i in range(count)])]
    ppermute x30, starting transfers between devices: 58.8 us -> 80.7 us  [to_partner(): lax.ppermute(block, ('node', 'local'), [(i, i ^ j) for i in range(count)])]
    all_to_all x2 -> x0, starting transfers between devices: 16.2 us -> none  [exchange(): lax.all_to_all(everything, axes, split_axis=0, concat_axis=0, tiled=True)]
    pallas_call x3 -> x4, Pallas kernels: 31.5 us -> 36.1 us  [the longest x2 21.8 us: expert(): call(kernel, 'expert', cost=work(12 * rows * model * hidden), in_specs=[V...]
    ppermute x2, waiting for transfers between devices: 3.22 us -> 0.01 us  [gathered(): shards.append(lax.ppermute(shard, 'edata', pairs))]
  transfers between devices with their start and end apart: 35 -> 33, of which waited for: 10 -> 9; matrix products, arithmetic and copies ran while one was open for 4% -> 5% of each run, Pallas kernels for 3% -> 14%
where the time goes in v10:
time: 243 us; the launch traced here: 241 us
  waiting for transfers between devices  95.3 us (39%)
  starting transfers between devices  81.4 us (33%)
  Pallas kernels  48.1 us (20%)
  other arithmetic  12 us (5%)
  local copies, waits for them, and re-layouts  3.35 us (1%)
    ppermute x30, waiting for transfers between devices, to_partner(): lax.ppermute(block, ('node', 'local'), [(i, i ^ j) for i in range(count)])  95.3 us
    ppermute x30, starting transfers between devices, to_partner(): lax.ppermute(block, ('node', 'local'), [(i, i ^ j) for i in range(count)])  80.7 us
    pallas_call x2, Pallas kernels, expert(): call(kernel, 'expert', cost=work(12 * rows * model * hidden), in_specs=[V...  21.8 us
    pallas_call x2, Pallas kernels, weight_grads(): call(kernel, 'weight_grads', cost=work(6 * count * rows * size * hidden),...  14.3 us
    add x2, other arithmetic, shards(): sum((p[:, columns].astype(F32) for p in parts))  10.4 us
    pallas_call x1, Pallas kernels, combine(): call(kernel, 'combine', in_specs=[SMEM] + [VMEM] * (len(operands) - 1), o...  6.23 us
    pallas_call x1, Pallas kernels, dispatch(): call(kernel, 'dispatch', in_specs=[SMEM] + [VMEM] * 4, out_specs=[VMEM] *...  5.78 us
  transfers between devices with their start and end apart: 33, of which 9 were waited for; matrix products, arithmetic and copies ran while one was open for 5% of the time, Pallas kernels for 14%

profile of v10, /device:TPU:0, one launch (start us, length us, event | category | flops | bytes accessed | tf_op | source)
XLA Modules:
  0.0 241.3 jit_solution(4200418097234343736)
XLA Ops:
  1.8 5.8 %dispatch.1 = (bf16[2,32,2048]{2,1,0:T(8,128)(2,1)}, bf16[2,32,2048]{2,1,0:T(8,128)(2,1)}, bf16[2,32,2048]{2,1,0:T(8,128)(2,1)}, bf16[2,32,2048]{2,1,0:T(8,128)(...) custom-call(s32[2]{0:T(128)} %pad_add_fusion.where_ref, ...), custom_call_target="tpu_custom_call" | custom-call | flops 1 | bytes 1 | tf_op jit(solution)/shard_map/dispatch/pallas_call | solution.py:112
  7.6 3.1 %collective-permute-start = (bf16[2,32,2048]{2,1,0:T(8,128)(2,1)}, bf16[2,32,2048]{2,1,0:T(8,128)(2,1)S(1)}, u32[]{:S(2)}, u32[]{:S(2)}) collective-permute-start(bf16[2,32,2048]{2,1,0:T(8,128)(2,1)} %get-tuple-element.103), channel_id=1, source_target_pairs={{0,2},{2,0},{4,6},{6,4},{8,10},{10,8},{12,14},{14,12},{16,18},{18,... | collective-permute-start | bytes 786440 | tf_op jit(solution)/shard_map/ppermute | solution.py:58
  10.6 2.6 %collective-permute-start.1 = (bf16[2,32,2048]{2,1,0:T(8,128)(2,1)}, bf16[2,32,2048]{2,1,0:T(8,128)(2,1)S(1)}, u32[]{:S(2)}, u32[]{:S(2)}) collective-permute-start(bf16[2,32,2048]{2,1,0:T(8,128)(2,1)} %get-tuple-element.104), channel_id=1, source_target_pairs={{0,4},{2,6},{4,0},{6,2},{8,12},{10,14},{12,8},{14,10},{16,20},{18,... | collective-permute-start | bytes 786440 | tf_op jit(solution)/shard_map/ppermute | solution.py:58
  13.2 1.8 collective-permute-start.5
  15.7 7.3 %collective-permute-done.refs_1_ = bf16[2,32,2048]{2,1,0:T(8,128)(2,1)S(1)} collective-permute-done((bf16[2,32,2048]{2,1,0:T(8,128)(2,1)}, bf16[2,32,2048]{2,1,0:T(8,128)(2,1)S(1)}, u32[]{:S(2)}, u32[]{:S(2)}) %collective-permute-start) | collective-permute-done | bytes 262176 | tf_op jit(solution)/shard_map/ppermute | solution.py:58
  22.9 2.7 %collective-permute-start.7 = (bf16[2,32,2048]{2,1,0:T(8,128)(2,1)}, bf16[2,32,2048]{2,1,0:T(8,128)(2,1)S(1)}, u32[]{:S(2)}, u32[]{:S(2)}) collective-permute-start(bf16[2,32,2048]{2,1,0:T(8,128)(2,1)} %get-tuple-element.111), channel_id=1, source_target_pairs={{0,12},{2,14},{4,8},{6,10},{8,4},{10,6},{12,0},{14,2},{16,28},{18,... | collective-permute-start | bytes 786440 | tf_op jit(solution)/shard_map/ppermute | solution.py:58
  25.6 6.6 %collective-permute-done.1.refs_2_ = bf16[2,32,2048]{2,1,0:T(8,128)(2,1)S(1)} collective-permute-done((bf16[2,32,2048]{2,1,0:T(8,128)(2,1)}, bf16[2,32,2048]{2,1,0:T(8,128)(2,1)S(1)}, u32[]{:S(2)}, u32[]{:S(2)}) %collective-permute-start.1) | collective-permute-done | bytes 262176 | tf_op jit(solution)/shard_map/ppermute | solution.py:58
  32.2 3.4 %collective-permute-start.8 = (bf16[2,32,2048]{2,1,0:T(8,128)(2,1)}, bf16[2,32,2048]{2,1,0:T(8,128)(2,1)S(1)}, u32[]{:S(2)}, u32[]{:S(2)}) collective-permute-start(bf16[2,32,2048]{2,1,0:T(8,128)(2,1)} %get-tuple-element.113), channel_id=1, source_target_pairs={{0,14},{2,12},{4,10},{6,8},{8,6},{10,4},{12,2},{14,0},{16,30},{18,... | collective-permute-start | bytes 786440 | tf_op jit(solution)/shard_map/ppermute | solution.py:58
  35.6 2.3 collective-permute-start.9
  38.4 20.8 %collective-permute-start.18 = (bf16[2,32,2048]{2,1,0:T(8,128)(2,1)}, bf16[2,32,2048]{2,1,0:T(8,128)(2,1)S(1)}, u32[]{:S(2)}, u32[]{:S(2)}) collective-permute-start(bf16[2,32,2048]{2,1,0:T(8,128)(2,1)} %get-tuple-element.134), channel_id=1, source_target_pairs={{0,18},{2,16},{4,22},{6,20},{8,26},{10,24},{12,30},{14,28},{16,2},... | collective-permute-start | bytes 786440 | tf_op jit(solution)/shard_map/ppermute | solution.py:58
  59.3 2.0 collective-permute-done.7.refs_6_
  62.1 11.0 %expert.2 = (bf16[2,32,2048]{2,1,0:T(8,128)(2,1)}, bf16[2,32,2048]{2,1,0:T(8,128)(2,1)}, bf16[2,32,2048]{2,1,0:T(8,128)(2,1)}, bf16[2,32,2048]{2,1,0:T(8,128)(2,...) custom-call(bf16[2,32,2048]{2,1,0:T(8,128)(2,1)} %get-tuple-element., ...), custom_call_target="tpu_custom_call" | custom-call | flops 4831838208 | bytes 12079595 | tf_op jit(solution)/shard_map/expert/pallas_call | solution.py:180
  73.0 7.2 %collective-permute-start.11 = (bf16[2,32,2048]{2,1,0:T(8,128)(2,1)}, bf16[2,32,2048]{2,1,0:T(8,128)(2,1)S(1)}, u32[]{:S(2)}, u32[]{:S(2)}) collective-permute-start(bf16[2,32,2048]{2,1,0:T(8,128)(2,1)} %get-tuple-element.122), channel_id=1, source_target_pairs={{0,4},{2,6},{4,0},{6,2},{8,12},{10,14},{12,8},{14,10},{16,20},{18,... | collective-permute-start | bytes 786440 | tf_op jit(solution)/shard_map/ppermute | solution.py:58
  81.6 4.1 %collective-permute-start.19 = (bf16[2,32,2048]{2,1,0:T(8,128)(2,1)S(1)}, bf16[2,32,2048]{2,1,0:T(8,128)(2,1)S(1)}, u32[]{:S(2)}, u32[]{:S(2)}) collective-permute-start(bf16[2,32,2048]{2,1,0:T(8,128)(2,1)S(1)} %copy-done.23), channel_id=1, source_target_pairs={{0,20},{2,22},{4,16},{6,18},{8,28},{10,30},{12,24},{14,26},{16,4},... | collective-permute-start | bytes 786440 | tf_op jit(solution)/shard_map/ppermute | solution.py:58
  86.9 24.3 %collective-permute-done.11.refs_2_ = bf16[2,32,2048]{2,1,0:T(8,128)(2,1)S(1)} collective-permute-done((bf16[2,32,2048]{2,1,0:T(8,128)(2,1)}, bf16[2,32,2048]{2,1,0:T(8,128)(2,1)S(1)}, u32[]{:S(2)}, u32[]{:S(2)}) %collective-permute-start.11) | collective-permute-done | bytes 262176 | tf_op jit(solution)/shard_map/ppermute | solution.py:58
  111.2 9.9 %collective-permute-start.21 = (bf16[2,32,2048]{2,1,0:T(8,128)(2,1)S(1)}, bf16[2,32,2048]{2,1,0:T(8,128)(2,1)S(1)}, u32[]{:S(2)}, u32[]{:S(2)}) collective-permute-start(bf16[2,32,2048]{2,1,0:T(8,128)(2,1)S(1)} %copy-done.20), channel_id=1, source_target_pairs={{0,26},{2,24},{4,30},{6,28},{8,18},{10,16},{12,22},{14,20},{16,10}... | collective-permute-start | bytes 786440 | tf_op jit(solution)/shard_map/ppermute | solution.py:58
  121.1 1.5 collective-permute-start.20
  122.6 6.4 %collective-permute-done.19.refs_2_ = bf16[2,32,2048]{2,1,0:T(8,128)(2,1)S(1)} collective-permute-done((bf16[2,32,2048]{2,1,0:T(8,128)(2,1)S(1)}, bf16[2,32,2048]{2,1,0:T(8,128)(2,1)S(1)}, u32[]{:S(2)}, u32[]{:S(2)}) %collective-permute-start.19) | collective-permute-done | bytes 262176 | tf_op jit(solution)/shard_map/ppermute | solution.py:58
  129.6 1.4 collective-permute-start.16
  131.0 20.5 %collective-permute-done.22.refs_6_ = bf16[2,32,2048]{2,1,0:T(8,128)(2,1)S(1)} collective-permute-done((bf16[2,32,2048]{2,1,0:T(8,128)(2,1)S(1)}, bf16[2,32,2048]{2,1,0:T(8,128)(2,1)S(1)}, u32[]{:S(2)}, u32[]{:S(2)}) %collective-permute-start.22) | collective-permute-done | bytes 262176 | tf_op jit(solution)/shard_map/ppermute | solution.py:58
  153.0 10.9 %expert.3 = (bf16[2,32,2048]{2,1,0:T(8,128)(2,1)}, bf16[2,32,2048]{2,1,0:T(8,128)(2,1)}, bf16[2,32,2048]{2,1,0:T(8,128)(2,1)}, bf16[2,32,2048]{2,1,0:T(8,128)(2,...) custom-call(bf16[2,32,2048]{2,1,0:T(8,128)(2,1)} %copy-done.25, ...), custom_call_target="tpu_custom_call" | custom-call | flops 4831838208 | bytes 12079595 | tf_op jit(solution)/shard_map/expert/pallas_call | solution.py:180
  164.5 7.3 %weight_grads.3 = bf16[1024,2304]{1,0:T(8,128)(2,1)} custom-call(bf16[256,768]{1,0:T(8,128)(2,1)} %get-tuple-element.165.refs_0_, bf16[256,768]{1,0:T(8,128)(2,1)} %get-tuple-element.166.refs_1_, bf16[256,1536]{1,0:T(8,128)(2,1)} %get-tuple-element.167.refs_2_, bf16[256,1536]{1,0:T(8,128)(2,1)} %get-tuple-element.168.refs_3_, ...), custom_call_target="tpu_custom_call" | custom-call | flops 2415919104 | bytes 6039797 | tf_op jit(solution)/shard_map/weight_grads/pallas_call | solution.py:216
  172.0 5.8 %collective-permute-start.27 = (bf16[2,32,2048]{2,1,0:T(8,128)(2,1)}, bf16[2,32,2048]{2,1,0:T(8,128)(2,1)S(1)}, u32[]{:S(2)}, u32[]{:S(2)}) collective-permute-start(bf16[2,32,2048]{2,1,0:T(8,128)(2,1)} %get-tuple-element.156), channel_id=1, source_target_pairs={{0,22},{2,20},{4,18},{6,16},{8,30},{10,28},{12,26},{14,24},{16,6},... | collective-permute-start | bytes 786440 | tf_op jit(solution)/shard_map/ppermute | solution.py:58
  180.0 12.1 %collective-permute-done.24.refs_8_ = bf16[2,32,2048]{2,1,0:T(8,128)(2,1)S(1)} collective-permute-done((bf16[2,32,2048]{2,1,0:T(8,128)(2,1)}, bf16[2,32,2048]{2,1,0:T(8,128)(2,1)S(1)}, u32[]{:S(2)}, u32[]{:S(2)}) %collective-permute-start.24) | collective-permute-done | bytes 262176 | tf_op jit(solution)/shard_map/ppermute | solution.py:58
  192.1 1.8 collective-permute-start.28
  193.9 15.7 %collective-permute-done.26.refs_10_ = bf16[2,32,2048]{2,1,0:T(8,128)(2,1)S(1)} collective-permute-done((bf16[2,32,2048]{2,1,0:T(8,128)(2,1)S(1)}, bf16[2,32,2048]{2,1,0:T(8,128)(2,1)S(1)}, u32[]{:S(2)}, u32[]{:S(2)}) %collective-permute-start.26) | collective-permute-done | bytes 262176 | tf_op jit(solution)/shard_map/ppermute | solution.py:58
  209.6 4.2 %collective-permute-start.31 = (bf16[2,32,2048]{2,1,0:T(8,128)(2,1)S(1)}, bf16[2,32,2048]{2,1,0:T(8,128)(2,1)S(1)}, u32[]{:S(2)}, u32[]{:S(2)}) collective-permute-start(bf16[2,32,2048]{2,1,0:T(8,128)(2,1)S(1)} %copy-done.29), channel_id=1, source_target_pairs={{0,30},{2,28},{4,26},{6,24},{8,22},{10,20},{12,18},{14,16},{16,14}... | collective-permute-start | bytes 786440 | tf_op jit(solution)/shard_map/ppermute | solution.py:58
  213.8 2.9 %collective-permute-start.29 = (bf16[2,32,2048]{2,1,0:T(8,128)(2,1)S(1)}, bf16[2,32,2048]{2,1,0:T(8,128)(2,1)S(1)}, u32[]{:S(2)}, u32[]{:S(2)}) collective-permute-start(bf16[2,32,2048]{2,1,0:T(8,128)(2,1)S(1)} %copy-done.27), channel_id=1, source_target_pairs={{0,26},{2,24},{4,30},{6,28},{8,18},{10,16},{12,22},{14,20},{16,10}... | collective-permute-start | bytes 786440 | tf_op jit(solution)/shard_map/ppermute | solution.py:58
  216.7 6.9 %weight_grads.2 = bf16[1024,2304]{1,0:T(8,128)(2,1)} custom-call(bf16[256,768]{1,0:T(8,128)(2,1)} %get-tuple-element.165.refs_0_, bf16[256,768]{1,0:T(8,128)(2,1)} %get-tuple-element.166.refs_1_, bf16[256,1536]{1,0:T(8,128)(2,1)} %get-tuple-element.167.refs_2_, bf16[256,1536]{1,0:T(8,128)(2,1)} %get-tuple-element.168.refs_3_, ...), custom_call_target="tpu_custom_call" | custom-call | flops 2415919104 | bytes 6039797 | tf_op jit(solution)/shard_map/weight_grads/pallas_call | solution.py:216
  223.7 6.5 %convert_add_fusion = f32[1024,1536]{1,0:T(8,128)} fusion(bf16[1024,2304]{1,0:T(8,128)(2,1)} %collective-permute-done.32, bf16[1024,2304]{1,0:T(8,128)(2,1)} %weight_grads.2), kind=kLoop, calls=%fused_computation | loop fusion | flops 4718592 | bytes 12582912 | tf_op jit(solution)/shard_map/add | solution.py:313
  230.1 3.9 %convert_add_fusion.1 = f32[1024,768]{1,0:T(8,128)} fusion(bf16[1024,2304]{1,0:T(8,128)(2,1)} %collective-permute-done.32, bf16[1024,2304]{1,0:T(8,128)(2,1)} %weight_grads.2), kind=kLoop, calls=%fused_computation.1 | loop fusion | flops 2359296 | bytes 6291456 | tf_op jit(solution)/shard_map/add | solution.py:313
  235.1 6.2 %combine.1 = (bf16[256,2048]{1,0:T(8,128)(2,1)}, bf16[256,2048]{1,0:T(8,128)(2,1)}, f32[8,256]{1,0:T(8,128)}) custom-call(s32[2]{0:T(128)} %pad_add_fusion.where_ref, bf16[512,256]{1,0:T(8,128)(2,1)} %get-tuple-element.100.pick_ref, bf16[256,512]{1,0:T(8,128)(2,1)} %bitcast.16, bf16[256,512]{1,0:T(8,128)(2,1)} %get-tuple-element.196.high_ref, ...), custom_call_target="tpu_custom_call" | custom-call | flops 1 | bytes 1 | tf_op jit(solution)/shard_map/combine/pallas_call | solution.py:264
  (136 shorter events, 11.5 us)
Async XLA Ops:
  0.6 12.6 %collective-permute-start.3 = (bf16[1024,1536]{1,0:T(8,128)(2,1)}, bf16[1024,1536]{1,0:T(8,128)(2,1)S(1)}, u32[]{:S(2)}, u32[]{:S(2)}) collective-permute-start(bf16[1024,1536]{1,0:T(8,128)(2,1)} %bitcast.20), channel_id=1, source_target_pairs={{1,0},{0,1},{3,2},{2,3},{5,4},{4,5},{7,6},{6,7},{9,8},{8,9},{11,10... | collective-permute-start | bytes 9437192 | tf_op jit(solution)/shard_map/ppermute | solution.py:45
  7.6 15.4 %collective-permute-start = (bf16[2,32,2048]{2,1,0:T(8,128)(2,1)}, bf16[2,32,2048]{2,1,0:T(8,128)(2,1)S(1)}, u32[]{:S(2)}, u32[]{:S(2)}) collective-permute-start(bf16[2,32,2048]{2,1,0:T(8,128)(2,1)} %get-tuple-element.103), channel_id=1, source_target_pairs={{0,2},{2,0},{4,6},{6,4},{8,10},{10,8},{12,14},{14,12},{16,18},{18,... | collective-permute-start | bytes 786440 | tf_op jit(solution)/shard_map/ppermute | solution.py:58
  10.6 21.6 %collective-permute-start.1 = (bf16[2,32,2048]{2,1,0:T(8,128)(2,1)}, bf16[2,32,2048]{2,1,0:T(8,128)(2,1)S(1)}, u32[]{:S(2)}, u32[]{:S(2)}) collective-permute-start(bf16[2,32,2048]{2,1,0:T(8,128)(2,1)} %get-tuple-element.104), channel_id=1, source_target_pairs={{0,4},{2,6},{4,0},{6,2},{8,12},{10,14},{12,8},{14,10},{16,20},{18,... | collective-permute-start | bytes 786440 | tf_op jit(solution)/shard_map/ppermute | solution.py:58
  13.2 22.4 %collective-permute-start.2 = (bf16[2,32,2048]{2,1,0:T(8,128)(2,1)}, bf16[2,32,2048]{2,1,0:T(8,128)(2,1)S(1)}, u32[]{:S(2)}, u32[]{:S(2)}) collective-permute-start(bf16[2,32,2048]{2,1,0:T(8,128)(2,1)} %get-tuple-element.105), channel_id=1, source_target_pairs={{0,6},{2,4},{4,2},{6,0},{8,14},{10,12},{12,10},{14,8},{16,22},{18,... | collective-permute-start | bytes 786440 | tf_op jit(solution)/shard_map/ppermute | solution.py:58
  13.2 24.7 %collective-permute-start.5 = (bf16[2,32,2048]{2,1,0:T(8,128)(2,1)}, bf16[2,32,2048]{2,1,0:T(8,128)(2,1)S(1)}, u32[]{:S(2)}, u32[]{:S(2)}) collective-permute-start(bf16[2,32,2048]{2,1,0:T(8,128)(2,1)} %get-tuple-element.107), channel_id=1, source_target_pairs={{0,8},{2,10},{4,12},{6,14},{8,0},{10,2},{12,4},{14,6},{16,24},{18,... | collective-permute-start | bytes 786440 | tf_op jit(solution)/shard_map/ppermute | solution.py:58
  15.0 23.4 %collective-permute-start.6 = (bf16[2,32,2048]{2,1,0:T(8,128)(2,1)}, bf16[2,32,2048]{2,1,0:T(8,128)(2,1)S(1)}, u32[]{:S(2)}, u32[]{:S(2)}) collective-permute-start(bf16[2,32,2048]{2,1,0:T(8,128)(2,1)} %get-tuple-element.109), channel_id=1, source_target_pairs={{0,10},{2,8},{4,14},{6,12},{8,2},{10,0},{12,6},{14,4},{16,26},{18,... | collective-permute-start | bytes 786440 | tf_op jit(solution)/shard_map/ppermute | solution.py:58
  22.9 38.3 %collective-permute-start.7 = (bf16[2,32,2048]{2,1,0:T(8,128)(2,1)}, bf16[2,32,2048]{2,1,0:T(8,128)(2,1)S(1)}, u32[]{:S(2)}, u32[]{:S(2)}) collective-permute-start(bf16[2,32,2048]{2,1,0:T(8,128)(2,1)} %get-tuple-element.111), channel_id=1, source_target_pairs={{0,12},{2,14},{4,8},{6,10},{8,4},{10,6},{12,0},{14,2},{16,28},{18,... | collective-permute-start | bytes 786440 | tf_op jit(solution)/shard_map/ppermute | solution.py:58
  32.2 29.0 %collective-permute-start.8 = (bf16[2,32,2048]{2,1,0:T(8,128)(2,1)}, bf16[2,32,2048]{2,1,0:T(8,128)(2,1)S(1)}, u32[]{:S(2)}, u32[]{:S(2)}) collective-permute-start(bf16[2,32,2048]{2,1,0:T(8,128)(2,1)} %get-tuple-element.113), channel_id=1, source_target_pairs={{0,14},{2,12},{4,10},{6,8},{8,6},{10,4},{12,2},{14,0},{16,30},{18,... | collective-permute-start | bytes 786440 | tf_op jit(solution)/shard_map/ppermute | solution.py:58
  35.6 45.9 %collective-permute-start.9 = (bf16[2,32,2048]{2,1,0:T(8,128)(2,1)}, bf16[2,32,2048]{2,1,0:T(8,128)(2,1)S(1)}, u32[]{:S(2)}, u32[]{:S(2)}) collective-permute-start(bf16[2,32,2048]{2,1,0:T(8,128)(2,1)} %get-tuple-element.120), channel_id=1, source_target_pairs={{0,22},{2,20},{4,18},{6,16},{8,30},{10,28},{12,26},{14,24},{16,6},... | collective-permute-start | bytes 786440 | tf_op jit(solution)/shard_map/ppermute | solution.py:58
  37.9 43.6 %collective-permute-start.17 = (bf16[2,32,2048]{2,1,0:T(8,128)(2,1)}, bf16[2,32,2048]{2,1,0:T(8,128)(2,1)S(1)}, u32[]{:S(2)}, u32[]{:S(2)}) collective-permute-start(bf16[2,32,2048]{2,1,0:T(8,128)(2,1)} %get-tuple-element.132), channel_id=1, source_target_pairs={{0,16},{2,18},{4,20},{6,22},{8,24},{10,26},{12,28},{14,30},{16,0},... | collective-permute-start | bytes 786440 | tf_op jit(solution)/shard_map/ppermute | solution.py:58
  38.4 47.2 %collective-permute-start.18 = (bf16[2,32,2048]{2,1,0:T(8,128)(2,1)}, bf16[2,32,2048]{2,1,0:T(8,128)(2,1)S(1)}, u32[]{:S(2)}, u32[]{:S(2)}) collective-permute-start(bf16[2,32,2048]{2,1,0:T(8,128)(2,1)} %get-tuple-element.134), channel_id=1, source_target_pairs={{0,18},{2,16},{4,22},{6,20},{8,26},{10,24},{12,30},{14,28},{16,2},... | collective-permute-start | bytes 786440 | tf_op jit(solution)/shard_map/ppermute | solution.py:58
  73.0 38.2 %collective-permute-start.11 = (bf16[2,32,2048]{2,1,0:T(8,128)(2,1)}, bf16[2,32,2048]{2,1,0:T(8,128)(2,1)S(1)}, u32[]{:S(2)}, u32[]{:S(2)}) collective-permute-start(bf16[2,32,2048]{2,1,0:T(8,128)(2,1)} %get-tuple-element.122), channel_id=1, source_target_pairs={{0,4},{2,6},{4,0},{6,2},{8,12},{10,14},{12,8},{14,10},{16,20},{18,... | collective-permute-start | bytes 786440 | tf_op jit(solution)/shard_map/ppermute | solution.py:58
  80.2 31.0 %collective-permute-start.12 = (bf16[2,32,2048]{2,1,0:T(8,128)(2,1)}, bf16[2,32,2048]{2,1,0:T(8,128)(2,1)S(1)}, u32[]{:S(2)}, u32[]{:S(2)}) collective-permute-start(bf16[2,32,2048]{2,1,0:T(8,128)(2,1)} %get-tuple-element.123), channel_id=1, source_target_pairs={{0,6},{2,4},{4,2},{6,0},{8,14},{10,12},{12,10},{14,8},{16,22},{18,... | collective-permute-start | bytes 786440 | tf_op jit(solution)/shard_map/ppermute | solution.py:58
  81.5 39.6 %collective-permute-start.10 = (bf16[2,32,2048]{2,1,0:T(8,128)(2,1)}, bf16[2,32,2048]{2,1,0:T(8,128)(2,1)S(1)}, u32[]{:S(2)}, u32[]{:S(2)}) collective-permute-start(bf16[2,32,2048]{2,1,0:T(8,128)(2,1)} %get-tuple-element.121), channel_id=1, source_target_pairs={{0,2},{2,0},{4,6},{6,4},{8,10},{10,8},{12,14},{14,12},{16,18},{18,... | collective-permute-start | bytes 786440 | tf_op jit(solution)/shard_map/ppermute | solution.py:58
  81.6 47.5 %collective-permute-start.19 = (bf16[2,32,2048]{2,1,0:T(8,128)(2,1)S(1)}, bf16[2,32,2048]{2,1,0:T(8,128)(2,1)S(1)}, u32[]{:S(2)}, u32[]{:S(2)}) collective-permute-start(bf16[2,32,2048]{2,1,0:T(8,128)(2,1)S(1)} %copy-done.23), channel_id=1, source_target_pairs={{0,20},{2,22},{4,16},{6,18},{8,28},{10,30},{12,24},{14,26},{16,4},... | collective-permute-start | bytes 786440 | tf_op jit(solution)/shard_map/ppermute | solution.py:58
  85.6 44.0 %collective-permute-start.23 = (bf16[2,32,2048]{2,1,0:T(8,128)(2,1)S(1)}, bf16[2,32,2048]{2,1,0:T(8,128)(2,1)S(1)}, u32[]{:S(2)}, u32[]{:S(2)}) collective-permute-start(bf16[2,32,2048]{2,1,0:T(8,128)(2,1)S(1)} %copy-done.22), channel_id=1, source_target_pairs={{0,30},{2,28},{4,26},{6,24},{8,22},{10,20},{12,18},{14,16},{16,14}... | collective-permute-start | bytes 786440 | tf_op jit(solution)/shard_map/ppermute | solution.py:58
  111.2 40.3 %collective-permute-start.22 = (bf16[2,32,2048]{2,1,0:T(8,128)(2,1)S(1)}, bf16[2,32,2048]{2,1,0:T(8,128)(2,1)S(1)}, u32[]{:S(2)}, u32[]{:S(2)}) collective-permute-start(bf16[2,32,2048]{2,1,0:T(8,128)(2,1)S(1)} %copy-done.21), channel_id=1, source_target_pairs={{0,28},{2,30},{4,24},{6,26},{8,20},{10,22},{12,16},{14,18},{16,12}... | collective-permute-start | bytes 786440 | tf_op jit(solution)/shard_map/ppermute | solution.py:58
  111.2 40.3 %collective-permute-start.21 = (bf16[2,32,2048]{2,1,0:T(8,128)(2,1)S(1)}, bf16[2,32,2048]{2,1,0:T(8,128)(2,1)S(1)}, u32[]{:S(2)}, u32[]{:S(2)}) collective-permute-start(bf16[2,32,2048]{2,1,0:T(8,128)(2,1)S(1)} %copy-done.20), channel_id=1, source_target_pairs={{0,26},{2,24},{4,30},{6,28},{8,18},{10,16},{12,22},{14,20},{16,10}... | collective-permute-start | bytes 786440 | tf_op jit(solution)/shard_map/ppermute | solution.py:58
  121.1 30.5 %collective-permute-start.20 = (bf16[2,32,2048]{2,1,0:T(8,128)(2,1)S(1)}, bf16[2,32,2048]{2,1,0:T(8,128)(2,1)S(1)}, u32[]{:S(2)}, u32[]{:S(2)}) collective-permute-start(bf16[2,32,2048]{2,1,0:T(8,128)(2,1)S(1)} %copy-done.19), channel_id=1, source_target_pairs={{0,24},{2,26},{4,28},{6,30},{8,16},{10,18},{12,20},{14,22},{16,8},... | collective-permute-start | bytes 786440 | tf_op jit(solution)/shard_map/ppermute | solution.py:58
  129.0 34.9 %collective-permute-start.13 = (bf16[2,32,2048]{2,1,0:T(8,128)(2,1)}, bf16[2,32,2048]{2,1,0:T(8,128)(2,1)S(1)}, u32[]{:S(2)}, u32[]{:S(2)}) collective-permute-start(bf16[2,32,2048]{2,1,0:T(8,128)(2,1)} %get-tuple-element.124), channel_id=1, source_target_pairs={{0,8},{2,10},{4,12},{6,14},{8,0},{10,2},{12,4},{14,6},{16,24},{18,... | collective-permute-start | bytes 786440 | tf_op jit(solution)/shard_map/ppermute | solution.py:58
  129.6 34.3 %collective-permute-start.16 = (bf16[2,32,2048]{2,1,0:T(8,128)(2,1)}, bf16[2,32,2048]{2,1,0:T(8,128)(2,1)S(1)}, u32[]{:S(2)}, u32[]{:S(2)}) collective-permute-start(bf16[2,32,2048]{2,1,0:T(8,128)(2,1)} %get-tuple-element.130), channel_id=1, source_target_pairs={{0,14},{2,12},{4,10},{6,8},{8,6},{10,4},{12,2},{14,0},{16,30},{18,... | collective-permute-start | bytes 786440 | tf_op jit(solution)/shard_map/ppermute | solution.py:58
  151.5 12.4 %collective-permute-start.15 = (bf16[2,32,2048]{2,1,0:T(8,128)(2,1)}, bf16[2,32,2048]{2,1,0:T(8,128)(2,1)S(1)}, u32[]{:S(2)}, u32[]{:S(2)}) collective-permute-start(bf16[2,32,2048]{2,1,0:T(8,128)(2,1)} %get-tuple-element.128), channel_id=1, source_target_pairs={{0,12},{2,14},{4,8},{6,10},{8,4},{10,6},{12,0},{14,2},{16,28},{18,... | collective-permute-start | bytes 786440 | tf_op jit(solution)/shard_map/ppermute | solution.py:58
  151.5 12.9 %collective-permute-start.14 = (bf16[2,32,2048]{2,1,0:T(8,128)(2,1)}, bf16[2,32,2048]{2,1,0:T(8,128)(2,1)S(1)}, u32[]{:S(2)}, u32[]{:S(2)}) collective-permute-start(bf16[2,32,2048]{2,1,0:T(8,128)(2,1)} %get-tuple-element.126), channel_id=1, source_target_pairs={{0,10},{2,8},{4,14},{6,12},{8,2},{10,0},{12,6},{14,4},{16,26},{18,... | collective-permute-start | bytes 786440 | tf_op jit(solution)/shard_map/ppermute | solution.py:58
  171.8 51.8 %collective-permute-start.32 = (bf16[1024,2304]{1,0:T(8,128)(2,1)}, bf16[1024,2304]{1,0:T(8,128)(2,1)}, u32[]{:S(2)}, u32[]{:S(2)}) collective-permute-start(bf16[1024,2304]{1,0:T(8,128)(2,1)} %weight_grads.3), channel_id=1, source_target_pairs={{0,1},{1,0},{2,3},{3,2},{4,5},{5,4},{6,7},{7,6},{8,9},{9,8},{10,11... | collective-permute-start | bytes 14155784 | tf_op jit(solution)/shard_map/ppermute | solution.py:51
  171.9 20.2 %collective-permute-start.24 = (bf16[2,32,2048]{2,1,0:T(8,128)(2,1)}, bf16[2,32,2048]{2,1,0:T(8,128)(2,1)S(1)}, u32[]{:S(2)}, u32[]{:S(2)}) collective-permute-start(bf16[2,32,2048]{2,1,0:T(8,128)(2,1)} %get-tuple-element.150), channel_id=1, source_target_pairs={{0,16},{2,18},{4,20},{6,22},{8,24},{10,26},{12,28},{14,30},{16,0},... | collective-permute-start | bytes 786440 | tf_op jit(solution)/shard_map/ppermute | solution.py:58
  172.0 21.9 %collective-permute-start.27 = (bf16[2,32,2048]{2,1,0:T(8,128)(2,1)}, bf16[2,32,2048]{2,1,0:T(8,128)(2,1)S(1)}, u32[]{:S(2)}, u32[]{:S(2)}) collective-permute-start(bf16[2,32,2048]{2,1,0:T(8,128)(2,1)} %get-tuple-element.156), channel_id=1, source_target_pairs={{0,22},{2,20},{4,18},{6,16},{8,30},{10,28},{12,26},{14,24},{16,6},... | collective-permute-start | bytes 786440 | tf_op jit(solution)/shard_map/ppermute | solution.py:58
  177.8 31.7 %collective-permute-start.26 = (bf16[2,32,2048]{2,1,0:T(8,128)(2,1)S(1)}, bf16[2,32,2048]{2,1,0:T(8,128)(2,1)S(1)}, u32[]{:S(2)}, u32[]{:S(2)}) collective-permute-start(bf16[2,32,2048]{2,1,0:T(8,128)(2,1)S(1)} %copy-done.37), channel_id=1, source_target_pairs={{0,20},{2,22},{4,16},{6,18},{8,28},{10,30},{12,24},{14,26},{16,4},... | collective-permute-start | bytes 786440 | tf_op jit(solution)/shard_map/ppermute | solution.py:58
  177.8 31.7 %collective-permute-start.25 = (bf16[2,32,2048]{2,1,0:T(8,128)(2,1)S(1)}, bf16[2,32,2048]{2,1,0:T(8,128)(2,1)S(1)}, u32[]{:S(2)}, u32[]{:S(2)}) collective-permute-start(bf16[2,32,2048]{2,1,0:T(8,128)(2,1)S(1)} %copy-done.34), channel_id=1, source_target_pairs={{0,18},{2,16},{4,22},{6,20},{8,26},{10,24},{12,30},{14,28},{16,2},... | collective-permute-start | bytes 786440 | tf_op jit(solution)/shard_map/ppermute | solution.py:58
  192.1 42.0 %collective-permute-start.28 = (bf16[2,32,2048]{2,1,0:T(8,128)(2,1)S(1)}, bf16[2,32,2048]{2,1,0:T(8,128)(2,1)S(1)}, u32[]{:S(2)}, u32[]{:S(2)}) collective-permute-start(bf16[2,32,2048]{2,1,0:T(8,128)(2,1)S(1)} %copy-done.30), channel_id=1, source_target_pairs={{0,24},{2,26},{4,28},{6,30},{8,16},{10,18},{12,20},{14,22},{16,8},... | collective-permute-start | bytes 786440 | tf_op jit(solution)/shard_map/ppermute | solution.py:58
  209.6 24.5 %collective-permute-start.31 = (bf16[2,32,2048]{2,1,0:T(8,128)(2,1)S(1)}, bf16[2,32,2048]{2,1,0:T(8,128)(2,1)S(1)}, u32[]{:S(2)}, u32[]{:S(2)}) collective-permute-start(bf16[2,32,2048]{2,1,0:T(8,128)(2,1)S(1)} %copy-done.29), channel_id=1, source_target_pairs={{0,30},{2,28},{4,26},{6,24},{8,22},{10,20},{12,18},{14,16},{16,14}... | collective-permute-start | bytes 786440 | tf_op jit(solution)/shard_map/ppermute | solution.py:58
  213.8 20.3 %collective-permute-start.30 = (bf16[2,32,2048]{2,1,0:T(8,128)(2,1)S(1)}, bf16[2,32,2048]{2,1,0:T(8,128)(2,1)S(1)}, u32[]{:S(2)}, u32[]{:S(2)}) collective-permute-start(bf16[2,32,2048]{2,1,0:T(8,128)(2,1)S(1)} %copy-done.28), channel_id=1, source_target_pairs={{0,28},{2,30},{4,24},{6,26},{8,20},{10,22},{12,16},{14,18},{16,12}... | collective-permute-start | bytes 786440 | tf_op jit(solution)/shard_map/ppermute | solution.py:58
  213.8 20.4 %collective-permute-start.29 = (bf16[2,32,2048]{2,1,0:T(8,128)(2,1)S(1)}, bf16[2,32,2048]{2,1,0:T(8,128)(2,1)S(1)}, u32[]{:S(2)}, u32[]{:S(2)}) collective-permute-start(bf16[2,32,2048]{2,1,0:T(8,128)(2,1)S(1)} %copy-done.27), channel_id=1, source_target_pairs={{0,26},{2,24},{4,30},{6,28},{8,18},{10,16},{12,22},{14,20},{16,10}... | collective-permute-start | bytes 786440 | tf_op jit(solution)/shard_map/ppermute | solution.py:58
  (46 other events, 1198.1 us)

commit v11 on v10

--- a/solution.py
+++ b/solution.py
@@ -287,26 +287,46 @@
     blocks, grad_rows, pick, slot_weight = dispatch(
         where, ids_t, gates.T, tokens, out_grad, groups, capacity
     )
-    for j in range(quarter, groups):
-        blocks[j] = after(blocks[j], *w_ins[1:], *w_outs[1:])
-    got = [to_partner(blocks[j], j) for j in range(half + quarter)]
-    sent, first = expert(got[:half], w_ins, w_outs)
-    for j in range(half + quarter, groups):
-        got.append(to_partner(after(blocks[j], sent[0]), j))
-    more, second = expert(got[half:], w_ins, w_outs)
-    back = []
-    for j, block in enumerate([*sent, *more]):
-        if j == 1:
-            block = after(block, got[half + quarter - 1])
-        elif j > WINDOW:
-            block = after(block, *back[max(1, j - WINDOW - 1) : j - WINDOW + 1])
-        back.append(to_partner(block, j))
+    planes = lax.axis_size("local")
+    hops = [min(j % planes, 2 if j % planes == planes // 2 else 1) for j in range(groups)]
+    low, high = range(half), range(half, groups)
+    late = sorted(high, key=lambda j: -hops[j])
+    early = [j for j in low if j]
+    arrived = []
+
+    def move(block, j, *needs):
+        if len(arrived) >= WINDOW:
+            needs += tuple(arrived[-WINDOW - 1 : len(arrived) - WINDOW + 1])
+        arrived.append(to_partner(after(block, *needs) if needs else block, j))
+        return arrived[-1]
+
+    got = {0: blocks[0]}
+    for i, j in enumerate(early):
+        got[j] = move(blocks[j], j, *(w_ins[1:] + w_outs[1:] if i == quarter - 1 else ()))
+    for j in late[:quarter]:
+        got[j] = move(blocks[j], j)
+    sent, first = expert([got[j] for j in low], w_ins, w_outs)
+    for j in late[quarter:]:
+        got[j] = move(blocks[j], j, sent[0])
+    more, second = expert([got[j] for j in high], w_ins, w_outs)
+    front = sorted(early, key=lambda j: -hops[j])
+    results = [*sent, *more]
+    back = {0: results[0]}
+    for i, j in enumerate(front + late):
+        back[j] = move(results[j], j, *(more[:1] if i >= WINDOW else ()))
 
     parts = []
+    hint = [back[j] for j in front]
     for shard in [*range(1, len(w_ins)), 0]:
-        hint = back[1:half] if shard > 0 else back[half : half + quarter]
         band = [after(first[0], *hint), *first[1:]]
         parts.append(weight_grads(shard, [band, second]))
+        hint = [parts[-1]]
+    middle = late[1 : quarter]
+    held = lax.optimization_barrier((*parts, *[back[j] for j in middle]))
+    parts = list(held[: len(parts)])
+    for j, block in zip(middle, held[len(parts) :]):
+        back[j] = block
+    back = [back[j] for j in range(groups)]
     parts = [parts[-1]] + [from_owner(p, step) for step, p in enumerate(parts[:-1], 1)]
     double = w_gate_up.shape[2]
     sums = [

time: 243 us -> 247 us (1.016)
  starting transfers between devices: 81.4 us -> 86.4 us
  waiting for transfers between devices: 95.3 us -> 98.1 us
    ppermute x30, starting transfers between devices: 80.7 us -> 85.8 us  [to_partner(): lax.ppermute(block, ('node', 'local'), [(i, i ^ j) for i in range(count)])]
    ppermute x30, waiting for transfers between devices: 95.3 us -> 98.1 us  [to_partner(): lax.ppermute(block, ('node', 'local'), [(i, i ^ j) for i in range(count)])]
  transfers between devices with their start and end apart: 33 -> 33, of which waited for: 9 -> 15; matrix products, arithmetic and copies ran while one was open for 5% -> 5% of each run, Pallas kernels for 14% -> 17%
where the time goes in v11:
time: 247 us
  waiting for transfers between devices  98.1 us (40%)
  starting transfers between devices  86.4 us (35%)
  Pallas kernels  47.9 us (19%)
  other arithmetic  12 us (5%)
    ppermute x30, waiting for transfers between devices, to_partner(): lax.ppermute(block, ('node', 'local'), [(i, i ^ j) for i in range(count)])  98.1 us
    ppermute x30, starting transfers between devices, to_partner(): lax.ppermute(block, ('node', 'local'), [(i, i ^ j) for i in range(count)])  85.8 us
    pallas_call x2, Pallas kernels, expert(): call(kernel, 'expert', cost=work(12 * rows * model * hidden), in_specs=[V...  21.9 us
    pallas_call x2, Pallas kernels, weight_grads(): call(kernel, 'weight_grads', cost=work(6 * count * rows * size * hidden),...  14 us
    add x2, other arithmetic, shards(): sum((p[:, columns].astype(F32) for p in parts))  10.4 us
    pallas_call x1, Pallas kernels, combine(): call(kernel, 'combine', in_specs=[SMEM] + [VMEM] * (len(operands) - 1), o...  6.23 us
    pallas_call x1, Pallas kernels, dispatch(): call(kernel, 'dispatch', in_specs=[SMEM] + [VMEM] * 4, out_specs=[VMEM] *...  5.77 us
  transfers between devices with their start and end apart: 33, of which 15 were waited for; matrix products, arithmetic and copies ran while one was open for 5% of the time, Pallas kernels for 17%

profile of v11, /device:TPU:0, one launch (start us, length us, event | category | flops | bytes accessed | tf_op | source)
XLA Modules:
  0.0 247.2 jit_solution(13000221267189270738)
XLA Ops:
  1.8 5.8 %dispatch.1 = (bf16[2,32,2048]{2,1,0:T(8,128)(2,1)}, bf16[2,32,2048]{2,1,0:T(8,128)(2,1)}, bf16[2,32,2048]{2,1,0:T(8,128)(2,1)}, bf16[2,32,2048]{2,1,0:T(8,128)(...) custom-call(s32[2]{0:T(128)} %pad_add_fusion.where_ref, ...), custom_call_target="tpu_custom_call" | custom-call | flops 1 | bytes 1 | tf_op jit(solution)/shard_map/dispatch/pallas_call | solution.py:112
  7.6 4.1 %collective-permute-start.1 = (bf16[2,32,2048]{2,1,0:T(8,128)(2,1)}, bf16[2,32,2048]{2,1,0:T(8,128)(2,1)S(1)}, u32[]{:S(2)}, u32[]{:S(2)}) collective-permute-start(bf16[2,32,2048]{2,1,0:T(8,128)(2,1)} %get-tuple-element.108), channel_id=1, source_target_pairs={{0,4},{2,6},{4,0},{6,2},{8,12},{10,14},{12,8},{14,10},{16,20},{18,... | collective-permute-start | bytes 786440 | tf_op jit(solution)/shard_map/ppermute | solution.py:58
  13.2 17.0 %collective-permute-done.1.refs_2_ = bf16[2,32,2048]{2,1,0:T(8,128)(2,1)S(1)} collective-permute-done((bf16[2,32,2048]{2,1,0:T(8,128)(2,1)}, bf16[2,32,2048]{2,1,0:T(8,128)(2,1)S(1)}, u32[]{:S(2)}, u32[]{:S(2)}) %collective-permute-start.1) | collective-permute-done | bytes 262176 | tf_op jit(solution)/shard_map/ppermute | solution.py:58
  30.2 4.1 %collective-permute-start.8 = (bf16[2,32,2048]{2,1,0:T(8,128)(2,1)}, bf16[2,32,2048]{2,1,0:T(8,128)(2,1)S(1)}, u32[]{:S(2)}, u32[]{:S(2)}) collective-permute-start(bf16[2,32,2048]{2,1,0:T(8,128)(2,1)} %get-tuple-element.117), channel_id=1, source_target_pairs={{0,14},{2,12},{4,10},{6,8},{8,6},{10,4},{12,2},{14,0},{16,30},{18,... | collective-permute-start | bytes 786440 | tf_op jit(solution)/shard_map/ppermute | solution.py:58
  34.3 10.3 %collective-permute-start.7 = (bf16[2,32,2048]{2,1,0:T(8,128)(2,1)}, bf16[2,32,2048]{2,1,0:T(8,128)(2,1)S(1)}, u32[]{:S(2)}, u32[]{:S(2)}) collective-permute-start(bf16[2,32,2048]{2,1,0:T(8,128)(2,1)} %get-tuple-element.115), channel_id=1, source_target_pairs={{0,12},{2,14},{4,8},{6,10},{8,4},{10,6},{12,0},{14,2},{16,28},{18,... | collective-permute-start | bytes 786440 | tf_op jit(solution)/shard_map/ppermute | solution.py:58
  46.7 19.1 %collective-permute-done.7.refs_6_ = bf16[2,32,2048]{2,1,0:T(8,128)(2,1)S(1)} collective-permute-done((bf16[2,32,2048]{2,1,0:T(8,128)(2,1)}, bf16[2,32,2048]{2,1,0:T(8,128)(2,1)S(1)}, u32[]{:S(2)}, u32[]{:S(2)}) %collective-permute-start.7) | collective-permute-done | bytes 262176 | tf_op jit(solution)/shard_map/ppermute | solution.py:58
  65.8 2.9 %collective-permute-start.12 = (bf16[2,32,2048]{2,1,0:T(8,128)(2,1)}, bf16[2,32,2048]{2,1,0:T(8,128)(2,1)S(1)}, u32[]{:S(2)}, u32[]{:S(2)}) collective-permute-start(bf16[2,32,2048]{2,1,0:T(8,128)(2,1)} %get-tuple-element.131), channel_id=1, source_target_pairs={{0,18},{2,16},{4,22},{6,20},{8,26},{10,24},{12,30},{14,28},{16,2},... | collective-permute-start | bytes 786440 | tf_op jit(solution)/shard_map/ppermute | solution.py:58
  68.7 3.3 %collective-permute-start.9 = (bf16[2,32,2048]{2,1,0:T(8,128)(2,1)}, bf16[2,32,2048]{2,1,0:T(8,128)(2,1)S(1)}, u32[]{:S(2)}, u32[]{:S(2)}) collective-permute-start(bf16[2,32,2048]{2,1,0:T(8,128)(2,1)} %get-tuple-element.125), channel_id=1, source_target_pairs={{0,20},{2,22},{4,16},{6,18},{8,28},{10,30},{12,24},{14,26},{16,4},... | collective-permute-start | bytes 786440 | tf_op jit(solution)/shard_map/ppermute | solution.py:58
  72.0 3.9 %collective-permute-start.10 = (bf16[2,32,2048]{2,1,0:T(8,128)(2,1)}, bf16[2,32,2048]{2,1,0:T(8,128)(2,1)S(1)}, u32[]{:S(2)}, u32[]{:S(2)}) collective-permute-start(bf16[2,32,2048]{2,1,0:T(8,128)(2,1)} %get-tuple-element.127), channel_id=1, source_target_pairs={{0,28},{2,30},{4,24},{6,26},{8,20},{10,22},{12,16},{14,18},{16,12}... | collective-permute-start | bytes 786440 | tf_op jit(solution)/shard_map/ppermute | solution.py:58
  76.1 11.0 %expert.2 = (bf16[2,32,2048]{2,1,0:T(8,128)(2,1)}, bf16[2,32,2048]{2,1,0:T(8,128)(2,1)}, bf16[2,32,2048]{2,1,0:T(8,128)(2,1)}, bf16[2,32,2048]{2,1,0:T(8,128)(2,...) custom-call(bf16[2,32,2048]{2,1,0:T(8,128)(2,1)} %get-tuple-element., ...), custom_call_target="tpu_custom_call" | custom-call | flops 4831838208 | bytes 12079595 | tf_op jit(solution)/shard_map/expert/pallas_call | solution.py:180
  87.0 18.1 %collective-permute-done.9.refs_2_ = bf16[2,32,2048]{2,1,0:T(8,128)(2,1)S(1)} collective-permute-done((bf16[2,32,2048]{2,1,0:T(8,128)(2,1)}, bf16[2,32,2048]{2,1,0:T(8,128)(2,1)S(1)}, u32[]{:S(2)}, u32[]{:S(2)}) %collective-permute-start.9) | collective-permute-done | bytes 262176 | tf_op jit(solution)/shard_map/ppermute | solution.py:58
  105.1 9.7 %collective-permute-start.11 = (bf16[2,32,2048]{2,1,0:T(8,128)(2,1)S(1)}, bf16[2,32,2048]{2,1,0:T(8,128)(2,1)S(1)}, u32[]{:S(2)}, u32[]{:S(2)}) collective-permute-start(bf16[2,32,2048]{2,1,0:T(8,128)(2,1)S(1)} %copy-done.22), channel_id=1, source_target_pairs={{0,30},{2,28},{4,26},{6,24},{8,22},{10,20},{12,18},{14,16},{16,14}... | collective-permute-start | bytes 786440 | tf_op jit(solution)/shard_map/ppermute | solution.py:58
  117.0 4.6 %collective-permute-done.11.refs_7_ = bf16[2,32,2048]{2,1,0:T(8,128)(2,1)S(1)} collective-permute-done((bf16[2,32,2048]{2,1,0:T(8,128)(2,1)S(1)}, bf16[2,32,2048]{2,1,0:T(8,128)(2,1)S(1)}, u32[]{:S(2)}, u32[]{:S(2)}) %collective-permute-start.11) | collective-permute-done | bytes 262176 | tf_op jit(solution)/shard_map/ppermute | solution.py:58
  121.5 6.8 %collective-permute-start.20 = (bf16[2,32,2048]{2,1,0:T(8,128)(2,1)}, bf16[2,32,2048]{2,1,0:T(8,128)(2,1)S(1)}, u32[]{:S(2)}, u32[]{:S(2)}) collective-permute-start(bf16[2,32,2048]{2,1,0:T(8,128)(2,1)} %get-tuple-element.147), channel_id=1, source_target_pairs={{0,12},{2,14},{4,8},{6,10},{8,4},{10,6},{12,0},{14,2},{16,28},{18,... | collective-permute-start | bytes 786440 | tf_op jit(solution)/shard_map/ppermute | solution.py:58
  128.4 4.2 %collective-permute-done.13.refs_0_ = bf16[2,32,2048]{2,1,0:T(8,128)(2,1)S(1)} collective-permute-done((bf16[2,32,2048]{2,1,0:T(8,128)(2,1)S(1)}, bf16[2,32,2048]{2,1,0:T(8,128)(2,1)S(1)}, u32[]{:S(2)}, u32[]{:S(2)}) %collective-permute-start.13) | collective-permute-done | bytes 262176 | tf_op jit(solution)/shard_map/ppermute | solution.py:58
  133.4 10.9 %expert.3 = (bf16[2,32,2048]{2,1,0:T(8,128)(2,1)}, bf16[2,32,2048]{2,1,0:T(8,128)(2,1)}, bf16[2,32,2048]{2,1,0:T(8,128)(2,1)}, bf16[2,32,2048]{2,1,0:T(8,128)(2,...) custom-call(bf16[2,32,2048]{2,1,0:T(8,128)(2,1)} %copy-done.40, ...), custom_call_target="tpu_custom_call" | custom-call | flops 4831838208 | bytes 12079595 | tf_op jit(solution)/shard_map/expert/pallas_call | solution.py:180
  147.2 2.7 %collective-permute-start.23 = (bf16[2,32,2048]{2,1,0:T(8,128)(2,1)S(1)}, bf16[2,32,2048]{2,1,0:T(8,128)(2,1)S(1)}, u32[]{:S(2)}, u32[]{:S(2)}) collective-permute-start(bf16[2,32,2048]{2,1,0:T(8,128)(2,1)S(1)} %copy-done.27), channel_id=1, source_target_pairs={{0,14},{2,12},{4,10},{6,8},{8,6},{10,4},{12,2},{14,0},{16,30},{18,... | collective-permute-start | bytes 786440 | tf_op jit(solution)/shard_map/ppermute | solution.py:58
  154.1 8.2 %collective-permute-start.19 = (bf16[2,32,2048]{2,1,0:T(8,128)(2,1)S(1)}, bf16[2,32,2048]{2,1,0:T(8,128)(2,1)S(1)}, u32[]{:S(2)}, u32[]{:S(2)}) collective-permute-start(bf16[2,32,2048]{2,1,0:T(8,128)(2,1)S(1)} %copy-done.25), channel_id=1, source_target_pairs={{0,6},{2,4},{4,2},{6,0},{8,14},{10,12},{12,10},{14,8},{16,22},{18,... | collective-permute-start | bytes 786440 | tf_op jit(solution)/shard_map/ppermute | solution.py:58
  162.3 4.3 %collective-permute-done.21.refs_4_ = bf16[2,32,2048]{2,1,0:T(8,128)(2,1)S(1)} collective-permute-done((bf16[2,32,2048]{2,1,0:T(8,128)(2,1)S(1)}, bf16[2,32,2048]{2,1,0:T(8,128)(2,1)S(1)}, u32[]{:S(2)}, u32[]{:S(2)}) %collective-permute-start.21) | collective-permute-done | bytes 262176 | tf_op jit(solution)/shard_map/ppermute | solution.py:58
  168.6 2.3 collective-permute-done.22.refs_5_
  170.9 8.7 %collective-permute-start.25 = (bf16[2,32,2048]{2,1,0:T(8,128)(2,1)}, bf16[2,32,2048]{2,1,0:T(8,128)(2,1)S(1)}, u32[]{:S(2)}, u32[]{:S(2)}) collective-permute-start(bf16[2,32,2048]{2,1,0:T(8,128)(2,1)} %get-tuple-element.156), channel_id=1, source_target_pairs={{0,18},{2,16},{4,22},{6,20},{8,26},{10,24},{12,30},{14,28},{16,2},... | collective-permute-start | bytes 786440 | tf_op jit(solution)/shard_map/ppermute | solution.py:58
  180.2 6.9 %weight_grads.2 = bf16[1024,2304]{1,0:T(8,128)(2,1)} custom-call(bf16[256,768]{1,0:T(8,128)(2,1)} %get-tuple-element.166.refs_0_, bf16[256,768]{1,0:T(8,128)(2,1)} %get-tuple-element.159.refs_1_, bf16[256,1536]{1,0:T(8,128)(2,1)} %get-tuple-element.160.refs_2_, bf16[256,1536]{1,0:T(8,128)(2,1)} %get-tuple-element.161.refs_3_, ...), custom_call_target="tpu_custom_call" | custom-call | flops 2415919104 | bytes 6039797 | tf_op jit(solution)/shard_map/weight_grads/pallas_call | solution.py:216
  187.3 7.1 %weight_grads.3 = bf16[1024,2304]{1,0:T(8,128)(2,1)} custom-call(bf16[256,768]{1,0:T(8,128)(2,1)} %get-tuple-element.166.refs_0_, bf16[256,768]{1,0:T(8,128)(2,1)} %get-tuple-element.159.refs_1_, bf16[256,1536]{1,0:T(8,128)(2,1)} %get-tuple-element.160.refs_2_, bf16[256,1536]{1,0:T(8,128)(2,1)} %get-tuple-element.161.refs_3_, ...), custom_call_target="tpu_custom_call" | custom-call | flops 2415919104 | bytes 6039797 | tf_op jit(solution)/shard_map/weight_grads/pallas_call | solution.py:216
  196.5 3.9 %collective-permute-start.28 = (bf16[2,32,2048]{2,1,0:T(8,128)(2,1)}, bf16[2,32,2048]{2,1,0:T(8,128)(2,1)S(1)}, u32[]{:S(2)}, u32[]{:S(2)}) collective-permute-start(bf16[2,32,2048]{2,1,0:T(8,128)(2,1)} %get-tuple-element.171), channel_id=1, source_target_pairs={{0,20},{2,22},{4,16},{6,18},{8,28},{10,30},{12,24},{14,26},{16,4},... | collective-permute-start | bytes 786440 | tf_op jit(solution)/shard_map/ppermute | solution.py:58
  201.7 11.6 %collective-permute-done.28.refs_10_ = bf16[2,32,2048]{2,1,0:T(8,128)(2,1)S(1)} collective-permute-done((bf16[2,32,2048]{2,1,0:T(8,128)(2,1)}, bf16[2,32,2048]{2,1,0:T(8,128)(2,1)S(1)}, u32[]{:S(2)}, u32[]{:S(2)}) %collective-permute-start.28) | collective-permute-done | bytes 262176 | tf_op jit(solution)/shard_map/ppermute | solution.py:58
  213.2 2.6 %collective-permute-start.31 = (bf16[2,32,2048]{2,1,0:T(8,128)(2,1)}, bf16[2,32,2048]{2,1,0:T(8,128)(2,1)S(1)}, u32[]{:S(2)}, u32[]{:S(2)}) collective-permute-start(bf16[2,32,2048]{2,1,0:T(8,128)(2,1)} %get-tuple-element.179), channel_id=1, source_target_pairs={{0,30},{2,28},{4,26},{6,24},{8,22},{10,20},{12,18},{14,16},{16,14}... | collective-permute-start | bytes 786440 | tf_op jit(solution)/shard_map/ppermute | solution.py:58
  217.3 3.3 %collective-permute-start.26 = (bf16[2,32,2048]{2,1,0:T(8,128)(2,1)S(1)}, bf16[2,32,2048]{2,1,0:T(8,128)(2,1)S(1)}, u32[]{:S(2)}, u32[]{:S(2)}) collective-permute-start(bf16[2,32,2048]{2,1,0:T(8,128)(2,1)S(1)} %copy-done.21), channel_id=1, source_target_pairs={{0,16},{2,18},{4,20},{6,22},{8,24},{10,26},{12,28},{14,30},{16,0},... | collective-permute-start | bytes 786440 | tf_op jit(solution)/shard_map/ppermute | solution.py:58
  220.6 6.5 %convert_add_fusion = f32[1024,1536]{1,0:T(8,128)} fusion(bf16[1024,2304]{1,0:T(8,128)(2,1)} %collective-permute-done.32, bf16[1024,2304]{1,0:T(8,128)(2,1)} %weight_grads.3), kind=kLoop, calls=%fused_computation | loop fusion | flops 4718592 | bytes 12582912 | tf_op jit(solution)/shard_map/add | solution.py:333
  227.1 3.9 %convert_add_fusion.1 = f32[1024,768]{1,0:T(8,128)} fusion(bf16[1024,2304]{1,0:T(8,128)(2,1)} %collective-permute-done.32, bf16[1024,2304]{1,0:T(8,128)(2,1)} %weight_grads.3), kind=kLoop, calls=%fused_computation.1 | loop fusion | flops 2359296 | bytes 6291456 | tf_op jit(solution)/shard_map/add | solution.py:333
  231.0 3.7 %collective-permute-done.29.refs_12_ = bf16[2,32,2048]{2,1,0:T(8,128)(2,1)S(1)} collective-permute-done((bf16[2,32,2048]{2,1,0:T(8,128)(2,1)}, bf16[2,32,2048]{2,1,0:T(8,128)(2,1)S(1)}, u32[]{:S(2)}, u32[]{:S(2)}) %collective-permute-start.29) | collective-permute-done | bytes 262176 | tf_op jit(solution)/shard_map/ppermute | solution.py:58
  234.7 5.5 %collective-permute-done.26.refs_8_ = bf16[2,32,2048]{2,1,0:T(8,128)(2,1)S(1)} collective-permute-done((bf16[2,32,2048]{2,1,0:T(8,128)(2,1)S(1)}, bf16[2,32,2048]{2,1,0:T(8,128)(2,1)S(1)}, u32[]{:S(2)}, u32[]{:S(2)}) %collective-permute-start.26) | collective-permute-done | bytes 262176 | tf_op jit(solution)/shard_map/ppermute | solution.py:58
  240.9 6.2 %combine.1 = (bf16[256,2048]{1,0:T(8,128)(2,1)}, bf16[256,2048]{1,0:T(8,128)(2,1)}, f32[8,256]{1,0:T(8,128)}) custom-call(s32[2]{0:T(128)} %pad_add_fusion.where_ref, bf16[512,256]{1,0:T(8,128)(2,1)} %get-tuple-element.104.pick_ref, bf16[256,512]{1,0:T(8,128)(2,1)} %bitcast.16, bf16[256,512]{1,0:T(8,128)(2,1)} %get-tuple-element.204.high_ref, ...), custom_call_target="tpu_custom_call" | custom-call | flops 1 | bytes 1 | tf_op jit(solution)/shard_map/combine/pallas_call | solution.py:264
  (132 shorter events, 23.1 us)
Async XLA Ops:
  0.6 44.0 %collective-permute-start.3 = (bf16[1024,1536]{1,0:T(8,128)(2,1)}, bf16[1024,1536]{1,0:T(8,128)(2,1)S(1)}, u32[]{:S(2)}, u32[]{:S(2)}) collective-permute-start(bf16[1024,1536]{1,0:T(8,128)(2,1)} %bitcast.20), channel_id=1, source_target_pairs={{1,0},{0,1},{3,2},{2,3},{5,4},{4,5},{7,6},{6,7},{9,8},{8,9},{11,10... | collective-permute-start | bytes 9437192 | tf_op jit(solution)/shard_map/ppermute | solution.py:45
  1.1 43.4 %collective-permute-start.4 = (bf16[1024,768]{1,0:T(8,128)(2,1)}, bf16[1024,768]{1,0:T(8,128)(2,1)}, u32[]{:S(2)}, u32[]{:S(2)}) collective-permute-start(bf16[1024,768]{1,0:T(8,128)(2,1)} %bitcast.23), channel_id=1, source_target_pairs={{1,0},{0,1},{3,2},{2,3},{5,4},{4,5},{7,6},{6,7},{9,8},{8,9},{11,10... | collective-permute-start | bytes 4718600 | tf_op jit(solution)/shard_map/ppermute | solution.py:45
  7.6 22.7 %collective-permute-start.1 = (bf16[2,32,2048]{2,1,0:T(8,128)(2,1)}, bf16[2,32,2048]{2,1,0:T(8,128)(2,1)S(1)}, u32[]{:S(2)}, u32[]{:S(2)}) collective-permute-start(bf16[2,32,2048]{2,1,0:T(8,128)(2,1)} %get-tuple-element.108), channel_id=1, source_target_pairs={{0,4},{2,6},{4,0},{6,2},{8,12},{10,14},{12,8},{14,10},{16,20},{18,... | collective-permute-start | bytes 786440 | tf_op jit(solution)/shard_map/ppermute | solution.py:58
  11.6 18.6 %collective-permute-start.2 = (bf16[2,32,2048]{2,1,0:T(8,128)(2,1)}, bf16[2,32,2048]{2,1,0:T(8,128)(2,1)S(1)}, u32[]{:S(2)}, u32[]{:S(2)}) collective-permute-start(bf16[2,32,2048]{2,1,0:T(8,128)(2,1)} %get-tuple-element.109), channel_id=1, source_target_pairs={{0,6},{2,4},{4,2},{6,0},{8,14},{10,12},{12,10},{14,8},{16,22},{18,... | collective-permute-start | bytes 786440 | tf_op jit(solution)/shard_map/ppermute | solution.py:58
  13.0 21.3 %collective-permute-start = (bf16[2,32,2048]{2,1,0:T(8,128)(2,1)}, bf16[2,32,2048]{2,1,0:T(8,128)(2,1)S(1)}, u32[]{:S(2)}, u32[]{:S(2)}) collective-permute-start(bf16[2,32,2048]{2,1,0:T(8,128)(2,1)} %get-tuple-element.107), channel_id=1, source_target_pairs={{0,2},{2,0},{4,6},{6,4},{8,10},{10,8},{12,14},{14,12},{16,18},{18,... | collective-permute-start | bytes 786440 | tf_op jit(solution)/shard_map/ppermute | solution.py:58
  30.2 16.4 %collective-permute-start.8 = (bf16[2,32,2048]{2,1,0:T(8,128)(2,1)}, bf16[2,32,2048]{2,1,0:T(8,128)(2,1)S(1)}, u32[]{:S(2)}, u32[]{:S(2)}) collective-permute-start(bf16[2,32,2048]{2,1,0:T(8,128)(2,1)} %get-tuple-element.117), channel_id=1, source_target_pairs={{0,14},{2,12},{4,10},{6,8},{8,6},{10,4},{12,2},{14,0},{16,30},{18,... | collective-permute-start | bytes 786440 | tf_op jit(solution)/shard_map/ppermute | solution.py:58
  34.3 31.5 %collective-permute-start.7 = (bf16[2,32,2048]{2,1,0:T(8,128)(2,1)}, bf16[2,32,2048]{2,1,0:T(8,128)(2,1)S(1)}, u32[]{:S(2)}, u32[]{:S(2)}) collective-permute-start(bf16[2,32,2048]{2,1,0:T(8,128)(2,1)} %get-tuple-element.115), channel_id=1, source_target_pairs={{0,12},{2,14},{4,8},{6,10},{8,4},{10,6},{12,0},{14,2},{16,28},{18,... | collective-permute-start | bytes 786440 | tf_op jit(solution)/shard_map/ppermute | solution.py:58
  44.6 21.2 %collective-permute-start.6 = (bf16[2,32,2048]{2,1,0:T(8,128)(2,1)}, bf16[2,32,2048]{2,1,0:T(8,128)(2,1)S(1)}, u32[]{:S(2)}, u32[]{:S(2)}) collective-permute-start(bf16[2,32,2048]{2,1,0:T(8,128)(2,1)} %get-tuple-element.113), channel_id=1, source_target_pairs={{0,10},{2,8},{4,14},{6,12},{8,2},{10,0},{12,6},{14,4},{16,26},{18,... | collective-permute-start | bytes 786440 | tf_op jit(solution)/shard_map/ppermute | solution.py:58
  44.6 24.1 %collective-permute-start.5 = (bf16[2,32,2048]{2,1,0:T(8,128)(2,1)}, bf16[2,32,2048]{2,1,0:T(8,128)(2,1)S(1)}, u32[]{:S(2)}, u32[]{:S(2)}) collective-permute-start(bf16[2,32,2048]{2,1,0:T(8,128)(2,1)} %get-tuple-element.111), channel_id=1, source_target_pairs={{0,8},{2,10},{4,12},{6,14},{8,0},{10,2},{12,4},{14,6},{16,24},{18,... | collective-permute-start | bytes 786440 | tf_op jit(solution)/shard_map/ppermute | solution.py:58
  65.8 51.1 %collective-permute-start.15 = (bf16[2,32,2048]{2,1,0:T(8,128)(2,1)}, bf16[2,32,2048]{2,1,0:T(8,128)(2,1)S(1)}, u32[]{:S(2)}, u32[]{:S(2)}) collective-permute-start(bf16[2,32,2048]{2,1,0:T(8,128)(2,1)} %get-tuple-element.136), channel_id=1, source_target_pairs={{0,22},{2,20},{4,18},{6,16},{8,30},{10,28},{12,26},{14,24},{16,6},... | collective-permute-start | bytes 786440 | tf_op jit(solution)/shard_map/ppermute | solution.py:58
  65.8 49.0 %collective-permute-start.12 = (bf16[2,32,2048]{2,1,0:T(8,128)(2,1)}, bf16[2,32,2048]{2,1,0:T(8,128)(2,1)S(1)}, u32[]{:S(2)}, u32[]{:S(2)}) collective-permute-start(bf16[2,32,2048]{2,1,0:T(8,128)(2,1)} %get-tuple-element.131), channel_id=1, source_target_pairs={{0,18},{2,16},{4,22},{6,20},{8,26},{10,24},{12,30},{14,28},{16,2},... | collective-permute-start | bytes 786440 | tf_op jit(solution)/shard_map/ppermute | solution.py:58
  68.7 36.4 %collective-permute-start.9 = (bf16[2,32,2048]{2,1,0:T(8,128)(2,1)}, bf16[2,32,2048]{2,1,0:T(8,128)(2,1)S(1)}, u32[]{:S(2)}, u32[]{:S(2)}) collective-permute-start(bf16[2,32,2048]{2,1,0:T(8,128)(2,1)} %get-tuple-element.125), channel_id=1, source_target_pairs={{0,20},{2,22},{4,16},{6,18},{8,28},{10,30},{12,24},{14,26},{16,4},... | collective-permute-start | bytes 786440 | tf_op jit(solution)/shard_map/ppermute | solution.py:58
  72.0 33.1 %collective-permute-start.10 = (bf16[2,32,2048]{2,1,0:T(8,128)(2,1)}, bf16[2,32,2048]{2,1,0:T(8,128)(2,1)S(1)}, u32[]{:S(2)}, u32[]{:S(2)}) collective-permute-start(bf16[2,32,2048]{2,1,0:T(8,128)(2,1)} %get-tuple-element.127), channel_id=1, source_target_pairs={{0,28},{2,30},{4,24},{6,26},{8,20},{10,22},{12,16},{14,18},{16,12}... | collective-permute-start | bytes 786440 | tf_op jit(solution)/shard_map/ppermute | solution.py:58
  105.1 11.8 %collective-permute-start.16 = (bf16[2,32,2048]{2,1,0:T(8,128)(2,1)S(1)}, bf16[2,32,2048]{2,1,0:T(8,128)(2,1)S(1)}, u32[]{:S(2)}, u32[]{:S(2)}) collective-permute-start(bf16[2,32,2048]{2,1,0:T(8,128)(2,1)S(1)} %copy-done.24), channel_id=1, source_target_pairs={{0,26},{2,24},{4,30},{6,28},{8,18},{10,16},{12,22},{14,20},{16,10}... | collective-permute-start | bytes 786440 | tf_op jit(solution)/shard_map/ppermute | solution.py:58
  105.1 16.4 %collective-permute-start.11 = (bf16[2,32,2048]{2,1,0:T(8,128)(2,1)S(1)}, bf16[2,32,2048]{2,1,0:T(8,128)(2,1)S(1)}, u32[]{:S(2)}, u32[]{:S(2)}) collective-permute-start(bf16[2,32,2048]{2,1,0:T(8,128)(2,1)S(1)} %copy-done.22), channel_id=1, source_target_pairs={{0,30},{2,28},{4,26},{6,24},{8,22},{10,20},{12,18},{14,16},{16,14}... | collective-permute-start | bytes 786440 | tf_op jit(solution)/shard_map/ppermute | solution.py:58
  114.8 17.7 %collective-permute-start.13 = (bf16[2,32,2048]{2,1,0:T(8,128)(2,1)S(1)}, bf16[2,32,2048]{2,1,0:T(8,128)(2,1)S(1)}, u32[]{:S(2)}, u32[]{:S(2)}) collective-permute-start(bf16[2,32,2048]{2,1,0:T(8,128)(2,1)S(1)} %copy-done.20), channel_id=1, source_target_pairs={{0,16},{2,18},{4,20},{6,22},{8,24},{10,26},{12,28},{14,30},{16,0},... | collective-permute-start | bytes 786440 | tf_op jit(solution)/shard_map/ppermute | solution.py:58
  116.9 15.7 %collective-permute-start.18 = (bf16[2,32,2048]{2,1,0:T(8,128)(2,1)S(1)}, bf16[2,32,2048]{2,1,0:T(8,128)(2,1)S(1)}, u32[]{:S(2)}, u32[]{:S(2)}) collective-permute-start(bf16[2,32,2048]{2,1,0:T(8,128)(2,1)S(1)} %copy-done.19), channel_id=1, source_target_pairs={{0,24},{2,26},{4,28},{6,30},{8,16},{10,18},{12,20},{14,22},{16,8},... | collective-permute-start | bytes 786440 | tf_op jit(solution)/shard_map/ppermute | solution.py:58
  121.5 24.6 %collective-permute-start.20 = (bf16[2,32,2048]{2,1,0:T(8,128)(2,1)}, bf16[2,32,2048]{2,1,0:T(8,128)(2,1)S(1)}, u32[]{:S(2)}, u32[]{:S(2)}) collective-permute-start(bf16[2,32,2048]{2,1,0:T(8,128)(2,1)} %get-tuple-element.147), channel_id=1, source_target_pairs={{0,12},{2,14},{4,8},{6,10},{8,4},{10,6},{12,0},{14,2},{16,28},{18,... | collective-permute-start | bytes 786440 | tf_op jit(solution)/shard_map/ppermute | solution.py:58
  128.4 18.8 %collective-permute-start.17 = (bf16[2,32,2048]{2,1,0:T(8,128)(2,1)}, bf16[2,32,2048]{2,1,0:T(8,128)(2,1)S(1)}, u32[]{:S(2)}, u32[]{:S(2)}) collective-permute-start(bf16[2,32,2048]{2,1,0:T(8,128)(2,1)} %get-tuple-element.139), channel_id=1, source_target_pairs={{0,4},{2,6},{4,0},{6,2},{8,12},{10,14},{12,8},{14,10},{16,20},{18,... | collective-permute-start | bytes 786440 | tf_op jit(solution)/shard_map/ppermute | solution.py:58
  132.6 19.6 %collective-permute-start.14 = (bf16[2,32,2048]{2,1,0:T(8,128)(2,1)}, bf16[2,32,2048]{2,1,0:T(8,128)(2,1)S(1)}, u32[]{:S(2)}, u32[]{:S(2)}) collective-permute-start(bf16[2,32,2048]{2,1,0:T(8,128)(2,1)} %get-tuple-element.133), channel_id=1, source_target_pairs={{0,2},{2,0},{4,6},{6,4},{8,10},{10,8},{12,14},{14,12},{16,18},{18,... | collective-permute-start | bytes 786440 | tf_op jit(solution)/shard_map/ppermute | solution.py:58
  147.2 15.1 %collective-permute-start.23 = (bf16[2,32,2048]{2,1,0:T(8,128)(2,1)S(1)}, bf16[2,32,2048]{2,1,0:T(8,128)(2,1)S(1)}, u32[]{:S(2)}, u32[]{:S(2)}) collective-permute-start(bf16[2,32,2048]{2,1,0:T(8,128)(2,1)S(1)} %copy-done.27), channel_id=1, source_target_pairs={{0,14},{2,12},{4,10},{6,8},{8,6},{10,4},{12,2},{14,0},{16,30},{18,... | collective-permute-start | bytes 786440 | tf_op jit(solution)/shard_map/ppermute | solution.py:58
  152.2 14.4 %collective-permute-start.21 = (bf16[2,32,2048]{2,1,0:T(8,128)(2,1)S(1)}, bf16[2,32,2048]{2,1,0:T(8,128)(2,1)S(1)}, u32[]{:S(2)}, u32[]{:S(2)}) collective-permute-start(bf16[2,32,2048]{2,1,0:T(8,128)(2,1)S(1)} %copy-done.26), channel_id=1, source_target_pairs={{0,8},{2,10},{4,12},{6,14},{8,0},{10,2},{12,4},{14,6},{16,24},{18,... | collective-permute-start | bytes 786440 | tf_op jit(solution)/shard_map/ppermute | solution.py:58
  154.1 14.6 %collective-permute-start.19 = (bf16[2,32,2048]{2,1,0:T(8,128)(2,1)S(1)}, bf16[2,32,2048]{2,1,0:T(8,128)(2,1)S(1)}, u32[]{:S(2)}, u32[]{:S(2)}) collective-permute-start(bf16[2,32,2048]{2,1,0:T(8,128)(2,1)S(1)} %copy-done.25), channel_id=1, source_target_pairs={{0,6},{2,4},{4,2},{6,0},{8,14},{10,12},{12,10},{14,8},{16,22},{18,... | collective-permute-start | bytes 786440 | tf_op jit(solution)/shard_map/ppermute | solution.py:58
  166.6 27.7 %collective-permute-start.27 = (bf16[2,32,2048]{2,1,0:T(8,128)(2,1)}, bf16[2,32,2048]{2,1,0:T(8,128)(2,1)S(1)}, u32[]{:S(2)}, u32[]{:S(2)}) collective-permute-start(bf16[2,32,2048]{2,1,0:T(8,128)(2,1)} %get-tuple-element.168), channel_id=1, source_target_pairs={{0,22},{2,20},{4,18},{6,16},{8,30},{10,28},{12,26},{14,24},{16,6},... | collective-permute-start | bytes 786440 | tf_op jit(solution)/shard_map/ppermute | solution.py:58
  170.9 23.4 %collective-permute-start.25 = (bf16[2,32,2048]{2,1,0:T(8,128)(2,1)}, bf16[2,32,2048]{2,1,0:T(8,128)(2,1)S(1)}, u32[]{:S(2)}, u32[]{:S(2)}) collective-permute-start(bf16[2,32,2048]{2,1,0:T(8,128)(2,1)} %get-tuple-element.156), channel_id=1, source_target_pairs={{0,18},{2,16},{4,22},{6,20},{8,26},{10,24},{12,30},{14,28},{16,2},... | collective-permute-start | bytes 786440 | tf_op jit(solution)/shard_map/ppermute | solution.py:58
  179.6 16.9 %collective-permute-start.24 = (bf16[2,32,2048]{2,1,0:T(8,128)(2,1)}, bf16[2,32,2048]{2,1,0:T(8,128)(2,1)S(1)}, u32[]{:S(2)}, u32[]{:S(2)}) collective-permute-start(bf16[2,32,2048]{2,1,0:T(8,128)(2,1)} %get-tuple-element.154), channel_id=1, source_target_pairs={{0,28},{2,30},{4,24},{6,26},{8,20},{10,22},{12,16},{14,18},{16,12}... | collective-permute-start | bytes 786440 | tf_op jit(solution)/shard_map/ppermute | solution.py:58
  196.5 24.1 %collective-permute-start.32 = (bf16[1024,2304]{1,0:T(8,128)(2,1)}, bf16[1024,2304]{1,0:T(8,128)(2,1)}, u32[]{:S(2)}, u32[]{:S(2)}) collective-permute-start(bf16[1024,2304]{1,0:T(8,128)(2,1)} %weight_grads.2), channel_id=1, source_target_pairs={{0,1},{1,0},{2,3},{3,2},{4,5},{5,4},{6,7},{7,6},{8,9},{9,8},{10,11... | collective-permute-start | bytes 14155784 | tf_op jit(solution)/shard_map/ppermute | solution.py:51
  196.5 16.7 %collective-permute-start.28 = (bf16[2,32,2048]{2,1,0:T(8,128)(2,1)}, bf16[2,32,2048]{2,1,0:T(8,128)(2,1)S(1)}, u32[]{:S(2)}, u32[]{:S(2)}) collective-permute-start(bf16[2,32,2048]{2,1,0:T(8,128)(2,1)} %get-tuple-element.171), channel_id=1, source_target_pairs={{0,20},{2,22},{4,16},{6,18},{8,28},{10,30},{12,24},{14,26},{16,4},... | collective-permute-start | bytes 786440 | tf_op jit(solution)/shard_map/ppermute | solution.py:58
  213.2 17.8 %collective-permute-start.30 = (bf16[2,32,2048]{2,1,0:T(8,128)(2,1)}, bf16[2,32,2048]{2,1,0:T(8,128)(2,1)S(1)}, u32[]{:S(2)}, u32[]{:S(2)}) collective-permute-start(bf16[2,32,2048]{2,1,0:T(8,128)(2,1)} %get-tuple-element.176), channel_id=1, source_target_pairs={{0,26},{2,24},{4,30},{6,28},{8,18},{10,16},{12,22},{14,20},{16,10}... | collective-permute-start | bytes 786440 | tf_op jit(solution)/shard_map/ppermute | solution.py:58
  213.2 17.8 %collective-permute-start.31 = (bf16[2,32,2048]{2,1,0:T(8,128)(2,1)}, bf16[2,32,2048]{2,1,0:T(8,128)(2,1)S(1)}, u32[]{:S(2)}, u32[]{:S(2)}) collective-permute-start(bf16[2,32,2048]{2,1,0:T(8,128)(2,1)} %get-tuple-element.179), channel_id=1, source_target_pairs={{0,30},{2,28},{4,26},{6,24},{8,22},{10,20},{12,18},{14,16},{16,14}... | collective-permute-start | bytes 786440 | tf_op jit(solution)/shard_map/ppermute | solution.py:58
  215.8 18.9 %collective-permute-start.29 = (bf16[2,32,2048]{2,1,0:T(8,128)(2,1)}, bf16[2,32,2048]{2,1,0:T(8,128)(2,1)S(1)}, u32[]{:S(2)}, u32[]{:S(2)}) collective-permute-start(bf16[2,32,2048]{2,1,0:T(8,128)(2,1)} %get-tuple-element.174), channel_id=1, source_target_pairs={{0,24},{2,26},{4,28},{6,30},{8,16},{10,18},{12,20},{14,22},{16,8},... | collective-permute-start | bytes 786440 | tf_op jit(solution)/shard_map/ppermute | solution.py:58
  217.3 22.9 %collective-permute-start.26 = (bf16[2,32,2048]{2,1,0:T(8,128)(2,1)S(1)}, bf16[2,32,2048]{2,1,0:T(8,128)(2,1)S(1)}, u32[]{:S(2)}, u32[]{:S(2)}) collective-permute-start(bf16[2,32,2048]{2,1,0:T(8,128)(2,1)S(1)} %copy-done.21), channel_id=1, source_target_pairs={{0,16},{2,18},{4,20},{6,22},{8,24},{10,26},{12,28},{14,30},{16,0},... | collective-permute-start | bytes 786440 | tf_op jit(solution)/shard_map/ppermute | solution.py:58
  (44 other events, 981.1 us)

commit v12 on v10

v12 whole, which is shorter than its diff:
```python
import jax
import jax.numpy as jnp
from jax import lax
from jax.experimental import pallas as pl
from jax.experimental.pallas import tpu as pltpu
from jax.sharding import PartitionSpec as P

EXP_DEV = 4
BF = jnp.bfloat16
F32 = jnp.float32
ROWS_IN = (((0,), (0,)), ((), ()))
COLS_IN = (((1,), (1,)), ((), ()))
LIMIT = 56 * 1024 * 1024
CHEAP = pl.CostEstimate(flops=1, bytes_accessed=1, transcendentals=0)
VMEM = pl.BlockSpec(memory_space=pltpu.VMEM)
SMEM = pl.BlockSpec(memory_space=pltpu.SMEM)


def call(kernel, name, cost=CHEAP, **more):
    return pl.pallas_call(
        kernel,
        compiler_params=pltpu.CompilerParams(vmem_limit_bytes=LIMIT),
        cost_estimate=cost,
        name=name,
        **more,
    )


def shape(*dims, kind=BF):
    return jax.ShapeDtypeStruct(dims, kind)


def after(value, *others):
    return lax.optimization_barrier((value, *others))[0]


def gathered(shard):
    count = lax.axis_size("edata")
    shards = [shard]
    for step in range(1, count):
        pairs = [((i + step) % count, i) for i in range(count)]
        shards.append(lax.ppermute(shard, "edata", pairs))
    return shards


def from_owner(piece, step):
    count = lax.axis_size("edata")
    return lax.ppermute(piece, "edata", [(i, (i + step) % count) for i in range(count)])


def over_planes(rows):
    planes = lax.axis_size("local")
    shaped = rows.reshape(planes, -1, rows.shape[-1])
    out = lax.all_to_all(shaped, "local", split_axis=0, concat_axis=0, tiled=True)
    return out.reshape(rows.shape)


def to_nodes(pieces):
    count = len(pieces)
    return [pieces[0]] + [
        lax.ppermute(pieces[d], "node", [(i, i ^ d) for i in range(count)]) for d in range(1, count)
    ]


def shard_at(s, turn, count, width):
    return pl.ds(pl.multiple_of((turn + s) % count * width, width), width)


def dispatch_x(where, numbers, ids_t, gates_t, tokens, nodes, planes, capacity):
    top, tok_rows = ids_t.shape
    model = tokens.shape[1]
    count = lax.axis_size("edata")
    width = model // count
    groups = nodes * planes
    slots = groups * capacity

    def kernel(where_ref, numbers_ref, ids_ref, gates_ref, x_ref, sent_ref, pick_ref, weight_ref):
        turn = where_ref[0]
        numbers = jnp.broadcast_to(numbers_ref[...], (groups, tok_rows))
        routed = jnp.zeros((groups, tok_rows), F32)
        weight = jnp.zeros((groups, tok_rows), F32)
        for k in range(top):
            chosen = ids_ref[k : k + 1, :] == numbers
            routed = jnp.where(chosen, 1.0, routed)
            weight += jnp.where(chosen, gates_ref[k : k + 1, :], 0.0)
        first = lax.broadcasted_iota(jnp.int32, (tok_rows, tok_rows), 0)
        second = lax.broadcasted_iota(jnp.int32, (tok_rows, tok_rows), 1)
        earlier = jnp.where(first < second, 1.0, 0.0).astype(BF)
        order = jnp.dot(routed.astype(BF), earlier, preferred_element_type=F32)
        order = jnp.where(routed > 0.0, order, -1.0)
        places = lax.broadcasted_iota(jnp.int32, (capacity, tok_rows), 0).astype(F32)
        for g in range(groups):
            hits = order[g : g + 1, :] == places
            here = slice(g * capacity, (g + 1) * capacity)
            pick_ref[here] = jnp.where(hits, 1.0, 0.0).astype(BF)
            weight_ref[here] = jnp.sum(
                jnp.where(hits, weight[g : g + 1, :], 0.0), axis=1, keepdims=True
            )
        for s in range(count):
            source = shard_at(s, turn, count, width)
            x = jnp.dot(pick_ref[...], x_ref[:, source], preferred_element_type=F32).astype(BF)
            sent_ref[:, :, :, s * width : (s + 1) * width] = x.reshape(
                planes, nodes, capacity, width
            )

    return call(
        kernel,
        "dispatch_x",
        in_specs=[SMEM] + [VMEM] * 4,
        out_specs=[VMEM] * 3,
        out_shape=[
            shape(planes, nodes, capacity, model),
            shape(slots, tok_rows),
            shape(slots, 1, kind=F32),
        ],
    )(where, numbers, ids_t, gates_t, tokens)


def dispatch_dy(where, pick, weight, out_grad, nodes, planes, capacity):
    slots, tok_rows = pick.shape
    model = out_grad.shape[1]
    count = lax.axis_size("edata")
    width = model // count

    def kernel(where_ref, pick_ref, weight_ref, grad_ref, sent_ref, rows_ref):
        turn = where_ref[0]
        for s in range(count):
            source = shard_at(s, turn, count, width)
            here = slice(s * width, (s + 1) * width)
            rows = jnp.dot(pick_ref[...], grad_ref[:, source], preferred_element_type=F32)
            rows_ref[:, here] = rows.astype(BF)
            sent_ref[:, :, :, here] = (
                (weight_ref[...] * rows).astype(BF).reshape(planes, nodes, capacity, width)
            )

    return call(
        kernel,
        "dispatch_dy",
        in_specs=[SMEM] + [VMEM] * 3,
        out_specs=[VMEM] * 2,
        out_shape=[shape(planes, nodes, capacity, model), shape(slots, model)],
    )(where, pick, weight, out_grad)


def split(rows):
    return [rows[:, d] for d in range(rows.shape[1])]


def pack(pieces):
    count = len(pieces)
    planes, capacity, width = pieces[0].shape
    tile = min(1024, width)

    def kernel(*refs):
        for d in range(count):
            refs[-1][:, d] = refs[d][...]

    return call(
        kernel,
        "pack",
        grid=(width // tile,),
        in_specs=[pl.BlockSpec((planes, capacity, tile), lambda i: (0, 0, i))] * count,
        out_specs=pl.BlockSpec((planes, count, capacity, tile), lambda i: (0, 0, 0, i)),
        out_shape=shape(planes, count, capacity, width),
    )(*pieces)


def product(left, weights):
    width = weights[0].shape[0]
    total = None
    for s, shard in enumerate(weights):
        one = jnp.dot(
            left[:, s * width : (s + 1) * width], shard[...], preferred_element_type=F32
        )
        total = one if total is None else total + one
    return total


def expert_forward(pieces, w_ins, w_outs):
    planes, capacity, model = pieces[0].shape
    nodes, count = len(pieces), len(w_ins)
    width = model // count
    double, hidden = w_ins[0].shape[1], w_outs[0].shape[1]
    size = planes * capacity
    band = min(2, nodes)

    def kernel(*refs):
        got, refs = refs[:nodes], refs[nodes:]
        ins, outs, refs = refs[:count], refs[count : 2 * count], refs[2 * count :]
        y_refs, (act_ref, inner_ref) = refs[:nodes], refs[nodes:]
        for first in range(0, nodes, band):
            here = slice(first * size, (first + band) * size)
            x = jnp.concatenate(
                [got[first + i][...].reshape(size, model) for i in range(band)], axis=0
            )
            act_ref[here] = product(x, ins)
            act_gate = act_ref[here, :hidden]
            inner_ref[here] = (act_gate * jax.nn.sigmoid(act_gate) * act_ref[here, hidden:]).astype(
                BF
            )
            for s in range(count):
                y = lax.dot_general(
                    inner_ref[here], outs[s][...], COLS_IN, preferred_element_type=F32
                ).astype(BF)
                for i in range(band):
                    part = y[i * size : (i + 1) * size].reshape(planes, capacity, width)
                    y_refs[first + i][:, :, s * width : (s + 1) * width] = part

    operands = (*pieces, *w_ins, *w_outs)
    results = call(
        kernel,
        "expert_forward",
        in_specs=[VMEM] * len(operands),
        out_specs=[VMEM] * (nodes + 2),
        out_shape=[
            *[shape(planes, capacity, model)] * nodes,
            shape(nodes * size, double, kind=F32),
            shape(nodes * size, hidden),
        ],
    )(*operands)
    return list(results[:nodes]), *results[nodes:]


def expert_backward(pieces, act, w_ins, w_outs):
    planes, capacity, model = pieces[0].shape
    nodes, count = len(pieces), len(w_ins)
    width = model // count
    double, hidden = w_ins[0].shape[1], w_outs[0].shape[1]
    size = planes * capacity
    band = min(2, nodes)

    def kernel(*refs):
        got, act_ref, refs = refs[:nodes], refs[nodes], refs[nodes + 1 :]
        ins, outs, refs = refs[:count], refs[count : 2 * count], refs[2 * count :]
        dx_refs, act_grad_ref = refs[:nodes], refs[nodes]
        for first in range(0, nodes, band):
            here = slice(first * size, (first + band) * size)
            dy = jnp.concatenate(
                [got[first + i][...].reshape(size, model) for i in range(band)], axis=0
            )
            inner_grad = product(dy, outs)
            act_gate = act_ref[here, :hidden]
            act_up = act_ref[here, hidden:]
            sig = jax.nn.sigmoid(act_gate)
            act_grad_ref[here, :hidden] = (
                inner_grad * act_up * sig * (1.0 + act_gate * (1.0 - sig))
            ).astype(BF)
            act_grad_ref[here, hidden:] = (inner_grad * (act_gate * sig)).astype(BF)
            for s in range(count):
                dx = lax.dot_general(
                    act_grad_ref[here], ins[s][...], COLS_IN, preferred_element_type=F32
                ).astype(BF)
                for i in range(band):
                    part = dx[i * size : (i + 1) * size].reshape(planes, capacity, width)
                    dx_refs[first + i][:, :, s * width : (s + 1) * width] = part

    operands = (*pieces, act, *w_ins, *w_outs)
    results = call(
        kernel,
        "expert_backward",
        in_specs=[VMEM] * len(operands),
        out_specs=[VMEM] * (nodes + 1),
        out_shape=[
            *[shape(planes, capacity, model)] * nodes,
            shape(nodes * size, double),
        ],
    )(*operands)
    return list(results[:nodes]), results[nodes]


def weight_grads(shard, xs, dys, inner, act_grad):
    nodes = len(xs)
    planes, capacity, model = xs[0].shape
    rows = planes * capacity
    hidden, double = inner.shape[1], act_grad.shape[1]
    size = model // lax.axis_size("edata")
    tile = min(256, size)
    steps = size // tile

    def kernel(*refs):
        x_refs, dy_refs, (inner_ref, act_grad_ref, out_ref) = (
            refs[:nodes],
            refs[nodes : 2 * nodes],
            refs[2 * nodes :],
        )
        for lefts, right, columns in (
            (x_refs, act_grad_ref, slice(0, double)),
            (dy_refs, inner_ref, slice(double, None)),
        ):
            left = jnp.concatenate([r[...].reshape(rows, tile) for r in lefts], axis=0)
            out_ref[:, columns] = lax.dot_general(
                left, right[...], ROWS_IN, preferred_element_type=F32
            ).astype(BF)

    tall = pl.BlockSpec((planes, capacity, tile), lambda i: (0, 0, shard * steps + i))
    return call(
        kernel,
        "weight_grads",
        grid=(steps,),
        in_specs=[tall] * (2 * nodes)
        + [
            pl.BlockSpec(inner.shape, lambda i: (0, 0)),
            pl.BlockSpec(act_grad.shape, lambda i: (0, 0)),
        ],
        out_specs=pl.BlockSpec((tile, double + hidden), lambda i: (i, 0)),
        out_shape=shape(size, double + hidden),
    )(*xs, *dys, inner, act_grad)


def combine_y(where, numbers, picks, ids_t, grad_rows, rows):
    pick, high_t, middle_t = picks
    slots, tok_rows = pick.shape
    planes, nodes, capacity, model = rows.shape
    groups = planes * nodes
    count = lax.axis_size("edata")
    width = model // count

    def kernel(where_ref, number_ref, pick_ref, high_ref, middle_ref, ids_ref, grad_ref, *refs):
        y_ref, mixed_ref, gate_grad_ref = refs
        turn = where_ref[0]
        dots = jnp.zeros((slots, 1), F32)
        for s in range(count):
            here = slice(s * width, (s + 1) * width)
            y = y_ref[:, :, :, here].reshape(slots, width)
            mixed_ref[:, shard_at(s, turn, count, width)] = (
                jnp.dot(high_ref[...], y, preferred_element_type=F32)
                + jnp.dot(middle_ref[...], y, preferred_element_type=F32)
            ).astype(BF)
            dots += jnp.sum(
                y.astype(F32) * grad_ref[:, here].astype(F32), axis=1, keepdims=True
            )
        by_token = pick_ref[...].astype(F32) * dots
        by_token = jnp.sum(by_token.reshape(groups, capacity, tok_rows), axis=1)
        ids = ids_ref[...]
        total = jnp.zeros(ids.shape, F32)
        for g in range(groups):
            total += jnp.where(ids == number_ref[g], by_token[g : g + 1], 0.0)
        gate_grad_ref[...] = total

    return call(
        kernel,
        "combine_y",
        in_specs=[SMEM, SMEM] + [VMEM] * 6,
        out_specs=[VMEM] * 2,
        out_shape=[shape(tok_rows, model), shape(*ids_t.shape, kind=F32)],
    )(where, numbers, pick, high_t, middle_t, ids_t, grad_rows, rows)


def combine_dx(where, pick_t, rows):
    tok_rows, slots = pick_t.shape
    planes, nodes, capacity, model = rows.shape
    count = lax.axis_size("edata")
    tile = min(512, model // count)
    steps = model // tile

    def kernel(where_ref, pick_ref, rows_ref, out_ref):
        out_ref[...] = jnp.dot(
            pick_ref[...], rows_ref[...].reshape(slots, tile), preferred_element_type=F32
        ).astype(BF)

    return call(
        kernel,
        "combine_dx",
        grid_spec=pltpu.PrefetchScalarGridSpec(
            num_scalar_prefetch=1,
            grid=(steps,),
            in_specs=[
                pl.BlockSpec((tok_rows, slots), lambda i, t: (0, 0)),
                pl.BlockSpec((planes, nodes, capacity, tile), lambda i, t: (0, 0, 0, i)),
            ],
            out_specs=pl.BlockSpec(
                (tok_rows, tile), lambda i, t: (0, (i + t[0] * (steps // count)) % steps)
            ),
        ),
        out_shape=shape(tok_rows, model),
    )(where, pick_t, rows)


def shards(tokens, out_grad, expert_ids, gates, w_gate_up, w_down):
    nodes, planes = lax.axis_size("node"), lax.axis_size("local")
    groups = nodes * planes
    tok_rows = tokens.shape[0]
    capacity = tok_rows * expert_ids.shape[1] // (EXP_DEV * groups)
    where = lax.axis_index("edata").astype(jnp.int32).reshape(1)
    w_ins = gathered(w_gate_up[0])
    w_outs = gathered(w_down[0])
    node = lax.axis_index("node") ^ jnp.arange(nodes, dtype=jnp.int32)
    numbers = jnp.arange(planes, dtype=jnp.int32)[:, None] + planes * node[None, :]
    numbers = numbers.reshape(-1)
    ids_t = expert_ids.T
    x_sent, pick, weight = dispatch_x(
        where, numbers[:, None], ids_t, gates.T, tokens, nodes, planes, capacity
    )
    dy_sent, grad_rows = dispatch_dy(where, pick, weight, out_grad, nodes, planes, capacity)
    x_mid = over_planes(x_sent)
    dy_mid = over_planes(after(dy_sent, x_mid))
    xs = to_nodes(split(x_mid))
    xs[0] = after(xs[0], *w_ins[1:], *w_outs[1:])
    ys, act, inner = expert_forward(xs, w_ins, w_outs)
    y_packed = pack(to_nodes(ys))
    y_packed, dy_mid = lax.optimization_barrier((y_packed, dy_mid))
    y_rows = over_planes(y_packed)
    dys = to_nodes(split(dy_mid))
    dxs, act_grad = expert_backward(dys, act, w_ins, w_outs)
    dxs = to_nodes(dxs)
    parts = [weight_grads(s, xs, dys, inner, act_grad) for s in range(1, len(w_ins))]
    held = lax.optimization_barrier((*dxs, *parts))
    dx_packed, parts = pack(held[:nodes]), held[nodes:]
    dx_packed, y_rows = lax.optimization_barrier((dx_packed, y_rows))
    dx_rows = over_planes(dx_packed)

    act_grad = after(act_grad, dx_packed)
    parts = [from_owner(p, step) for step, p in enumerate(parts, 1)]
    parts.append(weight_grads(0, xs, dys, inner, act_grad))
    double = w_gate_up.shape[2]
    sums = [
        sum(p[:, columns].astype(F32) for p in parts)
        for columns in (slice(0, double), slice(double, None))
    ]
    spread = pick.astype(F32) * after(weight, y_packed)
    high = lax.reduce_precision(spread, 8, 7)
    middle = (spread - high).astype(BF)
    mixed, gate_grad = combine_y(
        where, numbers, (pick, high.astype(BF).T, middle.T), ids_t, grad_rows, y_rows
    )
    held = lax.optimization_barrier((dx_rows, *sums, mixed, gate_grad, pick.T))
    dx_rows, grad_in, grad_down, mixed, gate_grad, pick_t = held
    token_grad = combine_dx(where, pick_t, dx_rows)
    return (mixed, token_grad, gate_grad.T, grad_in[None], grad_down[None])


def solution(mesh):
    rows = P(("node", "local", "edata"), None)
    weights = P(("node", "local"), "edata", None)
    return jax.shard_map(
        shards,
        mesh=mesh,
        in_specs=(rows, rows, rows, rows, weights, weights),
        out_specs=(rows, rows, rows, weights, weights),
        check_vma=False,
    )
```

time: 243 us -> 290 us (1.19)
  waiting for transfers between devices: 95.3 us -> 173 us
  starting transfers between devices: 81.4 us -> 34.4 us
  Pallas kernels: 48.1 us -> 59.8 us
  local copies, waits for them, and re-layouts: 3.35 us -> 10.1 us
    all_to_all x0 -> x4, waiting for transfers between devices: none -> 96.2 us  [over_planes(): lax.all_to_all(shaped, 'local', split_axis=0, concat_axis=0, tiled=True)]
    ppermute x30 -> x12, starting transfers between devices: 80.7 us -> 14 us  [to_nodes(): lax.ppermute(pieces[d], 'node', [(i, i ^ d) for i in range(count)])]
    all_to_all x0 -> x4, starting transfers between devices: none -> 20.4 us  [over_planes(): lax.all_to_all(shaped, 'local', split_axis=0, concat_axis=0, tiled=True)]
    ppermute x30 -> x12, waiting for transfers between devices: 95.3 us -> 77.2 us  [to_nodes(): lax.ppermute(pieces[d], 'node', [(i, i ^ d) for i in range(count)])]
    pallas_call x6 -> x10, Pallas kernels: 48.1 us -> 59.8 us  [the longest x2 14.1 us: weight_grads(): call(kernel, 'weight_grads', grid=(steps,), in_specs=[tall] * (2 * nodes)...]
    squeeze x0 -> x2, local copies, waits for them, and re-layouts: none -> 5.11 us  [split(): return [rows[:, d] for d in range(rows.shape[1])]]
  transfers between devices with their start and end apart: 33 -> 19, of which waited for: 9 -> 11; matrix products, arithmetic and copies ran while one was open for 5% -> 5% of each run, Pallas kernels for 14% -> 14%
where the time goes in v12:
time: 290 us; the launch traced here: 289 us
  waiting for transfers between devices  173 us (60%)
  Pallas kernels  59.8 us (21%)
  starting transfers between devices  34.4 us (12%)
  other arithmetic  10.7 us (4%)
  local copies, waits for them, and re-layouts  10.1 us (3%)
    all_to_all x4, waiting for transfers between devices, over_planes(): lax.all_to_all(shaped, 'local', split_axis=0, concat_axis=0, tiled=True)  96.2 us
    ppermute x12, waiting for transfers between devices, to_nodes(): lax.ppermute(pieces[d], 'node', [(i, i ^ d) for i in range(count)])  77.2 us
    all_to_all x4, starting transfers between devices, over_planes(): lax.all_to_all(shaped, 'local', split_axis=0, concat_axis=0, tiled=True)  20.4 us
    pallas_call x2, Pallas kernels, weight_grads(): call(kernel, 'weight_grads', grid=(steps,), in_specs=[tall] * (2 * nodes)...  14.1 us
    ppermute x12, starting transfers between devices, to_nodes(): lax.ppermute(pieces[d], 'node', [(i, i ^ d) for i in range(count)])  14 us
    pallas_call x1, Pallas kernels, expert_backward(): call(kernel, 'expert_backward', in_specs=[VMEM] * len(operands), out_spec...  12.1 us
    pallas_call x1, Pallas kernels, expert_forward(): call(kernel, 'expert_forward', in_specs=[VMEM] * len(operands), out_specs...  11.4 us
    add x2, other arithmetic, shards(): sum((p[:, columns].astype(F32) for p in parts))  9.59 us
  transfers between devices with their start and end apart: 19, of which 11 were waited for; matrix products, arithmetic and copies ran while one was open for 5% of the time, Pallas kernels for 14%

profile of v12, /device:TPU:0, one launch (start us, length us, event | category | flops | bytes accessed | tf_op | source)
XLA Modules:
  0.0 289.2 jit_solution(15987131525336473657)
XLA Ops:
  1.3 3.7 %dispatch_x.1 = (bf16[4,4,32,2048]{3,2,1,0:T(8,128)(2,1)}, bf16[512,256]{1,0:T(8,128)(2,1)}, f32[512,1]{1,0:T(8,128)}) custom-call(s32[1]{0:T(128)} %bitcast.where_ref, s32[16,1]{1,0:T(8,128)} %add.40.numbers_ref, s32[8,256]{1,0:T(8,128)} %bitcast.58, f32[8,256]{1,0:T(8,128)} %bitcast.60, bf16[256,2048]{1,0:T(8,128)(2,1)} %x_ref.1), custom_call_target="tpu_custom_call" | custom-call | flops 1 | bytes 1 | tf_op jit(solution)/shard_map/dispatch_x/pallas_call | solution.py:106
  5.1 6.3 %all-to-all-start = ((bf16[4,128,2048]{2,1,0:T(8,128)(2,1)}), bf16[4,128,2048]{2,1,0:T(8,128)(2,1)}, u32[]{:S(2)}, u32[]{:S(2)}) async-start(bf16[4,128,2048]{2,1,0:T(8,128)(2,1)} %bitcast.57), calls=%async_computation | async-start | bytes 4194304 | tf_op jit(solution)/shard_map/all_to_all | solution.py:54
  11.4 4.1 %dispatch_dy.1 = (bf16[4,4,32,2048]{3,2,1,0:T(8,128)(2,1)}, bf16[512,2048]{1,0:T(8,128)(2,1)}) custom-call(s32[1]{0:T(128)} %bitcast.where_ref, bf16[512,256]{1,0:T(8,128)(2,1)} %get-tuple-element.48.pick_ref, f32[512,1]{1,0:T(8,128)} %get-tuple-element.68.weight_ref, bf16[256,2048]{1,0:T(8,128)(2,1)} %grad_ref.1), custom_call_target="tpu_custom_call" | custom-call | flops 1 | bytes 1 | tf_op jit(solution)/shard_map/dispatch_dy/pallas_call | solution.py:136
  15.6 44.2 %all-to-all-done = bf16[4,128,2048]{2,1,0:T(8,128)(2,1)} async-done(((bf16[4,128,2048]{2,1,0:T(8,128)(2,1)}), bf16[4,128,2048]{2,1,0:T(8,128)(2,1)}, u32[]{:S(2)}, u32[]{:S(2)}) %all-to-all-start) | async-done | bytes 2097184 | tf_op jit(solution)/shard_map/all_to_all | solution.py:54
  59.7 4.4 %all-to-all-start.1 = ((bf16[4,128,2048]{2,1,0:T(8,128)(2,1)}), bf16[4,128,2048]{2,1,0:T(8,128)(2,1)}, u32[]{:S(2)}, u32[]{:S(2)}) async-start(bf16[4,128,2048]{2,1,0:T(8,128)(2,1)} %bitcast.56), calls=%async_computation.1 | async-start | bytes 4194304 | tf_op jit(solution)/shard_map/all_to_all | solution.py:54
  64.2 2.6 slice_bitcast_fusion.4
  66.9 2.4 collective-permute-start.4
  70.4 12.2 %collective-permute-done.4.refs_3_ = bf16[4,32,2048]{2,1,0:T(8,128)(2,1)S(1)} collective-permute-done((bf16[4,32,2048]{2,1,0:T(8,128)(2,1)S(1)}, bf16[4,32,2048]{2,1,0:T(8,128)(2,1)S(1)}, u32[]{:S(2)}, u32[]{:S(2)}) %collective-permute-start.4) | collective-permute-done | bytes 524320 | tf_op jit(solution)/shard_map/ppermute | solution.py:61
  82.5 10.8 %collective-permute-done.3.refs_2_ = bf16[4,32,2048]{2,1,0:T(8,128)(2,1)S(1)} collective-permute-done((bf16[4,32,2048]{2,1,0:T(8,128)(2,1)S(1)}, bf16[4,32,2048]{2,1,0:T(8,128)(2,1)S(1)}, u32[]{:S(2)}, u32[]{:S(2)}) %collective-permute-start.3) | collective-permute-done | bytes 524320 | tf_op jit(solution)/shard_map/ppermute | solution.py:61
  94.9 11.4 %expert_forward.1 = (bf16[4,32,2048]{2,1,0:T(8,128)(2,1)}, bf16[4,32,2048]{2,1,0:T(8,128)(2,1)}, bf16[4,32,2048]{2,1,0:T(8,128)(2,1)}, bf16[4,32,2048]{2,1,0:T(8...) custom-call(bf16[4,32,2048]{2,1,0:T(8,128)(2,1)} %get-tuple-element.43.refs_0_, ...), custom_call_target="tpu_custom_call" | custom-call | flops 1 | bytes 1 | tf_op jit(solution)/shard_map/expert_forward/pallas_call | solution.py:210
  106.3 1.5 collective-permute-start.5
  109.8 11.5 %collective-permute-done.5.refs_1_ = bf16[4,32,2048]{2,1,0:T(8,128)(2,1)S(1)} collective-permute-done((bf16[4,32,2048]{2,1,0:T(8,128)(2,1)}, bf16[4,32,2048]{2,1,0:T(8,128)(2,1)S(1)}, u32[]{:S(2)}, u32[]{:S(2)}) %collective-permute-start.5) | collective-permute-done | bytes 524320 | tf_op jit(solution)/shard_map/ppermute | solution.py:61
  121.3 11.5 %collective-permute-done.6.refs_2_ = bf16[4,32,2048]{2,1,0:T(8,128)(2,1)S(1)} collective-permute-done((bf16[4,32,2048]{2,1,0:T(8,128)(2,1)}, bf16[4,32,2048]{2,1,0:T(8,128)(2,1)S(1)}, u32[]{:S(2)}, u32[]{:S(2)}) %collective-permute-start.6) | collective-permute-done | bytes 524320 | tf_op jit(solution)/shard_map/ppermute | solution.py:61
  133.8 2.6 pack.2
  136.4 2.5 slice_bitcast_fusion
  140.9 1.5 collective-permute-start.8
  142.4 12.3 %collective-permute-done.10.refs_3_.refs_7_ = bf16[4,32,2048]{2,1,0:T(8,128)(2,1)S(1)} collective-permute-done((bf16[4,32,2048]{2,1,0:T(8,128)(2,1)S(1)}, bf16[4,32,2048]{2,1,0:T(8,128)(2,1)S(1)}, u32[]{:S(2)}, u32[]{:S(2)}) %collective-permute-start.10) | collective-permute-done | bytes 524320 | tf_op jit(solution)/shard_map/ppermute | solution.py:61
  154.7 9.0 %collective-permute-done.9.refs_2_.refs_6_ = bf16[4,32,2048]{2,1,0:T(8,128)(2,1)S(1)} collective-permute-done((bf16[4,32,2048]{2,1,0:T(8,128)(2,1)S(1)}, bf16[4,32,2048]{2,1,0:T(8,128)(2,1)S(1)}, u32[]{:S(2)}, u32[]{:S(2)}) %collective-permute-start.9) | collective-permute-done | bytes 524320 | tf_op jit(solution)/shard_map/ppermute | solution.py:61
  164.7 12.1 %expert_backward.1 = (bf16[4,32,2048]{2,1,0:T(8,128)(2,1)}, bf16[4,32,2048]{2,1,0:T(8,128)(2,1)}, bf16[4,32,2048]{2,1,0:T(8,128)(2,1)}, bf16[4,32,2048]{2,1,0:T(8,128)(2,1)}, bf16[512,1536]{1,0:T(8,128)(2,1)}) custom-call(bf16[4,32,2048]{2,1,0:T(8,128)(2,1)} %get-tuple-element.82.refs_0_.refs_4_, bf16[4,32,2048]{2,1,0:T(8,128)(2,1)} %copy-done.9, ...), custom_call_target="tpu_custom_call" | custom-call | flops 1 | bytes 1 | tf_op jit(solution)/shard_map/expert_backward/pallas_call | solution.py:258
  177.1 1.6 collective-permute-start.12
  180.2 5.0 %all-to-all-start.2 = ((bf16[4,128,2048]{2,1,0:T(8,128)(2,1)}), bf16[4,128,2048]{2,1,0:T(8,128)(2,1)S(1)}, u32[]{:S(2)}, u32[]{:S(2)}) async-start(bf16[4,128,2048]{2,1,0:T(8,128)(2,1)} %bitcast.17), calls=%async_computation.2 | async-start | bytes 4194304 | tf_op jit(solution)/shard_map/all_to_all | solution.py:54
  185.2 7.1 %weight_grads.2 = bf16[1024,2304]{1,0:T(8,128)(2,1)} custom-call(bf16[4,32,2048]{2,1,0:T(8,128)(2,1)} %get-tuple-element.43.refs_0_, bf16[4,32,2048]{2,1,0:T(8,128)(2,1)} %copy-done.6, bf16[4,32,2048]{2,1,0:T(8,128)(2,1)} %copy-done.5, bf16[4,32,2048]{2,1,0:T(8,128)(2,1)} %copy-done.4, bf16[4,32,2048]{2,1,0:T(8,128)(2,1)} %get-tuple-element.82.refs_0_.refs_4_, ...), custom_call_target="tpu_custom_call" | custom-call | flops 1 | bytes 1 | tf_op jit(solution)/shard_map/weight_grads/pallas_call | solution.py:296
  192.3 9.8 %collective-permute-done.13.refs_3_ = bf16[4,32,2048]{2,1,0:T(8,128)(2,1)} collective-permute-done((bf16[4,32,2048]{2,1,0:T(8,128)(2,1)}, bf16[4,32,2048]{2,1,0:T(8,128)(2,1)}, u32[]{:S(2)}, u32[]{:S(2)}) %collective-permute-start.13) | collective-permute-done | bytes 524320 | tf_op jit(solution)/shard_map/ppermute | solution.py:61
  202.2 2.7 pack.3
  204.8 27.9 %all-to-all-done.2 = bf16[4,128,2048]{2,1,0:T(8,128)(2,1)S(1)} async-done(((bf16[4,128,2048]{2,1,0:T(8,128)(2,1)}), bf16[4,128,2048]{2,1,0:T(8,128)(2,1)S(1)}, u32[]{:S(2)}, u32[]{:S(2)}) %all-to-all-start.2) | async-done | bytes 2097184 | tf_op jit(solution)/shard_map/all_to_all | solution.py:54
  232.8 4.6 %all-to-all-start.3 = ((bf16[4,128,2048]{2,1,0:T(8,128)(2,1)}), bf16[4,128,2048]{2,1,0:T(8,128)(2,1)}, u32[]{:S(2)}, u32[]{:S(2)}) async-start(bf16[4,128,2048]{2,1,0:T(8,128)(2,1)} %bitcast.49), calls=%async_computation.3 | async-start | bytes 4194304 | tf_op jit(solution)/shard_map/all_to_all | solution.py:54
  239.3 4.9 %combine_y.1 = (bf16[256,2048]{1,0:T(8,128)(2,1)}, f32[8,256]{1,0:T(8,128)}) custom-call(s32[1]{0:T(128)} %bitcast.where_ref, s32[16]{0:T(128)} %add.39.number_ref, bf16[512,256]{1,0:T(8,128)(2,1)} %get-tuple-element.48.pick_ref, bf16[256,512]{1,0:T(8,128)(2,1)} %get-tuple-element.88.high_ref, bf16[256,512]{1,0:T(8,128)(2,1)} %get-tuple-element.87.middle_ref, ...), custom_call_target="tpu_custom_call" | custom-call | flops 1 | bytes 1 | tf_op jit(solution)/shard_map/combine_y/pallas_call | solution.py:340
  244.2 7.0 %weight_grads.3 = bf16[1024,2304]{1,0:T(8,128)(2,1)} custom-call(bf16[4,32,2048]{2,1,0:T(8,128)(2,1)} %get-tuple-element.43.refs_0_, bf16[4,32,2048]{2,1,0:T(8,128)(2,1)} %copy-done.6, bf16[4,32,2048]{2,1,0:T(8,128)(2,1)} %copy-done.5, bf16[4,32,2048]{2,1,0:T(8,128)(2,1)} %copy-done.4, bf16[4,32,2048]{2,1,0:T(8,128)(2,1)} %get-tuple-element.82.refs_0_.refs_4_, ...), custom_call_target="tpu_custom_call" | custom-call | flops 1 | bytes 1 | tf_op jit(solution)/shard_map/weight_grads/pallas_call | solution.py:296
  251.3 4.0 %convert_add_fusion.1 = f32[1024,768]{1,0:T(8,128)} fusion(bf16[1024,2304]{1,0:T(8,128)(2,1)} %weight_grads.3, bf16[1024,2304]{1,0:T(8,128)(2,1)} %collective-permute-done.14), kind=kLoop, calls=%fused_computation.1 | loop fusion | flops 2359296 | bytes 6291456 | tf_op jit(solution)/shard_map/add | solution.py:417
  255.3 5.5 %convert_add_fusion = f32[1024,1536]{1,0:T(8,128)} fusion(bf16[1024,2304]{1,0:T(8,128)(2,1)S(1)} %copy-done, bf16[1024,2304]{1,0:T(8,128)(2,1)} %collective-permute-done.14), kind=kLoop, calls=%fused_computation | loop fusion | flops 4718592 | bytes 12582912 | tf_op jit(solution)/shard_map/add | solution.py:417
  260.9 24.1 %all-to-all-done.3 = bf16[4,128,2048]{2,1,0:T(8,128)(2,1)} async-done(((bf16[4,128,2048]{2,1,0:T(8,128)(2,1)}), bf16[4,128,2048]{2,1,0:T(8,128)(2,1)}, u32[]{:S(2)}, u32[]{:S(2)}) %all-to-all-start.3) | async-done | bytes 2097184 | tf_op jit(solution)/shard_map/all_to_all | solution.py:54
  285.0 4.2 %combine_dx.1 = bf16[256,2048]{1,0:T(8,128)(2,1)} custom-call(s32[1]{0:T(128)} %bitcast.where_ref, bf16[256,512]{1,0:T(8,128)(2,1)} %bitcast.55, bf16[4,4,32,2048]{3,2,1,0:T(8,128)(2,1)} %bitcast.20.rows_ref), custom_call_target="tpu_custom_call" | custom-call | flops 1 | bytes 1 | tf_op jit(solution)/shard_map/combine_dx/pallas_call | solution.py:361
  (63 shorter events, 13.1 us)
Async XLA Ops:
  0.6 10.8 %copy-start.1 = (bf16[1,1024,1536]{2,1,0:T(8,128)(2,1)S(1)}, bf16[1,1024,1536]{2,1,0:T(8,128)(2,1)}, u32[]{:S(2)}) copy-start(bf16[1,1024,1536]{2,1,0:T(8,128)(2,1)} %param.10) | copy-start | bytes 9437188
  5.1 54.6 %all-to-all-start = ((bf16[4,128,2048]{2,1,0:T(8,128)(2,1)}), bf16[4,128,2048]{2,1,0:T(8,128)(2,1)}, u32[]{:S(2)}, u32[]{:S(2)}) async-start(bf16[4,128,2048]{2,1,0:T(8,128)(2,1)} %bitcast.57), calls=%async_computation | async-start | bytes 4194304 | tf_op jit(solution)/shard_map/all_to_all | solution.py:54
  11.4 58.9 %collective-permute-start = (bf16[1024,1536]{1,0:T(8,128)(2,1)S(1)}, bf16[1024,1536]{1,0:T(8,128)(2,1)}, u32[]{:S(2)}, u32[]{:S(2)}) collective-permute-start(bf16[1024,1536]{1,0:T(8,128)(2,1)S(1)} %bitcast.47), channel_id=1, source_target_pairs={{1,0},{0,1},{3,2},{2,3},{5,4},{4,5},{7,6},{6,7},{9,8},{8,9},{11,10... | collective-permute-start | bytes 9437192 | tf_op jit(solution)/shard_map/ppermute | solution.py:42
  59.7 76.7 %all-to-all-start.1 = ((bf16[4,128,2048]{2,1,0:T(8,128)(2,1)}), bf16[4,128,2048]{2,1,0:T(8,128)(2,1)}, u32[]{:S(2)}, u32[]{:S(2)}) async-start(bf16[4,128,2048]{2,1,0:T(8,128)(2,1)} %bitcast.56), calls=%async_computation.1 | async-start | bytes 4194304 | tf_op jit(solution)/shard_map/all_to_all | solution.py:54
  64.2 6.2 %collective-permute-start.1 = (bf16[1024,768]{1,0:T(8,128)(2,1)}, bf16[1024,768]{1,0:T(8,128)(2,1)S(1)}, u32[]{:S(2)}, u32[]{:S(2)}) collective-permute-start(bf16[1024,768]{1,0:T(8,128)(2,1)} %bitcast.51), channel_id=1, source_target_pairs={{1,0},{0,1},{3,2},{2,3},{5,4},{4,5},{7,6},{6,7},{9,8},{8,9},{11,10... | collective-permute-start | bytes 4718600 | tf_op jit(solution)/shard_map/ppermute | solution.py:42
  66.9 15.7 %collective-permute-start.4 = (bf16[4,32,2048]{2,1,0:T(8,128)(2,1)S(1)}, bf16[4,32,2048]{2,1,0:T(8,128)(2,1)S(1)}, u32[]{:S(2)}, u32[]{:S(2)}) collective-permute-start(bf16[4,32,2048]{2,1,0:T(8,128)(2,1)S(1)} %get-tuple-element.83), channel_id=1, source_target_pairs={{0,24},{8,16},{16,8},{24,0},{1,25},{9,17},{17,9},{25,1},{2,26},{10... | collective-permute-start | bytes 1572872 | tf_op jit(solution)/shard_map/ppermute | solution.py:61
  69.3 24.0 %collective-permute-start.3 = (bf16[4,32,2048]{2,1,0:T(8,128)(2,1)S(1)}, bf16[4,32,2048]{2,1,0:T(8,128)(2,1)S(1)}, u32[]{:S(2)}, u32[]{:S(2)}) collective-permute-start(bf16[4,32,2048]{2,1,0:T(8,128)(2,1)S(1)} %get-tuple-element.84), channel_id=1, source_target_pairs={{0,16},{8,24},{16,0},{24,8},{1,17},{9,25},{17,1},{25,9},{2,18},{10... | collective-permute-start | bytes 1572872 | tf_op jit(solution)/shard_map/ppermute | solution.py:61
  69.8 23.6 %collective-permute-start.2 = (bf16[4,32,2048]{2,1,0:T(8,128)(2,1)S(1)}, bf16[4,32,2048]{2,1,0:T(8,128)(2,1)S(1)}, u32[]{:S(2)}, u32[]{:S(2)}) collective-permute-start(bf16[4,32,2048]{2,1,0:T(8,128)(2,1)S(1)} %get-tuple-element.85), channel_id=1, source_target_pairs={{0,8},{8,0},{16,24},{24,16},{1,9},{9,1},{17,25},{25,17},{2,10},{10... | collective-permute-start | bytes 1572872 | tf_op jit(solution)/shard_map/ppermute | solution.py:61
  70.4 23.1 %copy-start.3 = (bf16[1024,768]{1,0:T(8,128)(2,1)}, bf16[1024,768]{1,0:T(8,128)(2,1)S(1)}, u32[]{:S(2)}) copy-start(bf16[1024,768]{1,0:T(8,128)(2,1)S(1)} %collective-permute-done.1.refs_7_.refs_8_) | copy-start | bytes 4718596
  82.5 10.9 %copy-start.4 = (bf16[4,32,2048]{2,1,0:T(8,128)(2,1)}, bf16[4,32,2048]{2,1,0:T(8,128)(2,1)S(1)}, u32[]{:S(2)}) copy-start(bf16[4,32,2048]{2,1,0:T(8,128)(2,1)S(1)} %collective-permute-done.4.refs_3_) | copy-start | bytes 1572868
  106.3 15.0 %collective-permute-start.5 = (bf16[4,32,2048]{2,1,0:T(8,128)(2,1)}, bf16[4,32,2048]{2,1,0:T(8,128)(2,1)S(1)}, u32[]{:S(2)}, u32[]{:S(2)}) collective-permute-start(bf16[4,32,2048]{2,1,0:T(8,128)(2,1)} %get-tuple-element.45), channel_id=1, source_target_pairs={{0,8},{8,0},{16,24},{24,16},{1,9},{9,1},{17,25},{25,17},{2,10},{10... | collective-permute-start | bytes 1572872 | tf_op jit(solution)/shard_map/ppermute | solution.py:61
  107.8 25.0 %collective-permute-start.6 = (bf16[4,32,2048]{2,1,0:T(8,128)(2,1)}, bf16[4,32,2048]{2,1,0:T(8,128)(2,1)S(1)}, u32[]{:S(2)}, u32[]{:S(2)}) collective-permute-start(bf16[4,32,2048]{2,1,0:T(8,128)(2,1)} %get-tuple-element.46), channel_id=1, source_target_pairs={{0,16},{8,24},{16,0},{24,8},{1,17},{9,25},{17,1},{25,9},{2,18},{10... | collective-permute-start | bytes 1572872 | tf_op jit(solution)/shard_map/ppermute | solution.py:61
  108.6 24.2 %collective-permute-start.7 = (bf16[4,32,2048]{2,1,0:T(8,128)(2,1)}, bf16[4,32,2048]{2,1,0:T(8,128)(2,1)S(1)}, u32[]{:S(2)}, u32[]{:S(2)}) collective-permute-start(bf16[4,32,2048]{2,1,0:T(8,128)(2,1)} %get-tuple-element.47), channel_id=1, source_target_pairs={{0,24},{8,16},{16,8},{24,0},{1,25},{9,17},{17,9},{25,1},{2,26},{10... | collective-permute-start | bytes 1572872 | tf_op jit(solution)/shard_map/ppermute | solution.py:61
  121.3 11.5 %copy-start.15 = (bf16[4,32,2048]{2,1,0:T(8,128)(2,1)}, bf16[4,32,2048]{2,1,0:T(8,128)(2,1)S(1)}, u32[]{:S(2)}) copy-start(bf16[4,32,2048]{2,1,0:T(8,128)(2,1)S(1)} %collective-permute-done.5.refs_1_) | copy-start | bytes 1572868
  138.9 15.8 %collective-permute-start.10 = (bf16[4,32,2048]{2,1,0:T(8,128)(2,1)S(1)}, bf16[4,32,2048]{2,1,0:T(8,128)(2,1)S(1)}, u32[]{:S(2)}, u32[]{:S(2)}) collective-permute-start(bf16[4,32,2048]{2,1,0:T(8,128)(2,1)S(1)} %get-tuple-element.79), channel_id=1, source_target_pairs={{0,24},{8,16},{16,8},{24,0},{1,25},{9,17},{17,9},{25,1},{2,26},{10... | collective-permute-start | bytes 1572872 | tf_op jit(solution)/shard_map/ppermute | solution.py:61
  140.4 23.3 %collective-permute-start.9 = (bf16[4,32,2048]{2,1,0:T(8,128)(2,1)S(1)}, bf16[4,32,2048]{2,1,0:T(8,128)(2,1)S(1)}, u32[]{:S(2)}, u32[]{:S(2)}) collective-permute-start(bf16[4,32,2048]{2,1,0:T(8,128)(2,1)S(1)} %get-tuple-element.80), channel_id=1, source_target_pairs={{0,16},{8,24},{16,0},{24,8},{1,17},{9,25},{17,1},{25,9},{2,18},{10... | collective-permute-start | bytes 1572872 | tf_op jit(solution)/shard_map/ppermute | solution.py:61
  140.9 22.8 %collective-permute-start.8 = (bf16[4,32,2048]{2,1,0:T(8,128)(2,1)S(1)}, bf16[4,32,2048]{2,1,0:T(8,128)(2,1)S(1)}, u32[]{:S(2)}, u32[]{:S(2)}) collective-permute-start(bf16[4,32,2048]{2,1,0:T(8,128)(2,1)S(1)} %get-tuple-element.81), channel_id=1, source_target_pairs={{0,8},{8,0},{16,24},{24,16},{1,9},{9,1},{17,25},{25,17},{2,10},{10... | collective-permute-start | bytes 1572872 | tf_op jit(solution)/shard_map/ppermute | solution.py:61
  154.7 9.0 %copy-start.7 = (bf16[4,32,2048]{2,1,0:T(8,128)(2,1)}, bf16[4,32,2048]{2,1,0:T(8,128)(2,1)S(1)}, u32[]{:S(2)}) copy-start(bf16[4,32,2048]{2,1,0:T(8,128)(2,1)S(1)} %collective-permute-done.10.refs_3_.refs_7_) | copy-start | bytes 1572868
  163.7 1.0 copy-start.9
  176.8 15.5 %collective-permute-start.11 = (bf16[4,32,2048]{2,1,0:T(8,128)(2,1)}, bf16[4,32,2048]{2,1,0:T(8,128)(2,1)S(1)}, u32[]{:S(2)}, u32[]{:S(2)}) collective-permute-start(bf16[4,32,2048]{2,1,0:T(8,128)(2,1)} %get-tuple-element.55), channel_id=1, source_target_pairs={{0,8},{8,0},{16,24},{24,16},{1,9},{9,1},{17,25},{25,17},{2,10},{10... | collective-permute-start | bytes 1572872 | tf_op jit(solution)/shard_map/ppermute | solution.py:61
  177.1 15.2 %collective-permute-start.12 = (bf16[4,32,2048]{2,1,0:T(8,128)(2,1)}, bf16[4,32,2048]{2,1,0:T(8,128)(2,1)S(1)}, u32[]{:S(2)}, u32[]{:S(2)}) collective-permute-start(bf16[4,32,2048]{2,1,0:T(8,128)(2,1)} %get-tuple-element.56), channel_id=1, source_target_pairs={{0,16},{8,24},{16,0},{24,8},{1,17},{9,25},{17,1},{25,9},{2,18},{10... | collective-permute-start | bytes 1572872 | tf_op jit(solution)/shard_map/ppermute | solution.py:61
  178.8 23.4 %collective-permute-start.13 = (bf16[4,32,2048]{2,1,0:T(8,128)(2,1)}, bf16[4,32,2048]{2,1,0:T(8,128)(2,1)}, u32[]{:S(2)}, u32[]{:S(2)}) collective-permute-start(bf16[4,32,2048]{2,1,0:T(8,128)(2,1)} %get-tuple-element.57), channel_id=1, source_target_pairs={{0,24},{8,16},{16,8},{24,0},{1,25},{9,17},{17,9},{25,1},{2,26},{10... | collective-permute-start | bytes 1572872 | tf_op jit(solution)/shard_map/ppermute | solution.py:61
  180.2 52.5 %all-to-all-start.2 = ((bf16[4,128,2048]{2,1,0:T(8,128)(2,1)}), bf16[4,128,2048]{2,1,0:T(8,128)(2,1)S(1)}, u32[]{:S(2)}, u32[]{:S(2)}) async-start(bf16[4,128,2048]{2,1,0:T(8,128)(2,1)} %bitcast.17), calls=%async_computation.2 | async-start | bytes 4194304 | tf_op jit(solution)/shard_map/all_to_all | solution.py:54
  192.3 9.9 %copy-start.13 = (bf16[4,32,2048]{2,1,0:T(8,128)(2,1)}, bf16[4,32,2048]{2,1,0:T(8,128)(2,1)S(1)}, u32[]{:S(2)}) copy-start(bf16[4,32,2048]{2,1,0:T(8,128)(2,1)S(1)} %collective-permute-done.11.refs_1_) | copy-start | bytes 1572868
  192.3 9.8 %copy-start.14 = (bf16[4,32,2048]{2,1,0:T(8,128)(2,1)}, bf16[4,32,2048]{2,1,0:T(8,128)(2,1)S(1)}, u32[]{:S(2)}) copy-start(bf16[4,32,2048]{2,1,0:T(8,128)(2,1)S(1)} %collective-permute-done.12.refs_2_) | copy-start | bytes 1572868
  202.2 49.1 %collective-permute-start.14 = (bf16[1024,2304]{1,0:T(8,128)(2,1)}, bf16[1024,2304]{1,0:T(8,128)(2,1)}, u32[]{:S(2)}, u32[]{:S(2)}) collective-permute-start(bf16[1024,2304]{1,0:T(8,128)(2,1)} %weight_grads.2), channel_id=1, source_target_pairs={{0,1},{1,0},{2,3},{3,2},{4,5},{5,4},{6,7},{7,6},{8,9},{9,8},{10,11... | collective-permute-start | bytes 14155784 | tf_op jit(solution)/shard_map/ppermute | solution.py:48
  204.8 33.2 %copy-start.11 = (bf16[512,256]{1,0:T(8,128)(2,1)S(1)}, bf16[512,256]{1,0:T(8,128)(2,1)}, u32[]{:S(2)}) copy-start(bf16[512,256]{1,0:T(8,128)(2,1)} %get-tuple-element.48.pick_ref) | copy-start | bytes 786436
  204.8 33.4 %copy-start.12 = (f32[512,1]{1,0:T(8,128)S(1)}, f32[512,1]{1,0:T(8,128)}, u32[]{:S(2)}) copy-start(f32[512,1]{1,0:T(8,128)} %get-tuple-element.68.weight_ref) | copy-start | bytes 6148
  232.8 6.5 %copy-start.2 = (bf16[4,128,2048]{2,1,0:T(8,128)(2,1)}, bf16[4,128,2048]{2,1,0:T(8,128)(2,1)S(1)}, u32[]{:S(2)}) copy-start(bf16[4,128,2048]{2,1,0:T(8,128)(2,1)S(1)} %all-to-all-done.2) | copy-start | bytes 6291460
  232.8 52.2 %all-to-all-start.3 = ((bf16[4,128,2048]{2,1,0:T(8,128)(2,1)}), bf16[4,128,2048]{2,1,0:T(8,128)(2,1)}, u32[]{:S(2)}, u32[]{:S(2)}) async-start(bf16[4,128,2048]{2,1,0:T(8,128)(2,1)} %bitcast.49), calls=%async_computation.3 | async-start | bytes 4194304 | tf_op jit(solution)/shard_map/all_to_all | solution.py:54
  238.2 13.0 %copy-start.10 = (bf16[512,256]{0,1:T(8,128)(2,1)}, bf16[512,256]{0,1:T(8,128)(2,1)S(1)}, u32[]{:S(2)}) copy-start(bf16[512,256]{0,1:T(8,128)(2,1)S(1)} %copy.23) | copy-start | bytes 786436
  251.3 4.1 %copy-start = (bf16[1024,2304]{1,0:T(8,128)(2,1)S(1)}, bf16[1024,2304]{1,0:T(8,128)(2,1)}, u32[]{:S(2)}) copy-start(bf16[1024,2304]{1,0:T(8,128)(2,1)} %weight_grads.3) | copy-start | bytes 14155780
  (5 other events, 4.2 us)

commit v13 on v9

v13 whole, which is shorter than its diff:
```python
import jax
import jax.numpy as jnp
from jax import lax
from jax.experimental import pallas as pl
from jax.experimental.pallas import tpu as pltpu
from jax.sharding import PartitionSpec as P

EXP_DEV = 4
BF = jnp.bfloat16
F32 = jnp.float32
ROWS_IN = (((0,), (0,)), ((), ()))
COLS_IN = (((1,), (1,)), ((), ()))
LIMIT = 56 * 1024 * 1024
def work(flops):
    return pl.CostEstimate(flops=flops, bytes_accessed=flops // 200, transcendentals=0)


CHEAP = pl.CostEstimate(flops=1, bytes_accessed=1, transcendentals=0)
VMEM = pl.BlockSpec(memory_space=pltpu.VMEM)
SMEM = pl.BlockSpec(memory_space=pltpu.SMEM)

def call(kernel, name, cost=CHEAP, **more):
    return pl.pallas_call(
        kernel,
        compiler_params=pltpu.CompilerParams(vmem_limit_bytes=LIMIT),
        cost_estimate=cost,
        name=name,
        **more,
    )


def shape(*dims, kind=BF):
    return jax.ShapeDtypeStruct(dims, kind)


def after(value, *others):
    return lax.optimization_barrier((value, *others))[0]


def gathered(shard):
    count = lax.axis_size("edata")
    shards = [shard]
    for step in range(1, count):
        pairs = [((i + step) % count, i) for i in range(count)]
        shards.append(lax.ppermute(shard, "edata", pairs))
    return shards


def from_owner(piece, step):
    count = lax.axis_size("edata")
    return lax.ppermute(piece, "edata", [(i, (i + step) % count) for i in range(count)])


def to_all(rows):
    return lax.all_to_all(rows, ("node", "local"), split_axis=0, concat_axis=0, tiled=True)


def to_partner(block, j):
    count = lax.axis_size("node") * lax.axis_size("local")
    return lax.ppermute(block, ("node", "local"), [(i, i ^ j) for i in range(count)])


def slots_of(j, me, capacity):
    return pl.ds(pl.multiple_of((me ^ j) * capacity, capacity), capacity)


def shard_at(s, turn, count, width):
    return pl.ds(pl.multiple_of((turn + s) % count * width, width), width)


def dispatch_x(where, ids_t, gates_t, tokens, groups, capacity):
    top, tok_rows = ids_t.shape
    model = tokens.shape[1]
    count = lax.axis_size("edata")
    width = model // count
    slots = groups * capacity

    def kernel(where_ref, ids_ref, gates_ref, x_ref, sent_ref, pick_ref, weight_ref):
        turn = where_ref[1]
        numbers = lax.broadcasted_iota(jnp.int32, (groups, tok_rows), 0)
        routed = jnp.zeros((groups, tok_rows), F32)
        weight = jnp.zeros((groups, tok_rows), F32)
        for k in range(top):
            chosen = ids_ref[k : k + 1, :] == numbers
            routed = jnp.where(chosen, 1.0, routed)
            weight += jnp.where(chosen, gates_ref[k : k + 1, :], 0.0)
        first = lax.broadcasted_iota(jnp.int32, (tok_rows, tok_rows), 0)
        second = lax.broadcasted_iota(jnp.int32, (tok_rows, tok_rows), 1)
        earlier = jnp.where(first < second, 1.0, 0.0).astype(BF)
        order = jnp.dot(routed.astype(BF), earlier, preferred_element_type=F32)
        order = jnp.where(routed > 0.0, order, -1.0)
        places = lax.broadcasted_iota(jnp.int32, (capacity, tok_rows), 0).astype(F32)
        for g in range(groups):
            hits = order[g : g + 1, :] == places
            here = slice(g * capacity, (g + 1) * capacity)
            pick_ref[here] = jnp.where(hits, 1.0, 0.0).astype(BF)
            weight_ref[here] = jnp.sum(
                jnp.where(hits, weight[g : g + 1, :], 0.0), axis=1, keepdims=True
            )
        for s in range(count):
            source = shard_at(s, turn, count, width)
            x = jnp.dot(pick_ref[...], x_ref[:, source], preferred_element_type=F32).astype(BF)
            sent_ref[:, :, s * width : (s + 1) * width] = x.reshape(groups, capacity, width)

    return call(
        kernel,
        "dispatch_x",
        in_specs=[SMEM] + [VMEM] * 3,
        out_specs=[VMEM] * 3,
        out_shape=[
            shape(groups, capacity, model),
            shape(slots, tok_rows),
            shape(slots, 1, kind=F32),
        ],
    )(where, ids_t, gates_t, tokens)


def dispatch_dy(where, pick, weight, out_grad, groups, capacity):
    slots, tok_rows = pick.shape
    model = out_grad.shape[1]
    count = lax.axis_size("edata")
    width = model // count

    def kernel(where_ref, pick_ref, weight_ref, grad_ref, *refs):
        blocks, (rows_ref, relative_ref, dy_ref) = refs[:groups], refs[groups:]
        me, turn = where_ref[0], where_ref[1]
        for s in range(count):
            source = shard_at(s, turn, count, width)
            here = slice(s * width, (s + 1) * width)
            rows = jnp.dot(pick_ref[...], grad_ref[:, source], preferred_element_type=F32)
            rows_ref[:, here] = rows.astype(BF)
            dy_ref[:, here] = (weight_ref[...] * rows).astype(BF)
        for j, block in enumerate(blocks):
            block[...] = dy_ref[slots_of(j, me, capacity), :]
            relative_ref[j * capacity : (j + 1) * capacity] = pick_ref[slots_of(j, me, capacity), :]

    results = call(
        kernel,
        "dispatch_dy",
        in_specs=[SMEM] + [VMEM] * 3,
        out_specs=[VMEM] * (groups + 2),
        out_shape=[
            *[shape(capacity, model)] * groups,
            shape(slots, model),
            shape(slots, tok_rows),
        ],
        scratch_shapes=[pltpu.VMEM((slots, model), BF)],
    )(where, pick, weight, out_grad)
    return list(results[:groups]), *results[groups:]


def product(left, weights):
    width = weights[0].shape[0]
    total = None
    for s, shard in enumerate(weights):
        one = jnp.dot(
            left[:, s * width : (s + 1) * width], shard[...], preferred_element_type=F32
        )
        total = one if total is None else total + one
    return total


def expert_forward(got, w_ins, w_outs):
    groups, capacity, model = got.shape
    count = len(w_ins)
    width = model // count
    double, hidden = w_ins[0].shape[1], w_outs[0].shape[1]
    slots = groups * capacity
    many = max(1, 256 // capacity)

    def kernel(got_ref, *refs):
        ins, outs, (y_ref, act_ref, inner_ref) = refs[:count], refs[count:-3], refs[-3:]
        for first in range(0, groups, many):
            theirs = slice(first, first + many)
            band = slice(first * capacity, (first + many) * capacity)
            x = got_ref[theirs].reshape(many * capacity, model)
            act_ref[band] = product(x, ins)
            act_gate = act_ref[band, :hidden]
            inner_ref[band] = (
                act_gate * jax.nn.sigmoid(act_gate) * act_ref[band, hidden:]
            ).astype(BF)
            for s in range(count):
                y = lax.dot_general(
                    inner_ref[band], outs[s][...], COLS_IN, preferred_element_type=F32
                ).astype(BF)
                y_ref[theirs, :, s * width : (s + 1) * width] = y.reshape(many, capacity, width)

    operands = (got, *w_ins, *w_outs)
    return call(
        kernel,
        "expert_forward",
        cost=work(6 * slots * model * hidden),
        in_specs=[VMEM] * len(operands),
        out_specs=[VMEM] * 3,
        out_shape=[
            shape(groups, capacity, model),
            shape(slots, double, kind=F32),
            shape(slots, hidden),
        ],
    )(*operands)


def expert_backward(where, blocks, act, w_ins, w_outs):
    groups = len(blocks)
    capacity, model = blocks[0].shape
    count = len(w_ins)
    width = model // count
    double, hidden = w_ins[0].shape[1], w_outs[0].shape[1]
    slots = groups * capacity
    rows = min(256, slots)

    def kernel(where_ref, *refs):
        got, act_ref, refs = refs[:groups], refs[groups], refs[groups + 1 :]
        ins, outs, refs = refs[:count], refs[count : 2 * count], refs[2 * count :]
        sent, (act_grad_ref, dy_ref, dx_ref) = refs[:groups], refs[groups:]
        me = where_ref[0]
        for j, block in enumerate(got):
            dy_ref[slots_of(j, me, capacity), :] = block[...]
        for first in range(0, slots, rows):
            band = slice(first, first + rows)
            inner_grad = product(dy_ref[band], outs)
            act_gate = act_ref[band, :hidden]
            act_up = act_ref[band, hidden:]
            sig = jax.nn.sigmoid(act_gate)
            act_grad_ref[band, :hidden] = (
                inner_grad * act_up * sig * (1.0 + act_gate * (1.0 - sig))
            ).astype(BF)
            act_grad_ref[band, hidden:] = (inner_grad * (act_gate * sig)).astype(BF)
            for s in range(count):
                dx_ref[band, s * width : (s + 1) * width] = lax.dot_general(
                    act_grad_ref[band], ins[s][...], COLS_IN, preferred_element_type=F32
                ).astype(BF)
        for j, block in enumerate(sent):
            block[...] = dx_ref[slots_of(j, me, capacity), :]

    operands = (where, *blocks, act, *w_ins, *w_outs)
    results = call(
        kernel,
        "expert_backward",
        cost=work(6 * slots * model * hidden),
        in_specs=[SMEM] + [VMEM] * (len(operands) - 1),
        out_specs=[VMEM] * (groups + 2),
        out_shape=[
            *[shape(capacity, model)] * groups,
            shape(slots, double),
            shape(slots, model),
        ],
        scratch_shapes=[pltpu.VMEM((slots, model), BF)],
    )(*operands)
    return list(results[:groups]), *results[groups:]


def weight_grads(shard, got, dys, inner, act_grad):
    groups, capacity, _ = got.shape
    slots, model = dys.shape
    size = model // lax.axis_size("edata")
    double, hidden = act_grad.shape[1], inner.shape[1]
    tile = min(256, size)
    steps = size // tile

    def kernel(x_ref, dy_ref, inner_ref, act_grad_ref, out_ref):
        x = x_ref[...].reshape(slots, tile)
        out_ref[:, :double] = lax.dot_general(
            x, act_grad_ref[...], ROWS_IN, preferred_element_type=F32
        ).astype(BF)
        out_ref[:, double:] = lax.dot_general(
            dy_ref[...], inner_ref[...], ROWS_IN, preferred_element_type=F32
        ).astype(BF)

    return call(
        kernel,
        "weight_grads",
        cost=work(6 * slots * size * hidden),
        grid=(steps,),
        in_specs=[
            pl.BlockSpec((groups, capacity, tile), lambda i: (0, 0, shard * steps + i)),
            pl.BlockSpec((slots, tile), lambda i: (0, shard * steps + i)),
            pl.BlockSpec((slots, hidden), lambda i: (0, 0)),
            pl.BlockSpec((slots, double), lambda i: (0, 0)),
        ],
        out_specs=pl.BlockSpec((tile, double + hidden), lambda i: (i, 0)),
        out_shape=shape(size, double + hidden),
    )(got, dys, inner, act_grad)


def combine_y(where, picks, ids_t, grad_rows, rows):
    pick, high_t, middle_t = picks
    slots, tok_rows = pick.shape
    groups, capacity, model = rows.shape
    count = lax.axis_size("edata")
    width = model // count

    def kernel(where_ref, pick_ref, high_ref, middle_ref, ids_ref, grad_ref, *refs):
        y_ref, mixed_ref, gate_grad_ref = refs
        turn = where_ref[1]
        dots = jnp.zeros((slots, 1), F32)
        for s in range(count):
            here = slice(s * width, (s + 1) * width)
            y = y_ref[:, :, here].reshape(slots, width)
            mixed_ref[:, shard_at(s, turn, count, width)] = (
                jnp.dot(high_ref[...], y, preferred_element_type=F32)
                + jnp.dot(middle_ref[...], y, preferred_element_type=F32)
            ).astype(BF)
            dots += jnp.sum(
                y.astype(F32) * grad_ref[:, here].astype(F32), axis=1, keepdims=True
            )
        by_token = pick_ref[...].astype(F32) * dots
        by_token = jnp.sum(by_token.reshape(groups, capacity, tok_rows), axis=1)
        ids = ids_ref[...]
        total = jnp.zeros(ids.shape, F32)
        for g in range(groups):
            total += jnp.where(ids == g, by_token[g : g + 1], 0.0)
        gate_grad_ref[...] = total

    return call(
        kernel,
        "combine_y",
        in_specs=[SMEM] + [VMEM] * 6,
        out_specs=[VMEM] * 2,
        out_shape=[shape(tok_rows, model), shape(*ids_t.shape, kind=F32)],
    )(where, pick, high_t, middle_t, ids_t, grad_rows, rows)


def combine_dx(where, relative_t, blocks):
    tok_rows, slots = relative_t.shape
    capacity, model = blocks[0].shape
    count = lax.axis_size("edata")
    width = model // count

    def kernel(where_ref, relative_ref, *refs):
        blocks, out_ref = refs[:-1], refs[-1]
        for s in range(count):
            here = slice(s * width, (s + 1) * width)
            dx = jnp.concatenate([block[:, here] for block in blocks], axis=0)
            out_ref[:, shard_at(s, where_ref[1], count, width)] = jnp.dot(
                relative_ref[...], dx, preferred_element_type=F32
            ).astype(BF)

    return call(
        kernel,
        "combine_dx",
        in_specs=[SMEM] + [VMEM] * (1 + len(blocks)),
        out_specs=VMEM,
        out_shape=shape(tok_rows, model),
    )(where, relative_t, *blocks)


def shards(tokens, out_grad, expert_ids, gates, w_gate_up, w_down):
    groups = lax.axis_size("node") * lax.axis_size("local")
    tok_rows = tokens.shape[0]
    capacity = tok_rows * expert_ids.shape[1] // (EXP_DEV * groups)
    queued = min(5, groups - 1)
    where = jnp.stack([lax.axis_index(("node", "local")), lax.axis_index("edata")])
    where = where.astype(jnp.int32)
    w_ins = gathered(w_gate_up[0])
    w_outs = gathered(w_down[0])
    ids_t = expert_ids.T
    sent, pick, weight = dispatch_x(where, ids_t, gates.T, tokens, groups, capacity)
    got = to_all(sent)
    blocks, grad_rows, relative = dispatch_dy(where, pick, weight, out_grad, groups, capacity)
    blocks = [blocks[0], *(after(b, *w_ins[1:], *w_outs[1:]) for b in blocks[1:])]
    y_sent, act, inner = expert_forward(got, w_ins, w_outs)
    dys = [blocks[0]]
    for j in range(1, groups):
        needs = (inner, dys[j - queued]) if j > queued else ()
        dys.append(to_partner(after(blocks[j], *needs) if needs else blocks[j], j))
    y_got = to_all(after(y_sent, *dys[1:]))
    dxs, act_grad, dy_rows = expert_backward(where, dys, act, w_ins, w_outs)
    backs = [dxs[0]]
    for j in range(1, groups):
        needs = (y_got, backs[j - queued]) if j > queued else ()
        backs.append(to_partner(after(dxs[j], *needs) if needs else dxs[j], j))

    parts = []
    for shard in [*range(1, len(w_ins)), 0]:
        parts.append(weight_grads(shard, got, dy_rows, inner, act_grad))
    parts = [parts[-1]] + [from_owner(after(p, y_got), step) for step, p in enumerate(parts[:-1], 1)]
    double = w_gate_up.shape[2]
    sums = [
        sum(p[:, columns].astype(F32) for p in parts)
        for columns in (slice(0, double), slice(double, None))
    ]
    spread = pick.astype(F32) * after(weight, inner)
    high = lax.reduce_precision(spread, 8, 7)
    middle = (spread - high).astype(BF)
    mixed, gate_grad = combine_y(
        where, (pick, high.astype(BF).T, middle.T), ids_t, grad_rows, y_got
    )
    held = lax.optimization_barrier((*backs, *sums, mixed, gate_grad, relative.T))
    *backs, grad_in, grad_down, mixed, gate_grad, relative_t = held
    token_grad = combine_dx(where, relative_t, backs)
    return (mixed, token_grad, gate_grad.T, grad_in[None], grad_down[None])


def solution(mesh):
    rows = P(("node", "local", "edata"), None)
    weights = P(("node", "local"), "edata", None)
    return jax.shard_map(
        shards,
        mesh=mesh,
        in_specs=(rows, rows, rows, rows, weights, weights),
        out_specs=(rows, rows, rows, weights, weights),
        check_vma=False,
    )
```

time: 263 us -> 234 us (0.89)
  waiting for transfers between devices: 126 us -> 102 us
  starting transfers between devices: 75.7 us -> 60.7 us
  Pallas kernels: 43.2 us -> 54.4 us
    ppermute x30, waiting for transfers between devices: 123 us -> 28.5 us  [to_partner(): lax.ppermute(block, ('node', 'local'), [(i, i ^ j) for i in range(count)])]
    all_to_all x2, waiting for transfers between devices: 0.01 us -> 70.4 us  [to_all(): lax.all_to_all(rows, ('node', 'local'), split_axis=0, concat_axis=0, tile...]
    ppermute x30, starting transfers between devices: 58.8 us -> 47.5 us  [to_partner(): lax.ppermute(block, ('node', 'local'), [(i, i ^ j) for i in range(count)])]
    pallas_call x5 -> x8, Pallas kernels: 43.2 us -> 54.4 us  [the longest x2 13.8 us: weight_grads(): call(kernel, 'weight_grads', cost=work(6 * slots * size * hidden), grid=(...]
    all_to_all x2, starting transfers between devices: 16.2 us -> 12.6 us  [to_all(): lax.all_to_all(rows, ('node', 'local'), split_axis=0, concat_axis=0, tile...]
  transfers between devices with their start and end apart: 35 -> 35, of which waited for: 10 -> 10; matrix products, arithmetic and copies ran while one was open for 4% -> 5% of each run, Pallas kernels for 3% -> 20%
where the time goes in v13:
time: 234 us
  waiting for transfers between devices  102 us (44%)
  starting transfers between devices  60.7 us (26%)
  Pallas kernels  54.4 us (23%)
  other arithmetic  10.6 us (5%)
  local copies, waits for them, and re-layouts  4.4 us (2%)
    all_to_all x2, waiting for transfers between devices, to_all(): lax.all_to_all(rows, ('node', 'local'), split_axis=0, concat_axis=0, tile...  70.4 us
    ppermute x30, starting transfers between devices, to_partner(): lax.ppermute(block, ('node', 'local'), [(i, i ^ j) for i in range(count)])  47.5 us
    ppermute x30, waiting for transfers between devices, to_partner(): lax.ppermute(block, ('node', 'local'), [(i, i ^ j) for i in range(count)])  28.5 us
    pallas_call x2, Pallas kernels, weight_grads(): call(kernel, 'weight_grads', cost=work(6 * slots * size * hidden), grid=(...  13.8 us
    pallas_call x1, Pallas kernels, expert_backward(): call(kernel, 'expert_backward', cost=work(6 * slots * model * hidden), in...  13.4 us
    all_to_all x2, starting transfers between devices, to_all(): lax.all_to_all(rows, ('node', 'local'), split_axis=0, concat_axis=0, tile...  12.6 us
    pallas_call x1, Pallas kernels, expert_forward(): call(kernel, 'expert_forward', cost=work(6 * slots * model * hidden), in_...  11.2 us
    add x2, other arithmetic, shards(): sum((p[:, columns].astype(F32) for p in parts))  8.95 us
  transfers between devices with their start and end apart: 35, of which 10 were waited for; matrix products, arithmetic and copies ran while one was open for 5% of the time, Pallas kernels for 20%

profile of v13, /device:TPU:0, one launch (start us, length us, event | category | flops | bytes accessed | tf_op | source)
XLA Modules:
  0.0 233.6 jit_solution(4144383618019897182)
XLA Ops:
  1.3 3.5 %dispatch_x.1 = (bf16[16,32,2048]{2,1,0:T(8,128)(2,1)}, bf16[512,256]{1,0:T(8,128)(2,1)}, f32[512,1]{1,0:T(8,128)}) custom-call(s32[2]{0:T(128)} %pad_add_fusion.where_ref, s32[8,256]{1,0:T(8,128)} %bitcast.17, f32[8,256]{1,0:T(8,128)} %bitcast.19, bf16[256,2048]{1,0:T(8,128)(2,1)} %x_ref.1), custom_call_target="tpu_custom_call" | custom-call | flops 1 | bytes 1 | tf_op jit(solution)/shard_map/dispatch_x/pallas_call | solution.py:105
  4.8 8.3 %all-to-all-start = ((bf16[16,32,2048]{2,1,0:T(8,128)(2,1)}), bf16[16,32,2048]{2,1,0:T(8,128)(2,1)S(1)}, u32[]{:S(2)}, u32[]{:S(2)}) async-start(bf16[16,32,2048]{2,1,0:T(8,128)(2,1)} %get-tuple-element.123), calls=%async_computation | async-start | bytes 4194304 | tf_op jit(solution)/shard_map/all_to_all | solution.py:55
  13.7 4.2 %dispatch_dy.1 = (bf16[32,2048]{1,0:T(8,128)(2,1)}, bf16[32,2048]{1,0:T(8,128)(2,1)}, bf16[32,2048]{1,0:T(8,128)(2,1)}, bf16[32,2048]{1,0:T(8,128)(2,1)}, bf16[3...) custom-call(s32[2]{0:T(128)} %pad_add_fusion.where_ref, ...), custom_call_target="tpu_custom_call" | custom-call | flops 1 | bytes 1 | tf_op jit(solution)/shard_map/dispatch_dy/pallas_call | solution.py:137
  17.9 3.4 %collective-permute-done.1.refs_3_.refs_20_ = bf16[1024,768]{1,0:T(8,128)(2,1)S(1)} collective-permute-done((bf16[1024,768]{1,0:T(8,128)(2,1)}, bf16[1024,768]{1,0:T(8,128)(2,1)S(1)}, u32[]{:S(2)}, u32[]{:S(2)}) %collective-permute-start.1) | collective-permute-done | bytes 1572896 | tf_op jit(solution)/shard_map/ppermute | solution.py:45
  21.3 2.8 %collective-permute-start.6 = (bf16[32,2048]{1,0:T(8,128)(2,1)}, bf16[32,2048]{1,0:T(8,128)(2,1)S(1)}, u32[]{:S(2)}, u32[]{:S(2)}) collective-permute-start(bf16[32,2048]{1,0:T(8,128)(2,1)} %get-tuple-element.120), channel_id=1, source_target_pairs={{0,10},{2,8},{4,14},{6,12},{8,2},{10,0},{12,6},{14,4},{16,26},{18,... | collective-permute-start | bytes 393224 | tf_op jit(solution)/shard_map/ppermute | solution.py:60
  24.7 2.4 %collective-permute-start.4 = (bf16[32,2048]{1,0:T(8,128)(2,1)}, bf16[32,2048]{1,0:T(8,128)(2,1)S(1)}, u32[]{:S(2)}, u32[]{:S(2)}) collective-permute-start(bf16[32,2048]{1,0:T(8,128)(2,1)} %get-tuple-element.116), channel_id=1, source_target_pairs={{0,6},{2,4},{4,2},{6,0},{8,14},{10,12},{12,10},{14,8},{16,22},{18,... | collective-permute-start | bytes 393224 | tf_op jit(solution)/shard_map/ppermute | solution.py:60
  27.1 2.0 collective-permute-start.2
  29.1 40.7 %all-to-all-done.got_ref.x_ref = bf16[16,32,2048]{2,1,0:T(8,128)(2,1)S(1)} async-done(((bf16[16,32,2048]{2,1,0:T(8,128)(2,1)}), bf16[16,32,2048]{2,1,0:T(8,128)(2,1)S(1)}, u32[]{:S(2)}, u32[]{:S(2)}) %all-to-all-start) | async-done | bytes 2097184 | tf_op jit(solution)/shard_map/all_to_all | solution.py:55
  71.1 11.2 %expert_forward.1 = (bf16[16,32,2048]{2,1,0:T(8,128)(2,1)}, f32[512,1536]{1,0:T(8,128)}, bf16[512,768]{1,0:T(8,128)(2,1)}) custom-call(bf16[16,32,2048]{2,1,0:T(8,128)(2,1)} %copy-done.1, bf16[1024,1536]{1,0:T(8,128)(2,1)} %bitcast.21, bf16[1024,1536]{1,0:T(8,128)(2,1)} %copy-done.21, bf16[1024,768]{1,0:T(8,128)(2,1)} %bitcast.24, bf16[1024,768]{1,0:T(8,128)(2,1)} %copy-done.22), custom_call_target="tpu_custom_call" | custom-call | flops 4831838208 | bytes 24159192 | tf_op jit(solution)/shard_map/expert_forward/pallas_call | solution.py:189
  83.4 4.8 %collective-permute-start.10 = (bf16[32,2048]{1,0:T(8,128)(2,1)}, bf16[32,2048]{1,0:T(8,128)(2,1)S(1)}, u32[]{:S(2)}, u32[]{:S(2)}) collective-permute-start(bf16[32,2048]{1,0:T(8,128)(2,1)} %get-tuple-element.134), channel_id=1, source_target_pairs={{0,18},{2,16},{4,22},{6,20},{8,26},{10,24},{12,30},{14,28},{16,2},... | collective-permute-start | bytes 393224 | tf_op jit(solution)/shard_map/ppermute | solution.py:60
  88.3 6.7 %collective-permute-done.7.refs_6_ = bf16[32,2048]{1,0:T(8,128)(2,1)S(1)} collective-permute-done((bf16[32,2048]{1,0:T(8,128)(2,1)}, bf16[32,2048]{1,0:T(8,128)(2,1)S(1)}, u32[]{:S(2)}, u32[]{:S(2)}) %collective-permute-start.7) | collective-permute-done | bytes 131104 | tf_op jit(solution)/shard_map/ppermute | solution.py:60
  97.6 3.2 %collective-permute-start.14 = (bf16[32,2048]{1,0:T(8,128)(2,1)S(1)}, bf16[32,2048]{1,0:T(8,128)(2,1)S(1)}, u32[]{:S(2)}, u32[]{:S(2)}) collective-permute-start(bf16[32,2048]{1,0:T(8,128)(2,1)S(1)} %copy-done.32), channel_id=1, source_target_pairs={{0,26},{2,24},{4,30},{6,28},{8,18},{10,16},{12,22},{14,20},{16,10}... | collective-permute-start | bytes 393224 | tf_op jit(solution)/shard_map/ppermute | solution.py:60
  100.8 2.3 collective-permute-start.15
  103.1 3.1 %collective-permute-done.11.refs_10_ = bf16[32,2048]{1,0:T(8,128)(2,1)S(1)} collective-permute-done((bf16[32,2048]{1,0:T(8,128)(2,1)}, bf16[32,2048]{1,0:T(8,128)(2,1)S(1)}, u32[]{:S(2)}, u32[]{:S(2)}) %collective-permute-start.11) | collective-permute-done | bytes 131104 | tf_op jit(solution)/shard_map/ppermute | solution.py:60
  106.2 2.4 %collective-permute-start.16 = (bf16[32,2048]{1,0:T(8,128)(2,1)S(1)}, bf16[32,2048]{1,0:T(8,128)(2,1)S(1)}, u32[]{:S(2)}, u32[]{:S(2)}) collective-permute-start(bf16[32,2048]{1,0:T(8,128)(2,1)S(1)} %copy-done.30), channel_id=1, source_target_pairs={{0,30},{2,28},{4,26},{6,24},{8,22},{10,20},{12,18},{14,16},{16,14}... | collective-permute-start | bytes 393224 | tf_op jit(solution)/shard_map/ppermute | solution.py:60
  108.6 8.6 %collective-permute-done.15.refs_14_ = bf16[32,2048]{1,0:T(8,128)(2,1)S(1)} collective-permute-done((bf16[32,2048]{1,0:T(8,128)(2,1)S(1)}, bf16[32,2048]{1,0:T(8,128)(2,1)S(1)}, u32[]{:S(2)}, u32[]{:S(2)}) %collective-permute-start.15) | collective-permute-done | bytes 131104 | tf_op jit(solution)/shard_map/ppermute | solution.py:60
  118.5 4.3 %all-to-all-start.1 = ((bf16[16,32,2048]{2,1,0:T(8,128)(2,1)}), bf16[16,32,2048]{2,1,0:T(8,128)(2,1)S(1)}, u32[]{:S(2)}, u32[]{:S(2)}) async-start(bf16[16,32,2048]{2,1,0:T(8,128)(2,1)} %get-tuple-element.162), calls=%async_computation.1 | async-start | bytes 4194304 | tf_op jit(solution)/shard_map/all_to_all | solution.py:55
  122.9 13.4 %expert_backward.1 = (bf16[32,2048]{1,0:T(8,128)(2,1)}, bf16[32,2048]{1,0:T(8,128)(2,1)}, bf16[32,2048]{1,0:T(8,128)(2,1)}, bf16[32,2048]{1,0:T(8,128)(2,1)}, bf...) custom-call(s32[2]{0:T(128)} %pad_add_fusion.where_ref, ...), custom_call_target="tpu_custom_call" | custom-call | flops 4831838208 | bytes 24159192 | tf_op jit(solution)/shard_map/expert_backward/pallas_call | solution.py:237
  136.3 6.9 %weight_grads.3 = bf16[1024,2304]{1,0:T(8,128)(2,1)} custom-call(bf16[16,32,2048]{2,1,0:T(8,128)(2,1)} %copy-done.1, bf16[512,2048]{1,0:T(8,128)(2,1)} %get-tuple-element.182.dy_ref, bf16[512,768]{1,0:T(8,128)(2,1)} %get-tuple-element.124.inner_ref, bf16[512,1536]{1,0:T(8,128)(2,1)} %get-tuple-element.183.act_grad_ref), custom_call_target="tpu_custom_call" | custom-call | flops 2415919104 | bytes 12079595 | tf_op jit(solution)/shard_map/weight_grads/pallas_call | solution.py:270
  143.3 29.7 %all-to-all-done.1.refs_0_ = bf16[16,32,2048]{2,1,0:T(8,128)(2,1)S(1)} async-done(((bf16[16,32,2048]{2,1,0:T(8,128)(2,1)}), bf16[16,32,2048]{2,1,0:T(8,128)(2,1)S(1)}, u32[]{:S(2)}, u32[]{:S(2)}) %all-to-all-start.1) | async-done | bytes 2097184 | tf_op jit(solution)/shard_map/all_to_all | solution.py:55
  175.3 3.3 %collective-permute-start.19 = (bf16[32,2048]{1,0:T(8,128)(2,1)}, bf16[32,2048]{1,0:T(8,128)(2,1)S(1)}, u32[]{:S(2)}, u32[]{:S(2)}) collective-permute-start(bf16[32,2048]{1,0:T(8,128)(2,1)} %get-tuple-element.157), channel_id=1, source_target_pairs={{0,6},{2,4},{4,2},{6,0},{8,14},{10,12},{12,10},{14,8},{16,22},{18,... | collective-permute-start | bytes 393224 | tf_op jit(solution)/shard_map/ppermute | solution.py:60
  180.4 5.9 %collective-permute-done.18.refs_2_ = bf16[32,2048]{1,0:T(8,128)(2,1)S(1)} collective-permute-done((bf16[32,2048]{1,0:T(8,128)(2,1)}, bf16[32,2048]{1,0:T(8,128)(2,1)S(1)}, u32[]{:S(2)}, u32[]{:S(2)}) %collective-permute-start.18) | collective-permute-done | bytes 131104 | tf_op jit(solution)/shard_map/ppermute | solution.py:60
  189.4 5.9 %collective-permute-start.25 = (bf16[32,2048]{1,0:T(8,128)(2,1)}, bf16[32,2048]{1,0:T(8,128)(2,1)S(1)}, u32[]{:S(2)}, u32[]{:S(2)}) collective-permute-start(bf16[32,2048]{1,0:T(8,128)(2,1)} %get-tuple-element.169), channel_id=1, source_target_pairs={{0,18},{2,16},{4,22},{6,20},{8,26},{10,24},{12,30},{14,28},{16,2},... | collective-permute-start | bytes 393224 | tf_op jit(solution)/shard_map/ppermute | solution.py:60
  197.3 6.9 %weight_grads.2 = bf16[1024,2304]{1,0:T(8,128)(2,1)} custom-call(bf16[16,32,2048]{2,1,0:T(8,128)(2,1)} %copy-done.1, bf16[512,2048]{1,0:T(8,128)(2,1)} %get-tuple-element.182.dy_ref, bf16[512,768]{1,0:T(8,128)(2,1)} %get-tuple-element.124.inner_ref, bf16[512,1536]{1,0:T(8,128)(2,1)} %get-tuple-element.183.act_grad_ref), custom_call_target="tpu_custom_call" | custom-call | flops 2415919104 | bytes 12079595 | tf_op jit(solution)/shard_map/weight_grads/pallas_call | solution.py:270
  204.3 5.1 %combine_y.1 = (bf16[256,2048]{1,0:T(8,128)(2,1)}, f32[8,256]{1,0:T(8,128)}) custom-call(s32[2]{0:T(128)} %pad_add_fusion.where_ref, bf16[512,256]{1,0:T(8,128)(2,1)} %get-tuple-element.108.pick_ref, bf16[256,512]{1,0:T(8,128)(2,1)} %get-tuple-element.212.high_ref, bf16[256,512]{1,0:T(8,128)(2,1)} %get-tuple-element.211.middle_ref, s32[8,256]{1,0:T(8,128)} %bitcast.18, ...), custom_call_target="tpu_custom_call" | custom-call | flops 1 | bytes 1 | tf_op jit(solution)/shard_map/combine_y/pallas_call | solution.py:315
  209.3 2.0 collective-permute-start.27
  211.4 2.7 %collective-permute-start.28 = (bf16[32,2048]{1,0:T(8,128)(2,1)}, bf16[32,2048]{1,0:T(8,128)(2,1)S(1)}, u32[]{:S(2)}, u32[]{:S(2)}) collective-permute-start(bf16[32,2048]{1,0:T(8,128)(2,1)} %get-tuple-element.175), channel_id=1, source_target_pairs={{0,24},{2,26},{4,28},{6,30},{8,16},{10,18},{12,20},{14,22},{16,8},... | collective-permute-start | bytes 393224 | tf_op jit(solution)/shard_map/ppermute | solution.py:60
  214.0 2.1 collective-permute-start.29
  216.1 2.1 collective-permute-start.30
  220.0 5.6 %convert_add_fusion = f32[1024,1536]{1,0:T(8,128)} fusion(bf16[1024,2304]{1,0:T(8,128)(2,1)} %collective-permute-done.32, bf16[1024,2304]{1,0:T(8,128)(2,1)S(1)} %copy-done), kind=kLoop, calls=%fused_computation | loop fusion | flops 4718592 | bytes 12582912 | tf_op jit(solution)/shard_map/add | solution.py:380
  225.6 3.4 %convert_add_fusion.1 = f32[1024,768]{1,0:T(8,128)} fusion(bf16[1024,2304]{1,0:T(8,128)(2,1)} %collective-permute-done.32, bf16[1024,2304]{1,0:T(8,128)(2,1)S(1)} %copy-done), kind=kLoop, calls=%fused_computation.1 | loop fusion | flops 2359296 | bytes 6291456 | tf_op jit(solution)/shard_map/add | solution.py:380
  230.2 3.4 %combine_dx.1 = bf16[256,2048]{1,0:T(8,128)(2,1)} custom-call(s32[2]{0:T(128)} %pad_add_fusion.where_ref, bf16[256,512]{1,0:T(8,128)(2,1)} %bitcast.16, bf16[32,2048]{1,0:T(8,128)(2,1)} %get-tuple-element.192.refs_0_, bf16[32,2048]{1,0:T(8,128)(2,1)} %copy-done.6, bf16[32,2048]{1,0:T(8,128)(2,1)} %copy-done.7, bf16[32,2048]{1,0:T(8,128)(2,1)} %copy-done.8, ...), custom_call_target="tpu_custom_call" | custom-call | flops 1 | bytes 1 | tf_op jit(solution)/shard_map/combine_dx/pallas_call | solution.py:339
  (145 shorter events, 20.5 us)
Async XLA Ops:
  4.8 65.0 %all-to-all-start = ((bf16[16,32,2048]{2,1,0:T(8,128)(2,1)}), bf16[16,32,2048]{2,1,0:T(8,128)(2,1)S(1)}, u32[]{:S(2)}, u32[]{:S(2)}) async-start(bf16[16,32,2048]{2,1,0:T(8,128)(2,1)} %get-tuple-element.123), calls=%async_computation | async-start | bytes 4194304 | tf_op jit(solution)/shard_map/all_to_all | solution.py:55
  21.3 66.9 %collective-permute-start.6 = (bf16[32,2048]{1,0:T(8,128)(2,1)}, bf16[32,2048]{1,0:T(8,128)(2,1)S(1)}, u32[]{:S(2)}, u32[]{:S(2)}) collective-permute-start(bf16[32,2048]{1,0:T(8,128)(2,1)} %get-tuple-element.120), channel_id=1, source_target_pairs={{0,10},{2,8},{4,14},{6,12},{8,2},{10,0},{12,6},{14,4},{16,26},{18,... | collective-permute-start | bytes 393224 | tf_op jit(solution)/shard_map/ppermute | solution.py:60
  24.1 59.3 %collective-permute-start.5 = (bf16[32,2048]{1,0:T(8,128)(2,1)}, bf16[32,2048]{1,0:T(8,128)(2,1)S(1)}, u32[]{:S(2)}, u32[]{:S(2)}) collective-permute-start(bf16[32,2048]{1,0:T(8,128)(2,1)} %get-tuple-element.118), channel_id=1, source_target_pairs={{0,8},{2,10},{4,12},{6,14},{8,0},{10,2},{12,4},{14,6},{16,24},{18,... | collective-permute-start | bytes 393224 | tf_op jit(solution)/shard_map/ppermute | solution.py:60
  24.7 57.7 %collective-permute-start.4 = (bf16[32,2048]{1,0:T(8,128)(2,1)}, bf16[32,2048]{1,0:T(8,128)(2,1)S(1)}, u32[]{:S(2)}, u32[]{:S(2)}) collective-permute-start(bf16[32,2048]{1,0:T(8,128)(2,1)} %get-tuple-element.116), channel_id=1, source_target_pairs={{0,6},{2,4},{4,2},{6,0},{8,14},{10,12},{12,10},{14,8},{16,22},{18,... | collective-permute-start | bytes 393224 | tf_op jit(solution)/shard_map/ppermute | solution.py:60
  27.1 55.3 %collective-permute-start.3 = (bf16[32,2048]{1,0:T(8,128)(2,1)}, bf16[32,2048]{1,0:T(8,128)(2,1)S(1)}, u32[]{:S(2)}, u32[]{:S(2)}) collective-permute-start(bf16[32,2048]{1,0:T(8,128)(2,1)} %get-tuple-element.114), channel_id=1, source_target_pairs={{0,4},{2,6},{4,0},{6,2},{8,12},{10,14},{12,8},{14,10},{16,20},{18,... | collective-permute-start | bytes 393224 | tf_op jit(solution)/shard_map/ppermute | solution.py:60
  27.1 55.2 %collective-permute-start.2 = (bf16[32,2048]{1,0:T(8,128)(2,1)}, bf16[32,2048]{1,0:T(8,128)(2,1)S(1)}, u32[]{:S(2)}, u32[]{:S(2)}) collective-permute-start(bf16[32,2048]{1,0:T(8,128)(2,1)} %get-tuple-element.112), channel_id=1, source_target_pairs={{0,2},{2,0},{4,6},{6,4},{8,10},{10,8},{12,14},{14,12},{16,18},{18,... | collective-permute-start | bytes 393224 | tf_op jit(solution)/shard_map/ppermute | solution.py:60
  82.3 12.7 %collective-permute-start.7 = (bf16[32,2048]{1,0:T(8,128)(2,1)}, bf16[32,2048]{1,0:T(8,128)(2,1)S(1)}, u32[]{:S(2)}, u32[]{:S(2)}) collective-permute-start(bf16[32,2048]{1,0:T(8,128)(2,1)} %get-tuple-element.125), channel_id=1, source_target_pairs={{0,12},{2,14},{4,8},{6,10},{8,4},{10,6},{12,0},{14,2},{16,28},{18,... | collective-permute-start | bytes 393224 | tf_op jit(solution)/shard_map/ppermute | solution.py:60
  82.4 13.5 %collective-permute-start.8 = (bf16[32,2048]{1,0:T(8,128)(2,1)}, bf16[32,2048]{1,0:T(8,128)(2,1)S(1)}, u32[]{:S(2)}, u32[]{:S(2)}) collective-permute-start(bf16[32,2048]{1,0:T(8,128)(2,1)} %get-tuple-element.128), channel_id=1, source_target_pairs={{0,14},{2,12},{4,10},{6,8},{8,6},{10,4},{12,2},{14,0},{16,30},{18,... | collective-permute-start | bytes 393224 | tf_op jit(solution)/shard_map/ppermute | solution.py:60
  82.5 15.1 %collective-permute-start.9 = (bf16[32,2048]{1,0:T(8,128)(2,1)}, bf16[32,2048]{1,0:T(8,128)(2,1)S(1)}, u32[]{:S(2)}, u32[]{:S(2)}) collective-permute-start(bf16[32,2048]{1,0:T(8,128)(2,1)} %get-tuple-element.131), channel_id=1, source_target_pairs={{0,16},{2,18},{4,20},{6,22},{8,24},{10,26},{12,28},{14,30},{16,0},... | collective-permute-start | bytes 393224 | tf_op jit(solution)/shard_map/ppermute | solution.py:60
  83.4 17.4 %collective-permute-start.10 = (bf16[32,2048]{1,0:T(8,128)(2,1)}, bf16[32,2048]{1,0:T(8,128)(2,1)S(1)}, u32[]{:S(2)}, u32[]{:S(2)}) collective-permute-start(bf16[32,2048]{1,0:T(8,128)(2,1)} %get-tuple-element.134), channel_id=1, source_target_pairs={{0,18},{2,16},{4,22},{6,20},{8,26},{10,24},{12,30},{14,28},{16,2},... | collective-permute-start | bytes 393224 | tf_op jit(solution)/shard_map/ppermute | solution.py:60
  88.2 18.0 %collective-permute-start.11 = (bf16[32,2048]{1,0:T(8,128)(2,1)}, bf16[32,2048]{1,0:T(8,128)(2,1)S(1)}, u32[]{:S(2)}, u32[]{:S(2)}) collective-permute-start(bf16[32,2048]{1,0:T(8,128)(2,1)} %get-tuple-element.137), channel_id=1, source_target_pairs={{0,20},{2,22},{4,16},{6,18},{8,28},{10,30},{12,24},{14,26},{16,4},... | collective-permute-start | bytes 393224 | tf_op jit(solution)/shard_map/ppermute | solution.py:60
  95.0 13.5 %collective-permute-start.12 = (bf16[32,2048]{1,0:T(8,128)(2,1)S(1)}, bf16[32,2048]{1,0:T(8,128)(2,1)S(1)}, u32[]{:S(2)}, u32[]{:S(2)}) collective-permute-start(bf16[32,2048]{1,0:T(8,128)(2,1)S(1)} %copy-done.35), channel_id=1, source_target_pairs={{0,22},{2,20},{4,18},{6,16},{8,30},{10,28},{12,26},{14,24},{16,6},... | collective-permute-start | bytes 393224 | tf_op jit(solution)/shard_map/ppermute | solution.py:60
  95.9 12.6 %collective-permute-start.13 = (bf16[32,2048]{1,0:T(8,128)(2,1)S(1)}, bf16[32,2048]{1,0:T(8,128)(2,1)S(1)}, u32[]{:S(2)}, u32[]{:S(2)}) collective-permute-start(bf16[32,2048]{1,0:T(8,128)(2,1)S(1)} %copy-done.33), channel_id=1, source_target_pairs={{0,24},{2,26},{4,28},{6,30},{8,16},{10,18},{12,20},{14,22},{16,8},... | collective-permute-start | bytes 393224 | tf_op jit(solution)/shard_map/ppermute | solution.py:60
  97.6 11.0 %collective-permute-start.14 = (bf16[32,2048]{1,0:T(8,128)(2,1)S(1)}, bf16[32,2048]{1,0:T(8,128)(2,1)S(1)}, u32[]{:S(2)}, u32[]{:S(2)}) collective-permute-start(bf16[32,2048]{1,0:T(8,128)(2,1)S(1)} %copy-done.32), channel_id=1, source_target_pairs={{0,26},{2,24},{4,30},{6,28},{8,18},{10,16},{12,22},{14,20},{16,10}... | collective-permute-start | bytes 393224 | tf_op jit(solution)/shard_map/ppermute | solution.py:60
  100.8 16.4 %collective-permute-start.15 = (bf16[32,2048]{1,0:T(8,128)(2,1)S(1)}, bf16[32,2048]{1,0:T(8,128)(2,1)S(1)}, u32[]{:S(2)}, u32[]{:S(2)}) collective-permute-start(bf16[32,2048]{1,0:T(8,128)(2,1)S(1)} %copy-done.31), channel_id=1, source_target_pairs={{0,28},{2,30},{4,24},{6,26},{8,20},{10,22},{12,16},{14,18},{16,12}... | collective-permute-start | bytes 393224 | tf_op jit(solution)/shard_map/ppermute | solution.py:60
  106.2 11.1 %collective-permute-start.16 = (bf16[32,2048]{1,0:T(8,128)(2,1)S(1)}, bf16[32,2048]{1,0:T(8,128)(2,1)S(1)}, u32[]{:S(2)}, u32[]{:S(2)}) collective-permute-start(bf16[32,2048]{1,0:T(8,128)(2,1)S(1)} %copy-done.30), channel_id=1, source_target_pairs={{0,30},{2,28},{4,26},{6,24},{8,22},{10,20},{12,18},{14,16},{16,14}... | collective-permute-start | bytes 393224 | tf_op jit(solution)/shard_map/ppermute | solution.py:60
  118.5 54.5 %all-to-all-start.1 = ((bf16[16,32,2048]{2,1,0:T(8,128)(2,1)}), bf16[16,32,2048]{2,1,0:T(8,128)(2,1)S(1)}, u32[]{:S(2)}, u32[]{:S(2)}) async-start(bf16[16,32,2048]{2,1,0:T(8,128)(2,1)} %get-tuple-element.162), calls=%async_computation.1 | async-start | bytes 4194304 | tf_op jit(solution)/shard_map/all_to_all | solution.py:55
  173.0 45.2 %collective-permute-start.32 = (bf16[1024,2304]{1,0:T(8,128)(2,1)}, bf16[1024,2304]{1,0:T(8,128)(2,1)}, u32[]{:S(2)}, u32[]{:S(2)}) collective-permute-start(bf16[1024,2304]{1,0:T(8,128)(2,1)} %weight_grads.3), channel_id=1, source_target_pairs={{0,1},{1,0},{2,3},{3,2},{4,5},{5,4},{6,7},{7,6},{8,9},{9,8},{10,11... | collective-permute-start | bytes 14155784 | tf_op jit(solution)/shard_map/ppermute | solution.py:51
  173.0 13.2 %collective-permute-start.18 = (bf16[32,2048]{1,0:T(8,128)(2,1)}, bf16[32,2048]{1,0:T(8,128)(2,1)S(1)}, u32[]{:S(2)}, u32[]{:S(2)}) collective-permute-start(bf16[32,2048]{1,0:T(8,128)(2,1)} %get-tuple-element.156), channel_id=1, source_target_pairs={{0,4},{2,6},{4,0},{6,2},{8,12},{10,14},{12,8},{14,10},{16,20},{18,... | collective-permute-start | bytes 393224 | tf_op jit(solution)/shard_map/ppermute | solution.py:60
  175.3 11.9 %collective-permute-start.19 = (bf16[32,2048]{1,0:T(8,128)(2,1)}, bf16[32,2048]{1,0:T(8,128)(2,1)S(1)}, u32[]{:S(2)}, u32[]{:S(2)}) collective-permute-start(bf16[32,2048]{1,0:T(8,128)(2,1)} %get-tuple-element.157), channel_id=1, source_target_pairs={{0,6},{2,4},{4,2},{6,0},{8,14},{10,12},{12,10},{14,8},{16,22},{18,... | collective-permute-start | bytes 393224 | tf_op jit(solution)/shard_map/ppermute | solution.py:60
  178.6 10.3 %collective-permute-start.20 = (bf16[32,2048]{1,0:T(8,128)(2,1)}, bf16[32,2048]{1,0:T(8,128)(2,1)S(1)}, u32[]{:S(2)}, u32[]{:S(2)}) collective-permute-start(bf16[32,2048]{1,0:T(8,128)(2,1)} %get-tuple-element.158), channel_id=1, source_target_pairs={{0,8},{2,10},{4,12},{6,14},{8,0},{10,2},{12,4},{14,6},{16,24},{18,... | collective-permute-start | bytes 393224 | tf_op jit(solution)/shard_map/ppermute | solution.py:60
  180.4 9.1 %collective-permute-start.21 = (bf16[32,2048]{1,0:T(8,128)(2,1)}, bf16[32,2048]{1,0:T(8,128)(2,1)S(1)}, u32[]{:S(2)}, u32[]{:S(2)}) collective-permute-start(bf16[32,2048]{1,0:T(8,128)(2,1)} %get-tuple-element.159), channel_id=1, source_target_pairs={{0,10},{2,8},{4,14},{6,12},{8,2},{10,0},{12,6},{14,4},{16,26},{18,... | collective-permute-start | bytes 393224 | tf_op jit(solution)/shard_map/ppermute | solution.py:60
  186.2 11.1 %collective-permute-start.22 = (bf16[32,2048]{1,0:T(8,128)(2,1)S(1)}, bf16[32,2048]{1,0:T(8,128)(2,1)S(1)}, u32[]{:S(2)}, u32[]{:S(2)}) collective-permute-start(bf16[32,2048]{1,0:T(8,128)(2,1)S(1)} %copy-done.38), channel_id=1, source_target_pairs={{0,12},{2,14},{4,8},{6,10},{8,4},{10,6},{12,0},{14,2},{16,28},{18,... | collective-permute-start | bytes 393224 | tf_op jit(solution)/shard_map/ppermute | solution.py:60
  187.1 22.2 %collective-permute-start.23 = (bf16[32,2048]{1,0:T(8,128)(2,1)}, bf16[32,2048]{1,0:T(8,128)(2,1)S(1)}, u32[]{:S(2)}, u32[]{:S(2)}) collective-permute-start(bf16[32,2048]{1,0:T(8,128)(2,1)} %get-tuple-element.165), channel_id=1, source_target_pairs={{0,14},{2,12},{4,10},{6,8},{8,6},{10,4},{12,2},{14,0},{16,30},{18,... | collective-permute-start | bytes 393224 | tf_op jit(solution)/shard_map/ppermute | solution.py:60
  188.9 22.5 %collective-permute-start.24 = (bf16[32,2048]{1,0:T(8,128)(2,1)}, bf16[32,2048]{1,0:T(8,128)(2,1)S(1)}, u32[]{:S(2)}, u32[]{:S(2)}) collective-permute-start(bf16[32,2048]{1,0:T(8,128)(2,1)} %get-tuple-element.167), channel_id=1, source_target_pairs={{0,16},{2,18},{4,20},{6,22},{8,24},{10,26},{12,28},{14,30},{16,0},... | collective-permute-start | bytes 393224 | tf_op jit(solution)/shard_map/ppermute | solution.py:60
  189.4 24.6 %collective-permute-start.25 = (bf16[32,2048]{1,0:T(8,128)(2,1)}, bf16[32,2048]{1,0:T(8,128)(2,1)S(1)}, u32[]{:S(2)}, u32[]{:S(2)}) collective-permute-start(bf16[32,2048]{1,0:T(8,128)(2,1)} %get-tuple-element.169), channel_id=1, source_target_pairs={{0,18},{2,16},{4,22},{6,20},{8,26},{10,24},{12,30},{14,28},{16,2},... | collective-permute-start | bytes 393224 | tf_op jit(solution)/shard_map/ppermute | solution.py:60
  197.3 18.8 %collective-permute-start.26 = (bf16[32,2048]{1,0:T(8,128)(2,1)}, bf16[32,2048]{1,0:T(8,128)(2,1)S(1)}, u32[]{:S(2)}, u32[]{:S(2)}) collective-permute-start(bf16[32,2048]{1,0:T(8,128)(2,1)} %get-tuple-element.171), channel_id=1, source_target_pairs={{0,20},{2,22},{4,16},{6,18},{8,28},{10,30},{12,24},{14,26},{16,4},... | collective-permute-start | bytes 393224 | tf_op jit(solution)/shard_map/ppermute | solution.py:60
  209.3 19.6 %collective-permute-start.27 = (bf16[32,2048]{1,0:T(8,128)(2,1)}, bf16[32,2048]{1,0:T(8,128)(2,1)S(1)}, u32[]{:S(2)}, u32[]{:S(2)}) collective-permute-start(bf16[32,2048]{1,0:T(8,128)(2,1)} %get-tuple-element.173), channel_id=1, source_target_pairs={{0,22},{2,20},{4,18},{6,16},{8,30},{10,28},{12,26},{14,24},{16,6},... | collective-permute-start | bytes 393224 | tf_op jit(solution)/shard_map/ppermute | solution.py:60
  211.4 17.6 %collective-permute-start.28 = (bf16[32,2048]{1,0:T(8,128)(2,1)}, bf16[32,2048]{1,0:T(8,128)(2,1)S(1)}, u32[]{:S(2)}, u32[]{:S(2)}) collective-permute-start(bf16[32,2048]{1,0:T(8,128)(2,1)} %get-tuple-element.175), channel_id=1, source_target_pairs={{0,24},{2,26},{4,28},{6,30},{8,16},{10,18},{12,20},{14,22},{16,8},... | collective-permute-start | bytes 393224 | tf_op jit(solution)/shard_map/ppermute | solution.py:60
  214.0 15.0 %collective-permute-start.29 = (bf16[32,2048]{1,0:T(8,128)(2,1)}, bf16[32,2048]{1,0:T(8,128)(2,1)S(1)}, u32[]{:S(2)}, u32[]{:S(2)}) collective-permute-start(bf16[32,2048]{1,0:T(8,128)(2,1)} %get-tuple-element.177), channel_id=1, source_target_pairs={{0,26},{2,24},{4,30},{6,28},{8,18},{10,16},{12,22},{14,20},{16,10}... | collective-permute-start | bytes 393224 | tf_op jit(solution)/shard_map/ppermute | solution.py:60
  216.1 13.4 %collective-permute-start.30 = (bf16[32,2048]{1,0:T(8,128)(2,1)S(1)}, bf16[32,2048]{1,0:T(8,128)(2,1)S(1)}, u32[]{:S(2)}, u32[]{:S(2)}) collective-permute-start(bf16[32,2048]{1,0:T(8,128)(2,1)S(1)} %copy-done.24), channel_id=1, source_target_pairs={{0,28},{2,30},{4,24},{6,26},{8,20},{10,22},{12,16},{14,18},{16,12}... | collective-permute-start | bytes 393224 | tf_op jit(solution)/shard_map/ppermute | solution.py:60
  218.2 11.3 %collective-permute-start.31 = (bf16[32,2048]{1,0:T(8,128)(2,1)S(1)}, bf16[32,2048]{1,0:T(8,128)(2,1)S(1)}, u32[]{:S(2)}, u32[]{:S(2)}) collective-permute-start(bf16[32,2048]{1,0:T(8,128)(2,1)S(1)} %copy-done.23), channel_id=1, source_target_pairs={{0,30},{2,28},{4,26},{6,24},{8,22},{10,20},{12,18},{14,16},{16,14}... | collective-permute-start | bytes 393224 | tf_op jit(solution)/shard_map/ppermute | solution.py:60
  (49 other events, 1133.3 us)

commit v14 on v13

--- a/solution.py
+++ b/solution.py
@@ -359,10 +359,13 @@
     got = to_all(sent)
     blocks, grad_rows, relative = dispatch_dy(where, pick, weight, out_grad, groups, capacity)
     blocks = [blocks[0], *(after(b, *w_ins[1:], *w_outs[1:]) for b in blocks[1:])]
-    y_sent, act, inner = expert_forward(got, w_ins, w_outs)
     dys = [blocks[0]]
     for j in range(1, groups):
-        needs = (inner, dys[j - queued]) if j > queued else ()
+        needs = (dys[j - queued],) if j > queued else ()
+        if j == 2 * queued + 1:
+            y_sent, act, inner = expert_forward(after(got, *dys[1 : queued + 1]), w_ins, w_outs)
+        if j > 2 * queued:
+            needs += (inner,)
         dys.append(to_partner(after(blocks[j], *needs) if needs else blocks[j], j))
     y_got = to_all(after(y_sent, *dys[1:]))
     dxs, act_grad, dy_rows = expert_backward(where, dys, act, w_ins, w_outs)
@@ -374,7 +377,8 @@
     parts = []
     for shard in [*range(1, len(w_ins)), 0]:
         parts.append(weight_grads(shard, got, dy_rows, inner, act_grad))
-    parts = [parts[-1]] + [from_owner(after(p, y_got), step) for step, p in enumerate(parts[:-1], 1)]
+    *parts, y_got = lax.optimization_barrier((*parts, y_got))
+    parts = [parts[-1]] + [from_owner(p, step) for step, p in enumerate(parts[:-1], 1)]
     double = w_gate_up.shape[2]
     sums = [
         sum(p[:, columns].astype(F32) for p in parts)

time: 234 us -> 221 us (0.944)
  waiting for transfers between devices: 102 us -> 82.9 us
  starting transfers between devices: 60.7 us -> 68.1 us
    all_to_all x2, waiting for transfers between devices: 70.4 us -> 20.7 us  [to_all(): lax.all_to_all(rows, ('node', 'local'), split_axis=0, concat_axis=0, tile...]
    ppermute x30, waiting for transfers between devices: 28.5 us -> 58.9 us  [to_partner(): lax.ppermute(block, ('node', 'local'), [(i, i ^ j) for i in range(count)])]
    ppermute x30, starting transfers between devices: 47.5 us -> 52.2 us  [to_partner(): lax.ppermute(block, ('node', 'local'), [(i, i ^ j) for i in range(count)])]
    all_to_all x2, starting transfers between devices: 12.6 us -> 15.3 us  [to_all(): lax.all_to_all(rows, ('node', 'local'), split_axis=0, concat_axis=0, tile...]
  transfers between devices with their start and end apart: 35 -> 35, of which waited for: 10 -> 11; matrix products, arithmetic and copies ran while one was open for 5% -> 5% of each run, Pallas kernels for 20% -> 22%
where the time goes in v14:
time: 221 us
  waiting for transfers between devices  82.9 us (38%)
  starting transfers between devices  68.1 us (31%)
  Pallas kernels  54.3 us (25%)
  other arithmetic  10.5 us (5%)
  local copies, waits for them, and re-layouts  3.87 us (2%)
    ppermute x30, waiting for transfers between devices, to_partner(): lax.ppermute(block, ('node', 'local'), [(i, i ^ j) for i in range(count)])  58.9 us
    ppermute x30, starting transfers between devices, to_partner(): lax.ppermute(block, ('node', 'local'), [(i, i ^ j) for i in range(count)])  52.2 us
    all_to_all x2, waiting for transfers between devices, to_all(): lax.all_to_all(rows, ('node', 'local'), split_axis=0, concat_axis=0, tile...  20.7 us
    all_to_all x2, starting transfers between devices, to_all(): lax.all_to_all(rows, ('node', 'local'), split_axis=0, concat_axis=0, tile...  15.3 us
    pallas_call x2, Pallas kernels, weight_grads(): call(kernel, 'weight_grads', cost=work(6 * slots * size * hidden), grid=(...  13.8 us
    pallas_call x1, Pallas kernels, expert_backward(): call(kernel, 'expert_backward', cost=work(6 * slots * model * hidden), in...  13.4 us
    pallas_call x1, Pallas kernels, expert_forward(): call(kernel, 'expert_forward', cost=work(6 * slots * model * hidden), in_...  11.2 us
    add x2, other arithmetic, shards(): sum((p[:, columns].astype(F32) for p in parts))  8.95 us
  transfers between devices with their start and end apart: 35, of which 11 were waited for; matrix products, arithmetic and copies ran while one was open for 5% of the time, Pallas kernels for 22%

profile of v14, /device:TPU:0, one launch (start us, length us, event | category | flops | bytes accessed | tf_op | source)
XLA Modules:
  0.0 220.8 jit_solution(3185746255805661097)
XLA Ops:
  1.2 3.5 %dispatch_x.1 = (bf16[16,32,2048]{2,1,0:T(8,128)(2,1)}, bf16[512,256]{1,0:T(8,128)(2,1)}, f32[512,1]{1,0:T(8,128)}) custom-call(s32[2]{0:T(128)} %pad_add_fusion.where_ref, s32[8,256]{1,0:T(8,128)} %bitcast.17, f32[8,256]{1,0:T(8,128)} %bitcast.19, bf16[256,2048]{1,0:T(8,128)(2,1)} %x_ref.1), custom_call_target="tpu_custom_call" | custom-call | flops 1 | bytes 1 | tf_op jit(solution)/shard_map/dispatch_x/pallas_call | solution.py:105
  4.7 8.3 %all-to-all-start = ((bf16[16,32,2048]{2,1,0:T(8,128)(2,1)}), bf16[16,32,2048]{2,1,0:T(8,128)(2,1)S(1)}, u32[]{:S(2)}, u32[]{:S(2)}) async-start(bf16[16,32,2048]{2,1,0:T(8,128)(2,1)} %get-tuple-element.141), calls=%async_computation | async-start | bytes 4194304 | tf_op jit(solution)/shard_map/all_to_all | solution.py:55
  13.6 4.2 %dispatch_dy.1 = (bf16[32,2048]{1,0:T(8,128)(2,1)}, bf16[32,2048]{1,0:T(8,128)(2,1)}, bf16[32,2048]{1,0:T(8,128)(2,1)}, bf16[32,2048]{1,0:T(8,128)(2,1)}, bf16[3...) custom-call(s32[2]{0:T(128)} %pad_add_fusion.where_ref, ...), custom_call_target="tpu_custom_call" | custom-call | flops 1 | bytes 1 | tf_op jit(solution)/shard_map/dispatch_dy/pallas_call | solution.py:137
  17.8 3.4 %collective-permute-done.1.refs_3_.refs_20_ = bf16[1024,768]{1,0:T(8,128)(2,1)S(1)} collective-permute-done((bf16[1024,768]{1,0:T(8,128)(2,1)}, bf16[1024,768]{1,0:T(8,128)(2,1)S(1)}, u32[]{:S(2)}, u32[]{:S(2)}) %collective-permute-start.1) | collective-permute-done | bytes 1572896 | tf_op jit(solution)/shard_map/ppermute | solution.py:45
  21.2 2.8 %collective-permute-start.6 = (bf16[32,2048]{1,0:T(8,128)(2,1)}, bf16[32,2048]{1,0:T(8,128)(2,1)S(1)}, u32[]{:S(2)}, u32[]{:S(2)}) collective-permute-start(bf16[32,2048]{1,0:T(8,128)(2,1)} %get-tuple-element.123), channel_id=1, source_target_pairs={{0,10},{2,8},{4,14},{6,12},{8,2},{10,0},{12,6},{14,4},{16,26},{18,... | collective-permute-start | bytes 393224 | tf_op jit(solution)/shard_map/ppermute | solution.py:60
  24.6 2.4 %collective-permute-start.4 = (bf16[32,2048]{1,0:T(8,128)(2,1)}, bf16[32,2048]{1,0:T(8,128)(2,1)S(1)}, u32[]{:S(2)}, u32[]{:S(2)}) collective-permute-start(bf16[32,2048]{1,0:T(8,128)(2,1)} %get-tuple-element.119), channel_id=1, source_target_pairs={{0,6},{2,4},{4,2},{6,0},{8,14},{10,12},{12,10},{14,8},{16,22},{18,... | collective-permute-start | bytes 393224 | tf_op jit(solution)/shard_map/ppermute | solution.py:60
  26.9 2.0 collective-permute-start.2
  29.0 22.2 %collective-permute-done.6.refs_5_ = bf16[32,2048]{1,0:T(8,128)(2,1)S(1)} collective-permute-done((bf16[32,2048]{1,0:T(8,128)(2,1)}, bf16[32,2048]{1,0:T(8,128)(2,1)S(1)}, u32[]{:S(2)}, u32[]{:S(2)}) %collective-permute-start.6) | collective-permute-done | bytes 131104 | tf_op jit(solution)/shard_map/ppermute | solution.py:60
  51.2 6.4 %collective-permute-start.11 = (bf16[32,2048]{1,0:T(8,128)(2,1)}, bf16[32,2048]{1,0:T(8,128)(2,1)S(1)}, u32[]{:S(2)}, u32[]{:S(2)}) collective-permute-start(bf16[32,2048]{1,0:T(8,128)(2,1)} %get-tuple-element.138), channel_id=1, source_target_pairs={{0,20},{2,22},{4,16},{6,18},{8,28},{10,30},{12,24},{14,26},{16,4},... | collective-permute-start | bytes 393224 | tf_op jit(solution)/shard_map/ppermute | solution.py:60
  59.7 16.9 %collective-permute-done.3.refs_2_ = bf16[32,2048]{1,0:T(8,128)(2,1)S(1)} collective-permute-done((bf16[32,2048]{1,0:T(8,128)(2,1)}, bf16[32,2048]{1,0:T(8,128)(2,1)S(1)}, u32[]{:S(2)}, u32[]{:S(2)}) %collective-permute-start.3) | collective-permute-done | bytes 131104 | tf_op jit(solution)/shard_map/ppermute | solution.py:60
  79.4 11.2 %expert_forward.1 = (bf16[16,32,2048]{2,1,0:T(8,128)(2,1)}, f32[512,1536]{1,0:T(8,128)}, bf16[512,768]{1,0:T(8,128)(2,1)}) custom-call(bf16[16,32,2048]{2,1,0:T(8,128)(2,1)} %copy-done.1, bf16[1024,1536]{1,0:T(8,128)(2,1)} %bitcast.21, bf16[1024,1536]{1,0:T(8,128)(2,1)} %copy-done.18, bf16[1024,768]{1,0:T(8,128)(2,1)} %bitcast.24, bf16[1024,768]{1,0:T(8,128)(2,1)} %copy-done.19), custom_call_target="tpu_custom_call" | custom-call | flops 4831838208 | bytes 24159192 | tf_op jit(solution)/shard_map/expert_forward/pallas_call | solution.py:189
  90.7 4.1 %collective-permute-start.12 = (bf16[32,2048]{1,0:T(8,128)(2,1)S(1)}, bf16[32,2048]{1,0:T(8,128)(2,1)S(1)}, u32[]{:S(2)}, u32[]{:S(2)}) collective-permute-start(bf16[32,2048]{1,0:T(8,128)(2,1)S(1)} %copy-done.32), channel_id=1, source_target_pairs={{0,22},{2,20},{4,18},{6,16},{8,30},{10,28},{12,26},{14,24},{16,6},... | collective-permute-start | bytes 393224 | tf_op jit(solution)/shard_map/ppermute | solution.py:60
  97.2 2.1 collective-permute-start.15
  99.3 4.1 %collective-permute-start.16 = (bf16[32,2048]{1,0:T(8,128)(2,1)S(1)}, bf16[32,2048]{1,0:T(8,128)(2,1)S(1)}, u32[]{:S(2)}, u32[]{:S(2)}) collective-permute-start(bf16[32,2048]{1,0:T(8,128)(2,1)S(1)} %copy-done.26), channel_id=1, source_target_pairs={{0,30},{2,28},{4,26},{6,24},{8,22},{10,20},{12,18},{14,16},{16,14}... | collective-permute-start | bytes 393224 | tf_op jit(solution)/shard_map/ppermute | solution.py:60
  103.3 3.8 %collective-permute-done.13.refs_12_ = bf16[32,2048]{1,0:T(8,128)(2,1)S(1)} collective-permute-done((bf16[32,2048]{1,0:T(8,128)(2,1)S(1)}, bf16[32,2048]{1,0:T(8,128)(2,1)S(1)}, u32[]{:S(2)}, u32[]{:S(2)}) %collective-permute-start.13) | collective-permute-done | bytes 131104 | tf_op jit(solution)/shard_map/ppermute | solution.py:60
  107.1 3.3 %collective-permute-done.15.refs_14_ = bf16[32,2048]{1,0:T(8,128)(2,1)S(1)} collective-permute-done((bf16[32,2048]{1,0:T(8,128)(2,1)S(1)}, bf16[32,2048]{1,0:T(8,128)(2,1)S(1)}, u32[]{:S(2)}, u32[]{:S(2)}) %collective-permute-start.15) | collective-permute-done | bytes 131104 | tf_op jit(solution)/shard_map/ppermute | solution.py:60
  111.2 7.0 %all-to-all-start.1 = ((bf16[16,32,2048]{2,1,0:T(8,128)(2,1)}), bf16[16,32,2048]{2,1,0:T(8,128)(2,1)S(1)}, u32[]{:S(2)}, u32[]{:S(2)}) async-start(bf16[16,32,2048]{2,1,0:T(8,128)(2,1)} %get-tuple-element.166), calls=%async_computation.1 | async-start | bytes 4194304 | tf_op jit(solution)/shard_map/all_to_all | solution.py:55
  118.2 13.4 %expert_backward.1 = (bf16[32,2048]{1,0:T(8,128)(2,1)}, bf16[32,2048]{1,0:T(8,128)(2,1)}, bf16[32,2048]{1,0:T(8,128)(2,1)}, bf16[32,2048]{1,0:T(8,128)(2,1)}, bf...) custom-call(s32[2]{0:T(128)} %pad_add_fusion.where_ref, ...), custom_call_target="tpu_custom_call" | custom-call | flops 4831838208 | bytes 24159192 | tf_op jit(solution)/shard_map/expert_backward/pallas_call | solution.py:237
  131.6 6.9 %weight_grads.3 = bf16[1024,2304]{1,0:T(8,128)(2,1)} custom-call(bf16[16,32,2048]{2,1,0:T(8,128)(2,1)} %copy-done.1, bf16[512,2048]{1,0:T(8,128)(2,1)} %get-tuple-element.186.dy_ref, bf16[512,768]{1,0:T(8,128)(2,1)} %get-tuple-element.143.inner_ref, bf16[512,1536]{1,0:T(8,128)(2,1)} %get-tuple-element.187.act_grad_ref), custom_call_target="tpu_custom_call" | custom-call | flops 2415919104 | bytes 12079595 | tf_op jit(solution)/shard_map/weight_grads/pallas_call | solution.py:270
  138.5 6.9 %weight_grads.2 = bf16[1024,2304]{1,0:T(8,128)(2,1)} custom-call(bf16[16,32,2048]{2,1,0:T(8,128)(2,1)} %copy-done.1, bf16[512,2048]{1,0:T(8,128)(2,1)} %get-tuple-element.186.dy_ref, bf16[512,768]{1,0:T(8,128)(2,1)} %get-tuple-element.143.inner_ref, bf16[512,1536]{1,0:T(8,128)(2,1)} %get-tuple-element.187.act_grad_ref), custom_call_target="tpu_custom_call" | custom-call | flops 2415919104 | bytes 12079595 | tf_op jit(solution)/shard_map/weight_grads/pallas_call | solution.py:270
  145.5 20.7 %all-to-all-done.1.refs_0_ = bf16[16,32,2048]{2,1,0:T(8,128)(2,1)S(1)} async-done(((bf16[16,32,2048]{2,1,0:T(8,128)(2,1)}), bf16[16,32,2048]{2,1,0:T(8,128)(2,1)S(1)}, u32[]{:S(2)}, u32[]{:S(2)}) %all-to-all-start.1) | async-done | bytes 2097184 | tf_op jit(solution)/shard_map/all_to_all | solution.py:55
  167.3 3.3 %collective-permute-start.19 = (bf16[32,2048]{1,0:T(8,128)(2,1)}, bf16[32,2048]{1,0:T(8,128)(2,1)S(1)}, u32[]{:S(2)}, u32[]{:S(2)}) collective-permute-start(bf16[32,2048]{1,0:T(8,128)(2,1)} %get-tuple-element.161), channel_id=1, source_target_pairs={{0,6},{2,4},{4,2},{6,0},{8,14},{10,12},{12,10},{14,8},{16,22},{18,... | collective-permute-start | bytes 393224 | tf_op jit(solution)/shard_map/ppermute | solution.py:60
  170.6 2.6 %collective-permute-done.17.refs_1_ = bf16[32,2048]{1,0:T(8,128)(2,1)S(1)} collective-permute-done((bf16[32,2048]{1,0:T(8,128)(2,1)S(1)}, bf16[32,2048]{1,0:T(8,128)(2,1)S(1)}, u32[]{:S(2)}, u32[]{:S(2)}) %collective-permute-start.17) | collective-permute-done | bytes 131104 | tf_op jit(solution)/shard_map/ppermute | solution.py:60
  173.2 6.2 %collective-permute-done.18.refs_2_ = bf16[32,2048]{1,0:T(8,128)(2,1)S(1)} collective-permute-done((bf16[32,2048]{1,0:T(8,128)(2,1)S(1)}, bf16[32,2048]{1,0:T(8,128)(2,1)S(1)}, u32[]{:S(2)}, u32[]{:S(2)}) %collective-permute-start.18) | collective-permute-done | bytes 131104 | tf_op jit(solution)/shard_map/ppermute | solution.py:60
  182.7 5.6 %collective-permute-start.25 = (bf16[32,2048]{1,0:T(8,128)(2,1)}, bf16[32,2048]{1,0:T(8,128)(2,1)S(1)}, u32[]{:S(2)}, u32[]{:S(2)}) collective-permute-start(bf16[32,2048]{1,0:T(8,128)(2,1)} %get-tuple-element.173), channel_id=1, source_target_pairs={{0,18},{2,16},{4,22},{6,20},{8,26},{10,24},{12,30},{14,28},{16,2},... | collective-permute-start | bytes 393224 | tf_op jit(solution)/shard_map/ppermute | solution.py:60
  188.3 2.5 %collective-permute-done.22.refs_6_ = bf16[32,2048]{1,0:T(8,128)(2,1)} collective-permute-done((bf16[32,2048]{1,0:T(8,128)(2,1)}, bf16[32,2048]{1,0:T(8,128)(2,1)}, u32[]{:S(2)}, u32[]{:S(2)}) %collective-permute-start.22) | collective-permute-done | bytes 131104 | tf_op jit(solution)/shard_map/ppermute | solution.py:60
  191.7 4.9 %combine_y.1 = (bf16[256,2048]{1,0:T(8,128)(2,1)}, f32[8,256]{1,0:T(8,128)}) custom-call(s32[2]{0:T(128)} %pad_add_fusion.where_ref, bf16[512,256]{1,0:T(8,128)(2,1)} %get-tuple-element.111.pick_ref, bf16[256,512]{1,0:T(8,128)(2,1)} %get-tuple-element.218.high_ref, bf16[256,512]{1,0:T(8,128)(2,1)} %get-tuple-element.217.middle_ref, s32[8,256]{1,0:T(8,128)} %bitcast.18, ...), custom_call_target="tpu_custom_call" | custom-call | flops 1 | bytes 1 | tf_op jit(solution)/shard_map/combine_y/pallas_call | solution.py:315
  200.4 3.0 %collective-permute-start.29 = (bf16[32,2048]{1,0:T(8,128)(2,1)}, bf16[32,2048]{1,0:T(8,128)(2,1)S(1)}, u32[]{:S(2)}, u32[]{:S(2)}) collective-permute-start(bf16[32,2048]{1,0:T(8,128)(2,1)} %get-tuple-element.181), channel_id=1, source_target_pairs={{0,26},{2,24},{4,30},{6,28},{8,18},{10,16},{12,22},{14,20},{16,10}... | collective-permute-start | bytes 393224 | tf_op jit(solution)/shard_map/ppermute | solution.py:60
  205.0 2.0 collective-permute-start.31
  207.0 5.6 %convert_add_fusion = f32[1024,1536]{1,0:T(8,128)} fusion(bf16[1024,2304]{1,0:T(8,128)(2,1)} %collective-permute-done.32, bf16[1024,2304]{1,0:T(8,128)(2,1)S(1)} %copy-done), kind=kLoop, calls=%fused_computation | loop fusion | flops 4718592 | bytes 12582912 | tf_op jit(solution)/shard_map/add | solution.py:384
  212.6 3.4 %convert_add_fusion.1 = f32[1024,768]{1,0:T(8,128)} fusion(bf16[1024,2304]{1,0:T(8,128)(2,1)} %collective-permute-done.32, bf16[1024,2304]{1,0:T(8,128)(2,1)S(1)} %copy-done), kind=kLoop, calls=%fused_computation.1 | loop fusion | flops 2359296 | bytes 6291456 | tf_op jit(solution)/shard_map/add | solution.py:384
  217.4 3.4 %combine_dx.1 = bf16[256,2048]{1,0:T(8,128)(2,1)} custom-call(s32[2]{0:T(128)} %pad_add_fusion.where_ref, bf16[256,512]{1,0:T(8,128)(2,1)} %bitcast.16, bf16[32,2048]{1,0:T(8,128)(2,1)} %get-tuple-element.198.refs_0_, bf16[32,2048]{1,0:T(8,128)(2,1)} %copy-done.6, bf16[32,2048]{1,0:T(8,128)(2,1)} %copy-done.7, bf16[32,2048]{1,0:T(8,128)(2,1)} %copy-done.8, ...), custom_call_target="tpu_custom_call" | custom-call | flops 1 | bytes 1 | tf_op jit(solution)/shard_map/combine_dx/pallas_call | solution.py:339
  (133 shorter events, 21.9 us)
Async XLA Ops:
  4.7 73.4 %all-to-all-start = ((bf16[16,32,2048]{2,1,0:T(8,128)(2,1)}), bf16[16,32,2048]{2,1,0:T(8,128)(2,1)S(1)}, u32[]{:S(2)}, u32[]{:S(2)}) async-start(bf16[16,32,2048]{2,1,0:T(8,128)(2,1)} %get-tuple-element.141), calls=%async_computation | async-start | bytes 4194304 | tf_op jit(solution)/shard_map/all_to_all | solution.py:55
  21.2 30.0 %collective-permute-start.6 = (bf16[32,2048]{1,0:T(8,128)(2,1)}, bf16[32,2048]{1,0:T(8,128)(2,1)S(1)}, u32[]{:S(2)}, u32[]{:S(2)}) collective-permute-start(bf16[32,2048]{1,0:T(8,128)(2,1)} %get-tuple-element.123), channel_id=1, source_target_pairs={{0,10},{2,8},{4,14},{6,12},{8,2},{10,0},{12,6},{14,4},{16,26},{18,... | collective-permute-start | bytes 393224 | tf_op jit(solution)/shard_map/ppermute | solution.py:60
  24.0 33.5 %collective-permute-start.5 = (bf16[32,2048]{1,0:T(8,128)(2,1)}, bf16[32,2048]{1,0:T(8,128)(2,1)S(1)}, u32[]{:S(2)}, u32[]{:S(2)}) collective-permute-start(bf16[32,2048]{1,0:T(8,128)(2,1)} %get-tuple-element.121), channel_id=1, source_target_pairs={{0,8},{2,10},{4,12},{6,14},{8,0},{10,2},{12,4},{14,6},{16,24},{18,... | collective-permute-start | bytes 393224 | tf_op jit(solution)/shard_map/ppermute | solution.py:60
  24.6 33.7 %collective-permute-start.4 = (bf16[32,2048]{1,0:T(8,128)(2,1)}, bf16[32,2048]{1,0:T(8,128)(2,1)S(1)}, u32[]{:S(2)}, u32[]{:S(2)}) collective-permute-start(bf16[32,2048]{1,0:T(8,128)(2,1)} %get-tuple-element.119), channel_id=1, source_target_pairs={{0,6},{2,4},{4,2},{6,0},{8,14},{10,12},{12,10},{14,8},{16,22},{18,... | collective-permute-start | bytes 393224 | tf_op jit(solution)/shard_map/ppermute | solution.py:60
  26.9 49.7 %collective-permute-start.3 = (bf16[32,2048]{1,0:T(8,128)(2,1)}, bf16[32,2048]{1,0:T(8,128)(2,1)S(1)}, u32[]{:S(2)}, u32[]{:S(2)}) collective-permute-start(bf16[32,2048]{1,0:T(8,128)(2,1)} %get-tuple-element.117), channel_id=1, source_target_pairs={{0,4},{2,6},{4,0},{6,2},{8,12},{10,14},{12,8},{14,10},{16,20},{18,... | collective-permute-start | bytes 393224 | tf_op jit(solution)/shard_map/ppermute | solution.py:60
  26.9 50.7 %collective-permute-start.2 = (bf16[32,2048]{1,0:T(8,128)(2,1)}, bf16[32,2048]{1,0:T(8,128)(2,1)S(1)}, u32[]{:S(2)}, u32[]{:S(2)}) collective-permute-start(bf16[32,2048]{1,0:T(8,128)(2,1)} %get-tuple-element.115), channel_id=1, source_target_pairs={{0,2},{2,0},{4,6},{6,4},{8,10},{10,8},{12,14},{14,12},{16,18},{18,... | collective-permute-start | bytes 393224 | tf_op jit(solution)/shard_map/ppermute | solution.py:60
  51.2 39.4 %collective-permute-start.11 = (bf16[32,2048]{1,0:T(8,128)(2,1)}, bf16[32,2048]{1,0:T(8,128)(2,1)S(1)}, u32[]{:S(2)}, u32[]{:S(2)}) collective-permute-start(bf16[32,2048]{1,0:T(8,128)(2,1)} %get-tuple-element.138), channel_id=1, source_target_pairs={{0,20},{2,22},{4,16},{6,18},{8,28},{10,30},{12,24},{14,26},{16,4},... | collective-permute-start | bytes 393224 | tf_op jit(solution)/shard_map/ppermute | solution.py:60
  57.5 33.1 %collective-permute-start.10 = (bf16[32,2048]{1,0:T(8,128)(2,1)}, bf16[32,2048]{1,0:T(8,128)(2,1)S(1)}, u32[]{:S(2)}, u32[]{:S(2)}) collective-permute-start(bf16[32,2048]{1,0:T(8,128)(2,1)} %get-tuple-element.135), channel_id=1, source_target_pairs={{0,18},{2,16},{4,22},{6,20},{8,26},{10,24},{12,30},{14,28},{16,2},... | collective-permute-start | bytes 393224 | tf_op jit(solution)/shard_map/ppermute | solution.py:60
  58.2 32.4 %collective-permute-start.9 = (bf16[32,2048]{1,0:T(8,128)(2,1)}, bf16[32,2048]{1,0:T(8,128)(2,1)}, u32[]{:S(2)}, u32[]{:S(2)}) collective-permute-start(bf16[32,2048]{1,0:T(8,128)(2,1)} %get-tuple-element.132), channel_id=1, source_target_pairs={{0,16},{2,18},{4,20},{6,22},{8,24},{10,26},{12,28},{14,30},{16,0},... | collective-permute-start | bytes 393224 | tf_op jit(solution)/shard_map/ppermute | solution.py:60
  76.6 14.0 %collective-permute-start.8 = (bf16[32,2048]{1,0:T(8,128)(2,1)}, bf16[32,2048]{1,0:T(8,128)(2,1)}, u32[]{:S(2)}, u32[]{:S(2)}) collective-permute-start(bf16[32,2048]{1,0:T(8,128)(2,1)} %get-tuple-element.129), channel_id=1, source_target_pairs={{0,14},{2,12},{4,10},{6,8},{8,6},{10,4},{12,2},{14,0},{16,30},{18,... | collective-permute-start | bytes 393224 | tf_op jit(solution)/shard_map/ppermute | solution.py:60
  77.6 13.0 %collective-permute-start.7 = (bf16[32,2048]{1,0:T(8,128)(2,1)}, bf16[32,2048]{1,0:T(8,128)(2,1)}, u32[]{:S(2)}, u32[]{:S(2)}) collective-permute-start(bf16[32,2048]{1,0:T(8,128)(2,1)} %get-tuple-element.126), channel_id=1, source_target_pairs={{0,12},{2,14},{4,8},{6,10},{8,4},{10,6},{12,0},{14,2},{16,28},{18,... | collective-permute-start | bytes 393224 | tf_op jit(solution)/shard_map/ppermute | solution.py:60
  90.7 12.7 %collective-permute-start.12 = (bf16[32,2048]{1,0:T(8,128)(2,1)S(1)}, bf16[32,2048]{1,0:T(8,128)(2,1)S(1)}, u32[]{:S(2)}, u32[]{:S(2)}) collective-permute-start(bf16[32,2048]{1,0:T(8,128)(2,1)S(1)} %copy-done.32), channel_id=1, source_target_pairs={{0,22},{2,20},{4,18},{6,16},{8,30},{10,28},{12,26},{14,24},{16,6},... | collective-permute-start | bytes 393224 | tf_op jit(solution)/shard_map/ppermute | solution.py:60
  94.8 12.4 %collective-permute-start.13 = (bf16[32,2048]{1,0:T(8,128)(2,1)S(1)}, bf16[32,2048]{1,0:T(8,128)(2,1)S(1)}, u32[]{:S(2)}, u32[]{:S(2)}) collective-permute-start(bf16[32,2048]{1,0:T(8,128)(2,1)S(1)} %copy-done.31), channel_id=1, source_target_pairs={{0,24},{2,26},{4,28},{6,30},{8,16},{10,18},{12,20},{14,22},{16,8},... | collective-permute-start | bytes 393224 | tf_op jit(solution)/shard_map/ppermute | solution.py:60
  95.6 11.5 %collective-permute-start.14 = (bf16[32,2048]{1,0:T(8,128)(2,1)S(1)}, bf16[32,2048]{1,0:T(8,128)(2,1)S(1)}, u32[]{:S(2)}, u32[]{:S(2)}) collective-permute-start(bf16[32,2048]{1,0:T(8,128)(2,1)S(1)} %copy-done.29), channel_id=1, source_target_pairs={{0,26},{2,24},{4,30},{6,28},{8,18},{10,16},{12,22},{14,20},{16,10}... | collective-permute-start | bytes 393224 | tf_op jit(solution)/shard_map/ppermute | solution.py:60
  97.2 13.3 %collective-permute-start.15 = (bf16[32,2048]{1,0:T(8,128)(2,1)S(1)}, bf16[32,2048]{1,0:T(8,128)(2,1)S(1)}, u32[]{:S(2)}, u32[]{:S(2)}) collective-permute-start(bf16[32,2048]{1,0:T(8,128)(2,1)S(1)} %copy-done.28), channel_id=1, source_target_pairs={{0,28},{2,30},{4,24},{6,26},{8,20},{10,22},{12,16},{14,18},{16,12}... | collective-permute-start | bytes 393224 | tf_op jit(solution)/shard_map/ppermute | solution.py:60
  99.3 11.2 %collective-permute-start.16 = (bf16[32,2048]{1,0:T(8,128)(2,1)S(1)}, bf16[32,2048]{1,0:T(8,128)(2,1)S(1)}, u32[]{:S(2)}, u32[]{:S(2)}) collective-permute-start(bf16[32,2048]{1,0:T(8,128)(2,1)S(1)} %copy-done.26), channel_id=1, source_target_pairs={{0,30},{2,28},{4,26},{6,24},{8,22},{10,20},{12,18},{14,16},{16,14}... | collective-permute-start | bytes 393224 | tf_op jit(solution)/shard_map/ppermute | solution.py:60
  111.2 54.9 %all-to-all-start.1 = ((bf16[16,32,2048]{2,1,0:T(8,128)(2,1)}), bf16[16,32,2048]{2,1,0:T(8,128)(2,1)S(1)}, u32[]{:S(2)}, u32[]{:S(2)}) async-start(bf16[16,32,2048]{2,1,0:T(8,128)(2,1)} %get-tuple-element.166), calls=%async_computation.1 | async-start | bytes 4194304 | tf_op jit(solution)/shard_map/all_to_all | solution.py:55
  166.1 38.9 %collective-permute-start.32 = (bf16[1024,2304]{1,0:T(8,128)(2,1)}, bf16[1024,2304]{1,0:T(8,128)(2,1)}, u32[]{:S(2)}, u32[]{:S(2)}) collective-permute-start(bf16[1024,2304]{1,0:T(8,128)(2,1)} %weight_grads.2), channel_id=1, source_target_pairs={{0,1},{1,0},{2,3},{3,2},{4,5},{5,4},{6,7},{7,6},{8,9},{9,8},{10,11... | collective-permute-start | bytes 14155784 | tf_op jit(solution)/shard_map/ppermute | solution.py:51
  166.2 13.2 %collective-permute-start.18 = (bf16[32,2048]{1,0:T(8,128)(2,1)S(1)}, bf16[32,2048]{1,0:T(8,128)(2,1)S(1)}, u32[]{:S(2)}, u32[]{:S(2)}) collective-permute-start(bf16[32,2048]{1,0:T(8,128)(2,1)S(1)} %copy-done.34), channel_id=1, source_target_pairs={{0,4},{2,6},{4,0},{6,2},{8,12},{10,14},{12,8},{14,10},{16,20},{18,... | collective-permute-start | bytes 393224 | tf_op jit(solution)/shard_map/ppermute | solution.py:60
  167.3 13.3 %collective-permute-start.19 = (bf16[32,2048]{1,0:T(8,128)(2,1)}, bf16[32,2048]{1,0:T(8,128)(2,1)S(1)}, u32[]{:S(2)}, u32[]{:S(2)}) collective-permute-start(bf16[32,2048]{1,0:T(8,128)(2,1)} %get-tuple-element.161), channel_id=1, source_target_pairs={{0,6},{2,4},{4,2},{6,0},{8,14},{10,12},{12,10},{14,8},{16,22},{18,... | collective-permute-start | bytes 393224 | tf_op jit(solution)/shard_map/ppermute | solution.py:60
  170.6 11.6 %collective-permute-start.20 = (bf16[32,2048]{1,0:T(8,128)(2,1)}, bf16[32,2048]{1,0:T(8,128)(2,1)}, u32[]{:S(2)}, u32[]{:S(2)}) collective-permute-start(bf16[32,2048]{1,0:T(8,128)(2,1)} %get-tuple-element.162), channel_id=1, source_target_pairs={{0,8},{2,10},{4,12},{6,14},{8,0},{10,2},{12,4},{14,6},{16,24},{18,... | collective-permute-start | bytes 393224 | tf_op jit(solution)/shard_map/ppermute | solution.py:60
  173.2 9.5 %collective-permute-start.21 = (bf16[32,2048]{1,0:T(8,128)(2,1)}, bf16[32,2048]{1,0:T(8,128)(2,1)}, u32[]{:S(2)}, u32[]{:S(2)}) collective-permute-start(bf16[32,2048]{1,0:T(8,128)(2,1)} %get-tuple-element.163), channel_id=1, source_target_pairs={{0,10},{2,8},{4,14},{6,12},{8,2},{10,0},{12,6},{14,4},{16,26},{18,... | collective-permute-start | bytes 393224 | tf_op jit(solution)/shard_map/ppermute | solution.py:60
  179.4 11.4 %collective-permute-start.22 = (bf16[32,2048]{1,0:T(8,128)(2,1)}, bf16[32,2048]{1,0:T(8,128)(2,1)}, u32[]{:S(2)}, u32[]{:S(2)}) collective-permute-start(bf16[32,2048]{1,0:T(8,128)(2,1)} %get-tuple-element.167), channel_id=1, source_target_pairs={{0,12},{2,14},{4,8},{6,10},{8,4},{10,6},{12,0},{14,2},{16,28},{18,... | collective-permute-start | bytes 393224 | tf_op jit(solution)/shard_map/ppermute | solution.py:60
  180.6 16.0 %collective-permute-start.23 = (bf16[32,2048]{1,0:T(8,128)(2,1)}, bf16[32,2048]{1,0:T(8,128)(2,1)S(1)}, u32[]{:S(2)}, u32[]{:S(2)}) collective-permute-start(bf16[32,2048]{1,0:T(8,128)(2,1)} %get-tuple-element.169), channel_id=1, source_target_pairs={{0,14},{2,12},{4,10},{6,8},{8,6},{10,4},{12,2},{14,0},{16,30},{18,... | collective-permute-start | bytes 393224 | tf_op jit(solution)/shard_map/ppermute | solution.py:60
  182.1 16.3 %collective-permute-start.24 = (bf16[32,2048]{1,0:T(8,128)(2,1)}, bf16[32,2048]{1,0:T(8,128)(2,1)S(1)}, u32[]{:S(2)}, u32[]{:S(2)}) collective-permute-start(bf16[32,2048]{1,0:T(8,128)(2,1)} %get-tuple-element.171), channel_id=1, source_target_pairs={{0,16},{2,18},{4,20},{6,22},{8,24},{10,26},{12,28},{14,30},{16,0},... | collective-permute-start | bytes 393224 | tf_op jit(solution)/shard_map/ppermute | solution.py:60
  182.7 17.7 %collective-permute-start.25 = (bf16[32,2048]{1,0:T(8,128)(2,1)}, bf16[32,2048]{1,0:T(8,128)(2,1)S(1)}, u32[]{:S(2)}, u32[]{:S(2)}) collective-permute-start(bf16[32,2048]{1,0:T(8,128)(2,1)} %get-tuple-element.173), channel_id=1, source_target_pairs={{0,18},{2,16},{4,22},{6,20},{8,26},{10,24},{12,30},{14,28},{16,2},... | collective-permute-start | bytes 393224 | tf_op jit(solution)/shard_map/ppermute | solution.py:60
  190.8 12.6 %collective-permute-start.26 = (bf16[32,2048]{1,0:T(8,128)(2,1)}, bf16[32,2048]{1,0:T(8,128)(2,1)S(1)}, u32[]{:S(2)}, u32[]{:S(2)}) collective-permute-start(bf16[32,2048]{1,0:T(8,128)(2,1)} %get-tuple-element.175), channel_id=1, source_target_pairs={{0,20},{2,22},{4,16},{6,18},{8,28},{10,30},{12,24},{14,26},{16,4},... | collective-permute-start | bytes 393224 | tf_op jit(solution)/shard_map/ppermute | solution.py:60
  196.6 19.4 %collective-permute-start.27 = (bf16[32,2048]{1,0:T(8,128)(2,1)}, bf16[32,2048]{1,0:T(8,128)(2,1)S(1)}, u32[]{:S(2)}, u32[]{:S(2)}) collective-permute-start(bf16[32,2048]{1,0:T(8,128)(2,1)} %get-tuple-element.177), channel_id=1, source_target_pairs={{0,22},{2,20},{4,18},{6,16},{8,30},{10,28},{12,26},{14,24},{16,6},... | collective-permute-start | bytes 393224 | tf_op jit(solution)/shard_map/ppermute | solution.py:60
  198.4 17.6 %collective-permute-start.28 = (bf16[32,2048]{1,0:T(8,128)(2,1)}, bf16[32,2048]{1,0:T(8,128)(2,1)S(1)}, u32[]{:S(2)}, u32[]{:S(2)}) collective-permute-start(bf16[32,2048]{1,0:T(8,128)(2,1)} %get-tuple-element.179), channel_id=1, source_target_pairs={{0,24},{2,26},{4,28},{6,30},{8,16},{10,18},{12,20},{14,22},{16,8},... | collective-permute-start | bytes 393224 | tf_op jit(solution)/shard_map/ppermute | solution.py:60
  200.4 15.6 %collective-permute-start.29 = (bf16[32,2048]{1,0:T(8,128)(2,1)}, bf16[32,2048]{1,0:T(8,128)(2,1)S(1)}, u32[]{:S(2)}, u32[]{:S(2)}) collective-permute-start(bf16[32,2048]{1,0:T(8,128)(2,1)} %get-tuple-element.181), channel_id=1, source_target_pairs={{0,26},{2,24},{4,30},{6,28},{8,18},{10,16},{12,22},{14,20},{16,10}... | collective-permute-start | bytes 393224 | tf_op jit(solution)/shard_map/ppermute | solution.py:60
  203.4 13.3 %collective-permute-start.30 = (bf16[32,2048]{1,0:T(8,128)(2,1)}, bf16[32,2048]{1,0:T(8,128)(2,1)S(1)}, u32[]{:S(2)}, u32[]{:S(2)}) collective-permute-start(bf16[32,2048]{1,0:T(8,128)(2,1)} %get-tuple-element.183), channel_id=1, source_target_pairs={{0,28},{2,30},{4,24},{6,26},{8,20},{10,22},{12,16},{14,18},{16,12}... | collective-permute-start | bytes 393224 | tf_op jit(solution)/shard_map/ppermute | solution.py:60
  205.0 11.7 %collective-permute-start.31 = (bf16[32,2048]{1,0:T(8,128)(2,1)S(1)}, bf16[32,2048]{1,0:T(8,128)(2,1)S(1)}, u32[]{:S(2)}, u32[]{:S(2)}) collective-permute-start(bf16[32,2048]{1,0:T(8,128)(2,1)S(1)} %copy-done.20), channel_id=1, source_target_pairs={{0,30},{2,28},{4,26},{6,24},{8,22},{10,20},{12,18},{14,16},{16,14}... | collective-permute-start | bytes 393224 | tf_op jit(solution)/shard_map/ppermute | solution.py:60
  (43 other events, 1116.3 us)

commit v15 on v14

--- a/solution.py
+++ b/solution.py
@@ -371,8 +371,9 @@
     dxs, act_grad, dy_rows = expert_backward(where, dys, act, w_ins, w_outs)
     backs = [dxs[0]]
     for j in range(1, groups):
-        needs = (y_got, backs[j - queued]) if j > queued else ()
+        needs = (backs[j - queued],) if j > queued else ()
         backs.append(to_partner(after(dxs[j], *needs) if needs else dxs[j], j))
+    y_got = after(y_got, *backs[1 : queued + 1])
 
     parts = []
     for shard in [*range(1, len(w_ins)), 0]:

time: 221 us -> 228 us (1.032)
  starting transfers between devices: 68.1 us -> 74.1 us
    all_to_all x2, waiting for transfers between devices: 20.7 us -> 0.01 us  [to_all(): lax.all_to_all(rows, ('node', 'local'), split_axis=0, concat_axis=0, tile...]
    ppermute x30, waiting for transfers between devices: 58.9 us -> 79.2 us  [to_partner(): lax.ppermute(block, ('node', 'local'), [(i, i ^ j) for i in range(count)])]
    ppermute x30, starting transfers between devices: 52.2 us -> 61 us  [to_partner(): lax.ppermute(block, ('node', 'local'), [(i, i ^ j) for i in range(count)])]
    all_to_all x2, starting transfers between devices: 15.3 us -> 12.5 us  [to_all(): lax.all_to_all(rows, ('node', 'local'), split_axis=0, concat_axis=0, tile...]
  transfers between devices with their start and end apart: 35 -> 35, of which waited for: 11 -> 10; matrix products, arithmetic and copies ran while one was open for 5% -> 5% of each run, Pallas kernels for 22% -> 21%
where the time goes in v15:
time: 228 us
  waiting for transfers between devices  82.6 us (36%)
  starting transfers between devices  74.1 us (32%)
  Pallas kernels  54.3 us (24%)
  other arithmetic  10.6 us (5%)
  local copies, waits for them, and re-layouts  5.2 us (2%)
    ppermute x30, waiting for transfers between devices, to_partner(): lax.ppermute(block, ('node', 'local'), [(i, i ^ j) for i in range(count)])  79.2 us
    ppermute x30, starting transfers between devices, to_partner(): lax.ppermute(block, ('node', 'local'), [(i, i ^ j) for i in range(count)])  61 us
    pallas_call x2, Pallas kernels, weight_grads(): call(kernel, 'weight_grads', cost=work(6 * slots * size * hidden), grid=(...  13.8 us
    pallas_call x1, Pallas kernels, expert_backward(): call(kernel, 'expert_backward', cost=work(6 * slots * model * hidden), in...  13.4 us
    all_to_all x2, starting transfers between devices, to_all(): lax.all_to_all(rows, ('node', 'local'), split_axis=0, concat_axis=0, tile...  12.5 us
    pallas_call x1, Pallas kernels, expert_forward(): call(kernel, 'expert_forward', cost=work(6 * slots * model * hidden), in_...  11.2 us
    add x2, other arithmetic, shards(): sum((p[:, columns].astype(F32) for p in parts))  8.95 us
    pallas_call x1, Pallas kernels, combine_y(): call(kernel, 'combine_y', in_specs=[SMEM] + [VMEM] * 6, out_specs=[VMEM]...  4.9 us
  transfers between devices with their start and end apart: 35, of which 10 were waited for; matrix products, arithmetic and copies ran while one was open for 5% of the time, Pallas kernels for 21%

profile of v15, /device:TPU:0, one launch (start us, length us, event | category | flops | bytes accessed | tf_op | source)
XLA Modules:
  0.0 227.8 jit_solution(18069445219493743046)
XLA Ops:
  1.2 3.5 %dispatch_x.1 = (bf16[16,32,2048]{2,1,0:T(8,128)(2,1)}, bf16[512,256]{1,0:T(8,128)(2,1)}, f32[512,1]{1,0:T(8,128)}) custom-call(s32[2]{0:T(128)} %pad_add_fusion.where_ref, s32[8,256]{1,0:T(8,128)} %bitcast.17, f32[8,256]{1,0:T(8,128)} %bitcast.19, bf16[256,2048]{1,0:T(8,128)(2,1)} %x_ref.1), custom_call_target="tpu_custom_call" | custom-call | flops 1 | bytes 1 | tf_op jit(solution)/shard_map/dispatch_x/pallas_call | solution.py:105
  4.7 8.3 %all-to-all-start = ((bf16[16,32,2048]{2,1,0:T(8,128)(2,1)}), bf16[16,32,2048]{2,1,0:T(8,128)(2,1)S(1)}, u32[]{:S(2)}, u32[]{:S(2)}) async-start(bf16[16,32,2048]{2,1,0:T(8,128)(2,1)} %get-tuple-element.142), calls=%async_computation | async-start | bytes 4194304 | tf_op jit(solution)/shard_map/all_to_all | solution.py:55
  13.6 4.2 %dispatch_dy.1 = (bf16[32,2048]{1,0:T(8,128)(2,1)}, bf16[32,2048]{1,0:T(8,128)(2,1)}, bf16[32,2048]{1,0:T(8,128)(2,1)}, bf16[32,2048]{1,0:T(8,128)(2,1)}, bf16[3...) custom-call(s32[2]{0:T(128)} %pad_add_fusion.where_ref, ...), custom_call_target="tpu_custom_call" | custom-call | flops 1 | bytes 1 | tf_op jit(solution)/shard_map/dispatch_dy/pallas_call | solution.py:137
  17.8 3.4 %collective-permute-done.1.refs_3_.refs_20_ = bf16[1024,768]{1,0:T(8,128)(2,1)S(1)} collective-permute-done((bf16[1024,768]{1,0:T(8,128)(2,1)}, bf16[1024,768]{1,0:T(8,128)(2,1)S(1)}, u32[]{:S(2)}, u32[]{:S(2)}) %collective-permute-start.1) | collective-permute-done | bytes 1572896 | tf_op jit(solution)/shard_map/ppermute | solution.py:45
  21.2 2.8 %collective-permute-start.6 = (bf16[32,2048]{1,0:T(8,128)(2,1)}, bf16[32,2048]{1,0:T(8,128)(2,1)S(1)}, u32[]{:S(2)}, u32[]{:S(2)}) collective-permute-start(bf16[32,2048]{1,0:T(8,128)(2,1)} %get-tuple-element.124), channel_id=1, source_target_pairs={{0,10},{2,8},{4,14},{6,12},{8,2},{10,0},{12,6},{14,4},{16,26},{18,... | collective-permute-start | bytes 393224 | tf_op jit(solution)/shard_map/ppermute | solution.py:60
  24.6 2.4 %collective-permute-start.4 = (bf16[32,2048]{1,0:T(8,128)(2,1)}, bf16[32,2048]{1,0:T(8,128)(2,1)S(1)}, u32[]{:S(2)}, u32[]{:S(2)}) collective-permute-start(bf16[32,2048]{1,0:T(8,128)(2,1)} %get-tuple-element.120), channel_id=1, source_target_pairs={{0,6},{2,4},{4,2},{6,0},{8,14},{10,12},{12,10},{14,8},{16,22},{18,... | collective-permute-start | bytes 393224 | tf_op jit(solution)/shard_map/ppermute | solution.py:60
  29.0 22.2 %collective-permute-done.6.refs_5_ = bf16[32,2048]{1,0:T(8,128)(2,1)S(1)} collective-permute-done((bf16[32,2048]{1,0:T(8,128)(2,1)}, bf16[32,2048]{1,0:T(8,128)(2,1)S(1)}, u32[]{:S(2)}, u32[]{:S(2)}) %collective-permute-start.6) | collective-permute-done | bytes 131104 | tf_op jit(solution)/shard_map/ppermute | solution.py:60
  51.2 6.4 %collective-permute-start.11 = (bf16[32,2048]{1,0:T(8,128)(2,1)}, bf16[32,2048]{1,0:T(8,128)(2,1)S(1)}, u32[]{:S(2)}, u32[]{:S(2)}) collective-permute-start(bf16[32,2048]{1,0:T(8,128)(2,1)} %get-tuple-element.139), channel_id=1, source_target_pairs={{0,20},{2,22},{4,16},{6,18},{8,28},{10,30},{12,24},{14,26},{16,4},... | collective-permute-start | bytes 393224 | tf_op jit(solution)/shard_map/ppermute | solution.py:60
  59.7 16.9 %collective-permute-done.3.refs_2_ = bf16[32,2048]{1,0:T(8,128)(2,1)S(1)} collective-permute-done((bf16[32,2048]{1,0:T(8,128)(2,1)}, bf16[32,2048]{1,0:T(8,128)(2,1)S(1)}, u32[]{:S(2)}, u32[]{:S(2)}) %collective-permute-start.3) | collective-permute-done | bytes 131104 | tf_op jit(solution)/shard_map/ppermute | solution.py:60
  79.5 11.2 %expert_forward.1 = (bf16[16,32,2048]{2,1,0:T(8,128)(2,1)}, f32[512,1536]{1,0:T(8,128)}, bf16[512,768]{1,0:T(8,128)(2,1)}) custom-call(bf16[16,32,2048]{2,1,0:T(8,128)(2,1)} %copy-done.1, bf16[1024,1536]{1,0:T(8,128)(2,1)} %bitcast.21, bf16[1024,1536]{1,0:T(8,128)(2,1)} %copy-done.20, bf16[1024,768]{1,0:T(8,128)(2,1)} %bitcast.24, bf16[1024,768]{1,0:T(8,128)(2,1)} %copy-done.21), custom_call_target="tpu_custom_call" | custom-call | flops 4831838208 | bytes 24159192 | tf_op jit(solution)/shard_map/expert_forward/pallas_call | solution.py:189
  90.7 4.1 %collective-permute-start.16 = (bf16[32,2048]{1,0:T(8,128)(2,1)S(1)}, bf16[32,2048]{1,0:T(8,128)(2,1)S(1)}, u32[]{:S(2)}, u32[]{:S(2)}) collective-permute-start(bf16[32,2048]{1,0:T(8,128)(2,1)S(1)} %copy-done.33), channel_id=1, source_target_pairs={{0,30},{2,28},{4,26},{6,24},{8,22},{10,20},{12,18},{14,16},{16,14}... | collective-permute-start | bytes 393224 | tf_op jit(solution)/shard_map/ppermute | solution.py:60
  94.8 3.2 %collective-permute-start.15 = (bf16[32,2048]{1,0:T(8,128)(2,1)S(1)}, bf16[32,2048]{1,0:T(8,128)(2,1)S(1)}, u32[]{:S(2)}, u32[]{:S(2)}) collective-permute-start(bf16[32,2048]{1,0:T(8,128)(2,1)S(1)} %copy-done.32), channel_id=1, source_target_pairs={{0,28},{2,30},{4,24},{6,26},{8,20},{10,22},{12,16},{14,18},{16,12}... | collective-permute-start | bytes 393224 | tf_op jit(solution)/shard_map/ppermute | solution.py:60
  100.2 3.2 %collective-permute-start.12 = (bf16[32,2048]{1,0:T(8,128)(2,1)S(1)}, bf16[32,2048]{1,0:T(8,128)(2,1)S(1)}, u32[]{:S(2)}, u32[]{:S(2)}) collective-permute-start(bf16[32,2048]{1,0:T(8,128)(2,1)S(1)} %copy-done.27), channel_id=1, source_target_pairs={{0,22},{2,20},{4,18},{6,16},{8,30},{10,28},{12,26},{14,24},{16,6},... | collective-permute-start | bytes 393224 | tf_op jit(solution)/shard_map/ppermute | solution.py:60
  103.4 8.5 %collective-permute-done.15.refs_14_ = bf16[32,2048]{1,0:T(8,128)(2,1)S(1)} collective-permute-done((bf16[32,2048]{1,0:T(8,128)(2,1)S(1)}, bf16[32,2048]{1,0:T(8,128)(2,1)S(1)}, u32[]{:S(2)}, u32[]{:S(2)}) %collective-permute-start.15) | collective-permute-done | bytes 131104 | tf_op jit(solution)/shard_map/ppermute | solution.py:60
  113.3 4.2 %all-to-all-start.1 = ((bf16[16,32,2048]{2,1,0:T(8,128)(2,1)}), bf16[16,32,2048]{2,1,0:T(8,128)(2,1)S(1)}, u32[]{:S(2)}, u32[]{:S(2)}) async-start(bf16[16,32,2048]{2,1,0:T(8,128)(2,1)} %get-tuple-element.188), calls=%async_computation.1 | async-start | bytes 4194304 | tf_op jit(solution)/shard_map/all_to_all | solution.py:55
  117.5 13.4 %expert_backward.1 = (bf16[32,2048]{1,0:T(8,128)(2,1)}, bf16[32,2048]{1,0:T(8,128)(2,1)}, bf16[32,2048]{1,0:T(8,128)(2,1)}, bf16[32,2048]{1,0:T(8,128)(2,1)}, bf...) custom-call(s32[2]{0:T(128)} %pad_add_fusion.where_ref, ...), custom_call_target="tpu_custom_call" | custom-call | flops 4831838208 | bytes 24159192 | tf_op jit(solution)/shard_map/expert_backward/pallas_call | solution.py:237
  132.9 2.4 %collective-permute-start.18 = (bf16[32,2048]{1,0:T(8,128)(2,1)}, bf16[32,2048]{1,0:T(8,128)(2,1)S(1)}, u32[]{:S(2)}, u32[]{:S(2)}) collective-permute-start(bf16[32,2048]{1,0:T(8,128)(2,1)} %get-tuple-element.161), channel_id=1, source_target_pairs={{0,4},{2,6},{4,0},{6,2},{8,12},{10,14},{12,8},{14,10},{16,20},{18,... | collective-permute-start | bytes 393224 | tf_op jit(solution)/shard_map/ppermute | solution.py:60
  137.9 6.8 %weight_grads.3 = bf16[1024,2304]{1,0:T(8,128)(2,1)} custom-call(bf16[16,32,2048]{2,1,0:T(8,128)(2,1)} %copy-done.1, bf16[512,2048]{1,0:T(8,128)(2,1)} %get-tuple-element.185.dy_ref, bf16[512,768]{1,0:T(8,128)(2,1)} %get-tuple-element.144.inner_ref, bf16[512,1536]{1,0:T(8,128)(2,1)} %get-tuple-element.186.act_grad_ref), custom_call_target="tpu_custom_call" | custom-call | flops 2415919104 | bytes 12079595 | tf_op jit(solution)/shard_map/weight_grads/pallas_call | solution.py:270
  144.7 6.9 %weight_grads.2 = bf16[1024,2304]{1,0:T(8,128)(2,1)} custom-call(bf16[16,32,2048]{2,1,0:T(8,128)(2,1)} %copy-done.1, bf16[512,2048]{1,0:T(8,128)(2,1)} %get-tuple-element.185.dy_ref, bf16[512,768]{1,0:T(8,128)(2,1)} %get-tuple-element.144.inner_ref, bf16[512,1536]{1,0:T(8,128)(2,1)} %get-tuple-element.186.act_grad_ref), custom_call_target="tpu_custom_call" | custom-call | flops 2415919104 | bytes 12079595 | tf_op jit(solution)/shard_map/weight_grads/pallas_call | solution.py:270
  151.7 3.7 %collective-permute-done.17.refs_1_ = bf16[32,2048]{1,0:T(8,128)(2,1)S(1)} collective-permute-done((bf16[32,2048]{1,0:T(8,128)(2,1)}, bf16[32,2048]{1,0:T(8,128)(2,1)S(1)}, u32[]{:S(2)}, u32[]{:S(2)}) %collective-permute-start.17) | collective-permute-done | bytes 131104 | tf_op jit(solution)/shard_map/ppermute | solution.py:60
  155.4 19.5 %collective-permute-done.18.refs_2_ = bf16[32,2048]{1,0:T(8,128)(2,1)S(1)} collective-permute-done((bf16[32,2048]{1,0:T(8,128)(2,1)}, bf16[32,2048]{1,0:T(8,128)(2,1)S(1)}, u32[]{:S(2)}, u32[]{:S(2)}) %collective-permute-start.18) | collective-permute-done | bytes 131104 | tf_op jit(solution)/shard_map/ppermute | solution.py:60
  175.7 4.4 %collective-permute-start.26 = (bf16[32,2048]{1,0:T(8,128)(2,1)}, bf16[32,2048]{1,0:T(8,128)(2,1)}, u32[]{:S(2)}, u32[]{:S(2)}) collective-permute-start(bf16[32,2048]{1,0:T(8,128)(2,1)} %get-tuple-element.174), channel_id=1, source_target_pairs={{0,20},{2,22},{4,16},{6,18},{8,28},{10,30},{12,24},{14,26},{16,4},... | collective-permute-start | bytes 393224 | tf_op jit(solution)/shard_map/ppermute | solution.py:60
  181.8 2.7 %collective-permute-start.23 = (bf16[32,2048]{1,0:T(8,128)(2,1)}, bf16[32,2048]{1,0:T(8,128)(2,1)S(1)}, u32[]{:S(2)}, u32[]{:S(2)}) collective-permute-start(bf16[32,2048]{1,0:T(8,128)(2,1)} %get-tuple-element.168), channel_id=1, source_target_pairs={{0,14},{2,12},{4,10},{6,8},{8,6},{10,4},{12,2},{14,0},{16,30},{18,... | collective-permute-start | bytes 393224 | tf_op jit(solution)/shard_map/ppermute | solution.py:60
  184.6 2.5 %collective-permute-done.26.refs_10_ = bf16[32,2048]{1,0:T(8,128)(2,1)} collective-permute-done((bf16[32,2048]{1,0:T(8,128)(2,1)}, bf16[32,2048]{1,0:T(8,128)(2,1)}, u32[]{:S(2)}, u32[]{:S(2)}) %collective-permute-start.26) | collective-permute-done | bytes 131104 | tf_op jit(solution)/shard_map/ppermute | solution.py:60
  187.1 2.2 collective-permute-start.22
  193.8 8.0 %collective-permute-start.29 = (bf16[32,2048]{1,0:T(8,128)(2,1)}, bf16[32,2048]{1,0:T(8,128)(2,1)S(1)}, u32[]{:S(2)}, u32[]{:S(2)}) collective-permute-start(bf16[32,2048]{1,0:T(8,128)(2,1)} %get-tuple-element.180), channel_id=1, source_target_pairs={{0,26},{2,24},{4,30},{6,28},{8,18},{10,16},{12,22},{14,20},{16,10}... | collective-permute-start | bytes 393224 | tf_op jit(solution)/shard_map/ppermute | solution.py:60
  201.8 3.2 %collective-permute-done.22.refs_6_ = bf16[32,2048]{1,0:T(8,128)(2,1)S(1)} collective-permute-done((bf16[32,2048]{1,0:T(8,128)(2,1)}, bf16[32,2048]{1,0:T(8,128)(2,1)S(1)}, u32[]{:S(2)}, u32[]{:S(2)}) %collective-permute-start.22) | collective-permute-done | bytes 131104 | tf_op jit(solution)/shard_map/ppermute | solution.py:60
  207.1 4.9 %combine_y.1 = (bf16[256,2048]{1,0:T(8,128)(2,1)}, f32[8,256]{1,0:T(8,128)}) custom-call(s32[2]{0:T(128)} %pad_add_fusion.where_ref, bf16[512,256]{1,0:T(8,128)(2,1)} %get-tuple-element.112.pick_ref, bf16[256,512]{1,0:T(8,128)(2,1)} %get-tuple-element.220.high_ref, bf16[256,512]{1,0:T(8,128)(2,1)} %get-tuple-element.219.middle_ref, s32[8,256]{1,0:T(8,128)} %bitcast.18, ...), custom_call_target="tpu_custom_call" | custom-call | flops 1 | bytes 1 | tf_op jit(solution)/shard_map/combine_y/pallas_call | solution.py:315
  212.0 2.6 %collective-permute-start.27 = (bf16[32,2048]{1,0:T(8,128)(2,1)}, bf16[32,2048]{1,0:T(8,128)(2,1)S(1)}, u32[]{:S(2)}, u32[]{:S(2)}) collective-permute-start(bf16[32,2048]{1,0:T(8,128)(2,1)} %get-tuple-element.176), channel_id=1, source_target_pairs={{0,22},{2,20},{4,18},{6,16},{8,30},{10,28},{12,26},{14,24},{16,6},... | collective-permute-start | bytes 393224 | tf_op jit(solution)/shard_map/ppermute | solution.py:60
  214.6 5.6 %convert_add_fusion = f32[1024,1536]{1,0:T(8,128)} fusion(bf16[1024,2304]{1,0:T(8,128)(2,1)} %collective-permute-done.32, bf16[1024,2304]{1,0:T(8,128)(2,1)S(1)} %copy-done), kind=kLoop, calls=%fused_computation | loop fusion | flops 4718592 | bytes 12582912 | tf_op jit(solution)/shard_map/add | solution.py:385
  220.2 3.4 %convert_add_fusion.1 = f32[1024,768]{1,0:T(8,128)} fusion(bf16[1024,2304]{1,0:T(8,128)(2,1)} %collective-permute-done.32, bf16[1024,2304]{1,0:T(8,128)(2,1)S(1)} %copy-done), kind=kLoop, calls=%fused_computation.1 | loop fusion | flops 2359296 | bytes 6291456 | tf_op jit(solution)/shard_map/add | solution.py:385
  224.5 3.4 %combine_dx.1 = bf16[256,2048]{1,0:T(8,128)(2,1)} custom-call(s32[2]{0:T(128)} %pad_add_fusion.where_ref, bf16[256,512]{1,0:T(8,128)(2,1)} %bitcast.16, bf16[32,2048]{1,0:T(8,128)(2,1)} %get-tuple-element.200.refs_0_, bf16[32,2048]{1,0:T(8,128)(2,1)} %copy-done.6, bf16[32,2048]{1,0:T(8,128)(2,1)} %copy-done.7, bf16[32,2048]{1,0:T(8,128)(2,1)} %copy-done.8, ...), custom_call_target="tpu_custom_call" | custom-call | flops 1 | bytes 1 | tf_op jit(solution)/shard_map/combine_dx/pallas_call | solution.py:339
  (131 shorter events, 26.7 us)
Async XLA Ops:
  4.7 73.4 %all-to-all-start = ((bf16[16,32,2048]{2,1,0:T(8,128)(2,1)}), bf16[16,32,2048]{2,1,0:T(8,128)(2,1)S(1)}, u32[]{:S(2)}, u32[]{:S(2)}) async-start(bf16[16,32,2048]{2,1,0:T(8,128)(2,1)} %get-tuple-element.142), calls=%async_computation | async-start | bytes 4194304 | tf_op jit(solution)/shard_map/all_to_all | solution.py:55
  21.2 30.0 %collective-permute-start.6 = (bf16[32,2048]{1,0:T(8,128)(2,1)}, bf16[32,2048]{1,0:T(8,128)(2,1)S(1)}, u32[]{:S(2)}, u32[]{:S(2)}) collective-permute-start(bf16[32,2048]{1,0:T(8,128)(2,1)} %get-tuple-element.124), channel_id=1, source_target_pairs={{0,10},{2,8},{4,14},{6,12},{8,2},{10,0},{12,6},{14,4},{16,26},{18,... | collective-permute-start | bytes 393224 | tf_op jit(solution)/shard_map/ppermute | solution.py:60
  24.0 33.5 %collective-permute-start.5 = (bf16[32,2048]{1,0:T(8,128)(2,1)}, bf16[32,2048]{1,0:T(8,128)(2,1)S(1)}, u32[]{:S(2)}, u32[]{:S(2)}) collective-permute-start(bf16[32,2048]{1,0:T(8,128)(2,1)} %get-tuple-element.122), channel_id=1, source_target_pairs={{0,8},{2,10},{4,12},{6,14},{8,0},{10,2},{12,4},{14,6},{16,24},{18,... | collective-permute-start | bytes 393224 | tf_op jit(solution)/shard_map/ppermute | solution.py:60
  24.6 33.7 %collective-permute-start.4 = (bf16[32,2048]{1,0:T(8,128)(2,1)}, bf16[32,2048]{1,0:T(8,128)(2,1)S(1)}, u32[]{:S(2)}, u32[]{:S(2)}) collective-permute-start(bf16[32,2048]{1,0:T(8,128)(2,1)} %get-tuple-element.120), channel_id=1, source_target_pairs={{0,6},{2,4},{4,2},{6,0},{8,14},{10,12},{12,10},{14,8},{16,22},{18,... | collective-permute-start | bytes 393224 | tf_op jit(solution)/shard_map/ppermute | solution.py:60
  27.0 49.7 %collective-permute-start.3 = (bf16[32,2048]{1,0:T(8,128)(2,1)}, bf16[32,2048]{1,0:T(8,128)(2,1)S(1)}, u32[]{:S(2)}, u32[]{:S(2)}) collective-permute-start(bf16[32,2048]{1,0:T(8,128)(2,1)} %get-tuple-element.118), channel_id=1, source_target_pairs={{0,4},{2,6},{4,0},{6,2},{8,12},{10,14},{12,8},{14,10},{16,20},{18,... | collective-permute-start | bytes 393224 | tf_op jit(solution)/shard_map/ppermute | solution.py:60
  27.0 50.7 %collective-permute-start.2 = (bf16[32,2048]{1,0:T(8,128)(2,1)}, bf16[32,2048]{1,0:T(8,128)(2,1)S(1)}, u32[]{:S(2)}, u32[]{:S(2)}) collective-permute-start(bf16[32,2048]{1,0:T(8,128)(2,1)} %get-tuple-element.116), channel_id=1, source_target_pairs={{0,2},{2,0},{4,6},{6,4},{8,10},{10,8},{12,14},{14,12},{16,18},{18,... | collective-permute-start | bytes 393224 | tf_op jit(solution)/shard_map/ppermute | solution.py:60
  51.2 39.4 %collective-permute-start.11 = (bf16[32,2048]{1,0:T(8,128)(2,1)}, bf16[32,2048]{1,0:T(8,128)(2,1)S(1)}, u32[]{:S(2)}, u32[]{:S(2)}) collective-permute-start(bf16[32,2048]{1,0:T(8,128)(2,1)} %get-tuple-element.139), channel_id=1, source_target_pairs={{0,20},{2,22},{4,16},{6,18},{8,28},{10,30},{12,24},{14,26},{16,4},... | collective-permute-start | bytes 393224 | tf_op jit(solution)/shard_map/ppermute | solution.py:60
  57.6 37.2 %collective-permute-start.10 = (bf16[32,2048]{1,0:T(8,128)(2,1)}, bf16[32,2048]{1,0:T(8,128)(2,1)S(1)}, u32[]{:S(2)}, u32[]{:S(2)}) collective-permute-start(bf16[32,2048]{1,0:T(8,128)(2,1)} %get-tuple-element.136), channel_id=1, source_target_pairs={{0,18},{2,16},{4,22},{6,20},{8,26},{10,24},{12,30},{14,28},{16,2},... | collective-permute-start | bytes 393224 | tf_op jit(solution)/shard_map/ppermute | solution.py:60
  58.3 39.8 %collective-permute-start.9 = (bf16[32,2048]{1,0:T(8,128)(2,1)}, bf16[32,2048]{1,0:T(8,128)(2,1)}, u32[]{:S(2)}, u32[]{:S(2)}) collective-permute-start(bf16[32,2048]{1,0:T(8,128)(2,1)} %get-tuple-element.133), channel_id=1, source_target_pairs={{0,16},{2,18},{4,20},{6,22},{8,24},{10,26},{12,28},{14,30},{16,0},... | collective-permute-start | bytes 393224 | tf_op jit(solution)/shard_map/ppermute | solution.py:60
  76.6 21.4 %collective-permute-start.8 = (bf16[32,2048]{1,0:T(8,128)(2,1)}, bf16[32,2048]{1,0:T(8,128)(2,1)}, u32[]{:S(2)}, u32[]{:S(2)}) collective-permute-start(bf16[32,2048]{1,0:T(8,128)(2,1)} %get-tuple-element.130), channel_id=1, source_target_pairs={{0,14},{2,12},{4,10},{6,8},{8,6},{10,4},{12,2},{14,0},{16,30},{18,... | collective-permute-start | bytes 393224 | tf_op jit(solution)/shard_map/ppermute | solution.py:60
  77.7 22.5 %collective-permute-start.7 = (bf16[32,2048]{1,0:T(8,128)(2,1)}, bf16[32,2048]{1,0:T(8,128)(2,1)}, u32[]{:S(2)}, u32[]{:S(2)}) collective-permute-start(bf16[32,2048]{1,0:T(8,128)(2,1)} %get-tuple-element.127), channel_id=1, source_target_pairs={{0,12},{2,14},{4,8},{6,10},{8,4},{10,6},{12,0},{14,2},{16,28},{18,... | collective-permute-start | bytes 393224 | tf_op jit(solution)/shard_map/ppermute | solution.py:60
  90.7 12.7 %collective-permute-start.16 = (bf16[32,2048]{1,0:T(8,128)(2,1)S(1)}, bf16[32,2048]{1,0:T(8,128)(2,1)S(1)}, u32[]{:S(2)}, u32[]{:S(2)}) collective-permute-start(bf16[32,2048]{1,0:T(8,128)(2,1)S(1)} %copy-done.33), channel_id=1, source_target_pairs={{0,30},{2,28},{4,26},{6,24},{8,22},{10,20},{12,18},{14,16},{16,14}... | collective-permute-start | bytes 393224 | tf_op jit(solution)/shard_map/ppermute | solution.py:60
  94.8 17.1 %collective-permute-start.15 = (bf16[32,2048]{1,0:T(8,128)(2,1)S(1)}, bf16[32,2048]{1,0:T(8,128)(2,1)S(1)}, u32[]{:S(2)}, u32[]{:S(2)}) collective-permute-start(bf16[32,2048]{1,0:T(8,128)(2,1)S(1)} %copy-done.32), channel_id=1, source_target_pairs={{0,28},{2,30},{4,24},{6,26},{8,20},{10,22},{12,16},{14,18},{16,12}... | collective-permute-start | bytes 393224 | tf_op jit(solution)/shard_map/ppermute | solution.py:60
  98.0 13.9 %collective-permute-start.14 = (bf16[32,2048]{1,0:T(8,128)(2,1)S(1)}, bf16[32,2048]{1,0:T(8,128)(2,1)S(1)}, u32[]{:S(2)}, u32[]{:S(2)}) collective-permute-start(bf16[32,2048]{1,0:T(8,128)(2,1)S(1)} %copy-done.30), channel_id=1, source_target_pairs={{0,26},{2,24},{4,30},{6,28},{8,18},{10,16},{12,22},{14,20},{16,10}... | collective-permute-start | bytes 393224 | tf_op jit(solution)/shard_map/ppermute | solution.py:60
  98.1 13.8 %collective-permute-start.13 = (bf16[32,2048]{1,0:T(8,128)(2,1)S(1)}, bf16[32,2048]{1,0:T(8,128)(2,1)S(1)}, u32[]{:S(2)}, u32[]{:S(2)}) collective-permute-start(bf16[32,2048]{1,0:T(8,128)(2,1)S(1)} %copy-done.29), channel_id=1, source_target_pairs={{0,24},{2,26},{4,28},{6,30},{8,16},{10,18},{12,20},{14,22},{16,8},... | collective-permute-start | bytes 393224 | tf_op jit(solution)/shard_map/ppermute | solution.py:60
  100.2 11.7 %collective-permute-start.12 = (bf16[32,2048]{1,0:T(8,128)(2,1)S(1)}, bf16[32,2048]{1,0:T(8,128)(2,1)S(1)}, u32[]{:S(2)}, u32[]{:S(2)}) collective-permute-start(bf16[32,2048]{1,0:T(8,128)(2,1)S(1)} %copy-done.27), channel_id=1, source_target_pairs={{0,22},{2,20},{4,18},{6,16},{8,30},{10,28},{12,26},{14,24},{16,6},... | collective-permute-start | bytes 393224 | tf_op jit(solution)/shard_map/ppermute | solution.py:60
  113.3 61.6 %all-to-all-start.1 = ((bf16[16,32,2048]{2,1,0:T(8,128)(2,1)}), bf16[16,32,2048]{2,1,0:T(8,128)(2,1)S(1)}, u32[]{:S(2)}, u32[]{:S(2)}) async-start(bf16[16,32,2048]{2,1,0:T(8,128)(2,1)} %get-tuple-element.188), calls=%async_computation.1 | async-start | bytes 4194304 | tf_op jit(solution)/shard_map/all_to_all | solution.py:55
  131.0 24.5 %collective-permute-start.17 = (bf16[32,2048]{1,0:T(8,128)(2,1)}, bf16[32,2048]{1,0:T(8,128)(2,1)S(1)}, u32[]{:S(2)}, u32[]{:S(2)}) collective-permute-start(bf16[32,2048]{1,0:T(8,128)(2,1)} %get-tuple-element.160), channel_id=1, source_target_pairs={{0,2},{2,0},{4,6},{6,4},{8,10},{10,8},{12,14},{14,12},{16,18},{18,... | collective-permute-start | bytes 393224 | tf_op jit(solution)/shard_map/ppermute | solution.py:60
  132.9 42.0 %collective-permute-start.18 = (bf16[32,2048]{1,0:T(8,128)(2,1)}, bf16[32,2048]{1,0:T(8,128)(2,1)S(1)}, u32[]{:S(2)}, u32[]{:S(2)}) collective-permute-start(bf16[32,2048]{1,0:T(8,128)(2,1)} %get-tuple-element.161), channel_id=1, source_target_pairs={{0,4},{2,6},{4,0},{6,2},{8,12},{10,14},{12,8},{14,10},{16,20},{18,... | collective-permute-start | bytes 393224 | tf_op jit(solution)/shard_map/ppermute | solution.py:60
  135.3 39.6 %collective-permute-start.19 = (bf16[32,2048]{1,0:T(8,128)(2,1)}, bf16[32,2048]{1,0:T(8,128)(2,1)S(1)}, u32[]{:S(2)}, u32[]{:S(2)}) collective-permute-start(bf16[32,2048]{1,0:T(8,128)(2,1)} %get-tuple-element.162), channel_id=1, source_target_pairs={{0,6},{2,4},{4,2},{6,0},{8,14},{10,12},{12,10},{14,8},{16,22},{18,... | collective-permute-start | bytes 393224 | tf_op jit(solution)/shard_map/ppermute | solution.py:60
  135.4 39.5 %collective-permute-start.20 = (bf16[32,2048]{1,0:T(8,128)(2,1)}, bf16[32,2048]{1,0:T(8,128)(2,1)S(1)}, u32[]{:S(2)}, u32[]{:S(2)}) collective-permute-start(bf16[32,2048]{1,0:T(8,128)(2,1)} %get-tuple-element.163), channel_id=1, source_target_pairs={{0,8},{2,10},{4,12},{6,14},{8,0},{10,2},{12,4},{14,6},{16,24},{18,... | collective-permute-start | bytes 393224 | tf_op jit(solution)/shard_map/ppermute | solution.py:60
  137.3 37.6 %collective-permute-start.21 = (bf16[32,2048]{1,0:T(8,128)(2,1)}, bf16[32,2048]{1,0:T(8,128)(2,1)S(1)}, u32[]{:S(2)}, u32[]{:S(2)}) collective-permute-start(bf16[32,2048]{1,0:T(8,128)(2,1)} %get-tuple-element.164), channel_id=1, source_target_pairs={{0,10},{2,8},{4,14},{6,12},{8,2},{10,0},{12,6},{14,4},{16,26},{18,... | collective-permute-start | bytes 393224 | tf_op jit(solution)/shard_map/ppermute | solution.py:60
  175.0 37.0 %collective-permute-start.32 = (bf16[1024,2304]{1,0:T(8,128)(2,1)}, bf16[1024,2304]{1,0:T(8,128)(2,1)}, u32[]{:S(2)}, u32[]{:S(2)}) collective-permute-start(bf16[1024,2304]{1,0:T(8,128)(2,1)} %weight_grads.2), channel_id=1, source_target_pairs={{0,1},{1,0},{2,3},{3,2},{4,5},{5,4},{6,7},{7,6},{8,9},{9,8},{10,11... | collective-permute-start | bytes 14155784 | tf_op jit(solution)/shard_map/ppermute | solution.py:51
  175.7 11.4 %collective-permute-start.26 = (bf16[32,2048]{1,0:T(8,128)(2,1)}, bf16[32,2048]{1,0:T(8,128)(2,1)}, u32[]{:S(2)}, u32[]{:S(2)}) collective-permute-start(bf16[32,2048]{1,0:T(8,128)(2,1)} %get-tuple-element.174), channel_id=1, source_target_pairs={{0,20},{2,22},{4,16},{6,18},{8,28},{10,30},{12,24},{14,26},{16,4},... | collective-permute-start | bytes 393224 | tf_op jit(solution)/shard_map/ppermute | solution.py:60
  181.3 10.7 %collective-permute-start.25 = (bf16[32,2048]{1,0:T(8,128)(2,1)}, bf16[32,2048]{1,0:T(8,128)(2,1)S(1)}, u32[]{:S(2)}, u32[]{:S(2)}) collective-permute-start(bf16[32,2048]{1,0:T(8,128)(2,1)} %get-tuple-element.172), channel_id=1, source_target_pairs={{0,18},{2,16},{4,22},{6,20},{8,26},{10,24},{12,30},{14,28},{16,2},... | collective-permute-start | bytes 393224 | tf_op jit(solution)/shard_map/ppermute | solution.py:60
  181.8 12.0 %collective-permute-start.23 = (bf16[32,2048]{1,0:T(8,128)(2,1)}, bf16[32,2048]{1,0:T(8,128)(2,1)S(1)}, u32[]{:S(2)}, u32[]{:S(2)}) collective-permute-start(bf16[32,2048]{1,0:T(8,128)(2,1)} %get-tuple-element.168), channel_id=1, source_target_pairs={{0,14},{2,12},{4,10},{6,8},{8,6},{10,4},{12,2},{14,0},{16,30},{18,... | collective-permute-start | bytes 393224 | tf_op jit(solution)/shard_map/ppermute | solution.py:60
  187.1 18.0 %collective-permute-start.22 = (bf16[32,2048]{1,0:T(8,128)(2,1)}, bf16[32,2048]{1,0:T(8,128)(2,1)S(1)}, u32[]{:S(2)}, u32[]{:S(2)}) collective-permute-start(bf16[32,2048]{1,0:T(8,128)(2,1)} %get-tuple-element.166), channel_id=1, source_target_pairs={{0,12},{2,14},{4,8},{6,10},{8,4},{10,6},{12,0},{14,2},{16,28},{18,... | collective-permute-start | bytes 393224 | tf_op jit(solution)/shard_map/ppermute | solution.py:60
  192.0 31.6 %collective-permute-start.31 = (bf16[32,2048]{1,0:T(8,128)(2,1)}, bf16[32,2048]{1,0:T(8,128)(2,1)S(1)}, u32[]{:S(2)}, u32[]{:S(2)}) collective-permute-start(bf16[32,2048]{1,0:T(8,128)(2,1)} %get-tuple-element.184), channel_id=1, source_target_pairs={{0,30},{2,28},{4,26},{6,24},{8,22},{10,20},{12,18},{14,16},{16,14}... | collective-permute-start | bytes 393224 | tf_op jit(solution)/shard_map/ppermute | solution.py:60
  192.0 31.6 %collective-permute-start.30 = (bf16[32,2048]{1,0:T(8,128)(2,1)}, bf16[32,2048]{1,0:T(8,128)(2,1)S(1)}, u32[]{:S(2)}, u32[]{:S(2)}) collective-permute-start(bf16[32,2048]{1,0:T(8,128)(2,1)} %get-tuple-element.182), channel_id=1, source_target_pairs={{0,28},{2,30},{4,24},{6,26},{8,20},{10,22},{12,16},{14,18},{16,12}... | collective-permute-start | bytes 393224 | tf_op jit(solution)/shard_map/ppermute | solution.py:60
  193.8 29.8 %collective-permute-start.29 = (bf16[32,2048]{1,0:T(8,128)(2,1)}, bf16[32,2048]{1,0:T(8,128)(2,1)S(1)}, u32[]{:S(2)}, u32[]{:S(2)}) collective-permute-start(bf16[32,2048]{1,0:T(8,128)(2,1)} %get-tuple-element.180), channel_id=1, source_target_pairs={{0,26},{2,24},{4,30},{6,28},{8,18},{10,16},{12,22},{14,20},{16,10}... | collective-permute-start | bytes 393224 | tf_op jit(solution)/shard_map/ppermute | solution.py:60
  205.0 18.6 %collective-permute-start.28 = (bf16[32,2048]{1,0:T(8,128)(2,1)}, bf16[32,2048]{1,0:T(8,128)(2,1)S(1)}, u32[]{:S(2)}, u32[]{:S(2)}) collective-permute-start(bf16[32,2048]{1,0:T(8,128)(2,1)} %get-tuple-element.178), channel_id=1, source_target_pairs={{0,24},{2,26},{4,28},{6,30},{8,16},{10,18},{12,20},{14,22},{16,8},... | collective-permute-start | bytes 393224 | tf_op jit(solution)/shard_map/ppermute | solution.py:60
  212.0 11.7 %collective-permute-start.27 = (bf16[32,2048]{1,0:T(8,128)(2,1)}, bf16[32,2048]{1,0:T(8,128)(2,1)S(1)}, u32[]{:S(2)}, u32[]{:S(2)}) collective-permute-start(bf16[32,2048]{1,0:T(8,128)(2,1)} %get-tuple-element.176), channel_id=1, source_target_pairs={{0,22},{2,20},{4,18},{6,16},{8,30},{10,28},{12,26},{14,24},{16,6},... | collective-permute-start | bytes 393224 | tf_op jit(solution)/shard_map/ppermute | solution.py:60
  (42 other events, 1164.7 us)

commit v16 on v14

--- a/solution.py
+++ b/solution.py
@@ -122,29 +122,35 @@
     width = model // count
 
     def kernel(where_ref, pick_ref, weight_ref, grad_ref, *refs):
-        blocks, (rows_ref, relative_ref, dy_ref) = refs[:groups], refs[groups:]
+        blocks, refs = refs[:groups], refs[groups:]
+        rows_ref, relative_ref, weights_ref, all_rows_ref, dy_ref = refs
         me, turn = where_ref[0], where_ref[1]
         for s in range(count):
             source = shard_at(s, turn, count, width)
             here = slice(s * width, (s + 1) * width)
             rows = jnp.dot(pick_ref[...], grad_ref[:, source], preferred_element_type=F32)
-            rows_ref[:, here] = rows.astype(BF)
+            all_rows_ref[:, here] = rows.astype(BF)
             dy_ref[:, here] = (weight_ref[...] * rows).astype(BF)
         for j, block in enumerate(blocks):
-            block[...] = dy_ref[slots_of(j, me, capacity), :]
-            relative_ref[j * capacity : (j + 1) * capacity] = pick_ref[slots_of(j, me, capacity), :]
+            here = slice(j * capacity, (j + 1) * capacity)
+            there = slots_of(j, me, capacity)
+            block[...] = dy_ref[there, :]
+            rows_ref[here] = all_rows_ref[there, :]
+            relative_ref[here] = pick_ref[there, :]
+            weights_ref[here] = weight_ref[there, :]
 
     results = call(
         kernel,
         "dispatch_dy",
         in_specs=[SMEM] + [VMEM] * 3,
-        out_specs=[VMEM] * (groups + 2),
+        out_specs=[VMEM] * (groups + 3),
         out_shape=[
             *[shape(capacity, model)] * groups,
             shape(slots, model),
             shape(slots, tok_rows),
+            shape(slots, 1, kind=F32),
         ],
-        scratch_shapes=[pltpu.VMEM((slots, model), BF)],
+        scratch_shapes=[pltpu.VMEM((slots, model), BF)] * 2,
     )(where, pick, weight, out_grad)
     return list(results[:groups]), *results[groups:]
 
@@ -160,7 +166,7 @@
     return total
 
 
-def expert_forward(got, w_ins, w_outs):
+def expert_forward(where, got, w_ins, w_outs):
     groups, capacity, model = got.shape
     count = len(w_ins)
     width = model // count
@@ -168,8 +174,10 @@
     slots = groups * capacity
     many = max(1, 256 // capacity)
 
-    def kernel(got_ref, *refs):
-        ins, outs, (y_ref, act_ref, inner_ref) = refs[:count], refs[count:-3], refs[-3:]
+    def kernel(where_ref, got_ref, *refs):
+        ins, outs, refs = refs[:count], refs[count : 2 * count], refs[2 * count :]
+        sent, (act_ref, inner_ref, y_ref) = refs[:groups], refs[groups:]
+        me = where_ref[0]
         for first in range(0, groups, many):
             theirs = slice(first, first + many)
             band = slice(first * capacity, (first + many) * capacity)
@@ -180,24 +188,27 @@
                 act_gate * jax.nn.sigmoid(act_gate) * act_ref[band, hidden:]
             ).astype(BF)
             for s in range(count):
-                y = lax.dot_general(
+                y_ref[band, s * width : (s + 1) * width] = lax.dot_general(
                     inner_ref[band], outs[s][...], COLS_IN, preferred_element_type=F32
                 ).astype(BF)
-                y_ref[theirs, :, s * width : (s + 1) * width] = y.reshape(many, capacity, width)
-
-    operands = (got, *w_ins, *w_outs)
-    return call(
+        for j, block in enumerate(sent):
+            block[...] = y_ref[slots_of(j, me, capacity), :]
+
+    operands = (where, got, *w_ins, *w_outs)
+    results = call(
         kernel,
         "expert_forward",
         cost=work(6 * slots * model * hidden),
-        in_specs=[VMEM] * len(operands),
-        out_specs=[VMEM] * 3,
+        in_specs=[SMEM] + [VMEM] * (len(operands) - 1),
+        out_specs=[VMEM] * (groups + 2),
         out_shape=[
-            shape(groups, capacity, model),
+            *[shape(capacity, model)] * groups,
             shape(slots, double, kind=F32),
             shape(slots, hidden),
         ],
+        scratch_shapes=[pltpu.VMEM((slots, model), BF)],
     )(*operands)
+    return list(results[:groups]), *results[groups:]
 
 
 def expert_backward(where, blocks, act, w_ins, w_outs):
@@ -212,7 +223,7 @@
     def kernel(where_ref, *refs):
         got, act_ref, refs = refs[:groups], refs[groups], refs[groups + 1 :]
         ins, outs, refs = refs[:count], refs[count : 2 * count], refs[2 * count :]
-        sent, (act_grad_ref, dy_ref, dx_ref) = refs[:groups], refs[groups:]
+        dx_ref, act_grad_ref, dy_ref = refs
         me = where_ref[0]
         for j, block in enumerate(got):
             dy_ref[slots_of(j, me, capacity), :] = block[...]
@@ -227,27 +238,25 @@
             ).astype(BF)
             act_grad_ref[band, hidden:] = (inner_grad * (act_gate * sig)).astype(BF)
             for s in range(count):
-                dx_ref[band, s * width : (s + 1) * width] = lax.dot_general(
+                dx = lax.dot_general(
                     act_grad_ref[band], ins[s][...], COLS_IN, preferred_element_type=F32
                 ).astype(BF)
-        for j, block in enumerate(sent):
-            block[...] = dx_ref[slots_of(j, me, capacity), :]
+                theirs = slice(first // capacity, (first + rows) // capacity)
+                dx_ref[theirs, :, s * width : (s + 1) * width] = dx.reshape(-1, capacity, width)
 
     operands = (where, *blocks, act, *w_ins, *w_outs)
-    results = call(
+    return call(
         kernel,
         "expert_backward",
         cost=work(6 * slots * model * hidden),
         in_specs=[SMEM] + [VMEM] * (len(operands) - 1),
-        out_specs=[VMEM] * (groups + 2),
+        out_specs=[VMEM] * 3,
         out_shape=[
-            *[shape(capacity, model)] * groups,
+            shape(groups, capacity, model),
             shape(slots, double),
             shape(slots, model),
         ],
-        scratch_shapes=[pltpu.VMEM((slots, model), BF)],
     )(*operands)
-    return list(results[:groups]), *results[groups:]
 
 
 def weight_grads(shard, got, dys, inner, act_grad):
@@ -283,20 +292,21 @@
     )(got, dys, inner, act_grad)
 
 
-def combine_y(where, picks, ids_t, grad_rows, rows):
+def combine_y(where, picks, ids_t, grad_rows, blocks):
     pick, high_t, middle_t = picks
     slots, tok_rows = pick.shape
-    groups, capacity, model = rows.shape
+    groups = len(blocks)
+    capacity, model = blocks[0].shape
     count = lax.axis_size("edata")
     width = model // count
 
     def kernel(where_ref, pick_ref, high_ref, middle_ref, ids_ref, grad_ref, *refs):
-        y_ref, mixed_ref, gate_grad_ref = refs
-        turn = where_ref[1]
+        blocks, (mixed_ref, gate_grad_ref) = refs[:groups], refs[groups:]
+        me, turn = where_ref[0], where_ref[1]
         dots = jnp.zeros((slots, 1), F32)
         for s in range(count):
             here = slice(s * width, (s + 1) * width)
-            y = y_ref[:, :, here].reshape(slots, width)
+            y = jnp.concatenate([block[:, here] for block in blocks], axis=0)
             mixed_ref[:, shard_at(s, turn, count, width)] = (
                 jnp.dot(high_ref[...], y, preferred_element_type=F32)
                 + jnp.dot(middle_ref[...], y, preferred_element_type=F32)
@@ -308,41 +318,47 @@
         by_token = jnp.sum(by_token.reshape(groups, capacity, tok_rows), axis=1)
         ids = ids_ref[...]
         total = jnp.zeros(ids.shape, F32)
-        for g in range(groups):
-            total += jnp.where(ids == g, by_token[g : g + 1], 0.0)
+        for j in range(groups):
+            total += jnp.where(ids == (me ^ j), by_token[j : j + 1], 0.0)
         gate_grad_ref[...] = total
 
     return call(
         kernel,
         "combine_y",
-        in_specs=[SMEM] + [VMEM] * 6,
+        in_specs=[SMEM] + [VMEM] * (5 + groups),
         out_specs=[VMEM] * 2,
         out_shape=[shape(tok_rows, model), shape(*ids_t.shape, kind=F32)],
-    )(where, pick, high_t, middle_t, ids_t, grad_rows, rows)
-
-
-def combine_dx(where, relative_t, blocks):
-    tok_rows, slots = relative_t.shape
-    capacity, model = blocks[0].shape
-    count = lax.axis_size("edata")
-    width = model // count
-
-    def kernel(where_ref, relative_ref, *refs):
-        blocks, out_ref = refs[:-1], refs[-1]
-        for s in range(count):
-            here = slice(s * width, (s + 1) * width)
-            dx = jnp.concatenate([block[:, here] for block in blocks], axis=0)
-            out_ref[:, shard_at(s, where_ref[1], count, width)] = jnp.dot(
-                relative_ref[...], dx, preferred_element_type=F32
-            ).astype(BF)
+    )(where, pick, high_t, middle_t, ids_t, grad_rows, *blocks)
+
+
+def combine_dx(where, pick, rows):
+    slots, tok_rows = pick.shape
+    groups, capacity, model = rows.shape
+    count = lax.axis_size("edata")
+    tile = min(512, model // count)
+    steps = model // tile
+
+    def kernel(where_ref, pick_ref, rows_ref, out_ref):
+        out_ref[...] = lax.dot_general(
+            pick_ref[...], rows_ref[...].reshape(slots, tile), ROWS_IN, preferred_element_type=F32
+        ).astype(BF)
 
     return call(
         kernel,
         "combine_dx",
-        in_specs=[SMEM] + [VMEM] * (1 + len(blocks)),
-        out_specs=VMEM,
+        grid_spec=pltpu.PrefetchScalarGridSpec(
+            num_scalar_prefetch=1,
+            grid=(steps,),
+            in_specs=[
+                pl.BlockSpec((slots, tok_rows), lambda i, w: (0, 0)),
+                pl.BlockSpec((groups, capacity, tile), lambda i, w: (0, 0, i)),
+            ],
+            out_specs=pl.BlockSpec(
+                (tok_rows, tile), lambda i, w: (0, (i + w[1] * (steps // count)) % steps)
+            ),
+        ),
         out_shape=shape(tok_rows, model),
-    )(where, relative_t, *blocks)
+    )(where, pick, rows)
 
 
 def shards(tokens, out_grad, expert_ids, gates, w_gate_up, w_down):
@@ -357,42 +373,47 @@
     ids_t = expert_ids.T
     sent, pick, weight = dispatch_x(where, ids_t, gates.T, tokens, groups, capacity)
     got = to_all(sent)
-    blocks, grad_rows, relative = dispatch_dy(where, pick, weight, out_grad, groups, capacity)
+    blocks, grad_rows, relative, weights = dispatch_dy(where, pick, weight, out_grad, groups, capacity)
     blocks = [blocks[0], *(after(b, *w_ins[1:], *w_outs[1:]) for b in blocks[1:])]
     dys = [blocks[0]]
     for j in range(1, groups):
         needs = (dys[j - queued],) if j > queued else ()
         if j == 2 * queued + 1:
-            y_sent, act, inner = expert_forward(after(got, *dys[1 : queued + 1]), w_ins, w_outs)
+            held = after(got, *dys[1 : queued + 1])
+            y_sent, act, inner = expert_forward(where, held, w_ins, w_outs)
         if j > 2 * queued:
             needs += (inner,)
         dys.append(to_partner(after(blocks[j], *needs) if needs else blocks[j], j))
-    y_got = to_all(after(y_sent, *dys[1:]))
-    dxs, act_grad, dy_rows = expert_backward(where, dys, act, w_ins, w_outs)
-    backs = [dxs[0]]
+    dx_sent, act_grad, dy_rows = expert_backward(where, dys, act, w_ins, w_outs)
+    ys = [y_sent[0]]
     for j in range(1, groups):
-        needs = (y_got, backs[j - queued]) if j > queued else ()
-        backs.append(to_partner(after(dxs[j], *needs) if needs else dxs[j], j))
-
-    parts = []
-    for shard in [*range(1, len(w_ins)), 0]:
-        parts.append(weight_grads(shard, got, dy_rows, inner, act_grad))
-    *parts, y_got = lax.optimization_barrier((*parts, y_got))
-    parts = [parts[-1]] + [from_owner(p, step) for step, p in enumerate(parts[:-1], 1)]
+        needs = (ys[j - queued], dx_sent) if j > queued else (dys[groups - 1 - queued + j],)
+        if j == 2 * queued + 1:
+            held = after(inner, *ys[1 : queued + 1])
+            parts = [
+                weight_grads(shard, got, dy_rows, held, act_grad) for shard in range(1, len(w_ins))
+            ]
+        if j > 2 * queued:
+            needs += tuple(parts)
+        ys.append(to_partner(after(y_sent[j], *needs), j))
+    dx_got = to_all(after(dx_sent, *ys[1:]))
+
+    parts = [from_owner(p, step) for step, p in enumerate(parts, 1)]
+    parts.append(weight_grads(0, got, dy_rows, after(inner, *ys[1:]), act_grad))
     double = w_gate_up.shape[2]
     sums = [
         sum(p[:, columns].astype(F32) for p in parts)
         for columns in (slice(0, double), slice(double, None))
     ]
-    spread = pick.astype(F32) * after(weight, inner)
+    spread = relative.astype(F32) * after(weights, inner)
     high = lax.reduce_precision(spread, 8, 7)
     middle = (spread - high).astype(BF)
     mixed, gate_grad = combine_y(
-        where, (pick, high.astype(BF).T, middle.T), ids_t, grad_rows, y_got
+        where, (relative, high.astype(BF).T, middle.T), ids_t, grad_rows, ys
     )
-    held = lax.optimization_barrier((*backs, *sums, mixed, gate_grad, relative.T))
-    *backs, grad_in, grad_down, mixed, gate_grad, relative_t = held
-    token_grad = combine_dx(where, relative_t, backs)
+    held = lax.optimization_barrier((dx_got, *sums, mixed, gate_grad))
+    dx_got, grad_in, grad_down, mixed, gate_grad = held
+    token_grad = combine_dx(where, pick, dx_got)
     return (mixed, token_grad, gate_grad.T, grad_in[None], grad_down[None])
 
 

time: 221 us -> 243 us (1.100)
  starting transfers between devices: 68.1 us -> 79.2 us
  waiting for transfers between devices: 82.9 us -> 91.3 us
    ppermute x30, starting transfers between devices: 52.2 us -> 64.7 us  [to_partner(): lax.ppermute(block, ('node', 'local'), [(i, i ^ j) for i in range(count)])]
    all_to_all x2, waiting for transfers between devices: 20.7 us -> 25.8 us  [to_all(): lax.all_to_all(rows, ('node', 'local'), split_axis=0, concat_axis=0, tile...]
    ppermute x30, waiting for transfers between devices: 58.9 us -> 62.2 us  [to_partner(): lax.ppermute(block, ('node', 'local'), [(i, i ^ j) for i in range(count)])]
  transfers between devices with their start and end apart: 35 -> 35, of which waited for: 11 -> 11; matrix products, arithmetic and copies ran while one was open for 5% -> 4% of each run, Pallas kernels for 22% -> 17%
where the time goes in v16:
time: 243 us; the launch traced here: 242 us
  waiting for transfers between devices  91.3 us (38%)
  starting transfers between devices  79.2 us (33%)
  Pallas kernels  56 us (23%)
  other arithmetic  11.2 us (5%)
  local copies, waits for them, and re-layouts  3.6 us (1%)
    ppermute x30, starting transfers between devices, to_partner(): lax.ppermute(block, ('node', 'local'), [(i, i ^ j) for i in range(count)])  64.7 us
    ppermute x30, waiting for transfers between devices, to_partner(): lax.ppermute(block, ('node', 'local'), [(i, i ^ j) for i in range(count)])  62.2 us
    all_to_all x2, waiting for transfers between devices, to_all(): lax.all_to_all(rows, ('node', 'local'), split_axis=0, concat_axis=0, tile...  25.8 us
    pallas_call x2, Pallas kernels, weight_grads(): call(kernel, 'weight_grads', cost=work(6 * slots * size * hidden), grid=(...  14.2 us
    all_to_all x2, starting transfers between devices, to_all(): lax.all_to_all(rows, ('node', 'local'), split_axis=0, concat_axis=0, tile...  13.8 us
    pallas_call x1, Pallas kernels, expert_backward(): call(kernel, 'expert_backward', cost=work(6 * slots * model * hidden), in...  12.2 us
    pallas_call x1, Pallas kernels, expert_forward(): call(kernel, 'expert_forward', cost=work(6 * slots * model * hidden), in_...  12 us
    add x2, other arithmetic, shards(): sum((p[:, columns].astype(F32) for p in parts))  9.59 us
  transfers between devices with their start and end apart: 35, of which 11 were waited for; matrix products, arithmetic and copies ran while one was open for 4% of the time, Pallas kernels for 17%

profile of v16, /device:TPU:0, one launch (start us, length us, event | category | flops | bytes accessed | tf_op | source)
XLA Modules:
  0.0 242.3 jit_solution(3402071151062929332)
XLA Ops:
  1.2 3.5 %dispatch_x.1 = (bf16[16,32,2048]{2,1,0:T(8,128)(2,1)}, bf16[512,256]{1,0:T(8,128)(2,1)}, f32[512,1]{1,0:T(8,128)}) custom-call(s32[2]{0:T(128)} %pad_add_fusion.where_ref, s32[8,256]{1,0:T(8,128)} %bitcast.15, f32[8,256]{1,0:T(8,128)} %bitcast.17, bf16[256,2048]{1,0:T(8,128)(2,1)} %x_ref.1), custom_call_target="tpu_custom_call" | custom-call | flops 1 | bytes 1 | tf_op jit(solution)/shard_map/dispatch_x/pallas_call | solution.py:105
  4.7 8.3 %all-to-all-start = ((bf16[16,32,2048]{2,1,0:T(8,128)(2,1)}), bf16[16,32,2048]{2,1,0:T(8,128)(2,1)S(1)}, u32[]{:S(2)}, u32[]{:S(2)}) async-start(bf16[16,32,2048]{2,1,0:T(8,128)(2,1)} %get-tuple-element.130), calls=%async_computation | async-start | bytes 4194304 | tf_op jit(solution)/shard_map/all_to_all | solution.py:55
  13.6 4.3 %dispatch_dy.1 = (bf16[32,2048]{1,0:T(8,128)(2,1)}, bf16[32,2048]{1,0:T(8,128)(2,1)}, bf16[32,2048]{1,0:T(8,128)(2,1)}, bf16[32,2048]{1,0:T(8,128)(2,1)}, bf16[3...) custom-call(s32[2]{0:T(128)} %pad_add_fusion.where_ref, ...), custom_call_target="tpu_custom_call" | custom-call | flops 1 | bytes 1 | tf_op jit(solution)/shard_map/dispatch_dy/pallas_call | solution.py:142
  17.9 3.3 %collective-permute-done.1.refs_3_.refs_20_ = bf16[1024,768]{1,0:T(8,128)(2,1)S(1)} collective-permute-done((bf16[1024,768]{1,0:T(8,128)(2,1)}, bf16[1024,768]{1,0:T(8,128)(2,1)S(1)}, u32[]{:S(2)}, u32[]{:S(2)}) %collective-permute-start.1) | collective-permute-done | bytes 1572896 | tf_op jit(solution)/shard_map/ppermute | solution.py:45
  21.2 2.8 %collective-permute-start.6 = (bf16[32,2048]{1,0:T(8,128)(2,1)}, bf16[32,2048]{1,0:T(8,128)(2,1)S(1)}, u32[]{:S(2)}, u32[]{:S(2)}) collective-permute-start(bf16[32,2048]{1,0:T(8,128)(2,1)} %get-tuple-element.112), channel_id=1, source_target_pairs={{0,10},{2,8},{4,14},{6,12},{8,2},{10,0},{12,6},{14,4},{16,26},{18,... | collective-permute-start | bytes 393224 | tf_op jit(solution)/shard_map/ppermute | solution.py:60
  24.6 2.4 collective-permute-start.4
  29.0 22.2 %collective-permute-done.6.refs_5_ = bf16[32,2048]{1,0:T(8,128)(2,1)S(1)} collective-permute-done((bf16[32,2048]{1,0:T(8,128)(2,1)}, bf16[32,2048]{1,0:T(8,128)(2,1)S(1)}, u32[]{:S(2)}, u32[]{:S(2)}) %collective-permute-start.6) | collective-permute-done | bytes 131104 | tf_op jit(solution)/shard_map/ppermute | solution.py:60
  51.2 6.4 %collective-permute-start.11 = (bf16[32,2048]{1,0:T(8,128)(2,1)}, bf16[32,2048]{1,0:T(8,128)(2,1)S(1)}, u32[]{:S(2)}, u32[]{:S(2)}) collective-permute-start(bf16[32,2048]{1,0:T(8,128)(2,1)} %get-tuple-element.127), channel_id=1, source_target_pairs={{0,20},{2,22},{4,16},{6,18},{8,28},{10,30},{12,24},{14,26},{16,4},... | collective-permute-start | bytes 393224 | tf_op jit(solution)/shard_map/ppermute | solution.py:60
  59.7 16.9 %collective-permute-done.3.refs_2_ = bf16[32,2048]{1,0:T(8,128)(2,1)S(1)} collective-permute-done((bf16[32,2048]{1,0:T(8,128)(2,1)}, bf16[32,2048]{1,0:T(8,128)(2,1)S(1)}, u32[]{:S(2)}, u32[]{:S(2)}) %collective-permute-start.3) | collective-permute-done | bytes 131104 | tf_op jit(solution)/shard_map/ppermute | solution.py:60
  80.0 12.0 %expert_forward.1 = (bf16[32,2048]{1,0:T(8,128)(2,1)}, bf16[32,2048]{1,0:T(8,128)(2,1)}, bf16[32,2048]{1,0:T(8,128)(2,1)}, bf16[32,2048]{1,0:T(8,128)(2,1)}, bf1...) custom-call(s32[2]{0:T(128)} %pad_add_fusion.where_ref, ...), custom_call_target="tpu_custom_call" | custom-call | flops 4831838208 | bytes 24159192 | tf_op jit(solution)/shard_map/expert_forward/pallas_call | solution.py:198
  91.9 4.1 %collective-permute-start.12 = (bf16[32,2048]{1,0:T(8,128)(2,1)S(1)}, bf16[32,2048]{1,0:T(8,128)(2,1)S(1)}, u32[]{:S(2)}, u32[]{:S(2)}) collective-permute-start(bf16[32,2048]{1,0:T(8,128)(2,1)S(1)} %copy-done.40), channel_id=1, source_target_pairs={{0,22},{2,20},{4,18},{6,16},{8,30},{10,28},{12,26},{14,24},{16,6},... | collective-permute-start | bytes 393224 | tf_op jit(solution)/shard_map/ppermute | solution.py:60
  98.5 2.1 collective-permute-start.15
  100.6 4.1 %collective-permute-start.16 = (bf16[32,2048]{1,0:T(8,128)(2,1)S(1)}, bf16[32,2048]{1,0:T(8,128)(2,1)S(1)}, u32[]{:S(2)}, u32[]{:S(2)}) collective-permute-start(bf16[32,2048]{1,0:T(8,128)(2,1)S(1)} %copy-done.27), channel_id=1, source_target_pairs={{0,30},{2,28},{4,26},{6,24},{8,22},{10,20},{12,18},{14,16},{16,14}... | collective-permute-start | bytes 393224 | tf_op jit(solution)/shard_map/ppermute | solution.py:60
  105.8 3.1 %collective-permute-done.13.refs_12_ = bf16[32,2048]{1,0:T(8,128)(2,1)S(1)} collective-permute-done((bf16[32,2048]{1,0:T(8,128)(2,1)S(1)}, bf16[32,2048]{1,0:T(8,128)(2,1)S(1)}, u32[]{:S(2)}, u32[]{:S(2)}) %collective-permute-start.13) | collective-permute-done | bytes 131104 | tf_op jit(solution)/shard_map/ppermute | solution.py:60
  114.8 6.9 %collective-permute-start.21 = (bf16[32,2048]{1,0:T(8,128)(2,1)}, bf16[32,2048]{1,0:T(8,128)(2,1)S(1)}, u32[]{:S(2)}, u32[]{:S(2)}) collective-permute-start(bf16[32,2048]{1,0:T(8,128)(2,1)} %get-tuple-element.157), channel_id=1, source_target_pairs={{0,10},{2,8},{4,14},{6,12},{8,2},{10,0},{12,6},{14,4},{16,26},{18,... | collective-permute-start | bytes 393224 | tf_op jit(solution)/shard_map/ppermute | solution.py:60
  121.8 12.2 %expert_backward.1 = (bf16[16,32,2048]{2,1,0:T(8,128)(2,1)}, bf16[512,1536]{1,0:T(8,128)(2,1)}, bf16[512,2048]{1,0:T(8,128)(2,1)}) custom-call(s32[2]{0:T(128)} %pad_add_fusion.where_ref, bf16[32,2048]{1,0:T(8,128)(2,1)} %get-tuple-element.102.refs_0_, bf16[32,2048]{1,0:T(8,128)(2,1)} %copy-done.35, bf16[32,2048]{1,0:T(8,128)(2,1)} %copy-done.33, ...), custom_call_target="tpu_custom_call" | custom-call | flops 4831838208 | bytes 24159192 | tf_op jit(solution)/shard_map/expert_backward/pallas_call | solution.py:248
  134.1 7.4 %weight_grads.2 = bf16[1024,2304]{1,0:T(8,128)(2,1)} custom-call(bf16[16,32,2048]{2,1,0:T(8,128)(2,1)} %copy-done.1, bf16[512,2048]{1,0:T(8,128)(2,1)} %get-tuple-element.169.dy_ref, bf16[512,768]{1,0:T(8,128)(2,1)} %get-tuple-element.182.inner_ref, bf16[512,1536]{1,0:T(8,128)(2,1)} %get-tuple-element.171.act_grad_ref), custom_call_target="tpu_custom_call" | custom-call | flops 2415919104 | bytes 12079595 | tf_op jit(solution)/shard_map/weight_grads/pallas_call | solution.py:279
  143.5 2.5 %collective-permute-start.26 = (bf16[32,2048]{1,0:T(8,128)(2,1)S(1)}, bf16[32,2048]{1,0:T(8,128)(2,1)S(1)}, u32[]{:S(2)}, u32[]{:S(2)}) collective-permute-start(bf16[32,2048]{1,0:T(8,128)(2,1)S(1)} %copy-done.30), channel_id=1, source_target_pairs={{0,20},{2,22},{4,16},{6,18},{8,28},{10,30},{12,24},{14,26},{16,4},... | collective-permute-start | bytes 393224 | tf_op jit(solution)/shard_map/ppermute | solution.py:60
  146.2 2.4 %collective-permute-start.24 = (bf16[32,2048]{1,0:T(8,128)(2,1)S(1)}, bf16[32,2048]{1,0:T(8,128)(2,1)S(1)}, u32[]{:S(2)}, u32[]{:S(2)}) collective-permute-start(bf16[32,2048]{1,0:T(8,128)(2,1)S(1)} %copy-done.25), channel_id=1, source_target_pairs={{0,16},{2,18},{4,20},{6,22},{8,24},{10,26},{12,28},{14,30},{16,0},... | collective-permute-start | bytes 393224 | tf_op jit(solution)/shard_map/ppermute | solution.py:60
  148.6 5.7 %collective-permute-done.22.refs_6_ = bf16[32,2048]{1,0:T(8,128)(2,1)S(1)} collective-permute-done((bf16[32,2048]{1,0:T(8,128)(2,1)S(1)}, bf16[32,2048]{1,0:T(8,128)(2,1)S(1)}, u32[]{:S(2)}, u32[]{:S(2)}) %collective-permute-start.22) | collective-permute-done | bytes 131104 | tf_op jit(solution)/shard_map/ppermute | solution.py:60
  154.3 3.4 %collective-permute-start.23 = (bf16[32,2048]{1,0:T(8,128)(2,1)S(1)}, bf16[32,2048]{1,0:T(8,128)(2,1)S(1)}, u32[]{:S(2)}, u32[]{:S(2)}) collective-permute-start(bf16[32,2048]{1,0:T(8,128)(2,1)S(1)} %copy-done.24), channel_id=1, source_target_pairs={{0,14},{2,12},{4,10},{6,8},{8,6},{10,4},{12,2},{14,0},{16,30},{18,... | collective-permute-start | bytes 393224 | tf_op jit(solution)/shard_map/ppermute | solution.py:60
  162.5 2.9 %collective-permute-start.28 = (bf16[32,2048]{1,0:T(8,128)(2,1)S(1)}, bf16[32,2048]{1,0:T(8,128)(2,1)S(1)}, u32[]{:S(2)}, u32[]{:S(2)}) collective-permute-start(bf16[32,2048]{1,0:T(8,128)(2,1)S(1)} %copy-done.22), channel_id=1, source_target_pairs={{0,24},{2,26},{4,28},{6,30},{8,16},{10,18},{12,20},{14,22},{16,8},... | collective-permute-start | bytes 393224 | tf_op jit(solution)/shard_map/ppermute | solution.py:60
  165.4 3.9 %collective-permute-start.29 = (bf16[32,2048]{1,0:T(8,128)(2,1)S(1)}, bf16[32,2048]{1,0:T(8,128)(2,1)}, u32[]{:S(2)}, u32[]{:S(2)}) collective-permute-start(bf16[32,2048]{1,0:T(8,128)(2,1)S(1)} %copy-done.21), channel_id=1, source_target_pairs={{0,26},{2,24},{4,30},{6,28},{8,18},{10,16},{12,22},{14,20},{16,10}... | collective-permute-start | bytes 393224 | tf_op jit(solution)/shard_map/ppermute | solution.py:60
  170.2 3.3 %collective-permute-start.31 = (bf16[32,2048]{1,0:T(8,128)(2,1)S(1)}, bf16[32,2048]{1,0:T(8,128)(2,1)}, u32[]{:S(2)}, u32[]{:S(2)}) collective-permute-start(bf16[32,2048]{1,0:T(8,128)(2,1)S(1)} %copy-done.19), channel_id=1, source_target_pairs={{0,30},{2,28},{4,26},{6,24},{8,22},{10,20},{12,18},{14,16},{16,14}... | collective-permute-start | bytes 393224 | tf_op jit(solution)/shard_map/ppermute | solution.py:60
  173.6 8.6 %collective-permute-done.30.refs_14_ = bf16[32,2048]{1,0:T(8,128)(2,1)} collective-permute-done((bf16[32,2048]{1,0:T(8,128)(2,1)S(1)}, bf16[32,2048]{1,0:T(8,128)(2,1)}, u32[]{:S(2)}, u32[]{:S(2)}) %collective-permute-start.30) | collective-permute-done | bytes 131104 | tf_op jit(solution)/shard_map/ppermute | solution.py:60
  182.2 5.5 %all-to-all-start.1 = ((bf16[16,32,2048]{2,1,0:T(8,128)(2,1)}), bf16[16,32,2048]{2,1,0:T(8,128)(2,1)S(1)}, u32[]{:S(2)}, u32[]{:S(2)}) async-start(bf16[16,32,2048]{2,1,0:T(8,128)(2,1)} %get-tuple-element.181), calls=%async_computation.1 | async-start | bytes 4194304 | tf_op jit(solution)/shard_map/all_to_all | solution.py:55
  189.0 4.9 %combine_y.1 = (bf16[256,2048]{1,0:T(8,128)(2,1)}, f32[8,256]{1,0:T(8,128)}) custom-call(s32[2]{0:T(128)} %pad_add_fusion.where_ref, bf16[512,256]{1,0:T(8,128)(2,1)} %get-tuple-element.183.pick_ref, bf16[256,512]{1,0:T(8,128)(2,1)} %get-tuple-element.196.high_ref, bf16[256,512]{1,0:T(8,128)(2,1)} %get-tuple-element.195.middle_ref, s32[8,256]{1,0:T(8,128)} %bitcast.16, ...), custom_call_target="tpu_custom_call" | custom-call | flops 1 | bytes 1 | tf_op jit(solution)/shard_map/combine_y/pallas_call | solution.py:325
  193.9 6.8 %weight_grads.3 = bf16[1024,2304]{1,0:T(8,128)(2,1)} custom-call(bf16[16,32,2048]{2,1,0:T(8,128)(2,1)} %copy-done.1, bf16[512,2048]{1,0:T(8,128)(2,1)} %get-tuple-element.169.dy_ref, bf16[512,768]{1,0:T(8,128)(2,1)} %get-tuple-element.182.inner_ref, bf16[512,1536]{1,0:T(8,128)(2,1)} %get-tuple-element.171.act_grad_ref), custom_call_target="tpu_custom_call" | custom-call | flops 2415919104 | bytes 12079595 | tf_op jit(solution)/shard_map/weight_grads/pallas_call | solution.py:279
  200.7 4.0 %convert_add_fusion.1 = f32[1024,768]{1,0:T(8,128)} fusion(bf16[1024,2304]{1,0:T(8,128)(2,1)} %weight_grads.3, bf16[1024,2304]{1,0:T(8,128)(2,1)} %collective-permute-done.32), kind=kLoop, calls=%fused_computation.1 | loop fusion | flops 2359296 | bytes 6291456 | tf_op jit(solution)/shard_map/add | solution.py:405
  204.7 5.5 %convert_add_fusion = f32[1024,1536]{1,0:T(8,128)} fusion(bf16[1024,2304]{1,0:T(8,128)(2,1)S(1)} %copy-done, bf16[1024,2304]{1,0:T(8,128)(2,1)} %collective-permute-done.32), kind=kLoop, calls=%fused_computation | loop fusion | flops 4718592 | bytes 12582912 | tf_op jit(solution)/shard_map/add | solution.py:405
  210.3 25.8 %all-to-all-done.1.rows_ref = bf16[16,32,2048]{2,1,0:T(8,128)(2,1)S(1)} async-done(((bf16[16,32,2048]{2,1,0:T(8,128)(2,1)}), bf16[16,32,2048]{2,1,0:T(8,128)(2,1)S(1)}, u32[]{:S(2)}, u32[]{:S(2)}) %all-to-all-start.1) | async-done | bytes 2097184 | tf_op jit(solution)/shard_map/all_to_all | solution.py:55
  237.4 4.9 %combine_dx.1 = bf16[256,2048]{1,0:T(8,128)(2,1)} custom-call(s32[2]{0:T(128)} %pad_add_fusion.where_ref, bf16[512,256]{1,0:T(8,128)(2,1)} %get-tuple-element.100.pick_ref, bf16[16,32,2048]{2,1,0:T(8,128)(2,1)} %copy-done.2), custom_call_target="tpu_custom_call" | custom-call | flops 1 | bytes 1 | tf_op jit(solution)/shard_map/combine_dx/pallas_call | solution.py:346
  (144 shorter events, 29.0 us)
Async XLA Ops:
  4.7 73.9 %all-to-all-start = ((bf16[16,32,2048]{2,1,0:T(8,128)(2,1)}), bf16[16,32,2048]{2,1,0:T(8,128)(2,1)S(1)}, u32[]{:S(2)}, u32[]{:S(2)}) async-start(bf16[16,32,2048]{2,1,0:T(8,128)(2,1)} %get-tuple-element.130), calls=%async_computation | async-start | bytes 4194304 | tf_op jit(solution)/shard_map/all_to_all | solution.py:55
  13.0 8.2 %collective-permute-start = (bf16[1024,1536]{1,0:T(8,128)(2,1)}, bf16[1024,1536]{1,0:T(8,128)(2,1)S(1)}, u32[]{:S(2)}, u32[]{:S(2)}) collective-permute-start(bf16[1024,1536]{1,0:T(8,128)(2,1)} %bitcast.18), channel_id=1, source_target_pairs={{1,0},{0,1},{3,2},{2,3},{5,4},{4,5},{7,6},{6,7},{9,8},{8,9},{11,10... | collective-permute-start | bytes 9437192 | tf_op jit(solution)/shard_map/ppermute | solution.py:45
  21.2 30.0 %collective-permute-start.6 = (bf16[32,2048]{1,0:T(8,128)(2,1)}, bf16[32,2048]{1,0:T(8,128)(2,1)S(1)}, u32[]{:S(2)}, u32[]{:S(2)}) collective-permute-start(bf16[32,2048]{1,0:T(8,128)(2,1)} %get-tuple-element.112), channel_id=1, source_target_pairs={{0,10},{2,8},{4,14},{6,12},{8,2},{10,0},{12,6},{14,4},{16,26},{18,... | collective-permute-start | bytes 393224 | tf_op jit(solution)/shard_map/ppermute | solution.py:60
  24.0 33.5 %collective-permute-start.5 = (bf16[32,2048]{1,0:T(8,128)(2,1)}, bf16[32,2048]{1,0:T(8,128)(2,1)S(1)}, u32[]{:S(2)}, u32[]{:S(2)}) collective-permute-start(bf16[32,2048]{1,0:T(8,128)(2,1)} %get-tuple-element.110), channel_id=1, source_target_pairs={{0,8},{2,10},{4,12},{6,14},{8,0},{10,2},{12,4},{14,6},{16,24},{18,... | collective-permute-start | bytes 393224 | tf_op jit(solution)/shard_map/ppermute | solution.py:60
  24.6 33.7 %collective-permute-start.4 = (bf16[32,2048]{1,0:T(8,128)(2,1)}, bf16[32,2048]{1,0:T(8,128)(2,1)S(1)}, u32[]{:S(2)}, u32[]{:S(2)}) collective-permute-start(bf16[32,2048]{1,0:T(8,128)(2,1)} %get-tuple-element.108), channel_id=1, source_target_pairs={{0,6},{2,4},{4,2},{6,0},{8,14},{10,12},{12,10},{14,8},{16,22},{18,... | collective-permute-start | bytes 393224 | tf_op jit(solution)/shard_map/ppermute | solution.py:60
  26.9 49.7 %collective-permute-start.3 = (bf16[32,2048]{1,0:T(8,128)(2,1)}, bf16[32,2048]{1,0:T(8,128)(2,1)S(1)}, u32[]{:S(2)}, u32[]{:S(2)}) collective-permute-start(bf16[32,2048]{1,0:T(8,128)(2,1)} %get-tuple-element.106), channel_id=1, source_target_pairs={{0,4},{2,6},{4,0},{6,2},{8,12},{10,14},{12,8},{14,10},{16,20},{18,... | collective-permute-start | bytes 393224 | tf_op jit(solution)/shard_map/ppermute | solution.py:60
  26.9 50.7 %collective-permute-start.2 = (bf16[32,2048]{1,0:T(8,128)(2,1)}, bf16[32,2048]{1,0:T(8,128)(2,1)S(1)}, u32[]{:S(2)}, u32[]{:S(2)}) collective-permute-start(bf16[32,2048]{1,0:T(8,128)(2,1)} %get-tuple-element.104), channel_id=1, source_target_pairs={{0,2},{2,0},{4,6},{6,4},{8,10},{10,8},{12,14},{14,12},{16,18},{18,... | collective-permute-start | bytes 393224 | tf_op jit(solution)/shard_map/ppermute | solution.py:60
  51.2 49.4 %collective-permute-start.11 = (bf16[32,2048]{1,0:T(8,128)(2,1)}, bf16[32,2048]{1,0:T(8,128)(2,1)S(1)}, u32[]{:S(2)}, u32[]{:S(2)}) collective-permute-start(bf16[32,2048]{1,0:T(8,128)(2,1)} %get-tuple-element.127), channel_id=1, source_target_pairs={{0,20},{2,22},{4,16},{6,18},{8,28},{10,30},{12,24},{14,26},{16,4},... | collective-permute-start | bytes 393224 | tf_op jit(solution)/shard_map/ppermute | solution.py:60
  57.5 40.9 %collective-permute-start.10 = (bf16[32,2048]{1,0:T(8,128)(2,1)}, bf16[32,2048]{1,0:T(8,128)(2,1)S(1)}, u32[]{:S(2)}, u32[]{:S(2)}) collective-permute-start(bf16[32,2048]{1,0:T(8,128)(2,1)} %get-tuple-element.124), channel_id=1, source_target_pairs={{0,18},{2,16},{4,22},{6,20},{8,26},{10,24},{12,30},{14,28},{16,2},... | collective-permute-start | bytes 393224 | tf_op jit(solution)/shard_map/ppermute | solution.py:60
  58.2 38.7 %collective-permute-start.9 = (bf16[32,2048]{1,0:T(8,128)(2,1)}, bf16[32,2048]{1,0:T(8,128)(2,1)}, u32[]{:S(2)}, u32[]{:S(2)}) collective-permute-start(bf16[32,2048]{1,0:T(8,128)(2,1)} %get-tuple-element.121), channel_id=1, source_target_pairs={{0,16},{2,18},{4,20},{6,22},{8,24},{10,26},{12,28},{14,30},{16,0},... | collective-permute-start | bytes 393224 | tf_op jit(solution)/shard_map/ppermute | solution.py:60
  76.6 19.4 %collective-permute-start.8 = (bf16[32,2048]{1,0:T(8,128)(2,1)}, bf16[32,2048]{1,0:T(8,128)(2,1)}, u32[]{:S(2)}, u32[]{:S(2)}) collective-permute-start(bf16[32,2048]{1,0:T(8,128)(2,1)} %get-tuple-element.118), channel_id=1, source_target_pairs={{0,14},{2,12},{4,10},{6,8},{8,6},{10,4},{12,2},{14,0},{16,30},{18,... | collective-permute-start | bytes 393224 | tf_op jit(solution)/shard_map/ppermute | solution.py:60
  78.3 13.6 %collective-permute-start.7 = (bf16[32,2048]{1,0:T(8,128)(2,1)}, bf16[32,2048]{1,0:T(8,128)(2,1)}, u32[]{:S(2)}, u32[]{:S(2)}) collective-permute-start(bf16[32,2048]{1,0:T(8,128)(2,1)} %get-tuple-element.115), channel_id=1, source_target_pairs={{0,12},{2,14},{4,8},{6,10},{8,4},{10,6},{12,0},{14,2},{16,28},{18,... | collective-permute-start | bytes 393224 | tf_op jit(solution)/shard_map/ppermute | solution.py:60
  91.9 12.8 %collective-permute-start.12 = (bf16[32,2048]{1,0:T(8,128)(2,1)S(1)}, bf16[32,2048]{1,0:T(8,128)(2,1)S(1)}, u32[]{:S(2)}, u32[]{:S(2)}) collective-permute-start(bf16[32,2048]{1,0:T(8,128)(2,1)S(1)} %copy-done.40), channel_id=1, source_target_pairs={{0,22},{2,20},{4,18},{6,16},{8,30},{10,28},{12,26},{14,24},{16,6},... | collective-permute-start | bytes 393224 | tf_op jit(solution)/shard_map/ppermute | solution.py:60
  96.0 12.9 %collective-permute-start.13 = (bf16[32,2048]{1,0:T(8,128)(2,1)S(1)}, bf16[32,2048]{1,0:T(8,128)(2,1)S(1)}, u32[]{:S(2)}, u32[]{:S(2)}) collective-permute-start(bf16[32,2048]{1,0:T(8,128)(2,1)S(1)} %copy-done.38), channel_id=1, source_target_pairs={{0,24},{2,26},{4,28},{6,30},{8,16},{10,18},{12,20},{14,22},{16,8},... | collective-permute-start | bytes 393224 | tf_op jit(solution)/shard_map/ppermute | solution.py:60
  96.9 13.8 %collective-permute-start.14 = (bf16[32,2048]{1,0:T(8,128)(2,1)S(1)}, bf16[32,2048]{1,0:T(8,128)(2,1)S(1)}, u32[]{:S(2)}, u32[]{:S(2)}) collective-permute-start(bf16[32,2048]{1,0:T(8,128)(2,1)S(1)} %copy-done.36), channel_id=1, source_target_pairs={{0,26},{2,24},{4,30},{6,28},{8,18},{10,16},{12,22},{14,20},{16,10}... | collective-permute-start | bytes 393224 | tf_op jit(solution)/shard_map/ppermute | solution.py:60
  98.5 15.5 %collective-permute-start.15 = (bf16[32,2048]{1,0:T(8,128)(2,1)S(1)}, bf16[32,2048]{1,0:T(8,128)(2,1)S(1)}, u32[]{:S(2)}, u32[]{:S(2)}) collective-permute-start(bf16[32,2048]{1,0:T(8,128)(2,1)S(1)} %copy-done.31), channel_id=1, source_target_pairs={{0,28},{2,30},{4,24},{6,26},{8,20},{10,22},{12,16},{14,18},{16,12}... | collective-permute-start | bytes 393224 | tf_op jit(solution)/shard_map/ppermute | solution.py:60
  100.6 14.2 %collective-permute-start.16 = (bf16[32,2048]{1,0:T(8,128)(2,1)S(1)}, bf16[32,2048]{1,0:T(8,128)(2,1)S(1)}, u32[]{:S(2)}, u32[]{:S(2)}) collective-permute-start(bf16[32,2048]{1,0:T(8,128)(2,1)S(1)} %copy-done.27), channel_id=1, source_target_pairs={{0,30},{2,28},{4,26},{6,24},{8,22},{10,20},{12,18},{14,16},{16,14}... | collective-permute-start | bytes 393224 | tf_op jit(solution)/shard_map/ppermute | solution.py:60
  104.7 29.2 %collective-permute-start.17 = (bf16[32,2048]{1,0:T(8,128)(2,1)}, bf16[32,2048]{1,0:T(8,128)(2,1)S(1)}, u32[]{:S(2)}, u32[]{:S(2)}) collective-permute-start(bf16[32,2048]{1,0:T(8,128)(2,1)} %get-tuple-element.149), channel_id=1, source_target_pairs={{0,2},{2,0},{4,6},{6,4},{8,10},{10,8},{12,14},{14,12},{16,18},{18,... | collective-permute-start | bytes 393224 | tf_op jit(solution)/shard_map/ppermute | solution.py:60
  108.9 25.0 %collective-permute-start.18 = (bf16[32,2048]{1,0:T(8,128)(2,1)}, bf16[32,2048]{1,0:T(8,128)(2,1)S(1)}, u32[]{:S(2)}, u32[]{:S(2)}) collective-permute-start(bf16[32,2048]{1,0:T(8,128)(2,1)} %get-tuple-element.151), channel_id=1, source_target_pairs={{0,4},{2,6},{4,0},{6,2},{8,12},{10,14},{12,8},{14,10},{16,20},{18,... | collective-permute-start | bytes 393224 | tf_op jit(solution)/shard_map/ppermute | solution.py:60
  110.7 23.2 %collective-permute-start.19 = (bf16[32,2048]{1,0:T(8,128)(2,1)}, bf16[32,2048]{1,0:T(8,128)(2,1)S(1)}, u32[]{:S(2)}, u32[]{:S(2)}) collective-permute-start(bf16[32,2048]{1,0:T(8,128)(2,1)} %get-tuple-element.153), channel_id=1, source_target_pairs={{0,6},{2,4},{4,2},{6,0},{8,14},{10,12},{12,10},{14,8},{16,22},{18,... | collective-permute-start | bytes 393224 | tf_op jit(solution)/shard_map/ppermute | solution.py:60
  114.0 20.0 %collective-permute-start.20 = (bf16[32,2048]{1,0:T(8,128)(2,1)}, bf16[32,2048]{1,0:T(8,128)(2,1)S(1)}, u32[]{:S(2)}, u32[]{:S(2)}) collective-permute-start(bf16[32,2048]{1,0:T(8,128)(2,1)} %get-tuple-element.155), channel_id=1, source_target_pairs={{0,8},{2,10},{4,12},{6,14},{8,0},{10,2},{12,4},{14,6},{16,24},{18,... | collective-permute-start | bytes 393224 | tf_op jit(solution)/shard_map/ppermute | solution.py:60
  114.8 19.2 %collective-permute-start.21 = (bf16[32,2048]{1,0:T(8,128)(2,1)}, bf16[32,2048]{1,0:T(8,128)(2,1)S(1)}, u32[]{:S(2)}, u32[]{:S(2)}) collective-permute-start(bf16[32,2048]{1,0:T(8,128)(2,1)} %get-tuple-element.157), channel_id=1, source_target_pairs={{0,10},{2,8},{4,14},{6,12},{8,2},{10,0},{12,6},{14,4},{16,26},{18,... | collective-permute-start | bytes 393224 | tf_op jit(solution)/shard_map/ppermute | solution.py:60
  141.6 59.1 %collective-permute-start.32 = (bf16[1024,2304]{1,0:T(8,128)(2,1)}, bf16[1024,2304]{1,0:T(8,128)(2,1)}, u32[]{:S(2)}, u32[]{:S(2)}) collective-permute-start(bf16[1024,2304]{1,0:T(8,128)(2,1)} %weight_grads.2), channel_id=1, source_target_pairs={{0,1},{1,0},{2,3},{3,2},{4,5},{5,4},{6,7},{7,6},{8,9},{9,8},{10,11... | collective-permute-start | bytes 14155784 | tf_op jit(solution)/shard_map/ppermute | solution.py:51
  141.7 12.6 %collective-permute-start.22 = (bf16[32,2048]{1,0:T(8,128)(2,1)S(1)}, bf16[32,2048]{1,0:T(8,128)(2,1)S(1)}, u32[]{:S(2)}, u32[]{:S(2)}) collective-permute-start(bf16[32,2048]{1,0:T(8,128)(2,1)S(1)} %copy-done.34), channel_id=1, source_target_pairs={{0,12},{2,14},{4,8},{6,10},{8,4},{10,6},{12,0},{14,2},{16,28},{18,... | collective-permute-start | bytes 393224 | tf_op jit(solution)/shard_map/ppermute | solution.py:60
  143.5 15.2 %collective-permute-start.26 = (bf16[32,2048]{1,0:T(8,128)(2,1)S(1)}, bf16[32,2048]{1,0:T(8,128)(2,1)S(1)}, u32[]{:S(2)}, u32[]{:S(2)}) collective-permute-start(bf16[32,2048]{1,0:T(8,128)(2,1)S(1)} %copy-done.30), channel_id=1, source_target_pairs={{0,20},{2,22},{4,16},{6,18},{8,28},{10,30},{12,24},{14,26},{16,4},... | collective-permute-start | bytes 393224 | tf_op jit(solution)/shard_map/ppermute | solution.py:60
  146.0 14.7 %collective-permute-start.25 = (bf16[32,2048]{1,0:T(8,128)(2,1)S(1)}, bf16[32,2048]{1,0:T(8,128)(2,1)S(1)}, u32[]{:S(2)}, u32[]{:S(2)}) collective-permute-start(bf16[32,2048]{1,0:T(8,128)(2,1)S(1)} %copy-done.26), channel_id=1, source_target_pairs={{0,18},{2,16},{4,22},{6,20},{8,26},{10,24},{12,30},{14,28},{16,2},... | collective-permute-start | bytes 393224 | tf_op jit(solution)/shard_map/ppermute | solution.py:60
  146.2 14.5 %collective-permute-start.24 = (bf16[32,2048]{1,0:T(8,128)(2,1)S(1)}, bf16[32,2048]{1,0:T(8,128)(2,1)S(1)}, u32[]{:S(2)}, u32[]{:S(2)}) collective-permute-start(bf16[32,2048]{1,0:T(8,128)(2,1)S(1)} %copy-done.25), channel_id=1, source_target_pairs={{0,16},{2,18},{4,20},{6,22},{8,24},{10,26},{12,28},{14,30},{16,0},... | collective-permute-start | bytes 393224 | tf_op jit(solution)/shard_map/ppermute | solution.py:60
  158.7 11.5 %collective-permute-start.27 = (bf16[32,2048]{1,0:T(8,128)(2,1)S(1)}, bf16[32,2048]{1,0:T(8,128)(2,1)S(1)}, u32[]{:S(2)}, u32[]{:S(2)}) collective-permute-start(bf16[32,2048]{1,0:T(8,128)(2,1)S(1)} %copy-done.23), channel_id=1, source_target_pairs={{0,22},{2,20},{4,18},{6,16},{8,30},{10,28},{12,26},{14,24},{16,6},... | collective-permute-start | bytes 393224 | tf_op jit(solution)/shard_map/ppermute | solution.py:60
  162.5 11.1 %collective-permute-start.28 = (bf16[32,2048]{1,0:T(8,128)(2,1)S(1)}, bf16[32,2048]{1,0:T(8,128)(2,1)S(1)}, u32[]{:S(2)}, u32[]{:S(2)}) collective-permute-start(bf16[32,2048]{1,0:T(8,128)(2,1)S(1)} %copy-done.22), channel_id=1, source_target_pairs={{0,24},{2,26},{4,28},{6,30},{8,16},{10,18},{12,20},{14,22},{16,8},... | collective-permute-start | bytes 393224 | tf_op jit(solution)/shard_map/ppermute | solution.py:60
  169.3 12.9 %collective-permute-start.30 = (bf16[32,2048]{1,0:T(8,128)(2,1)S(1)}, bf16[32,2048]{1,0:T(8,128)(2,1)}, u32[]{:S(2)}, u32[]{:S(2)}) collective-permute-start(bf16[32,2048]{1,0:T(8,128)(2,1)S(1)} %copy-done.20), channel_id=1, source_target_pairs={{0,28},{2,30},{4,24},{6,26},{8,20},{10,22},{12,16},{14,18},{16,12}... | collective-permute-start | bytes 393224 | tf_op jit(solution)/shard_map/ppermute | solution.py:60
  170.2 12.0 %collective-permute-start.31 = (bf16[32,2048]{1,0:T(8,128)(2,1)S(1)}, bf16[32,2048]{1,0:T(8,128)(2,1)}, u32[]{:S(2)}, u32[]{:S(2)}) collective-permute-start(bf16[32,2048]{1,0:T(8,128)(2,1)S(1)} %copy-done.19), channel_id=1, source_target_pairs={{0,30},{2,28},{4,26},{6,24},{8,22},{10,20},{12,18},{14,16},{16,14}... | collective-permute-start | bytes 393224 | tf_op jit(solution)/shard_map/ppermute | solution.py:60
  182.2 53.9 %all-to-all-start.1 = ((bf16[16,32,2048]{2,1,0:T(8,128)(2,1)}), bf16[16,32,2048]{2,1,0:T(8,128)(2,1)S(1)}, u32[]{:S(2)}, u32[]{:S(2)}) async-start(bf16[16,32,2048]{2,1,0:T(8,128)(2,1)} %get-tuple-element.181), calls=%async_computation.1 | async-start | bytes 4194304 | tf_op jit(solution)/shard_map/all_to_all | solution.py:55
  (49 other events, 1328.9 us)

commit v17 on v14

--- a/solution.py
+++ b/solution.py
@@ -362,11 +362,9 @@
     dys = [blocks[0]]
     for j in range(1, groups):
         needs = (dys[j - queued],) if j > queued else ()
-        if j == 2 * queued + 1:
-            y_sent, act, inner = expert_forward(after(got, *dys[1 : queued + 1]), w_ins, w_outs)
-        if j > 2 * queued:
-            needs += (inner,)
         dys.append(to_partner(after(blocks[j], *needs) if needs else blocks[j], j))
+    held = after(got, *dys[1 : groups - queued])
+    y_sent, act, inner = expert_forward(held, w_ins, w_outs)
     y_got = to_all(after(y_sent, *dys[1:]))
     dxs, act_grad, dy_rows = expert_backward(where, dys, act, w_ins, w_outs)
     backs = [dxs[0]]

time: 221 us -> 220 us (level)
  starting transfers between devices: 68.1 us -> 64.9 us
  waiting for transfers between devices: 82.9 us -> 85.2 us
    ppermute x30, waiting for transfers between devices: 58.9 us -> 62.1 us  [to_partner(): lax.ppermute(block, ('node', 'local'), [(i, i ^ j) for i in range(count)])]
where the time goes in v17:
time: 220 us
  waiting for transfers between devices  85.2 us (39%)
  starting transfers between devices  64.9 us (30%)
  Pallas kernels  54.3 us (25%)
  other arithmetic  10.6 us (5%)
  local copies, waits for them, and re-layouts  3.78 us (2%)
    ppermute x30, waiting for transfers between devices, to_partner(): lax.ppermute(block, ('node', 'local'), [(i, i ^ j) for i in range(count)])  62.1 us
    ppermute x30, starting transfers between devices, to_partner(): lax.ppermute(block, ('node', 'local'), [(i, i ^ j) for i in range(count)])  50.6 us
    all_to_all x2, waiting for transfers between devices, to_all(): lax.all_to_all(rows, ('node', 'local'), split_axis=0, concat_axis=0, tile...  19.8 us
    pallas_call x2, Pallas kernels, weight_grads(): call(kernel, 'weight_grads', cost=work(6 * slots * size * hidden), grid=(...  13.8 us
    all_to_all x2, starting transfers between devices, to_all(): lax.all_to_all(rows, ('node', 'local'), split_axis=0, concat_axis=0, tile...  13.8 us
    pallas_call x1, Pallas kernels, expert_backward(): call(kernel, 'expert_backward', cost=work(6 * slots * model * hidden), in...  13.4 us
    pallas_call x1, Pallas kernels, expert_forward(): call(kernel, 'expert_forward', cost=work(6 * slots * model * hidden), in_...  11.2 us
    add x2, other arithmetic, shards(): sum((p[:, columns].astype(F32) for p in parts))  8.95 us
  transfers between devices with their start and end apart: 35, of which 11 were waited for; matrix products, arithmetic and copies ran while one was open for 5% of the time, Pallas kernels for 22%

profile of v17, /device:TPU:0, one launch (start us, length us, event | category | flops | bytes accessed | tf_op | source)
XLA Modules:
  0.0 219.8 jit_solution(320517992558616126)
XLA Ops:
  1.3 3.5 %dispatch_x.1 = (bf16[16,32,2048]{2,1,0:T(8,128)(2,1)}, bf16[512,256]{1,0:T(8,128)(2,1)}, f32[512,1]{1,0:T(8,128)}) custom-call(s32[2]{0:T(128)} %pad_add_fusion.where_ref, s32[8,256]{1,0:T(8,128)} %bitcast.17, f32[8,256]{1,0:T(8,128)} %bitcast.19, bf16[256,2048]{1,0:T(8,128)(2,1)} %x_ref.1), custom_call_target="tpu_custom_call" | custom-call | flops 1 | bytes 1 | tf_op jit(solution)/shard_map/dispatch_x/pallas_call | solution.py:105
  4.7 8.3 %all-to-all-start = ((bf16[16,32,2048]{2,1,0:T(8,128)(2,1)}), bf16[16,32,2048]{2,1,0:T(8,128)(2,1)S(1)}, u32[]{:S(2)}, u32[]{:S(2)}) async-start(bf16[16,32,2048]{2,1,0:T(8,128)(2,1)} %get-tuple-element.154), calls=%async_computation | async-start | bytes 4194304 | tf_op jit(solution)/shard_map/all_to_all | solution.py:55
  13.6 4.2 %dispatch_dy.1 = (bf16[32,2048]{1,0:T(8,128)(2,1)}, bf16[32,2048]{1,0:T(8,128)(2,1)}, bf16[32,2048]{1,0:T(8,128)(2,1)}, bf16[32,2048]{1,0:T(8,128)(2,1)}, bf16[3...) custom-call(s32[2]{0:T(128)} %pad_add_fusion.where_ref, ...), custom_call_target="tpu_custom_call" | custom-call | flops 1 | bytes 1 | tf_op jit(solution)/shard_map/dispatch_dy/pallas_call | solution.py:137
  17.8 3.4 %collective-permute-done.1.refs_3_.refs_20_ = bf16[1024,768]{1,0:T(8,128)(2,1)S(1)} collective-permute-done((bf16[1024,768]{1,0:T(8,128)(2,1)}, bf16[1024,768]{1,0:T(8,128)(2,1)S(1)}, u32[]{:S(2)}, u32[]{:S(2)}) %collective-permute-start.1) | collective-permute-done | bytes 1572896 | tf_op jit(solution)/shard_map/ppermute | solution.py:45
  21.2 2.8 %collective-permute-start.6 = (bf16[32,2048]{1,0:T(8,128)(2,1)}, bf16[32,2048]{1,0:T(8,128)(2,1)S(1)}, u32[]{:S(2)}, u32[]{:S(2)}) collective-permute-start(bf16[32,2048]{1,0:T(8,128)(2,1)} %get-tuple-element.123), channel_id=1, source_target_pairs={{0,10},{2,8},{4,14},{6,12},{8,2},{10,0},{12,6},{14,4},{16,26},{18,... | collective-permute-start | bytes 393224 | tf_op jit(solution)/shard_map/ppermute | solution.py:60
  24.6 2.4 %collective-permute-start.4 = (bf16[32,2048]{1,0:T(8,128)(2,1)}, bf16[32,2048]{1,0:T(8,128)(2,1)S(1)}, u32[]{:S(2)}, u32[]{:S(2)}) collective-permute-start(bf16[32,2048]{1,0:T(8,128)(2,1)} %get-tuple-element.119), channel_id=1, source_target_pairs={{0,6},{2,4},{4,2},{6,0},{8,14},{10,12},{12,10},{14,8},{16,22},{18,... | collective-permute-start | bytes 393224 | tf_op jit(solution)/shard_map/ppermute | solution.py:60
  27.0 2.0 collective-permute-start.2
  29.0 22.2 %collective-permute-done.6.refs_5_ = bf16[32,2048]{1,0:T(8,128)(2,1)S(1)} collective-permute-done((bf16[32,2048]{1,0:T(8,128)(2,1)}, bf16[32,2048]{1,0:T(8,128)(2,1)S(1)}, u32[]{:S(2)}, u32[]{:S(2)}) %collective-permute-start.6) | collective-permute-done | bytes 131104 | tf_op jit(solution)/shard_map/ppermute | solution.py:60
  51.2 6.4 %collective-permute-start.11 = (bf16[32,2048]{1,0:T(8,128)(2,1)}, bf16[32,2048]{1,0:T(8,128)(2,1)S(1)}, u32[]{:S(2)}, u32[]{:S(2)}) collective-permute-start(bf16[32,2048]{1,0:T(8,128)(2,1)} %get-tuple-element.138), channel_id=1, source_target_pairs={{0,20},{2,22},{4,16},{6,18},{8,28},{10,30},{12,24},{14,26},{16,4},... | collective-permute-start | bytes 393224 | tf_op jit(solution)/shard_map/ppermute | solution.py:60
  59.7 16.9 %collective-permute-done.3.refs_2_ = bf16[32,2048]{1,0:T(8,128)(2,1)S(1)} collective-permute-done((bf16[32,2048]{1,0:T(8,128)(2,1)}, bf16[32,2048]{1,0:T(8,128)(2,1)S(1)}, u32[]{:S(2)}, u32[]{:S(2)}) %collective-permute-start.3) | collective-permute-done | bytes 131104 | tf_op jit(solution)/shard_map/ppermute | solution.py:60
  78.0 2.0 collective-permute-done.11.refs_10_
  80.0 2.1 collective-permute-start.16
  82.1 3.1 %collective-permute-start.15 = (bf16[32,2048]{1,0:T(8,128)(2,1)}, bf16[32,2048]{1,0:T(8,128)(2,1)}, u32[]{:S(2)}, u32[]{:S(2)}) collective-permute-start(bf16[32,2048]{1,0:T(8,128)(2,1)} %get-tuple-element.150), channel_id=1, source_target_pairs={{0,28},{2,30},{4,24},{6,26},{8,20},{10,22},{12,16},{14,18},{16,12}... | collective-permute-start | bytes 393224 | tf_op jit(solution)/shard_map/ppermute | solution.py:60
  88.6 8.4 %collective-permute-done.7.refs_6_ = bf16[32,2048]{1,0:T(8,128)(2,1)S(1)} collective-permute-done((bf16[32,2048]{1,0:T(8,128)(2,1)}, bf16[32,2048]{1,0:T(8,128)(2,1)S(1)}, u32[]{:S(2)}, u32[]{:S(2)}) %collective-permute-start.7) | collective-permute-done | bytes 131104 | tf_op jit(solution)/shard_map/ppermute | solution.py:60
  96.9 2.5 %collective-permute-start.12 = (bf16[32,2048]{1,0:T(8,128)(2,1)}, bf16[32,2048]{1,0:T(8,128)(2,1)}, u32[]{:S(2)}, u32[]{:S(2)}) collective-permute-start(bf16[32,2048]{1,0:T(8,128)(2,1)} %get-tuple-element.141), channel_id=1, source_target_pairs={{0,22},{2,20},{4,18},{6,16},{8,30},{10,28},{12,26},{14,24},{16,6},... | collective-permute-start | bytes 393224 | tf_op jit(solution)/shard_map/ppermute | solution.py:60
  100.8 11.2 %expert_forward.1 = (bf16[16,32,2048]{2,1,0:T(8,128)(2,1)}, f32[512,1536]{1,0:T(8,128)}, bf16[512,768]{1,0:T(8,128)(2,1)}) custom-call(bf16[16,32,2048]{2,1,0:T(8,128)(2,1)} %copy-done.1, bf16[1024,1536]{1,0:T(8,128)(2,1)} %bitcast.21, bf16[1024,1536]{1,0:T(8,128)(2,1)} %copy-done.18, bf16[1024,768]{1,0:T(8,128)(2,1)} %bitcast.24, bf16[1024,768]{1,0:T(8,128)(2,1)} %copy-done.19), custom_call_target="tpu_custom_call" | custom-call | flops 4831838208 | bytes 24159192 | tf_op jit(solution)/shard_map/expert_forward/pallas_call | solution.py:189
  112.8 5.5 %all-to-all-start.1 = ((bf16[16,32,2048]{2,1,0:T(8,128)(2,1)}), bf16[16,32,2048]{2,1,0:T(8,128)(2,1)S(1)}, u32[]{:S(2)}, u32[]{:S(2)}) async-start(bf16[16,32,2048]{2,1,0:T(8,128)(2,1)} %get-tuple-element.165), calls=%async_computation.1 | async-start | bytes 4194304 | tf_op jit(solution)/shard_map/all_to_all | solution.py:55
  118.2 13.4 %expert_backward.1 = (bf16[32,2048]{1,0:T(8,128)(2,1)}, bf16[32,2048]{1,0:T(8,128)(2,1)}, bf16[32,2048]{1,0:T(8,128)(2,1)}, bf16[32,2048]{1,0:T(8,128)(2,1)}, bf...) custom-call(s32[2]{0:T(128)} %pad_add_fusion.where_ref, ...), custom_call_target="tpu_custom_call" | custom-call | flops 4831838208 | bytes 24159192 | tf_op jit(solution)/shard_map/expert_backward/pallas_call | solution.py:237
  131.6 6.9 %weight_grads.3 = bf16[1024,2304]{1,0:T(8,128)(2,1)} custom-call(bf16[16,32,2048]{2,1,0:T(8,128)(2,1)} %copy-done.1, bf16[512,2048]{1,0:T(8,128)(2,1)} %get-tuple-element.185.dy_ref, bf16[512,768]{1,0:T(8,128)(2,1)} %get-tuple-element.186.inner_ref, bf16[512,1536]{1,0:T(8,128)(2,1)} %get-tuple-element.187.act_grad_ref), custom_call_target="tpu_custom_call" | custom-call | flops 2415919104 | bytes 12079595 | tf_op jit(solution)/shard_map/weight_grads/pallas_call | solution.py:270
  138.5 6.9 %weight_grads.2 = bf16[1024,2304]{1,0:T(8,128)(2,1)} custom-call(bf16[16,32,2048]{2,1,0:T(8,128)(2,1)} %copy-done.1, bf16[512,2048]{1,0:T(8,128)(2,1)} %get-tuple-element.185.dy_ref, bf16[512,768]{1,0:T(8,128)(2,1)} %get-tuple-element.186.inner_ref, bf16[512,1536]{1,0:T(8,128)(2,1)} %get-tuple-element.187.act_grad_ref), custom_call_target="tpu_custom_call" | custom-call | flops 2415919104 | bytes 12079595 | tf_op jit(solution)/shard_map/weight_grads/pallas_call | solution.py:270
  145.4 19.8 %all-to-all-done.1.refs_0_ = bf16[16,32,2048]{2,1,0:T(8,128)(2,1)S(1)} async-done(((bf16[16,32,2048]{2,1,0:T(8,128)(2,1)}), bf16[16,32,2048]{2,1,0:T(8,128)(2,1)S(1)}, u32[]{:S(2)}, u32[]{:S(2)}) %all-to-all-start.1) | async-done | bytes 2097184 | tf_op jit(solution)/shard_map/all_to_all | solution.py:55
  165.9 3.8 %collective-permute-start.19 = (bf16[32,2048]{1,0:T(8,128)(2,1)}, bf16[32,2048]{1,0:T(8,128)(2,1)S(1)}, u32[]{:S(2)}, u32[]{:S(2)}) collective-permute-start(bf16[32,2048]{1,0:T(8,128)(2,1)} %get-tuple-element.160), channel_id=1, source_target_pairs={{0,6},{2,4},{4,2},{6,0},{8,14},{10,12},{12,10},{14,8},{16,22},{18,... | collective-permute-start | bytes 393224 | tf_op jit(solution)/shard_map/ppermute | solution.py:60
  169.7 2.6 %collective-permute-done.17.refs_1_ = bf16[32,2048]{1,0:T(8,128)(2,1)S(1)} collective-permute-done((bf16[32,2048]{1,0:T(8,128)(2,1)S(1)}, bf16[32,2048]{1,0:T(8,128)(2,1)S(1)}, u32[]{:S(2)}, u32[]{:S(2)}) %collective-permute-start.17) | collective-permute-done | bytes 131104 | tf_op jit(solution)/shard_map/ppermute | solution.py:60
  172.3 6.2 %collective-permute-done.18.refs_2_ = bf16[32,2048]{1,0:T(8,128)(2,1)S(1)} collective-permute-done((bf16[32,2048]{1,0:T(8,128)(2,1)S(1)}, bf16[32,2048]{1,0:T(8,128)(2,1)S(1)}, u32[]{:S(2)}, u32[]{:S(2)}) %collective-permute-start.18) | collective-permute-done | bytes 131104 | tf_op jit(solution)/shard_map/ppermute | solution.py:60
  181.7 5.8 %collective-permute-start.25 = (bf16[32,2048]{1,0:T(8,128)(2,1)}, bf16[32,2048]{1,0:T(8,128)(2,1)S(1)}, u32[]{:S(2)}, u32[]{:S(2)}) collective-permute-start(bf16[32,2048]{1,0:T(8,128)(2,1)} %get-tuple-element.172), channel_id=1, source_target_pairs={{0,18},{2,16},{4,22},{6,20},{8,26},{10,24},{12,30},{14,28},{16,2},... | collective-permute-start | bytes 393224 | tf_op jit(solution)/shard_map/ppermute | solution.py:60
  187.4 2.5 %collective-permute-done.22.refs_6_ = bf16[32,2048]{1,0:T(8,128)(2,1)} collective-permute-done((bf16[32,2048]{1,0:T(8,128)(2,1)}, bf16[32,2048]{1,0:T(8,128)(2,1)}, u32[]{:S(2)}, u32[]{:S(2)}) %collective-permute-start.22) | collective-permute-done | bytes 131104 | tf_op jit(solution)/shard_map/ppermute | solution.py:60
  190.8 4.9 %combine_y.1 = (bf16[256,2048]{1,0:T(8,128)(2,1)}, f32[8,256]{1,0:T(8,128)}) custom-call(s32[2]{0:T(128)} %pad_add_fusion.where_ref, bf16[512,256]{1,0:T(8,128)(2,1)} %get-tuple-element.111.pick_ref, bf16[256,512]{1,0:T(8,128)(2,1)} %get-tuple-element.218.high_ref, bf16[256,512]{1,0:T(8,128)(2,1)} %get-tuple-element.217.middle_ref, s32[8,256]{1,0:T(8,128)} %bitcast.18, ...), custom_call_target="tpu_custom_call" | custom-call | flops 1 | bytes 1 | tf_op jit(solution)/shard_map/combine_y/pallas_call | solution.py:315
  199.5 3.1 %collective-permute-start.29 = (bf16[32,2048]{1,0:T(8,128)(2,1)}, bf16[32,2048]{1,0:T(8,128)(2,1)S(1)}, u32[]{:S(2)}, u32[]{:S(2)}) collective-permute-start(bf16[32,2048]{1,0:T(8,128)(2,1)} %get-tuple-element.180), channel_id=1, source_target_pairs={{0,26},{2,24},{4,30},{6,28},{8,18},{10,16},{12,22},{14,20},{16,10}... | collective-permute-start | bytes 393224 | tf_op jit(solution)/shard_map/ppermute | solution.py:60
  204.1 2.0 collective-permute-start.31
  206.1 5.6 %convert_add_fusion = f32[1024,1536]{1,0:T(8,128)} fusion(bf16[1024,2304]{1,0:T(8,128)(2,1)} %collective-permute-done.32, bf16[1024,2304]{1,0:T(8,128)(2,1)S(1)} %copy-done), kind=kLoop, calls=%fused_computation | loop fusion | flops 4718592 | bytes 12582912 | tf_op jit(solution)/shard_map/add | solution.py:382
  211.7 3.4 %convert_add_fusion.1 = f32[1024,768]{1,0:T(8,128)} fusion(bf16[1024,2304]{1,0:T(8,128)(2,1)} %collective-permute-done.32, bf16[1024,2304]{1,0:T(8,128)(2,1)S(1)} %copy-done), kind=kLoop, calls=%fused_computation.1 | loop fusion | flops 2359296 | bytes 6291456 | tf_op jit(solution)/shard_map/add | solution.py:382
  216.4 3.4 %combine_dx.1 = bf16[256,2048]{1,0:T(8,128)(2,1)} custom-call(s32[2]{0:T(128)} %pad_add_fusion.where_ref, bf16[256,512]{1,0:T(8,128)(2,1)} %bitcast.16, bf16[32,2048]{1,0:T(8,128)(2,1)} %get-tuple-element.198.refs_0_, bf16[32,2048]{1,0:T(8,128)(2,1)} %copy-done.6, bf16[32,2048]{1,0:T(8,128)(2,1)} %copy-done.7, bf16[32,2048]{1,0:T(8,128)(2,1)} %copy-done.8, ...), custom_call_target="tpu_custom_call" | custom-call | flops 1 | bytes 1 | tf_op jit(solution)/shard_map/combine_dx/pallas_call | solution.py:339
  (121 shorter events, 22.1 us)
Async XLA Ops:
  4.7 94.7 %all-to-all-start = ((bf16[16,32,2048]{2,1,0:T(8,128)(2,1)}), bf16[16,32,2048]{2,1,0:T(8,128)(2,1)S(1)}, u32[]{:S(2)}, u32[]{:S(2)}) async-start(bf16[16,32,2048]{2,1,0:T(8,128)(2,1)} %get-tuple-element.154), calls=%async_computation | async-start | bytes 4194304 | tf_op jit(solution)/shard_map/all_to_all | solution.py:55
  21.2 30.0 %collective-permute-start.6 = (bf16[32,2048]{1,0:T(8,128)(2,1)}, bf16[32,2048]{1,0:T(8,128)(2,1)S(1)}, u32[]{:S(2)}, u32[]{:S(2)}) collective-permute-start(bf16[32,2048]{1,0:T(8,128)(2,1)} %get-tuple-element.123), channel_id=1, source_target_pairs={{0,10},{2,8},{4,14},{6,12},{8,2},{10,0},{12,6},{14,4},{16,26},{18,... | collective-permute-start | bytes 393224 | tf_op jit(solution)/shard_map/ppermute | solution.py:60
  24.1 33.5 %collective-permute-start.5 = (bf16[32,2048]{1,0:T(8,128)(2,1)}, bf16[32,2048]{1,0:T(8,128)(2,1)S(1)}, u32[]{:S(2)}, u32[]{:S(2)}) collective-permute-start(bf16[32,2048]{1,0:T(8,128)(2,1)} %get-tuple-element.121), channel_id=1, source_target_pairs={{0,8},{2,10},{4,12},{6,14},{8,0},{10,2},{12,4},{14,6},{16,24},{18,... | collective-permute-start | bytes 393224 | tf_op jit(solution)/shard_map/ppermute | solution.py:60
  24.6 33.7 %collective-permute-start.4 = (bf16[32,2048]{1,0:T(8,128)(2,1)}, bf16[32,2048]{1,0:T(8,128)(2,1)S(1)}, u32[]{:S(2)}, u32[]{:S(2)}) collective-permute-start(bf16[32,2048]{1,0:T(8,128)(2,1)} %get-tuple-element.119), channel_id=1, source_target_pairs={{0,6},{2,4},{4,2},{6,0},{8,14},{10,12},{12,10},{14,8},{16,22},{18,... | collective-permute-start | bytes 393224 | tf_op jit(solution)/shard_map/ppermute | solution.py:60
  27.0 49.7 %collective-permute-start.3 = (bf16[32,2048]{1,0:T(8,128)(2,1)}, bf16[32,2048]{1,0:T(8,128)(2,1)S(1)}, u32[]{:S(2)}, u32[]{:S(2)}) collective-permute-start(bf16[32,2048]{1,0:T(8,128)(2,1)} %get-tuple-element.117), channel_id=1, source_target_pairs={{0,4},{2,6},{4,0},{6,2},{8,12},{10,14},{12,8},{14,10},{16,20},{18,... | collective-permute-start | bytes 393224 | tf_op jit(solution)/shard_map/ppermute | solution.py:60
  27.0 50.7 %collective-permute-start.2 = (bf16[32,2048]{1,0:T(8,128)(2,1)}, bf16[32,2048]{1,0:T(8,128)(2,1)S(1)}, u32[]{:S(2)}, u32[]{:S(2)}) collective-permute-start(bf16[32,2048]{1,0:T(8,128)(2,1)} %get-tuple-element.115), channel_id=1, source_target_pairs={{0,2},{2,0},{4,6},{6,4},{8,10},{10,8},{12,14},{14,12},{16,18},{18,... | collective-permute-start | bytes 393224 | tf_op jit(solution)/shard_map/ppermute | solution.py:60
  51.2 28.8 %collective-permute-start.11 = (bf16[32,2048]{1,0:T(8,128)(2,1)}, bf16[32,2048]{1,0:T(8,128)(2,1)S(1)}, u32[]{:S(2)}, u32[]{:S(2)}) collective-permute-start(bf16[32,2048]{1,0:T(8,128)(2,1)} %get-tuple-element.138), channel_id=1, source_target_pairs={{0,20},{2,22},{4,16},{6,18},{8,28},{10,30},{12,24},{14,26},{16,4},... | collective-permute-start | bytes 393224 | tf_op jit(solution)/shard_map/ppermute | solution.py:60
  57.6 24.5 %collective-permute-start.10 = (bf16[32,2048]{1,0:T(8,128)(2,1)}, bf16[32,2048]{1,0:T(8,128)(2,1)S(1)}, u32[]{:S(2)}, u32[]{:S(2)}) collective-permute-start(bf16[32,2048]{1,0:T(8,128)(2,1)} %get-tuple-element.135), channel_id=1, source_target_pairs={{0,18},{2,16},{4,22},{6,20},{8,26},{10,24},{12,30},{14,28},{16,2},... | collective-permute-start | bytes 393224 | tf_op jit(solution)/shard_map/ppermute | solution.py:60
  58.3 27.0 %collective-permute-start.9 = (bf16[32,2048]{1,0:T(8,128)(2,1)}, bf16[32,2048]{1,0:T(8,128)(2,1)S(1)}, u32[]{:S(2)}, u32[]{:S(2)}) collective-permute-start(bf16[32,2048]{1,0:T(8,128)(2,1)} %get-tuple-element.132), channel_id=1, source_target_pairs={{0,16},{2,18},{4,20},{6,22},{8,24},{10,26},{12,28},{14,30},{16,0},... | collective-permute-start | bytes 393224 | tf_op jit(solution)/shard_map/ppermute | solution.py:60
  76.7 10.5 %collective-permute-start.8 = (bf16[32,2048]{1,0:T(8,128)(2,1)}, bf16[32,2048]{1,0:T(8,128)(2,1)S(1)}, u32[]{:S(2)}, u32[]{:S(2)}) collective-permute-start(bf16[32,2048]{1,0:T(8,128)(2,1)} %get-tuple-element.129), channel_id=1, source_target_pairs={{0,14},{2,12},{4,10},{6,8},{8,6},{10,4},{12,2},{14,0},{16,30},{18,... | collective-permute-start | bytes 393224 | tf_op jit(solution)/shard_map/ppermute | solution.py:60
  77.7 19.2 %collective-permute-start.7 = (bf16[32,2048]{1,0:T(8,128)(2,1)}, bf16[32,2048]{1,0:T(8,128)(2,1)S(1)}, u32[]{:S(2)}, u32[]{:S(2)}) collective-permute-start(bf16[32,2048]{1,0:T(8,128)(2,1)} %get-tuple-element.126), channel_id=1, source_target_pairs={{0,12},{2,14},{4,8},{6,10},{8,4},{10,6},{12,0},{14,2},{16,28},{18,... | collective-permute-start | bytes 393224 | tf_op jit(solution)/shard_map/ppermute | solution.py:60
  80.0 32.0 %collective-permute-start.16 = (bf16[32,2048]{1,0:T(8,128)(2,1)}, bf16[32,2048]{1,0:T(8,128)(2,1)S(1)}, u32[]{:S(2)}, u32[]{:S(2)}) collective-permute-start(bf16[32,2048]{1,0:T(8,128)(2,1)} %get-tuple-element.153), channel_id=1, source_target_pairs={{0,30},{2,28},{4,26},{6,24},{8,22},{10,20},{12,18},{14,16},{16,14}... | collective-permute-start | bytes 393224 | tf_op jit(solution)/shard_map/ppermute | solution.py:60
  82.1 29.9 %collective-permute-start.15 = (bf16[32,2048]{1,0:T(8,128)(2,1)}, bf16[32,2048]{1,0:T(8,128)(2,1)}, u32[]{:S(2)}, u32[]{:S(2)}) collective-permute-start(bf16[32,2048]{1,0:T(8,128)(2,1)} %get-tuple-element.150), channel_id=1, source_target_pairs={{0,28},{2,30},{4,24},{6,26},{8,20},{10,22},{12,16},{14,18},{16,12}... | collective-permute-start | bytes 393224 | tf_op jit(solution)/shard_map/ppermute | solution.py:60
  85.2 26.8 %collective-permute-start.14 = (bf16[32,2048]{1,0:T(8,128)(2,1)}, bf16[32,2048]{1,0:T(8,128)(2,1)}, u32[]{:S(2)}, u32[]{:S(2)}) collective-permute-start(bf16[32,2048]{1,0:T(8,128)(2,1)} %get-tuple-element.147), channel_id=1, source_target_pairs={{0,26},{2,24},{4,30},{6,28},{8,18},{10,16},{12,22},{14,20},{16,10}... | collective-permute-start | bytes 393224 | tf_op jit(solution)/shard_map/ppermute | solution.py:60
  87.2 24.9 %collective-permute-start.13 = (bf16[32,2048]{1,0:T(8,128)(2,1)}, bf16[32,2048]{1,0:T(8,128)(2,1)}, u32[]{:S(2)}, u32[]{:S(2)}) collective-permute-start(bf16[32,2048]{1,0:T(8,128)(2,1)} %get-tuple-element.144), channel_id=1, source_target_pairs={{0,24},{2,26},{4,28},{6,30},{8,16},{10,18},{12,20},{14,22},{16,8},... | collective-permute-start | bytes 393224 | tf_op jit(solution)/shard_map/ppermute | solution.py:60
  96.9 15.1 %collective-permute-start.12 = (bf16[32,2048]{1,0:T(8,128)(2,1)}, bf16[32,2048]{1,0:T(8,128)(2,1)}, u32[]{:S(2)}, u32[]{:S(2)}) collective-permute-start(bf16[32,2048]{1,0:T(8,128)(2,1)} %get-tuple-element.141), channel_id=1, source_target_pairs={{0,22},{2,20},{4,18},{6,16},{8,30},{10,28},{12,26},{14,24},{16,6},... | collective-permute-start | bytes 393224 | tf_op jit(solution)/shard_map/ppermute | solution.py:60
  112.8 52.5 %all-to-all-start.1 = ((bf16[16,32,2048]{2,1,0:T(8,128)(2,1)}), bf16[16,32,2048]{2,1,0:T(8,128)(2,1)S(1)}, u32[]{:S(2)}, u32[]{:S(2)}) async-start(bf16[16,32,2048]{2,1,0:T(8,128)(2,1)} %get-tuple-element.165), calls=%async_computation.1 | async-start | bytes 4194304 | tf_op jit(solution)/shard_map/all_to_all | solution.py:55
  165.2 38.9 %collective-permute-start.32 = (bf16[1024,2304]{1,0:T(8,128)(2,1)}, bf16[1024,2304]{1,0:T(8,128)(2,1)}, u32[]{:S(2)}, u32[]{:S(2)}) collective-permute-start(bf16[1024,2304]{1,0:T(8,128)(2,1)} %weight_grads.2), channel_id=1, source_target_pairs={{0,1},{1,0},{2,3},{3,2},{4,5},{5,4},{6,7},{7,6},{8,9},{9,8},{10,11... | collective-permute-start | bytes 14155784 | tf_op jit(solution)/shard_map/ppermute | solution.py:51
  165.3 13.2 %collective-permute-start.18 = (bf16[32,2048]{1,0:T(8,128)(2,1)S(1)}, bf16[32,2048]{1,0:T(8,128)(2,1)S(1)}, u32[]{:S(2)}, u32[]{:S(2)}) collective-permute-start(bf16[32,2048]{1,0:T(8,128)(2,1)S(1)} %copy-done.32), channel_id=1, source_target_pairs={{0,4},{2,6},{4,0},{6,2},{8,12},{10,14},{12,8},{14,10},{16,20},{18,... | collective-permute-start | bytes 393224 | tf_op jit(solution)/shard_map/ppermute | solution.py:60
  165.9 13.7 %collective-permute-start.19 = (bf16[32,2048]{1,0:T(8,128)(2,1)}, bf16[32,2048]{1,0:T(8,128)(2,1)S(1)}, u32[]{:S(2)}, u32[]{:S(2)}) collective-permute-start(bf16[32,2048]{1,0:T(8,128)(2,1)} %get-tuple-element.160), channel_id=1, source_target_pairs={{0,6},{2,4},{4,2},{6,0},{8,14},{10,12},{12,10},{14,8},{16,22},{18,... | collective-permute-start | bytes 393224 | tf_op jit(solution)/shard_map/ppermute | solution.py:60
  169.7 11.5 %collective-permute-start.20 = (bf16[32,2048]{1,0:T(8,128)(2,1)}, bf16[32,2048]{1,0:T(8,128)(2,1)}, u32[]{:S(2)}, u32[]{:S(2)}) collective-permute-start(bf16[32,2048]{1,0:T(8,128)(2,1)} %get-tuple-element.161), channel_id=1, source_target_pairs={{0,8},{2,10},{4,12},{6,14},{8,0},{10,2},{12,4},{14,6},{16,24},{18,... | collective-permute-start | bytes 393224 | tf_op jit(solution)/shard_map/ppermute | solution.py:60
  172.3 9.4 %collective-permute-start.21 = (bf16[32,2048]{1,0:T(8,128)(2,1)}, bf16[32,2048]{1,0:T(8,128)(2,1)}, u32[]{:S(2)}, u32[]{:S(2)}) collective-permute-start(bf16[32,2048]{1,0:T(8,128)(2,1)} %get-tuple-element.162), channel_id=1, source_target_pairs={{0,10},{2,8},{4,14},{6,12},{8,2},{10,0},{12,6},{14,4},{16,26},{18,... | collective-permute-start | bytes 393224 | tf_op jit(solution)/shard_map/ppermute | solution.py:60
  178.5 11.4 %collective-permute-start.22 = (bf16[32,2048]{1,0:T(8,128)(2,1)}, bf16[32,2048]{1,0:T(8,128)(2,1)}, u32[]{:S(2)}, u32[]{:S(2)}) collective-permute-start(bf16[32,2048]{1,0:T(8,128)(2,1)} %get-tuple-element.166), channel_id=1, source_target_pairs={{0,12},{2,14},{4,8},{6,10},{8,4},{10,6},{12,0},{14,2},{16,28},{18,... | collective-permute-start | bytes 393224 | tf_op jit(solution)/shard_map/ppermute | solution.py:60
  179.7 16.0 %collective-permute-start.23 = (bf16[32,2048]{1,0:T(8,128)(2,1)}, bf16[32,2048]{1,0:T(8,128)(2,1)S(1)}, u32[]{:S(2)}, u32[]{:S(2)}) collective-permute-start(bf16[32,2048]{1,0:T(8,128)(2,1)} %get-tuple-element.168), channel_id=1, source_target_pairs={{0,14},{2,12},{4,10},{6,8},{8,6},{10,4},{12,2},{14,0},{16,30},{18,... | collective-permute-start | bytes 393224 | tf_op jit(solution)/shard_map/ppermute | solution.py:60
  181.2 16.3 %collective-permute-start.24 = (bf16[32,2048]{1,0:T(8,128)(2,1)}, bf16[32,2048]{1,0:T(8,128)(2,1)S(1)}, u32[]{:S(2)}, u32[]{:S(2)}) collective-permute-start(bf16[32,2048]{1,0:T(8,128)(2,1)} %get-tuple-element.170), channel_id=1, source_target_pairs={{0,16},{2,18},{4,20},{6,22},{8,24},{10,26},{12,28},{14,30},{16,0},... | collective-permute-start | bytes 393224 | tf_op jit(solution)/shard_map/ppermute | solution.py:60
  181.7 17.8 %collective-permute-start.25 = (bf16[32,2048]{1,0:T(8,128)(2,1)}, bf16[32,2048]{1,0:T(8,128)(2,1)S(1)}, u32[]{:S(2)}, u32[]{:S(2)}) collective-permute-start(bf16[32,2048]{1,0:T(8,128)(2,1)} %get-tuple-element.172), channel_id=1, source_target_pairs={{0,18},{2,16},{4,22},{6,20},{8,26},{10,24},{12,30},{14,28},{16,2},... | collective-permute-start | bytes 393224 | tf_op jit(solution)/shard_map/ppermute | solution.py:60
  189.9 12.6 %collective-permute-start.26 = (bf16[32,2048]{1,0:T(8,128)(2,1)}, bf16[32,2048]{1,0:T(8,128)(2,1)S(1)}, u32[]{:S(2)}, u32[]{:S(2)}) collective-permute-start(bf16[32,2048]{1,0:T(8,128)(2,1)} %get-tuple-element.174), channel_id=1, source_target_pairs={{0,20},{2,22},{4,16},{6,18},{8,28},{10,30},{12,24},{14,26},{16,4},... | collective-permute-start | bytes 393224 | tf_op jit(solution)/shard_map/ppermute | solution.py:60
  195.7 19.4 %collective-permute-start.27 = (bf16[32,2048]{1,0:T(8,128)(2,1)}, bf16[32,2048]{1,0:T(8,128)(2,1)S(1)}, u32[]{:S(2)}, u32[]{:S(2)}) collective-permute-start(bf16[32,2048]{1,0:T(8,128)(2,1)} %get-tuple-element.176), channel_id=1, source_target_pairs={{0,22},{2,20},{4,18},{6,16},{8,30},{10,28},{12,26},{14,24},{16,6},... | collective-permute-start | bytes 393224 | tf_op jit(solution)/shard_map/ppermute | solution.py:60
  197.5 17.6 %collective-permute-start.28 = (bf16[32,2048]{1,0:T(8,128)(2,1)}, bf16[32,2048]{1,0:T(8,128)(2,1)S(1)}, u32[]{:S(2)}, u32[]{:S(2)}) collective-permute-start(bf16[32,2048]{1,0:T(8,128)(2,1)} %get-tuple-element.178), channel_id=1, source_target_pairs={{0,24},{2,26},{4,28},{6,30},{8,16},{10,18},{12,20},{14,22},{16,8},... | collective-permute-start | bytes 393224 | tf_op jit(solution)/shard_map/ppermute | solution.py:60
  199.5 15.6 %collective-permute-start.29 = (bf16[32,2048]{1,0:T(8,128)(2,1)}, bf16[32,2048]{1,0:T(8,128)(2,1)S(1)}, u32[]{:S(2)}, u32[]{:S(2)}) collective-permute-start(bf16[32,2048]{1,0:T(8,128)(2,1)} %get-tuple-element.180), channel_id=1, source_target_pairs={{0,26},{2,24},{4,30},{6,28},{8,18},{10,16},{12,22},{14,20},{16,10}... | collective-permute-start | bytes 393224 | tf_op jit(solution)/shard_map/ppermute | solution.py:60
  202.5 13.2 %collective-permute-start.30 = (bf16[32,2048]{1,0:T(8,128)(2,1)}, bf16[32,2048]{1,0:T(8,128)(2,1)S(1)}, u32[]{:S(2)}, u32[]{:S(2)}) collective-permute-start(bf16[32,2048]{1,0:T(8,128)(2,1)} %get-tuple-element.182), channel_id=1, source_target_pairs={{0,28},{2,30},{4,24},{6,26},{8,20},{10,22},{12,16},{14,18},{16,12}... | collective-permute-start | bytes 393224 | tf_op jit(solution)/shard_map/ppermute | solution.py:60
  204.1 11.6 %collective-permute-start.31 = (bf16[32,2048]{1,0:T(8,128)(2,1)S(1)}, bf16[32,2048]{1,0:T(8,128)(2,1)S(1)}, u32[]{:S(2)}, u32[]{:S(2)}) collective-permute-start(bf16[32,2048]{1,0:T(8,128)(2,1)S(1)} %copy-done.20), channel_id=1, source_target_pairs={{0,30},{2,28},{4,26},{6,24},{8,22},{10,20},{12,18},{14,16},{16,14}... | collective-permute-start | bytes 393224 | tf_op jit(solution)/shard_map/ppermute | solution.py:60
  (37 other events, 930.1 us)
